TPU v7x, 32 devices: a whole 2x2x4 slice. The times are simulated.
32 devices in a mesh: parts: 2 (over y), pool: 4 (over z), tp: 2 (over x), sub: 2 (over core).
Axes of the slice: x: 2, y: 2, z: 4, core: 2. Of those that a mesh axis runs over, the one named last changes fastest.
Arguments:
- deltas: bfloat16 [32, 2, 512, 1024], P(('parts', 'pool'), None, 'sub', 'tp'), parts along dimension 0, may hold values from -6 to 6
- anchors: bfloat16 [32, 2, 32, 1024], P(('parts', 'pool'), None, 'sub', 'tp'), parts along dimension 0, may hold values from -6 to 6
- chan_scale: bfloat16 [32, 2, 1024], P(('parts', 'pool'), None, 'tp'), parts along dimension 0, may hold values from 0.049804688 to 0.5
- lengths: int32 [32], P(('parts', 'pool')), parts along dimension 0, may hold values from 128 to 512, as said below
- route: int32 [32], P(('parts', 'pool')), parts along dimension 0, may hold values from 0 to 3, as said below
- new_query: bfloat16 [32, 4, 8192], P(('parts', 'pool'), None, ('tp', 'sub')), parts along dimension 0, may hold values from -32 to 32
- new_kv: bfloat16 [32, 2, 4, 1024], P(('parts', 'pool'), None, None, 'tp'), parts along dimension 0, may hold values from -8 to 8
Outputs:
- cache: bfloat16 [32, 2, 512, 1024], P(('parts', 'pool'), None, 'sub', 'tp'), parts along dimension 0
- attended: bfloat16 [32, 4, 8192], P(('parts', 'pool'), None, ('tp', 'sub')), parts along dimension 0
There are 2 independent parts, one for each index of `parts`. A program takes and returns all parts, laid end to end along the dimension named above; each array names one. Nothing has to cross between parts.
Inputs may be any that keep to these rules, and one draw needn't show every extreme that they name: `lengths`: multiples of 128; every draw holds a request of length 512. `route`: each prefill index sends exactly 1 of its requests to every decode group.
All inputs are finite; a program needn't handle non-finite values.
Results may differ from a plain program's by a relative error of at most 0.003.
Values may be sent and summed in bfloat16 or wider, within the bound.
No kernel may reach another device: no remote copies, remote signals or barrier semaphores. Data moves between devices by JAX's collectives and lax.ppermute only.
A program may use at most 64 MiB of HBM per device.

v0:
```python
import math

import jax
import jax.numpy as jnp
from jax import lax
from jax.sharding import PartitionSpec as P

HEAD_DIM = 128
Q_PER_KV = 8


def rebuild(delta, anchor, scale, length, offset):
    span = delta.shape[2]
    repeat = span // anchor.shape[2]
    full = jnp.repeat(anchor.astype(jnp.float32), repeat, axis=2)
    value = full + scale.astype(jnp.float32)[:, :, None, :] * delta.astype(jnp.float32)
    position = offset + jnp.arange(span, dtype=jnp.int32)
    keep = position[None, :] < length[:, None]
    value = jnp.where(keep[:, None, :, None], value, jnp.float32(0.0))
    return value.astype(jnp.bfloat16)


def body(deltas, anchors, chan_scale, lengths, route, new_query, new_kv):
    groups = lax.axis_size("pool")
    count = route.shape[0]
    slots_each = count // groups
    local = jnp.arange(count, dtype=jnp.int32)
    earlier = (route[:, None] == route[None, :]) & (local[None, :] < local[:, None])
    rank = jnp.sum(earlier.astype(jnp.int32), axis=1)
    place = route * slots_each + rank
    order = jnp.sum(jnp.where(place[None, :] == local[:, None], local[None, :], 0), axis=1)
    span = deltas.shape[2]
    sub_index = lax.axis_index("sub")
    offset = sub_index * span
    sent_len = jnp.take(lengths, order, axis=0)
    sent_delta = jnp.take(deltas, order, axis=0)
    sent_anchor = jnp.take(anchors, order, axis=0)
    sent_scale = jnp.take(chan_scale, order, axis=0)
    moved = (
        lax.all_to_all(sent_delta, "pool", split_axis=0, concat_axis=0, tiled=True),
        lax.all_to_all(sent_anchor, "pool", split_axis=0, concat_axis=0, tiled=True),
        lax.all_to_all(sent_scale, "pool", split_axis=0, concat_axis=0, tiled=True),
        lax.all_to_all(sent_len, "pool", split_axis=0, concat_axis=0, tiled=True),
    )
    got_len = moved[3]
    cache = rebuild(moved[0], moved[1], moved[2], got_len, offset)
    channels = deltas.shape[3]
    heads = channels // HEAD_DIM
    q_local = new_query.shape[2] // HEAD_DIM
    steps_now = new_query.shape[1]
    factor = 1.0 / math.sqrt(HEAD_DIM)
    steps_idx = jnp.arange(steps_now, dtype=jnp.int32)
    whole = lax.all_gather(cache, "sub", axis=2, tiled=True)
    total_len = whole.shape[2]
    first_head = sub_index * q_local
    kv_index = (first_head + jnp.arange(q_local, dtype=jnp.int32)) // Q_PER_KV
    queries = new_query.reshape(count, steps_now, q_local, HEAD_DIM)
    keys = jnp.take(whole[:, 0].reshape(count, total_len, heads, HEAD_DIM), kv_index, axis=2)
    values = jnp.take(whole[:, 1].reshape(count, total_len, heads, HEAD_DIM), kv_index, axis=2)
    new_keys = jnp.take(new_kv[:, 0].reshape(count, steps_now, heads, HEAD_DIM), kv_index, axis=2)
    new_values = jnp.take(new_kv[:, 1].reshape(count, steps_now, heads, HEAD_DIM), kv_index, axis=2)
    old_scores = (
        jnp.einsum("rtqd,rsqd->rqts", queries, keys, preferred_element_type=jnp.float32) * factor
    )
    new_scores = (
        jnp.einsum("rtqd,ruqd->rqtu", queries, new_keys, preferred_element_type=jnp.float32)
        * factor
    )
    position = jnp.arange(total_len, dtype=jnp.int32)
    live = (position[None, :] < got_len[:, None])[:, None, None, :]
    causal = (steps_idx[None, :] <= steps_idx[:, None])[None, None, :, :]
    old_scores = jnp.where(live, old_scores, jnp.float32(-1e30))
    new_scores = jnp.where(causal, new_scores, jnp.float32(-1e30))
    top = jnp.maximum(jnp.max(old_scores, axis=-1), jnp.max(new_scores, axis=-1))
    old_weights = jnp.where(live, jnp.exp(old_scores - top[..., None]), jnp.float32(0.0))
    new_weights = jnp.where(causal, jnp.exp(new_scores - top[..., None]), jnp.float32(0.0))
    total = jnp.sum(old_weights, axis=-1) + jnp.sum(new_weights, axis=-1)
    summed = jnp.einsum(
        "rqts,rsqd->rqtd",
        old_weights.astype(jnp.bfloat16),
        values,
        preferred_element_type=jnp.float32,
    )
    summed = summed + jnp.einsum(
        "rqtu,ruqd->rqtd",
        new_weights.astype(jnp.bfloat16),
        new_values,
        preferred_element_type=jnp.float32,
    )
    result = summed / total[..., None]
    result = jnp.transpose(result, (0, 2, 1, 3)).reshape(count, steps_now, q_local * HEAD_DIM)
    return (cache, result.astype(jnp.bfloat16))


def solution(mesh):
    placed = (
        P(("parts", "pool"), None, "sub", "tp"),
        P(("parts", "pool"), None, "sub", "tp"),
        P(("parts", "pool"), None, "tp"),
        P(("parts", "pool")),
        P(("parts", "pool")),
        P(("parts", "pool"), None, ("tp", "sub")),
        P(("parts", "pool"), None, None, "tp"),
    )
    return jax.shard_map(
        body,
        mesh=mesh,
        in_specs=placed,
        out_specs=(
            P(("parts", "pool"), None, "sub", "tp"),
            P(("parts", "pool"), None, ("tp", "sub")),
        ),
        check_vma=False,
    )
```

profile of v0, /device:TPU:9, one launch (start us, length us, event | category | flops | bytes accessed | tf_op | source)
XLA Modules:
  0.0 163.1 jit_solution(5580487669293208105)
XLA Ops:
  7.2 0.0 copy-start
  7.2 1.0 convert_reduce_fusion
  8.2 0.7 add.79
  8.8 0.1 select_reduce_fusion
  9.0 1.3 gather_fusion
  10.3 0.7 copy.76
  10.9 4.8 %all-to-all-start = ((s32[4,1,1]{2,1,0:T(1,128)}), s32[4,1,1]{2,1,0:T(1,128)S(1)}, u32[]{:S(2)}, u32[]{:S(2)}) async-start(s32[4,1,1]{2,1,0:T(1,128)} %copy.76), calls=%async_computation | async-start | bytes 4096 | tf_op jit(solution)/shard_map/all_to_all | solution.py:43
  15.7 1.5 gather_fusion.1
  17.2 1.3 gather_fusion.2
  18.5 0.7 broadcast_select_fusion.2
  19.1 0.0 all-to-all-done
  19.1 4.5 %all-to-all-start.2 = ((bf16[4,2,512]{2,1,0:T(2,128)(2,1)}), bf16[4,2,512]{2,1,0:T(2,128)(2,1)S(1)}, u32[]{:S(2)}, u32[]{:S(2)}) async-start(bf16[4,2,512]{2,1,0:T(2,128)(2,1)} %broadcast_select_fusion.2), calls=%async_computation.2 | async-start | bytes 16384 | tf_op jit(solution)/shard_map/all_to_all | solution.py:42
  23.7 0.7 broadcast_select_fusion.1
  24.4 0.0 copy-done
  24.4 2.0 %gather_fusion.3 = bf16[4,2,256,512]{3,2,1,0:T(8,128)(2,1)} fusion(bf16[4,2,256,512]{3,2,1,0:T(8,128)(2,1)S(1)} %copy-done, s32[1024]{0:T(1024)S(1)} %pad_clamp_fusion.1), kind=kCustom, calls=%fused_computation.7 | custom fusion | bytes 4194320 | tf_op jit(solution)/shard_map/jit(_take)/gather | solution.py:36
  26.4 0.6 all-to-all-done.2
  27.0 4.4 %all-to-all-start.1 = ((bf16[4,2,16,512]{3,2,1,0:T(8,128)(2,1)}), bf16[4,2,16,512]{3,2,1,0:T(8,128)(2,1)S(1)}, u32[]{:S(2)}, u32[]{:S(2)}) async-start(bf16[4,2,16,512]{3,2,1,0:T(8,128)(2,1)} %broadcast_select_fusion.1), calls=%async_computation.1 | async-start | bytes 262144 | tf_op jit(solution)/shard_map/all_to_all | solution.py:41
  31.4 3.2 %broadcast_select_fusion = bf16[4,2,256,512]{3,2,1,0:T(8,128)(2,1)} fusion(bf16[4,2,256,512]{3,2,1,0:T(8,128)(2,1)} %gather_fusion.3, pred[4]{0:T(512)(128)(4,1)S(1)} %compare_and_fusion.1), kind=kLoop, calls=%fused_computation.17 | loop fusion | flops 1048576 | bytes 4194308 | tf_op jit(solution)/shard_map/jit(_take)/select_n | solution.py:36
  34.6 1.1 all-to-all-done.1
  35.7 4.9 %all-to-all-start.3 = ((bf16[4,2,256,512]{3,2,1,0:T(8,128)(2,1)}), bf16[4,2,256,512]{3,2,1,0:T(8,128)(2,1)}, u32[]{:S(2)}, u32[]{:S(2)}) async-start(bf16[4,2,256,512]{3,2,1,0:T(8,128)(2,1)} %broadcast_select_fusion), calls=%async_computation.3 | async-start | bytes 4194304 | tf_op jit(solution)/shard_map/all_to_all | solution.py:40
  40.6 0.0 copy-start.2
  40.6 0.0 copy-start.1
  40.6 0.0 all-gather.2.cloned.1.call-start
  40.6 0.2 reduce
  40.8 0.1 broadcast_compare_fusion
  40.9 41.0 %all-to-all-done.3 = bf16[4,2,256,512]{3,2,1,0:T(8,128)(2,1)} async-done(((bf16[4,2,256,512]{3,2,1,0:T(8,128)(2,1)}), bf16[4,2,256,512]{3,2,1,0:T(8,128)(2,1)}, u32[]{:S(2)}, u32[]{:S(2)}) %all-to-all-start.3) | async-done | bytes 2097184 | tf_op jit(solution)/shard_map/all_to_all | solution.py:40
  81.8 3.6 %fusion.5 = bf16[4,2,256,512]{3,2,1,0:T(8,128)(2,1)} fusion(bf16[4,2,256,512]{3,2,1,0:T(8,128)(2,1)} %all-to-all-done.3, f32[4,2,512]{2,1,0:T(2,128)S(1)} %convert_element_type.29, f32[4,2,16,512]{3,2,1,0:T(8,128)S(1)} %convert_element_type.28, pred[4,256]{1,0:T(4,128)(4,1)S(1)} %broadcast_compare_fusion), kind=kLoop, calls=%fused_computation.16 | loop fusion | flops 5242880 | bytes 4473856 | tf_op jit(solution)/shard_map/convert_element_type | solution.py:20
  85.4 0.0 all-gather.2.cloned.1.call-update
  85.5 0.0 copy-done.2
  85.5 0.6 gather_fusion.7
  86.1 0.6 gather_fusion.5
  86.8 0.1 select_bitcast_fusion.2
  86.9 0.0 copy-done.1
  86.9 0.2 fusion.25
  87.1 0.2 copy.82
  87.3 0.1 fusion.30
  87.4 0.1 copy.83
  87.5 0.1 iota_compare_fusion
  87.6 18.6 %all-gather.2.cloned.1.call-done = bf16[4,2,512,512]{3,2,1,0:T(8,128)(2,1)} async-done(((bf16[4,2,256,512]{3,2,1,0:T(8,128)(2,1)}), bf16[4,2,512,512]{3,2,1,0:T(8,128)(2,1)}) %all-gather.2.cloned.1.call-update) | async-done | bytes 4194320 | tf_op jit(solution)/shard_map/all_gather | solution.py:53
  106.2 4.6 %fusion.36 = (bf16[4,1,512,512]{3,2,1,0:T(8,128)(2,1)}, bf16[4,1,512,512]{3,2,1,0:T(8,128)(2,1)}) fusion(bf16[4,2,512,512]{3,2,1,0:T(8,128)(2,1)} %all-gather.2.cloned.1.call-done), kind=kLoop, calls=%fused_computation.73 | loop fusion | bytes 8388608 | tf_op jit(solution)/shard_map/slice | solution.py:58
  110.8 4.0 %reshape_squeeze.14 = bf16[4,512,4,128]{3,2,1,0:T(4,128)(2,1)} reshape(bf16[4,1,512,512]{3,2,1,0:T(8,128)(2,1)} %get-tuple-element.5) | data formatting | bytes 4194304 | tf_op jit(solution)/shard_map/reshape;squeeze | solution.py:59
  114.8 3.3 %copy.84 = bf16[4,512,4,128]{3,1,2,0:T(8,128)(2,1)} copy(bf16[4,512,4,128]{3,2,1,0:T(4,128)(2,1)} %reshape_squeeze.14) | data formatting | bytes 4194304 | tf_op jit(solution)/shard_map/reshape;squeeze | solution.py:59
  118.1 6.4 %gather_fusion.6 = bf16[16,4,512,128]{3,2,1,0:T(8,128)(2,1)} fusion(bf16[4,512,4,128]{3,1,2,0:T(8,128)(2,1)} %copy.84, s32[1024]{0:T(1024)S(1)} %pad_clamp_fusion), kind=kCustom, calls=%fused_computation.2.clone | custom fusion | bytes 16777280 | tf_op jit(solution)/shard_map/jit(_take)/gather | solution.py:59
  124.4 4.0 %reshape_squeeze.12 = bf16[4,512,4,128]{3,2,1,0:T(4,128)(2,1)} reshape(bf16[4,1,512,512]{3,2,1,0:T(8,128)(2,1)} %get-tuple-element.4) | data formatting | bytes 4194304 | tf_op jit(solution)/shard_map/reshape;squeeze | solution.py:58
  128.4 3.4 %copy.77 = bf16[4,512,4,128]{3,1,2,0:T(8,128)(2,1)} copy(bf16[4,512,4,128]{3,2,1,0:T(4,128)(2,1)} %reshape_squeeze.12) | data formatting | bytes 4194304 | tf_op jit(solution)/shard_map/reshape;squeeze | solution.py:58
  131.8 6.3 %gather_fusion.4 = bf16[16,4,512,128]{3,2,1,0:T(8,128)(2,1)} fusion(bf16[4,512,4,128]{3,1,2,0:T(8,128)(2,1)} %copy.77, s32[1024]{0:T(1024)S(1)} %pad_clamp_fusion), kind=kCustom, calls=%fused_computation.clone | custom fusion | bytes 16777280 | tf_op jit(solution)/shard_map/jit(_take)/gather | solution.py:58
  138.1 9.4 %select_bitcast_fusion.1 = (bf16[4,512,16,128]{3,1,0,2:T(8,128)(2,1)S(1)}, bf16[4,512,16,128]{3,1,0,2:T(8,128)(2,1)}) fusion(bf16[16,4,512,128]{3,2,1,0:T(8,128)(2,1)} %gather_fusion.4, pred[16]{0:T(512)(128)(4,1)S(1)} %compare_and_fusion, bf16[16,4,512,128]{3,2,1,0:T(8,128)(2,1)} %gather_fusion.6), kind=kLoop, calls=%fused_computation.13 | loop fusion | flops 8388608 | bytes 33554448 | tf_op jit(solution)/shard_map/jit(_take)/select_n | solution.py:58
  147.5 2.3 %fusion.37 = (f32[4,16,4]{2,1,0:T(8,128)S(1)}, f32[4,16,4,512]{3,2,1,0:T(4,128)S(1)}) fusion(bf16[4,4,2048]{2,1,0:T(4,128)(2,1)S(1)} %copy-done.1, bf16[4,512,16,128]{3,1,0,2:T(8,128)(2,1)S(1)} %get-tuple-element.12, pred[4,512]{1,0:T(4,128)(4,1)S(1)} %iota_compare_fusion), kind=kOutput, calls=%fused_computation.74 | convolution fusion | flops 33947392 | bytes 8981504 | tf_op jit(solution)/shard_map/rtqd,rsqd->rqts/dot_general | solution.py:63
  149.9 0.1 copy.86
  150.0 0.4 fusion.19
  150.4 0.1 fusion.31
  150.5 0.1 copy.89
  150.6 0.2 copy.87
  150.8 4.6 %fusion = f32[4,16,4,128]{3,2,1,0:T(4,128)S(1)} fusion(bf16[4,512,16,128]{3,1,0,2:T(8,128)(2,1)} %get-tuple-element.13, f32[4,16,4,512]{3,2,1,0:T(4,128)S(1)} %get-tuple-element.15, f32[4,16,4]{2,1,0:T(8,128)S(1)} %max.7, pred[4,512]{1,0:T(4,128)(4,1)S(1)} %iota_compare_fusion), kind=kOutput, calls=%fused_computation.8 | convolution fusion | flops 33947648 | bytes 9047040 | tf_op jit(solution)/shard_map/rqts,rsqd->rqtd/dot_general | solution.py:78
  155.4 0.8 fusion.12
  (14 shorter events, 0.1 us)
Async XLA Ops:
  7.2 17.2 %copy-start = (bf16[4,2,256,512]{3,2,1,0:T(8,128)(2,1)S(1)}, bf16[4,2,256,512]{3,2,1,0:T(8,128)(2,1)}, u32[]{:S(2)}) copy-start(bf16[4,2,256,512]{3,2,1,0:T(8,128)(2,1)} %param.11) | copy-start | bytes 6291460
  10.9 8.2 %all-to-all-start = ((s32[4,1,1]{2,1,0:T(1,128)}), s32[4,1,1]{2,1,0:T(1,128)S(1)}, u32[]{:S(2)}, u32[]{:S(2)}) async-start(s32[4,1,1]{2,1,0:T(1,128)} %copy.76), calls=%async_computation | async-start | bytes 4096 | tf_op jit(solution)/shard_map/all_to_all | solution.py:43
  19.1 7.8 %all-to-all-start.2 = ((bf16[4,2,512]{2,1,0:T(2,128)(2,1)}), bf16[4,2,512]{2,1,0:T(2,128)(2,1)S(1)}, u32[]{:S(2)}, u32[]{:S(2)}) async-start(bf16[4,2,512]{2,1,0:T(2,128)(2,1)} %broadcast_select_fusion.2), calls=%async_computation.2 | async-start | bytes 16384 | tf_op jit(solution)/shard_map/all_to_all | solution.py:42
  27.0 8.7 %all-to-all-start.1 = ((bf16[4,2,16,512]{3,2,1,0:T(8,128)(2,1)}), bf16[4,2,16,512]{3,2,1,0:T(8,128)(2,1)S(1)}, u32[]{:S(2)}, u32[]{:S(2)}) async-start(bf16[4,2,16,512]{3,2,1,0:T(8,128)(2,1)} %broadcast_select_fusion.1), calls=%async_computation.1 | async-start | bytes 262144 | tf_op jit(solution)/shard_map/all_to_all | solution.py:41
  35.7 46.1 %all-to-all-start.3 = ((bf16[4,2,256,512]{3,2,1,0:T(8,128)(2,1)}), bf16[4,2,256,512]{3,2,1,0:T(8,128)(2,1)}, u32[]{:S(2)}, u32[]{:S(2)}) async-start(bf16[4,2,256,512]{3,2,1,0:T(8,128)(2,1)} %broadcast_select_fusion), calls=%async_computation.3 | async-start | bytes 4194304 | tf_op jit(solution)/shard_map/all_to_all | solution.py:40
  40.6 44.9 %copy-start.2 = (bf16[4,2,4,512]{3,2,1,0:T(4,128)(2,1)S(1)}, bf16[4,2,4,512]{3,2,1,0:T(4,128)(2,1)}, u32[]{:S(2)}) copy-start(bf16[4,2,4,512]{3,2,1,0:T(4,128)(2,1)} %param.17) | copy-start | bytes 98308
  40.6 46.3 %copy-start.1 = (bf16[4,4,2048]{2,1,0:T(4,128)(2,1)S(1)}, bf16[4,4,2048]{2,1,0:T(4,128)(2,1)}, u32[]{:S(2)}) copy-start(bf16[4,4,2048]{2,1,0:T(4,128)(2,1)} %param.16) | copy-start | bytes 196612
  40.6 65.6 %all-gather.2.cloned.1.call-start = ((), (), s32[]{:S(2)}) async-start(), calls=%async_computation.4 | async-start | bytes 6291456 | tf_op jit(solution)/shard_map/all_gather | solution.py:53
Sparse Core Ops, SparseCore 0:
  85.6 20.5 all-gather.1
where the time goes:
time: 165 us; the launch traced here: 163 us
  waiting for transfers between devices  61.3 us (37%)
  local copies, waits for them, and re-layouts  40.6 us (25%)
  other arithmetic  20.5 us (12%)
  starting transfers between devices  18.6 us (11%)
  between operations  14.2 us (9%)
  matrix products  8.02 us (5%)
    all_to_all x1, waiting for transfers between devices, body(): lax.all_to_all(sent_delta, 'pool', split_axis=0, concat_axis=0, tiled=True)  41 us
    all_gather x1, waiting for transfers between devices, body(): whole = lax.all_gather(cache, 'sub', axis=2, tiled=True)  18.6 us
    select_n x2, other arithmetic, body(): jnp.take(whole[:, 0].reshape(count, total_len, heads, HEAD_DIM), kv_index...  9.42 us
    another operation x2, local copies, waits for them, and re-layouts, body(): whole[:, 0].reshape(count, total_len, heads, HEAD_DIM)  7.36 us
    another operation x2, local copies, waits for them, and re-layouts, body(): whole[:, 1].reshape(count, total_len, heads, HEAD_DIM)  7.29 us
    gather x1, local copies, waits for them, and re-layouts, body(): jnp.take(whole[:, 1].reshape(count, total_len, heads, HEAD_DIM), kv_index...  6.35 us
    gather x1, local copies, waits for them, and re-layouts, body(): jnp.take(whole[:, 0].reshape(count, total_len, heads, HEAD_DIM), kv_index...  6.34 us
    all_to_all x1, starting transfers between devices, body(): lax.all_to_all(sent_delta, 'pool', split_axis=0, concat_axis=0, tiled=True)  4.88 us
  transfers between devices with their start and end apart: 5, of which 4 were waited for; matrix products, arithmetic and copies ran while one was open for 7% of the time, Pallas kernels for 0%

commit v1 on v0

v1 whole, which is shorter than its diff:
```python
import functools
import math

import jax
import jax.numpy as jnp
from jax import lax
from jax.experimental import pallas as pl
from jax.experimental.pallas import tpu as pltpu
from jax.sharding import PartitionSpec as P

HEAD_DIM = 128
Q_PER_KV = 8
TILE = 16
PAD_STEPS = 8
BF = jnp.bfloat16
F32 = jnp.float32


def partner_to(z, k, n):
    return z ^ k if n & (n - 1) == 0 else (z + k) % n


def partner_from(z, k, n):
    return z ^ k if n & (n - 1) == 0 else (z + n - k) % n


def side_block(scale, length):
    shape = (TILE, scale.shape[-1])
    row = lax.broadcasted_iota(jnp.int32, shape, 0)
    scale = scale.astype(F32)
    out = jnp.where(row == 0, scale[0:1, :], jnp.float32(0.0))
    out = jnp.where(row == 1, scale[1:2, :], out)
    out = jnp.where(row == 2, length.astype(F32), out)
    return out.astype(BF)


def pack_kernel(n, route, lengths, place, deltas, anchors, scale, *rest):
    outs, (side, sems) = rest[: 2 * n], rest[2 * n:]
    count = route.shape[0]
    span, rows = deltas.shape[2], anchors.shape[2]
    z = place[0]
    copies = []
    for k in list(range(1, n)) + [0]:
        key_msg, value_msg = outs[2 * k], outs[2 * k + 1]
        dest = partner_to(z, k, n)
        index = jnp.int32(0)
        for j in range(count):
            index = jnp.where(route[j] == dest, jnp.int32(j), index)
        side[k] = side_block(scale[index], lengths[index])
        moves = [
            (deltas.at[index, 0], key_msg.at[pl.ds(0, span)]),
            (anchors.at[index, 0], key_msg.at[pl.ds(span, rows)]),
            (anchors.at[index, 1], key_msg.at[pl.ds(span + rows, rows)]),
            (side.at[k], key_msg.at[pl.ds(span + 2 * rows, TILE)]),
            (deltas.at[index, 1], value_msg),
        ]
        for i, (src, dst) in enumerate(moves):
            copy = pltpu.make_async_copy(src, dst, sems.at[k, i])
            copy.start()
            copies.append(copy)
    for copy in copies:
        copy.wait()


def pack(route, lengths, place, deltas, anchors, scale, n):
    span, channels = deltas.shape[2:]
    rows = anchors.shape[2]
    tall = span + 2 * rows + TILE
    smem = pl.BlockSpec(memory_space=pltpu.SMEM)
    anywhere = pl.BlockSpec(memory_space=pl.ANY)
    shapes = []
    for _ in range(n):
        shapes.append(jax.ShapeDtypeStruct((tall, channels), BF))
        shapes.append(jax.ShapeDtypeStruct((span, channels), BF))
    return pl.pallas_call(
        functools.partial(pack_kernel, n),
        out_shape=shapes,
        in_specs=[smem, smem, smem, anywhere, anywhere, pl.BlockSpec(memory_space=pltpu.VMEM)],
        out_specs=[anywhere] * (2 * n),
        scratch_shapes=[
            pltpu.VMEM((n, TILE, channels), BF),
            pltpu.SemaphoreType.DMA((n, 5)),
        ],
        cost_estimate=pl.CostEstimate(flops=0, bytes_accessed=4 * n * span * channels * 2, transcendentals=0),
    )(route, lengths, place, deltas, anchors, scale)


def rebuild_kernel(which, width, place, *refs):
    delta, anchor, side, cache, mine, theirs = refs[-6:]
    span = delta.shape[0]
    rows = anchor.shape[0]
    repeat = span // rows
    scale = side[which:which + 1, :].astype(F32)
    length = side[2:3, :].astype(F32)
    base = place[2] * span
    mine_at, theirs_at = place[3], place[4]
    blocks = delta.shape[1] // width
    for i in range(rows):
        part = pl.ds(i * repeat, repeat)
        value = anchor[i:i + 1, :].astype(F32) + scale * delta[part, :].astype(F32)
        keep = (base + i * repeat).astype(F32) < length
        value = jnp.where(keep, value, jnp.float32(0.0)).astype(BF)
        cache[0, 0, part, :] = value
        for out, at in ((mine, mine_at), (theirs, theirs_at)):
            piece = value[:, :width]
            for b in range(1, blocks):
                piece = jnp.where(at == b, value[:, b * width:(b + 1) * width], piece)
            out[part, :] = piece


def rebuild(which, k, place, delta, anchor_msg, cache, count, width, span, rows):
    channels = delta.shape[1]
    n_prefetch = 1
    grid = (1,)
    in_specs = [
        pl.BlockSpec((span, channels), lambda i, p: (0, 0)),
        pl.BlockSpec((rows, channels), lambda i, p: (span // rows + which, 0)),
        pl.BlockSpec((TILE, channels), lambda i, p: ((span + 2 * rows) // TILE, 0)),
    ]
    args = [place, delta, anchor_msg, anchor_msg]
    aliases = {}
    if cache is not None:
        in_specs = [pl.BlockSpec(memory_space=pl.ANY)] + in_specs
        args = [place, cache, delta, anchor_msg, anchor_msg]
        aliases = {1: 0}
    return pl.pallas_call(
        functools.partial(rebuild_kernel, which, width),
        grid_spec=pltpu.PrefetchScalarGridSpec(
            num_scalar_prefetch=n_prefetch,
            grid=grid,
            in_specs=in_specs,
            out_specs=[
                pl.BlockSpec((1, 1, span, channels), lambda i, p: (p[5 + k], which, 0, 0)),
                pl.BlockSpec((span, width), lambda i, p: (0, 0)),
                pl.BlockSpec((span, width), lambda i, p: (0, 0)),
            ],
        ),
        out_shape=[
            jax.ShapeDtypeStruct((count, 2, span, channels), BF),
            jax.ShapeDtypeStruct((span, width), BF),
            jax.ShapeDtypeStruct((span, width), BF),
        ],
        input_output_aliases=aliases,
        cost_estimate=pl.CostEstimate(
            flops=4 * span * channels, bytes_accessed=6 * span * channels, transcendentals=0
        ),
    )(*args)


def attend_kernel(steps, place, *refs):
    query, new_kv, side, key_mine, key_other, value_mine, value_other, out = refs[-8:]
    heads, wide = query.shape[1], query.shape[2]
    group = wide // PAD_STEPS
    span = key_mine.shape[0]
    fresh = new_kv.shape[2]
    factor = 1.0 / math.sqrt(HEAD_DIM)
    length = side[2:3, :span].astype(F32) if side.shape[1] >= span else None
    if length is None:
        length = jnp.broadcast_to(side[2:3, 0:1].astype(F32), (1, span))
    spot = lax.broadcasted_iota(jnp.int32, (1, span), 1)
    live_mine = (spot + place[2] * span).astype(F32) < length
    live_other = (spot + (1 - place[2]) * span).astype(F32) < length
    step = lax.broadcasted_iota(jnp.int32, (wide, fresh), 0) % PAD_STEPS
    token = lax.broadcasted_iota(jnp.int32, (wide, fresh), 1)
    causal = (token <= step) & (token < steps)
    nt = (((1,), (1,)), ((), ()))
    low = jnp.float32(-1e30)
    for j in range(heads):
        lanes = slice(j * HEAD_DIM, (j + 1) * HEAD_DIM)
        q = query[0, j]
        s0 = lax.dot_general(q, key_mine[:, lanes], nt, preferred_element_type=F32) * factor
        s1 = lax.dot_general(q, key_other[:, lanes], nt, preferred_element_type=F32) * factor
        s2 = lax.dot_general(q, new_kv[0, 0, :, lanes], nt, preferred_element_type=F32) * factor
        s0 = jnp.where(live_mine, s0, low)
        s1 = jnp.where(live_other, s1, low)
        s2 = jnp.where(causal, s2, low)
        top = jnp.maximum(
            jnp.max(jnp.maximum(s0, s1), axis=1, keepdims=True), jnp.max(s2, axis=1, keepdims=True)
        )
        w0 = jnp.where(live_mine, jnp.exp(s0 - top), jnp.float32(0.0))
        w1 = jnp.where(live_other, jnp.exp(s1 - top), jnp.float32(0.0))
        w2 = jnp.where(causal, jnp.exp(s2 - top), jnp.float32(0.0))
        total = jnp.sum(w0 + w1, axis=1, keepdims=True) + jnp.sum(w2, axis=1, keepdims=True)
        acc = jnp.dot(w0.astype(BF), value_mine[:, lanes], preferred_element_type=F32)
        acc = acc + jnp.dot(w1.astype(BF), value_other[:, lanes], preferred_element_type=F32)
        acc = acc + jnp.dot(w2.astype(BF), new_kv[0, 1, :, lanes], preferred_element_type=F32)
        acc = (acc / total).astype(BF)
        for g in range(group):
            at = (j * group + g) * HEAD_DIM
            out[0, :, at:at + HEAD_DIM] = acc[g * PAD_STEPS:g * PAD_STEPS + steps, :]


def attend(k, place, query, new_kv, msg, keys, values, attended, count, steps, span, rows, width):
    heads, wide = query.shape[1:3]
    fresh = new_kv.shape[2]
    channels = msg.shape[1]
    full = pl.BlockSpec((span, width), lambda i, p: (0, 0))
    in_specs = [
        pl.BlockSpec((1, heads, wide, HEAD_DIM), lambda i, p: (p[5 + k], 0, 0, 0)),
        pl.BlockSpec((1, 2, fresh, width), lambda i, p: (p[5 + k], 0, 0, p[3])),
        pl.BlockSpec((TILE, channels), lambda i, p: ((span + 2 * rows) // TILE, 0)),
        full, full, full, full,
    ]
    args = [query, new_kv, msg, *keys, *values]
    aliases = {}
    if attended is not None:
        in_specs = [pl.BlockSpec(memory_space=pl.ANY)] + in_specs
        args = [attended] + args
        aliases = {1: 0}
    outer = heads * (wide // PAD_STEPS) * HEAD_DIM
    return pl.pallas_call(
        functools.partial(attend_kernel, steps),
        grid_spec=pltpu.PrefetchScalarGridSpec(
            num_scalar_prefetch=1,
            grid=(1,),
            in_specs=in_specs,
            out_specs=pl.BlockSpec((1, steps, outer), lambda i, p: (p[5 + k], 0, 0)),
        ),
        out_shape=jax.ShapeDtypeStruct((count, steps, outer), BF),
        input_output_aliases=aliases,
        cost_estimate=pl.CostEstimate(
            flops=8 * heads * wide * span * HEAD_DIM,
            bytes_accessed=8 * span * width,
            transcendentals=2 * heads * wide * span,
        ),
    )(place, *args)


def body(deltas, anchors, chan_scale, lengths, route, new_query, new_kv):
    n = lax.axis_size("pool")
    count, _, span, channels = deltas.shape
    rows = anchors.shape[2]
    steps = new_query.shape[1]
    q_local = new_query.shape[2] // HEAD_DIM
    heads = max(1, q_local // Q_PER_KV)
    group = q_local // heads
    width = heads * HEAD_DIM
    z = lax.axis_index("pool")
    sub = lax.axis_index("sub")
    mine_at = (sub * q_local) // Q_PER_KV // heads
    theirs_at = ((1 - sub) * q_local) // Q_PER_KV // heads
    place = jnp.stack(
        [z, z, sub, mine_at, theirs_at] + [partner_from(z, k, n) for k in range(n)]
    ).astype(jnp.int32)

    query = new_query.reshape(count, steps, heads, group, HEAD_DIM).transpose(0, 2, 3, 1, 4)
    query = jnp.pad(query, ((0, 0),) * 3 + ((0, PAD_STEPS - steps), (0, 0)))
    query = query.reshape(count, heads, group * PAD_STEPS, HEAD_DIM)
    fresh = jnp.pad(new_kv, ((0, 0), (0, 0), (0, TILE - steps), (0, 0)))

    packed = pack(route, lengths, place, deltas, anchors, chan_scale, n)
    order = sorted(range(1, n), key=lambda k: (k == 1, k))
    key_msg, value_msg = [packed[0]] + [None] * (n - 1), [packed[1]] + [None] * (n - 1)
    for msgs, at in ((key_msg, 0), (value_msg, 1)):
        for k in order:
            perm = [(i, partner_to(i, k, n)) for i in range(n)]
            msgs[k] = lax.ppermute(packed[2 * k + at], "pool", perm)

    swap = [(0, 1), (1, 0)]
    cache = None
    keys, values = [None] * n, [None] * n
    use = [0, 1] + [k for k in order if k != 1] if n > 1 else [0]
    for which, msgs, made in ((0, key_msg, keys), (1, value_msg, values)):
        for k in use:
            cache, mine, theirs = rebuild(
                which, k, place, msgs[k], key_msg[k], cache, count, width, span, rows
            )
            made[k] = (mine, lax.ppermute(theirs, "sub", swap))
    attended = None
    for k in use:
        attended = attend(
            k, place, query, fresh, key_msg[k], keys[k], values[k], attended,
            count, steps, span, rows, width,
        )
    return cache, attended


def solution(mesh):
    placed = (
        P(("parts", "pool"), None, "sub", "tp"),
        P(("parts", "pool"), None, "sub", "tp"),
        P(("parts", "pool"), None, "tp"),
        P(("parts", "pool")),
        P(("parts", "pool")),
        P(("parts", "pool"), None, ("tp", "sub")),
        P(("parts", "pool"), None, None, "tp"),
    )
    return jax.shard_map(
        body,
        mesh=mesh,
        in_specs=placed,
        out_specs=(
            P(("parts", "pool"), None, "sub", "tp"),
            P(("parts", "pool"), None, ("tp", "sub")),
        ),
        check_vma=False,
    )
```

time: 165 us -> 148 us (0.90)
  Pallas kernels: 0 us -> 102 us
  waiting for transfers between devices: 61.3 us -> 16.3 us
  local copies, waits for them, and re-layouts: 40.6 us -> 6.16 us
  other arithmetic: 20.5 us -> 0 us
  between operations: 14.2 us -> 0.82 us
  matrix products: 8.02 us -> 0 us
  starting transfers between devices: 18.6 us -> 21.9 us
    pallas_call x0 -> x13, Pallas kernels: none -> 102 us  [the longest x1 69.5 us: pack(): pl.pallas_call(functools.partial(pack_kernel, n), out_shape=shapes, in_sp...]
    all_to_all x4 -> x0, waiting for transfers between devices: 42.7 us -> none  [the longest x1 41 us: body(): lax.all_to_all(sent_delta, 'pool', split_axis=0, concat_axis=0, tiled=True)]
    ppermute x0 -> x14, starting transfers between devices: none -> 21.9 us  [the longest x8 14.2 us: body(): made[k] = (mine, lax.ppermute(theirs, 'sub', swap))]
    gather x8 -> x0, local copies, waits for them, and re-layouts: 20 us -> none  [the longest x1 6.35 us: body(): jnp.take(whole[:, 1].reshape(count, total_len, heads, HEAD_DIM), kv_index...]
    all_to_all x4 -> x0, starting transfers between devices: 18.6 us -> none  [the longest x1 4.88 us: body(): lax.all_to_all(sent_delta, 'pool', split_axis=0, concat_axis=0, tiled=True)]
    all_gather x1 -> x0, waiting for transfers between devices: 18.6 us -> none  [body(): whole = lax.all_gather(cache, 'sub', axis=2, tiled=True)]
    ppermute x0 -> x14, waiting for transfers between devices: none -> 16.3 us  [the longest x6 16.3 us: body(): msgs[k] = lax.ppermute(packed[2 * k + at], 'pool', perm)]
    select_n x8 -> x0, other arithmetic: 14.1 us -> none  [the longest x2 9.42 us: body(): jnp.take(whole[:, 0].reshape(count, total_len, heads, HEAD_DIM), kv_index...]
  transfers between devices with their start and end apart: 5 -> 14, of which waited for: 4 -> 2; matrix products, arithmetic and copies ran while one was open for 7% -> 1% of each run, Pallas kernels for 0% -> 20%
where the time goes in v1:
time: 148 us; the launch traced here: 147 us
  Pallas kernels  102 us (69%)
  starting transfers between devices  21.9 us (15%)
  waiting for transfers between devices  16.3 us (11%)
  local copies, waits for them, and re-layouts  6.16 us (4%)
    pallas_call x1, Pallas kernels, pack(): pl.pallas_call(functools.partial(pack_kernel, n), out_shape=shapes, in_sp...  69.5 us
    pallas_call x8, Pallas kernels, rebuild(): pl.pallas_call(functools.partial(rebuild_kernel, which, width), grid_spec...  20.4 us
    ppermute x6, waiting for transfers between devices, body(): msgs[k] = lax.ppermute(packed[2 * k + at], 'pool', perm)  16.3 us
    ppermute x8, starting transfers between devices, body(): made[k] = (mine, lax.ppermute(theirs, 'sub', swap))  14.2 us
    pallas_call x4, Pallas kernels, attend(): pl.pallas_call(functools.partial(attend_kernel, steps), grid_spec=pltpu.P...  12.4 us
    ppermute x6, starting transfers between devices, body(): msgs[k] = lax.ppermute(packed[2 * k + at], 'pool', perm)  7.63 us
    unnamed x38, local copies, waits for them, and re-layouts  4.19 us
  transfers between devices with their start and end apart: 14, of which 2 were waited for; matrix products, arithmetic and copies ran while one was open for 1% of the time, Pallas kernels for 20%

profile of v1, /device:TPU:9, one launch (start us, length us, event | category | flops | bytes accessed | tf_op | source)
XLA Modules:
  0.0 147.5 jit_solution(8236545821562782196)
XLA Ops:
  0.7 0.6 stack.33.place
  1.3 69.5 %shard_map.86 = (bf16[304,512]{1,0:T(8,128)(2,1)}, bf16[256,512]{1,0:T(8,128)(2,1)}, bf16[304,512]{1,0:T(8,128)(2,1)}, bf16[256,512]{1,0:T(8,128)(2,1)}, bf16[30...) custom-call(s32[4]{0:T(128)} %route.1, s32[4]{0:T(128)} %lengths.1, ...), custom_call_target="tpu_custom_call" | custom-call | bytes 4194304 | tf_op jit(solution)/shard_map/pallas_call | solution.py:75
  70.8 0.1 collective-permute-start
  70.9 2.5 %collective-permute-start.1 = (bf16[304,512]{1,0:T(8,128)(2,1)}, bf16[304,512]{1,0:T(8,128)(2,1)S(1)}, u32[]{:S(2)}, u32[]{:S(2)}) collective-permute-start(bf16[304,512]{1,0:T(8,128)(2,1)} %get-tuple-element.38), channel_id=1, source_target_pairs={{0,8},{4,12},{8,0},{12,4},{1,9},{5,13},{9,1},{13,5},{2,10},{6,14},... | collective-permute-start | bytes 933896 | tf_op jit(solution)/shard_map/ppermute | solution.py:257
  73.4 0.2 collective-permute-start.2
  73.6 1.1 collective-permute-start.3
  74.7 2.1 %collective-permute-start.4 = (bf16[256,512]{1,0:T(8,128)(2,1)}, bf16[256,512]{1,0:T(8,128)(2,1)S(1)}, u32[]{:S(2)}, u32[]{:S(2)}) collective-permute-start(bf16[256,512]{1,0:T(8,128)(2,1)} %get-tuple-element.46), channel_id=1, source_target_pairs={{0,8},{4,12},{8,0},{12,4},{1,9},{5,13},{9,1},{13,5},{2,10},{6,14},... | collective-permute-start | bytes 786440 | tf_op jit(solution)/shard_map/ppermute | solution.py:257
  76.8 6.7 %collective-permute-done.refs_1_.refs_2_.refs_3_ = bf16[304,512]{1,0:T(8,128)(2,1)S(1)} collective-permute-done((bf16[304,512]{1,0:T(8,128)(2,1)}, bf16[304,512]{1,0:T(8,128)(2,1)S(1)}, u32[]{:S(2)}, u32[]{:S(2)}) %collective-permute-start) | collective-permute-done | bytes 311328 | tf_op jit(solution)/shard_map/ppermute | solution.py:257
  83.5 1.7 %collective-permute-start.5 = (bf16[256,512]{1,0:T(8,128)(2,1)}, bf16[256,512]{1,0:T(8,128)(2,1)S(1)}, u32[]{:S(2)}, u32[]{:S(2)}) collective-permute-start(bf16[256,512]{1,0:T(8,128)(2,1)} %get-tuple-element.48), channel_id=1, source_target_pairs={{0,12},{4,8},{8,4},{12,0},{1,13},{5,9},{9,5},{13,1},{2,14},{6,10},... | collective-permute-start | bytes 786440 | tf_op jit(solution)/shard_map/ppermute | solution.py:257
  85.2 2.6 %shard_map.87 = (bf16[4,2,256,512]{3,2,1,0:T(8,128)(2,1)}, bf16[256,256]{1,0:T(8,128)(2,1)}, bf16[256,256]{1,0:T(8,128)(2,1)}) custom-call(s32[9]{0:T(128)} %stack.33.place, bf16[304,512]{1,0:T(8,128)(2,1)} %get-tuple-element.34.refs_0_.refs_1_.refs_2_.refs_3_, bf16[304,512]{1,0:T(8,128)(2,1)} %get-tuple-element.34.refs_0_.refs_1_.refs_2_.refs_3_, ...), custom_call_target="tpu_custom_call" | custom-call | flops 524288 | bytes 786432 | tf_op jit(solution)/shard_map/pallas_call | solution.py:126
  87.8 0.0 collective-permute-done.1.refs_1_.refs_2_.refs_3_
  87.8 8.4 %collective-permute-start.6 = (bf16[256,256]{1,0:T(8,128)(2,1)}, bf16[256,256]{1,0:T(8,128)(2,1)S(1)}, u32[]{:S(2)}, u32[]{:S(2)}) collective-permute-start(bf16[256,256]{1,0:T(8,128)(2,1)} %get-tuple-element.51), channel_id=1, source_target_pairs={{0,1},{1,0},{2,3},{3,2},{4,5},{5,4},{6,7},{7,6},{8,9},{9,8},{10,11... | collective-permute-start | bytes 393224 | tf_op jit(solution)/shard_map/ppermute | solution.py:268
  96.1 0.0 copy-done.2
  96.1 2.6 %shard_map.88 = (bf16[4,2,256,512]{3,2,1,0:T(8,128)(2,1)}, bf16[256,256]{1,0:T(8,128)(2,1)}, bf16[256,256]{1,0:T(8,128)(2,1)}) custom-call(s32[9]{0:T(128)} %stack.33.place, bf16[4,2,256,512]{3,2,1,0:T(8,128)(2,1)} %get-tuple-element.35.refs_0_, bf16[304,512]{1,0:T(8,128)(2,1)} %copy-done.2, ...), custom_call_target="tpu_custom_call", output_to_operand_aliasing={{0}: (1, {})} | custom-call | flops 524288 | bytes 786432 | tf_op jit(solution)/shard_map/pallas_call | solution.py:126
  98.7 0.0 copy-done.1
  98.7 2.6 %shard_map.89 = (bf16[4,2,256,512]{3,2,1,0:T(8,128)(2,1)}, bf16[256,256]{1,0:T(8,128)(2,1)}, bf16[256,256]{1,0:T(8,128)(2,1)}) custom-call(s32[9]{0:T(128)} %stack.33.place, bf16[4,2,256,512]{3,2,1,0:T(8,128)(2,1)} %get-tuple-element.37.refs_0_, bf16[304,512]{1,0:T(8,128)(2,1)} %copy-done.1, ...), custom_call_target="tpu_custom_call", output_to_operand_aliasing={{0}: (1, {})} | custom-call | flops 524288 | bytes 786432 | tf_op jit(solution)/shard_map/pallas_call | solution.py:126
  101.2 9.5 %collective-permute-done.2.refs_1_.refs_2_.refs_3_ = bf16[304,512]{1,0:T(8,128)(2,1)S(1)} collective-permute-done((bf16[304,512]{1,0:T(8,128)(2,1)}, bf16[304,512]{1,0:T(8,128)(2,1)S(1)}, u32[]{:S(2)}, u32[]{:S(2)}) %collective-permute-start.2) | collective-permute-done | bytes 311328 | tf_op jit(solution)/shard_map/ppermute | solution.py:257
  110.8 0.7 copy-done
  111.5 2.5 %shard_map.90 = (bf16[4,2,256,512]{3,2,1,0:T(8,128)(2,1)}, bf16[256,256]{1,0:T(8,128)(2,1)}, bf16[256,256]{1,0:T(8,128)(2,1)}) custom-call(s32[9]{0:T(128)} %stack.33.place, bf16[4,2,256,512]{3,2,1,0:T(8,128)(2,1)} %get-tuple-element.39.refs_0_, bf16[304,512]{1,0:T(8,128)(2,1)} %copy-done, ...), custom_call_target="tpu_custom_call", output_to_operand_aliasing={{0}: (1, {})} | custom-call | flops 524288 | bytes 786432 | tf_op jit(solution)/shard_map/pallas_call | solution.py:126
  114.0 2.6 %shard_map.91 = (bf16[4,2,256,512]{3,2,1,0:T(8,128)(2,1)}, bf16[256,256]{1,0:T(8,128)(2,1)}, bf16[256,256]{1,0:T(8,128)(2,1)}) custom-call(s32[9]{0:T(128)} %stack.33.place, bf16[4,2,256,512]{3,2,1,0:T(8,128)(2,1)} %get-tuple-element.41.refs_0_, bf16[256,512]{1,0:T(8,128)(2,1)} %get-tuple-element.42.refs_1_, ...), custom_call_target="tpu_custom_call", output_to_operand_aliasing={{0}: (1, {})} | custom-call | flops 524288 | bytes 786432 | tf_op jit(solution)/shard_map/pallas_call | solution.py:126
  116.6 4.0 %collective-permute-start.7 = (bf16[256,256]{1,0:T(8,128)(2,1)}, bf16[256,256]{1,0:T(8,128)(2,1)S(1)}, u32[]{:S(2)}, u32[]{:S(2)}) collective-permute-start(bf16[256,256]{1,0:T(8,128)(2,1)} %get-tuple-element.53), channel_id=1, source_target_pairs={{0,1},{1,0},{2,3},{3,2},{4,5},{5,4},{6,7},{7,6},{8,9},{9,8},{10,11... | collective-permute-start | bytes 393224 | tf_op jit(solution)/shard_map/ppermute | solution.py:268
  120.7 0.0 collective-permute-done.3.refs_1_
  120.7 0.7 copy-done.5
  121.4 2.5 %shard_map.92 = (bf16[4,2,256,512]{3,2,1,0:T(8,128)(2,1)}, bf16[256,256]{1,0:T(8,128)(2,1)}, bf16[256,256]{1,0:T(8,128)(2,1)}) custom-call(s32[9]{0:T(128)} %stack.33.place, bf16[4,2,256,512]{3,2,1,0:T(8,128)(2,1)} %get-tuple-element.43.refs_0_, bf16[256,512]{1,0:T(8,128)(2,1)} %copy-done.5, ...), custom_call_target="tpu_custom_call", output_to_operand_aliasing={{0}: (1, {})} | custom-call | flops 524288 | bytes 786432 | tf_op jit(solution)/shard_map/pallas_call | solution.py:126
  123.9 0.0 collective-permute-start.9
  123.9 0.0 collective-permute-done.4.refs_1_
  123.9 0.0 copy-start.4
  123.9 0.0 copy-done.18
  123.9 0.6 collective-permute-start.8
  124.5 0.1 copy-done.4
  124.6 2.5 %shard_map.93 = (bf16[4,2,256,512]{3,2,1,0:T(8,128)(2,1)}, bf16[256,256]{1,0:T(8,128)(2,1)}, bf16[256,256]{1,0:T(8,128)(2,1)}) custom-call(s32[9]{0:T(128)} %stack.33.place, bf16[4,2,256,512]{3,2,1,0:T(8,128)(2,1)} %get-tuple-element.45.refs_0_, bf16[256,512]{1,0:T(8,128)(2,1)} %copy-done.4, ...), custom_call_target="tpu_custom_call", output_to_operand_aliasing={{0}: (1, {})} | custom-call | flops 524288 | bytes 786432 | tf_op jit(solution)/shard_map/pallas_call | solution.py:126
  127.2 0.0 collective-permute-done.6.refs_4_
  127.2 0.0 copy-start.12
  127.2 0.6 collective-permute-start.11
  127.8 0.0 collective-permute-done.5.refs_1_
  127.8 0.0 copy-done.17
  127.8 0.1 collective-permute-start.10
  127.9 0.6 copy-done.3
  128.5 2.6 %shard_map.94 = (bf16[4,2,256,512]{3,2,1,0:T(8,128)(2,1)}, bf16[256,256]{1,0:T(8,128)(2,1)}, bf16[256,256]{1,0:T(8,128)(2,1)}) custom-call(s32[9]{0:T(128)} %stack.33.place, bf16[4,2,256,512]{3,2,1,0:T(8,128)(2,1)} %get-tuple-element.47.refs_0_, bf16[256,512]{1,0:T(8,128)(2,1)} %copy-done.3, ...), custom_call_target="tpu_custom_call", output_to_operand_aliasing={{0}: (1, {})} | custom-call | flops 524288 | bytes 786432 | tf_op jit(solution)/shard_map/pallas_call | solution.py:126
  131.0 0.0 collective-permute-done.7.refs_6_
  131.0 0.1 collective-permute-start.13
  131.1 0.0 collective-permute-done.9.refs_7_
  131.1 0.0 copy-start.6
  131.1 0.0 copy-done.16
  131.1 0.5 collective-permute-start.12
  131.6 0.0 copy-done.15
  131.6 0.7 pad.9.refs_1_.refs_2_
  132.3 0.0 copy-done.14
  132.3 0.7 pad_bitcast_fusion.refs_0_.refs_1_
  133.0 3.1 %shard_map.95.refs_0_ = bf16[4,4,2048]{2,1,0:T(4,128)(2,1)} custom-call(s32[9]{0:T(128)} %stack.33.place, bf16[4,2,64,128]{3,2,1,0:T(8,128)(2,1)} %pad_bitcast_fusion.refs_0_.refs_1_, bf16[4,2,16,512]{3,2,1,0:T(8,128)(2,1)} %pad.9.refs_1_.refs_2_, bf16[304,512]{1,0:T(8,128)(2,1)} %get-tuple-element.34.refs_0_.refs_1_.refs_2_.refs_3_, ...), custom_call_target="tpu_custom_call" | custom-call | flops 33554432 | bytes 524288 | tf_op jit(solution)/shard_map/pallas_call | solution.py:211
  136.1 0.0 collective-permute-done.8.refs_5_
  136.1 0.0 copy-done.6
  136.1 0.6 copy-done.8
  136.8 3.1 %shard_map.96.refs_0_ = bf16[4,4,2048]{2,1,0:T(4,128)(2,1)} custom-call(s32[9]{0:T(128)} %stack.33.place, bf16[4,4,2048]{2,1,0:T(4,128)(2,1)} %shard_map.95.refs_0_, bf16[4,2,64,128]{3,2,1,0:T(8,128)(2,1)} %pad_bitcast_fusion.refs_0_.refs_1_, bf16[4,2,16,512]{3,2,1,0:T(8,128)(2,1)} %pad.9.refs_1_.refs_2_, ...), custom_call_target="tpu_custom_call", output_to_operand_aliasing={{}: (1, {})} | custom-call | flops 33554432 | bytes 524288 | tf_op jit(solution)/shard_map/pallas_call | solution.py:211
  139.9 0.0 collective-permute-done.11.refs_7_
  139.9 0.0 collective-permute-done.10.refs_5_
  139.9 0.6 copy-done.7
  140.5 0.1 copy-done.10
  140.6 3.1 %shard_map.97.refs_0_ = bf16[4,4,2048]{2,1,0:T(4,128)(2,1)} custom-call(s32[9]{0:T(128)} %stack.33.place, bf16[4,4,2048]{2,1,0:T(4,128)(2,1)} %shard_map.96.refs_0_, bf16[4,2,64,128]{3,2,1,0:T(8,128)(2,1)} %pad_bitcast_fusion.refs_0_.refs_1_, bf16[4,2,16,512]{3,2,1,0:T(8,128)(2,1)} %pad.9.refs_1_.refs_2_, ...), custom_call_target="tpu_custom_call", output_to_operand_aliasing={{}: (1, {})} | custom-call | flops 33554432 | bytes 524288 | tf_op jit(solution)/shard_map/pallas_call | solution.py:211
  143.7 0.0 collective-permute-done.13.refs_7_
  143.7 0.0 collective-permute-done.12.refs_5_
  143.7 0.6 copy-done.9
  144.3 0.1 copy-done.11
  144.4 3.1 %shard_map.98 = bf16[4,4,2048]{2,1,0:T(4,128)(2,1)} custom-call(s32[9]{0:T(128)} %stack.33.place, bf16[4,4,2048]{2,1,0:T(4,128)(2,1)} %shard_map.97.refs_0_, bf16[4,2,64,128]{3,2,1,0:T(8,128)(2,1)} %pad_bitcast_fusion.refs_0_.refs_1_, bf16[4,2,16,512]{3,2,1,0:T(8,128)(2,1)} %pad.9.refs_1_.refs_2_, ...), custom_call_target="tpu_custom_call", output_to_operand_aliasing={{}: (1, {})} | custom-call | flops 33554432 | bytes 524288 | tf_op jit(solution)/shard_map/pallas_call | solution.py:211
  (18 shorter events, 0.0 us)
Async XLA Ops:
  70.8 12.6 %collective-permute-start = (bf16[304,512]{1,0:T(8,128)(2,1)}, bf16[304,512]{1,0:T(8,128)(2,1)S(1)}, u32[]{:S(2)}, u32[]{:S(2)}) collective-permute-start(bf16[304,512]{1,0:T(8,128)(2,1)} %get-tuple-element.36), channel_id=1, source_target_pairs={{0,4},{4,0},{8,12},{12,8},{1,5},{5,1},{9,13},{13,9},{2,6},{6,2},{1... | collective-permute-start | bytes 933896 | tf_op jit(solution)/shard_map/ppermute | solution.py:257
  70.9 16.8 %collective-permute-start.1 = (bf16[304,512]{1,0:T(8,128)(2,1)}, bf16[304,512]{1,0:T(8,128)(2,1)S(1)}, u32[]{:S(2)}, u32[]{:S(2)}) collective-permute-start(bf16[304,512]{1,0:T(8,128)(2,1)} %get-tuple-element.38), channel_id=1, source_target_pairs={{0,8},{4,12},{8,0},{12,4},{1,9},{5,13},{9,1},{13,5},{2,10},{6,14},... | collective-permute-start | bytes 933896 | tf_op jit(solution)/shard_map/ppermute | solution.py:257
  73.4 37.4 %collective-permute-start.2 = (bf16[304,512]{1,0:T(8,128)(2,1)}, bf16[304,512]{1,0:T(8,128)(2,1)S(1)}, u32[]{:S(2)}, u32[]{:S(2)}) collective-permute-start(bf16[304,512]{1,0:T(8,128)(2,1)} %get-tuple-element.40), channel_id=1, source_target_pairs={{0,12},{4,8},{8,4},{12,0},{1,13},{5,9},{9,5},{13,1},{2,14},{6,10},... | collective-permute-start | bytes 933896 | tf_op jit(solution)/shard_map/ppermute | solution.py:257
  73.6 47.1 %collective-permute-start.3 = (bf16[256,512]{1,0:T(8,128)(2,1)}, bf16[256,512]{1,0:T(8,128)(2,1)S(1)}, u32[]{:S(2)}, u32[]{:S(2)}) collective-permute-start(bf16[256,512]{1,0:T(8,128)(2,1)} %get-tuple-element.44), channel_id=1, source_target_pairs={{0,4},{4,0},{8,12},{12,8},{1,5},{5,1},{9,13},{13,9},{2,6},{6,2},{1... | collective-permute-start | bytes 786440 | tf_op jit(solution)/shard_map/ppermute | solution.py:257
  74.7 49.2 %collective-permute-start.4 = (bf16[256,512]{1,0:T(8,128)(2,1)}, bf16[256,512]{1,0:T(8,128)(2,1)S(1)}, u32[]{:S(2)}, u32[]{:S(2)}) collective-permute-start(bf16[256,512]{1,0:T(8,128)(2,1)} %get-tuple-element.46), channel_id=1, source_target_pairs={{0,8},{4,12},{8,0},{12,4},{1,9},{5,13},{9,1},{13,5},{2,10},{6,14},... | collective-permute-start | bytes 786440 | tf_op jit(solution)/shard_map/ppermute | solution.py:257
  83.5 12.7 %copy-start.2 = (bf16[304,512]{1,0:T(8,128)(2,1)}, bf16[304,512]{1,0:T(8,128)(2,1)S(1)}, u32[]{:S(2)}) copy-start(bf16[304,512]{1,0:T(8,128)(2,1)S(1)} %collective-permute-done.refs_1_.refs_2_.refs_3_) | copy-start | bytes 933892
  83.5 44.3 %collective-permute-start.5 = (bf16[256,512]{1,0:T(8,128)(2,1)}, bf16[256,512]{1,0:T(8,128)(2,1)S(1)}, u32[]{:S(2)}, u32[]{:S(2)}) collective-permute-start(bf16[256,512]{1,0:T(8,128)(2,1)} %get-tuple-element.48), channel_id=1, source_target_pairs={{0,12},{4,8},{8,4},{12,0},{1,13},{5,9},{9,5},{13,1},{2,14},{6,10},... | collective-permute-start | bytes 786440 | tf_op jit(solution)/shard_map/ppermute | solution.py:257
  87.8 10.9 %copy-start.1 = (bf16[304,512]{1,0:T(8,128)(2,1)}, bf16[304,512]{1,0:T(8,128)(2,1)S(1)}, u32[]{:S(2)}) copy-start(bf16[304,512]{1,0:T(8,128)(2,1)S(1)} %collective-permute-done.1.refs_1_.refs_2_.refs_3_) | copy-start | bytes 933892
  87.8 39.4 %collective-permute-start.6 = (bf16[256,256]{1,0:T(8,128)(2,1)}, bf16[256,256]{1,0:T(8,128)(2,1)S(1)}, u32[]{:S(2)}, u32[]{:S(2)}) collective-permute-start(bf16[256,256]{1,0:T(8,128)(2,1)} %get-tuple-element.51), channel_id=1, source_target_pairs={{0,1},{1,0},{2,3},{3,2},{4,5},{5,4},{6,7},{7,6},{8,9},{9,8},{10,11... | collective-permute-start | bytes 393224 | tf_op jit(solution)/shard_map/ppermute | solution.py:268
  110.8 0.7 copy-start
  116.6 7.3 %copy-start.18 = (bf16[256,256]{1,0:T(8,128)(2,1)S(1)}, bf16[256,256]{1,0:T(8,128)(2,1)}, u32[]{:S(2)}) copy-start(bf16[256,256]{1,0:T(8,128)(2,1)} %get-tuple-element.55) | copy-start | bytes 393220
  116.6 14.4 %collective-permute-start.7 = (bf16[256,256]{1,0:T(8,128)(2,1)}, bf16[256,256]{1,0:T(8,128)(2,1)S(1)}, u32[]{:S(2)}, u32[]{:S(2)}) collective-permute-start(bf16[256,256]{1,0:T(8,128)(2,1)} %get-tuple-element.53), channel_id=1, source_target_pairs={{0,1},{1,0},{2,3},{3,2},{4,5},{5,4},{6,7},{7,6},{8,9},{9,8},{10,11... | collective-permute-start | bytes 393224 | tf_op jit(solution)/shard_map/ppermute | solution.py:268
  120.7 0.7 copy-start.5
  123.9 3.9 %copy-start.17 = (bf16[256,256]{1,0:T(8,128)(2,1)S(1)}, bf16[256,256]{1,0:T(8,128)(2,1)}, u32[]{:S(2)}) copy-start(bf16[256,256]{1,0:T(8,128)(2,1)} %get-tuple-element.59) | copy-start | bytes 393220
  123.9 7.2 %collective-permute-start.9 = (bf16[256,256]{1,0:T(8,128)(2,1)}, bf16[256,256]{1,0:T(8,128)(2,1)S(1)}, u32[]{:S(2)}, u32[]{:S(2)}) collective-permute-start(bf16[256,256]{1,0:T(8,128)(2,1)} %get-tuple-element.57), channel_id=1, source_target_pairs={{0,1},{1,0},{2,3},{3,2},{4,5},{5,4},{6,7},{7,6},{8,9},{9,8},{10,11... | collective-permute-start | bytes 393224 | tf_op jit(solution)/shard_map/ppermute | solution.py:268
  123.9 0.7 copy-start.4
  123.9 12.2 %collective-permute-start.8 = (bf16[256,256]{1,0:T(8,128)(2,1)S(1)}, bf16[256,256]{1,0:T(8,128)(2,1)S(1)}, u32[]{:S(2)}, u32[]{:S(2)}) collective-permute-start(bf16[256,256]{1,0:T(8,128)(2,1)S(1)} %copy-done.18), channel_id=1, source_target_pairs={{0,1},{1,0},{2,3},{3,2},{4,5},{5,4},{6,7},{7,6},{8,9},{9,8},{10,11... | collective-permute-start | bytes 393224 | tf_op jit(solution)/shard_map/ppermute | solution.py:268
  127.2 3.9 %copy-start.16 = (bf16[256,256]{1,0:T(8,128)(2,1)S(1)}, bf16[256,256]{1,0:T(8,128)(2,1)}, u32[]{:S(2)}) copy-start(bf16[256,256]{1,0:T(8,128)(2,1)} %get-tuple-element.63) | copy-start | bytes 393220
  127.2 4.5 %copy-start.15 = (bf16[4,2,4,512]{3,2,1,0:T(4,128)(2,1)S(1)}, bf16[4,2,4,512]{3,2,1,0:T(4,128)(2,1)}, u32[]{:S(2)}) copy-start(bf16[4,2,4,512]{3,2,1,0:T(4,128)(2,1)} %param.13) | copy-start | bytes 98308
  127.2 5.1 %copy-start.14 = (bf16[4,4,2048]{2,1,0:T(4,128)(2,1)S(1)}, bf16[4,4,2048]{2,1,0:T(4,128)(2,1)}, u32[]{:S(2)}) copy-start(bf16[4,4,2048]{2,1,0:T(4,128)(2,1)} %param.12) | copy-start | bytes 196612
  127.2 5.8 %copy-start.12 = (bf16[256,256]{1,0:T(8,128)(2,1)}, bf16[256,256]{1,0:T(8,128)(2,1)S(1)}, u32[]{:S(2)}) copy-start(bf16[256,256]{1,0:T(8,128)(2,1)S(1)} %collective-permute-done.6.refs_4_) | copy-start | bytes 393220
  127.2 12.7 %collective-permute-start.11 = (bf16[256,256]{1,0:T(8,128)(2,1)}, bf16[256,256]{1,0:T(8,128)(2,1)S(1)}, u32[]{:S(2)}, u32[]{:S(2)}) collective-permute-start(bf16[256,256]{1,0:T(8,128)(2,1)} %get-tuple-element.61), channel_id=1, source_target_pairs={{0,1},{1,0},{2,3},{3,2},{4,5},{5,4},{6,7},{7,6},{8,9},{9,8},{10,11... | collective-permute-start | bytes 393224 | tf_op jit(solution)/shard_map/ppermute | solution.py:268
  127.8 0.7 copy-start.3
  127.8 12.1 %collective-permute-start.10 = (bf16[256,256]{1,0:T(8,128)(2,1)S(1)}, bf16[256,256]{1,0:T(8,128)(2,1)S(1)}, u32[]{:S(2)}, u32[]{:S(2)}) collective-permute-start(bf16[256,256]{1,0:T(8,128)(2,1)S(1)} %copy-done.17), channel_id=1, source_target_pairs={{0,1},{1,0},{2,3},{3,2},{4,5},{5,4},{6,7},{7,6},{8,9},{9,8},{10,11... | collective-permute-start | bytes 393224 | tf_op jit(solution)/shard_map/ppermute | solution.py:268
  131.0 2.0 %copy-start.13 = (bf16[256,256]{1,0:T(8,128)(2,1)}, bf16[256,256]{1,0:T(8,128)(2,1)S(1)}, u32[]{:S(2)}) copy-start(bf16[256,256]{1,0:T(8,128)(2,1)S(1)} %collective-permute-done.7.refs_6_) | copy-start | bytes 393220
  131.0 12.7 %collective-permute-start.13 = (bf16[256,256]{1,0:T(8,128)(2,1)}, bf16[256,256]{1,0:T(8,128)(2,1)S(1)}, u32[]{:S(2)}, u32[]{:S(2)}) collective-permute-start(bf16[256,256]{1,0:T(8,128)(2,1)} %get-tuple-element.65), channel_id=1, source_target_pairs={{0,1},{1,0},{2,3},{3,2},{4,5},{5,4},{6,7},{7,6},{8,9},{9,8},{10,11... | collective-permute-start | bytes 393224 | tf_op jit(solution)/shard_map/ppermute | solution.py:268
  131.1 5.0 %copy-start.6 = (bf16[256,256]{1,0:T(8,128)(2,1)}, bf16[256,256]{1,0:T(8,128)(2,1)S(1)}, u32[]{:S(2)}) copy-start(bf16[256,256]{1,0:T(8,128)(2,1)S(1)} %collective-permute-done.9.refs_7_) | copy-start | bytes 393220
  131.1 12.6 %collective-permute-start.12 = (bf16[256,256]{1,0:T(8,128)(2,1)S(1)}, bf16[256,256]{1,0:T(8,128)(2,1)S(1)}, u32[]{:S(2)}, u32[]{:S(2)}) collective-permute-start(bf16[256,256]{1,0:T(8,128)(2,1)S(1)} %copy-done.16), channel_id=1, source_target_pairs={{0,1},{1,0},{2,3},{3,2},{4,5},{5,4},{6,7},{7,6},{8,9},{9,8},{10,11... | collective-permute-start | bytes 393224 | tf_op jit(solution)/shard_map/ppermute | solution.py:268
  136.1 0.7 copy-start.8
  139.9 0.6 copy-start.7
  139.9 0.7 copy-start.10
  143.7 0.6 copy-start.9
  143.7 0.7 copy-start.11

commit v2 on v1

v2 whole, which is shorter than its diff:
```python
import functools
import math

import jax
import jax.numpy as jnp
from jax import lax
from jax.experimental import pallas as pl
from jax.experimental.pallas import tpu as pltpu
from jax.sharding import PartitionSpec as P

HEAD_DIM = 128
Q_PER_KV = 8
TILE = 16
PAD_STEPS = 8
BF = jnp.bfloat16
F32 = jnp.float32


def ring_of(n):
    return (0, 2, 3, 1) if n == 4 else tuple(range(n))


def shifts_of(n):
    return sorted(range(1, n), key=lambda k: (min(k, n - k), k))


def pick(values, at):
    out = jnp.int32(values[0])
    for i, value in enumerate(values[1:], 1):
        out = jnp.where(at == i, jnp.int32(value), out)
    return out


def far(n, k):
    ring = ring_of(n)
    return tuple(ring[(ring.index(z) + k) % n] for z in range(n))


def vmem(x):
    return pltpu.with_memory_space_constraint(x, pltpu.VMEM)


IN_VMEM = pl.BlockSpec(memory_space=pltpu.VMEM)
IN_SMEM = pl.BlockSpec(memory_space=pltpu.SMEM)
IN_HBM = pl.BlockSpec(memory_space=pltpu.HBM)
LIMIT = pltpu.CompilerParams(vmem_limit_bytes=16 * 1024 * 1024)


def side_block(scale, length):
    shape = (TILE, scale.shape[-1])
    row = lax.broadcasted_iota(jnp.int32, shape, 0)
    scale = scale.astype(F32)
    out = jnp.where(row == 0, scale[0:1, :], jnp.float32(0.0))
    out = jnp.where(row == 1, scale[1:2, :], out)
    out = jnp.where(row == 2, length.astype(F32), out)
    return out.astype(BF)


def pack_kernel(n, order, route, lengths, deltas, anchors, scale, *rest):
    outs, sems = rest[:-1], rest[-1]
    count = route.shape[0]
    span, rows = deltas.shape[2], anchors.shape[2]
    z = lax.axis_index("pool")
    copies = []
    for at, k in enumerate(order):
        key_msg, value_msg = outs[2 * at], outs[2 * at + 1]
        dest = pick(far(n, k), z)
        index = jnp.int32(0)
        for j in range(count):
            index = jnp.where(route[j] == dest, jnp.int32(j), index)
        moves = [
            (deltas.at[index, 0], key_msg.at[pl.ds(0, span)]),
            (anchors.at[index, 0], key_msg.at[pl.ds(span, rows)]),
            (anchors.at[index, 1], key_msg.at[pl.ds(span + rows, rows)]),
            (deltas.at[index, 1], value_msg),
        ]
        for i, (src, dst) in enumerate(moves):
            copy = pltpu.make_async_copy(src, dst, sems.at[at, i])
            copy.start()
            copies.append(copy)
        key_msg[pl.ds(span + 2 * rows, TILE), :] = side_block(scale[index], lengths[index])
    for copy in copies:
        copy.wait()


def pack(route, lengths, deltas, anchors, scale, n, order):
    span, channels = deltas.shape[2:]
    tall = span + 2 * anchors.shape[2] + TILE
    shapes = []
    for _ in order:
        shapes += [pltpu.VMEM((tall, channels), BF), pltpu.VMEM((span, channels), BF)]
    return pl.pallas_call(
        functools.partial(pack_kernel, n, order),
        out_shape=shapes,
        in_specs=[IN_SMEM, IN_SMEM, IN_HBM, IN_HBM, IN_VMEM],
        out_specs=[IN_VMEM] * len(shapes),
        scratch_shapes=[pltpu.SemaphoreType.DMA((len(order), 4))],
        compiler_params=LIMIT,
        cost_estimate=pl.CostEstimate(
            flops=0, bytes_accessed=4 * len(order) * span * channels * 2, transcendentals=0
        ),
    )(route, lengths, deltas, anchors, scale)


def rebuild_kernel(n, k, which, rows, delta, key_msg, *refs):
    cache, mine, theirs, made, sem = refs[-5:]
    span, channels = delta.shape[0] if which else key_msg.shape[0] - 2 * rows - TILE, key_msg.shape[1]
    width = mine.shape[1]
    repeat = span // rows
    sub = lax.axis_index("sub")
    row = pick(far(n, n - k), lax.axis_index("pool"))
    side = span + 2 * rows
    scale = key_msg[side + which:side + which + 1, :].astype(F32)
    length = key_msg[side + 2:side + 3, :].astype(F32)
    base = sub * span
    for i in range(rows):
        part = pl.ds(i * repeat, repeat)
        at = span + which * rows + i
        anchor = key_msg[at:at + 1, :].astype(F32)
        value = anchor + scale * delta[part, :].astype(F32)
        keep = (base + i * repeat).astype(F32) < length
        made[part, :] = jnp.where(keep, value, jnp.float32(0.0)).astype(BF)
    copy = pltpu.make_async_copy(made, cache.at[row, which], sem)
    copy.start()
    if width == channels:
        mine[...] = made[...]
        theirs[...] = made[...]
    else:
        @pl.when(sub == 0)
        def _():
            mine[...] = made[:, :width]
            theirs[...] = made[:, width:]

        @pl.when(sub != 0)
        def _():
            mine[...] = made[:, width:]
            theirs[...] = made[:, :width]
    copy.wait()


def rebuild(which, k, n, delta, key_msg, cache, count, width, span, rows):
    channels = delta.shape[1]
    args = [vmem(delta), vmem(key_msg)]
    in_specs = [IN_VMEM, IN_VMEM]
    aliases = {}
    if cache is not None:
        args.append(cache)
        in_specs.append(IN_HBM)
        aliases = {2: 0}
    return pl.pallas_call(
        functools.partial(rebuild_kernel, n, k, which, rows),
        in_specs=in_specs,
        out_specs=[IN_HBM, IN_VMEM, IN_VMEM],
        out_shape=[
            pltpu.HBM((count, 2, span, channels), BF),
            pltpu.VMEM((span, width), BF),
            pltpu.VMEM((span, width), BF),
        ],
        scratch_shapes=[pltpu.VMEM((span, channels), BF), pltpu.SemaphoreType.DMA],
        input_output_aliases=aliases,
        compiler_params=LIMIT,
        cost_estimate=pl.CostEstimate(
            flops=4 * span * channels, bytes_accessed=6 * span * channels, transcendentals=0
        ),
    )(*args)


def attend_kernel(n, k, steps, rows, query, new_kv, key_msg, key_mine, key_other, value_mine, value_other, *refs):
    out, made, sem = refs[-3:]
    heads, wide = query.shape[1], query.shape[2]
    group = wide // PAD_STEPS
    span, width = key_mine.shape
    fresh = new_kv.shape[2]
    factor = 1.0 / math.sqrt(HEAD_DIM)
    sub = lax.axis_index("sub")
    row = pick(far(n, n - k), lax.axis_index("pool"))
    side = span + 2 * rows
    length = key_msg[side + 2:side + 3, 0:1].astype(F32)
    spot = lax.broadcasted_iota(jnp.int32, (1, span), 1)
    live_mine = (spot + sub * span).astype(F32) < length
    live_other = (spot + (1 - sub) * span).astype(F32) < length
    step = lax.broadcasted_iota(jnp.int32, (wide, fresh), 0) % PAD_STEPS
    token = lax.broadcasted_iota(jnp.int32, (wide, fresh), 1)
    causal = (token <= step) & (token < steps)
    nt = (((1,), (1,)), ((), ()))
    low = jnp.float32(-1e30)
    for j in range(heads):
        lanes = slice(j * HEAD_DIM, (j + 1) * HEAD_DIM)
        q = query[row, j]
        new_key, new_value = new_kv[row, 0, :, lanes], new_kv[row, 1, :, lanes]
        s0 = lax.dot_general(q, key_mine[:, lanes], nt, preferred_element_type=F32) * factor
        s1 = lax.dot_general(q, key_other[:, lanes], nt, preferred_element_type=F32) * factor
        s2 = lax.dot_general(q, new_key, nt, preferred_element_type=F32) * factor
        s0 = jnp.where(live_mine, s0, low)
        s1 = jnp.where(live_other, s1, low)
        s2 = jnp.where(causal, s2, low)
        top = jnp.maximum(
            jnp.max(jnp.maximum(s0, s1), axis=1, keepdims=True), jnp.max(s2, axis=1, keepdims=True)
        )
        w0 = jnp.where(live_mine, jnp.exp(s0 - top), jnp.float32(0.0))
        w1 = jnp.where(live_other, jnp.exp(s1 - top), jnp.float32(0.0))
        w2 = jnp.where(causal, jnp.exp(s2 - top), jnp.float32(0.0))
        total = jnp.sum(w0 + w1, axis=1, keepdims=True) + jnp.sum(w2, axis=1, keepdims=True)
        acc = jnp.dot(w0.astype(BF), value_mine[:, lanes], preferred_element_type=F32)
        acc = acc + jnp.dot(w1.astype(BF), value_other[:, lanes], preferred_element_type=F32)
        acc = acc + jnp.dot(w2.astype(BF), new_value, preferred_element_type=F32)
        acc = (acc / total).astype(BF)
        for g in range(group):
            at = (j * group + g) * HEAD_DIM
            made[:, at:at + HEAD_DIM] = acc[g * PAD_STEPS:g * PAD_STEPS + steps, :]
    copy = pltpu.make_async_copy(made, out.at[row], sem)
    copy.start()
    copy.wait()


def attend(k, n, query, new_kv, msg, keys, values, attended, count, steps, span, rows):
    heads, wide = query.shape[1:3]
    args = [vmem(x) for x in (query, new_kv, msg, *keys, *values)]
    in_specs = [IN_VMEM] * len(args)
    aliases = {}
    if attended is not None:
        aliases = {len(args): 0}
        args.append(attended)
        in_specs.append(IN_HBM)
    outer = heads * (wide // PAD_STEPS) * HEAD_DIM
    return pl.pallas_call(
        functools.partial(attend_kernel, n, k, steps, rows),
        in_specs=in_specs,
        out_specs=IN_HBM,
        out_shape=pltpu.HBM((count, steps, outer), BF),
        scratch_shapes=[pltpu.VMEM((steps, outer), BF), pltpu.SemaphoreType.DMA],
        input_output_aliases=aliases,
        compiler_params=LIMIT,
        cost_estimate=pl.CostEstimate(
            flops=8 * heads * wide * span * HEAD_DIM,
            bytes_accessed=8 * span * keys[0].shape[1],
            transcendentals=2 * heads * wide * span,
        ),
    )(*args)


def body(deltas, anchors, chan_scale, lengths, route, new_query, new_kv):
    n = lax.axis_size("pool")
    count, _, span, channels = deltas.shape
    rows = anchors.shape[2]
    steps = new_query.shape[1]
    q_local = new_query.shape[2] // HEAD_DIM
    heads = max(1, q_local // Q_PER_KV)
    group = q_local // heads
    width = heads * HEAD_DIM
    sub = lax.axis_index("sub")

    query = new_query.reshape(count, steps, heads, group, HEAD_DIM).transpose(0, 2, 3, 1, 4)
    query = jnp.pad(query, ((0, 0),) * 3 + ((0, PAD_STEPS - steps), (0, 0)))
    query = query.reshape(count, heads, group * PAD_STEPS, HEAD_DIM)
    fresh = new_kv if width == channels else jnp.where(
        sub == 0, new_kv[..., :width], new_kv[..., channels - width:]
    )
    fresh = jnp.pad(fresh, ((0, 0), (0, 0), (0, TILE - steps), (0, 0)))

    order = shifts_of(n)
    packed = pack(route, lengths, deltas, anchors, chan_scale, n, order + [0])
    key_msg, value_msg = {0: packed[-2]}, {0: packed[-1]}
    for at, k in enumerate(order):
        perm = list(enumerate(far(n, k)))
        key_msg[k] = lax.ppermute(packed[2 * at], "pool", perm)
        value_msg[k] = lax.ppermute(packed[2 * at + 1], "pool", perm)

    swap = [(0, 1), (1, 0)]
    cache = attended = None
    for k in [0] + order:
        parts = []
        for which, msg in ((0, key_msg[k]), (1, value_msg[k])):
            cache, mine, theirs = rebuild(
                which, k, n, msg, key_msg[k], cache, count, width, span, rows
            )
            parts.append((mine, lax.ppermute(theirs, "sub", swap)))
        attended = attend(
            k, n, query, fresh, key_msg[k], *parts, attended, count, steps, span, rows
        )
    return cache, attended


def solution(mesh):
    placed = (
        P(("parts", "pool"), None, "sub", "tp"),
        P(("parts", "pool"), None, "sub", "tp"),
        P(("parts", "pool"), None, "tp"),
        P(("parts", "pool")),
        P(("parts", "pool")),
        P(("parts", "pool"), None, ("tp", "sub")),
        P(("parts", "pool"), None, None, "tp"),
    )
    return jax.shard_map(
        body,
        mesh=mesh,
        in_specs=placed,
        out_specs=(
            P(("parts", "pool"), None, "sub", "tp"),
            P(("parts", "pool"), None, ("tp", "sub")),
        ),
        check_vma=False,
    )
```

time: 148 us -> 66.7 us (0.45)
  Pallas kernels: 102 us -> 14.4 us
  waiting for transfers between devices: 16.3 us -> 32.7 us
  starting transfers between devices: 21.9 us -> 14 us
  local copies, waits for them, and re-layouts: 6.16 us -> 4.54 us
    pallas_call x13, Pallas kernels: 102 us -> 14.4 us  [the longest x8 8.02 us: rebuild(): pl.pallas_call(functools.partial(rebuild_kernel, n, k, which, rows), in_s...]
    ppermute x14, waiting for transfers between devices: 16.3 us -> 32.7 us  [the longest x3 18.6 us: body(): key_msg[k] = lax.ppermute(packed[2 * at], 'pool', perm)]
    ppermute x14, starting transfers between devices: 21.9 us -> 14 us  [the longest x8 6.63 us: body(): parts.append((mine, lax.ppermute(theirs, 'sub', swap)))]
    unnamed x38 -> x14, local copies, waits for them, and re-layouts: 4.19 us -> 4.5 us
  transfers between devices with their start and end apart: 14 -> 14, of which waited for: 2 -> 5; matrix products, arithmetic and copies ran while one was open for 1% -> 0% of each run, Pallas kernels for 20% -> 18%
where the time goes in v2:
time: 66.7 us; the launch traced here: 66.5 us
  waiting for transfers between devices  32.7 us (49%)
  Pallas kernels  14.4 us (22%)
  starting transfers between devices  14 us (21%)
  local copies, waits for them, and re-layouts  4.54 us (7%)
  between operations  0.84 us (1%)
    ppermute x3, waiting for transfers between devices, body(): key_msg[k] = lax.ppermute(packed[2 * at], 'pool', perm)  18.6 us
    ppermute x3, waiting for transfers between devices, body(): value_msg[k] = lax.ppermute(packed[2 * at + 1], 'pool', perm)  14.1 us
    pallas_call x8, Pallas kernels, rebuild(): pl.pallas_call(functools.partial(rebuild_kernel, n, k, which, rows), in_s...  8.02 us
    ppermute x8, starting transfers between devices, body(): parts.append((mine, lax.ppermute(theirs, 'sub', swap)))  6.63 us
    pallas_call x4, Pallas kernels, attend(): pl.pallas_call(functools.partial(attend_kernel, n, k, steps, rows), in_sp...  5.27 us
    unnamed x14, local copies, waits for them, and re-layouts  4.5 us
    ppermute x3, starting transfers between devices, body(): key_msg[k] = lax.ppermute(packed[2 * at], 'pool', perm)  3.71 us
    ppermute x3, starting transfers between devices, body(): value_msg[k] = lax.ppermute(packed[2 * at + 1], 'pool', perm)  3.66 us
  transfers between devices with their start and end apart: 14, of which 5 were waited for; matrix products, arithmetic and copies ran while one was open for 0% of the time, Pallas kernels for 18%

profile of v2, /device:TPU:9, one launch (start us, length us, event | category | flops | bytes accessed | tf_op | source)
XLA Modules:
  0.0 66.5 jit_solution(14094644455292222254)
XLA Ops:
  0.6 0.0 copy-start
  0.6 1.6 %copy-done = bf16[4,2,256,512]{3,2,1,0:T(8,128)(2,1)S(1)} copy-done((bf16[4,2,256,512]{3,2,1,0:T(8,128)(2,1)S(1)}, bf16[4,2,256,512]{3,2,1,0:T(8,128)(2,1)}, u32[]{:S(2)}) %copy-start) | copy-done | bytes 2097176
  2.2 0.0 copy-start.1
  2.2 0.9 %copy-done.1 = bf16[4,2,16,512]{3,2,1,0:T(8,128)(2,1)S(1)} copy-done((bf16[4,2,16,512]{3,2,1,0:T(8,128)(2,1)S(1)}, bf16[4,2,16,512]{3,2,1,0:T(8,128)(2,1)}, u32[]{:S(2)}) %copy-start.1) | copy-done | bytes 131096
  3.1 0.0 copy-start.2
  3.1 0.7 %copy-done.2 = bf16[4,2,512]{2,1,0:T(2,128)(2,1)S(1)} copy-done((bf16[4,2,512]{2,1,0:T(2,128)(2,1)S(1)}, bf16[4,2,512]{2,1,0:T(2,128)(2,1)}, u32[]{:S(2)}) %copy-start.2) | copy-done | bytes 8216
  3.8 0.0 copy-start.3
  3.8 0.7 copy-done.3
  4.5 0.0 copy-start.4
  4.5 0.7 copy-done.4
  5.1 1.1 %shard_map.86 = (bf16[304,512]{1,0:T(8,128)(2,1)S(1)}, bf16[256,512]{1,0:T(8,128)(2,1)S(1)}, bf16[304,512]{1,0:T(8,128)(2,1)S(1)}, bf16[256,512]{1,0:T(8,128)(2,...) custom-call(s32[4]{0:T(128)S(1)} %copy-done.3, ...), custom_call_target="tpu_custom_call" | custom-call | bytes 4194304 | tf_op jit(solution)/shard_map/pallas_call | solution.py:92
  6.2 0.1 collective-permute-start.5
  6.3 2.4 %collective-permute-start.3 = (bf16[304,512]{1,0:T(8,128)(2,1)S(1)}, bf16[304,512]{1,0:T(8,128)(2,1)S(1)}, u32[]{:S(2)}, u32[]{:S(2)}) collective-permute-start(bf16[304,512]{1,0:T(8,128)(2,1)S(1)} %get-tuple-element.37), channel_id=1, source_target_pairs={{0,4},{4,12},{8,0},{12,8},{1,5},{5,13},{9,1},{13,9},{2,6},{6,14},{... | collective-permute-start | bytes 933896 | tf_op jit(solution)/shard_map/ppermute | solution.py:266
  8.7 0.1 collective-permute-start.4
  8.8 2.3 %collective-permute-start.2 = (bf16[256,512]{1,0:T(8,128)(2,1)S(1)}, bf16[256,512]{1,0:T(8,128)(2,1)S(1)}, u32[]{:S(2)}, u32[]{:S(2)}) collective-permute-start(bf16[256,512]{1,0:T(8,128)(2,1)S(1)} %get-tuple-element.36), channel_id=1, source_target_pairs={{0,4},{4,12},{8,0},{12,8},{1,5},{5,13},{9,1},{13,9},{2,6},{6,14},{... | collective-permute-start | bytes 786440 | tf_op jit(solution)/shard_map/ppermute | solution.py:267
  11.0 1.3 %collective-permute-start.1 = (bf16[304,512]{1,0:T(8,128)(2,1)S(1)}, bf16[304,512]{1,0:T(8,128)(2,1)S(1)}, u32[]{:S(2)}, u32[]{:S(2)}) collective-permute-start(bf16[304,512]{1,0:T(8,128)(2,1)S(1)} %get-tuple-element.35), channel_id=1, source_target_pairs={{0,12},{4,8},{8,4},{12,0},{1,13},{5,9},{9,5},{13,1},{2,14},{6,10},... | collective-permute-start | bytes 933896 | tf_op jit(solution)/shard_map/ppermute | solution.py:266
  12.3 3.1 %collective-permute-done.5.delta.key_msg = bf16[304,512]{1,0:T(8,128)(2,1)S(1)} collective-permute-done((bf16[304,512]{1,0:T(8,128)(2,1)S(1)}, bf16[304,512]{1,0:T(8,128)(2,1)S(1)}, u32[]{:S(2)}, u32[]{:S(2)}) %collective-permute-start.5) | collective-permute-done | bytes 311328 | tf_op jit(solution)/shard_map/ppermute | solution.py:266
  15.5 1.3 %collective-permute-start = (bf16[256,512]{1,0:T(8,128)(2,1)S(1)}, bf16[256,512]{1,0:T(8,128)(2,1)S(1)}, u32[]{:S(2)}, u32[]{:S(2)}) collective-permute-start(bf16[256,512]{1,0:T(8,128)(2,1)S(1)} %get-tuple-element.34), channel_id=1, source_target_pairs={{0,12},{4,8},{8,4},{12,0},{1,13},{5,9},{9,5},{13,1},{2,14},{6,10},... | collective-permute-start | bytes 786440 | tf_op jit(solution)/shard_map/ppermute | solution.py:267
  16.8 0.8 %shard_map.87 = (bf16[4,2,256,512]{3,2,1,0:T(8,128)(2,1)}, bf16[256,256]{1,0:T(8,128)(2,1)S(1)}, bf16[256,256]{1,0:T(8,128)(2,1)S(1)}) custom-call(bf16[304,512]{1,0:T(8,128)(2,1)S(1)} %get-tuple-element.41.delta.key_msg, bf16[304,512]{1,0:T(8,128)(2,1)S(1)} %get-tuple-element.41.delta.key_msg), custom_call_target="tpu_custom_call" | custom-call | flops 524288 | bytes 786432 | tf_op jit(solution)/shard_map/pallas_call | solution.py:150
  17.6 1.5 %shard_map.88 = (bf16[4,2,256,512]{3,2,1,0:T(8,128)(2,1)}, bf16[256,256]{1,0:T(8,128)(2,1)S(1)}, bf16[256,256]{1,0:T(8,128)(2,1)}) custom-call(bf16[256,512]{1,0:T(8,128)(2,1)S(1)} %get-tuple-element.40.delta, bf16[304,512]{1,0:T(8,128)(2,1)S(1)} %get-tuple-element.41.delta.key_msg, ...), custom_call_target="tpu_custom_call", output_to_operand_aliasing={{0}: (2, {})} | custom-call | flops 524288 | bytes 786432 | tf_op jit(solution)/shard_map/pallas_call | solution.py:150
  19.1 0.8 %shard_map.89 = (bf16[4,2,256,512]{3,2,1,0:T(8,128)(2,1)}, bf16[256,256]{1,0:T(8,128)(2,1)S(1)}, bf16[256,256]{1,0:T(8,128)(2,1)S(1)}) custom-call(bf16[304,512]{1,0:T(8,128)(2,1)S(1)} %collective-permute-done.5.delta.key_msg, bf16[304,512]{1,0:T(8,128)(2,1)S(1)} %collective-permute-done.5.delta.key_msg, ...), custom_call_target="tpu_custom_call", output_to_operand_aliasing={{0}: (2, {})} | custom-call | flops 524288 | bytes 786432 | tf_op jit(solution)/shard_map/pallas_call | solution.py:150
  19.9 7.8 %collective-permute-done.4.delta = bf16[256,512]{1,0:T(8,128)(2,1)S(1)} collective-permute-done((bf16[256,512]{1,0:T(8,128)(2,1)S(1)}, bf16[256,512]{1,0:T(8,128)(2,1)S(1)}, u32[]{:S(2)}, u32[]{:S(2)}) %collective-permute-start.4) | collective-permute-done | bytes 262176 | tf_op jit(solution)/shard_map/ppermute | solution.py:267
  27.8 2.7 %collective-permute-start.13 = (bf16[256,256]{1,0:T(8,128)(2,1)}, bf16[256,256]{1,0:T(8,128)(2,1)S(1)}, u32[]{:S(2)}, u32[]{:S(2)}) collective-permute-start(bf16[256,256]{1,0:T(8,128)(2,1)} %get-tuple-element.65), channel_id=1, source_target_pairs={{0,1},{1,0},{2,3},{3,2},{4,5},{5,4},{6,7},{7,6},{8,9},{9,8},{10,11... | collective-permute-start | bytes 393224 | tf_op jit(solution)/shard_map/ppermute | solution.py:277
  30.5 1.5 %shard_map.90 = (bf16[4,2,256,512]{3,2,1,0:T(8,128)(2,1)}, bf16[256,256]{1,0:T(8,128)(2,1)S(1)}, bf16[256,256]{1,0:T(8,128)(2,1)}) custom-call(bf16[256,512]{1,0:T(8,128)(2,1)S(1)} %collective-permute-done.4.delta, bf16[304,512]{1,0:T(8,128)(2,1)S(1)} %collective-permute-done.5.delta.key_msg, ...), custom_call_target="tpu_custom_call", output_to_operand_aliasing={{0}: (2, {})} | custom-call | flops 524288 | bytes 786432 | tf_op jit(solution)/shard_map/pallas_call | solution.py:150
  32.0 2.0 %collective-permute-done.2.delta = bf16[256,512]{1,0:T(8,128)(2,1)S(1)} collective-permute-done((bf16[256,512]{1,0:T(8,128)(2,1)S(1)}, bf16[256,512]{1,0:T(8,128)(2,1)S(1)}, u32[]{:S(2)}, u32[]{:S(2)}) %collective-permute-start.2) | collective-permute-done | bytes 262176 | tf_op jit(solution)/shard_map/ppermute | solution.py:267
  34.0 2.2 %collective-permute-start.12 = (bf16[256,256]{1,0:T(8,128)(2,1)S(1)}, bf16[256,256]{1,0:T(8,128)(2,1)S(1)}, u32[]{:S(2)}, u32[]{:S(2)}) collective-permute-start(bf16[256,256]{1,0:T(8,128)(2,1)S(1)} %get-tuple-element.63), channel_id=1, source_target_pairs={{0,1},{1,0},{2,3},{3,2},{4,5},{5,4},{6,7},{7,6},{8,9},{9,8},{10,11... | collective-permute-start | bytes 393224 | tf_op jit(solution)/shard_map/ppermute | solution.py:277
  36.2 0.0 collective-permute-done.3.delta.key_msg
  36.2 0.0 collective-permute-start.11
  36.2 0.8 %shard_map.91 = (bf16[4,2,256,512]{3,2,1,0:T(8,128)(2,1)}, bf16[256,256]{1,0:T(8,128)(2,1)S(1)}, bf16[256,256]{1,0:T(8,128)(2,1)S(1)}) custom-call(bf16[304,512]{1,0:T(8,128)(2,1)S(1)} %collective-permute-done.3.delta.key_msg, bf16[304,512]{1,0:T(8,128)(2,1)S(1)} %collective-permute-done.3.delta.key_msg, ...), custom_call_target="tpu_custom_call", output_to_operand_aliasing={{0}: (2, {})} | custom-call | flops 524288 | bytes 786432 | tf_op jit(solution)/shard_map/pallas_call | solution.py:150
  37.1 0.8 %shard_map.92 = (bf16[4,2,256,512]{3,2,1,0:T(8,128)(2,1)}, bf16[256,256]{1,0:T(8,128)(2,1)S(1)}, bf16[256,256]{1,0:T(8,128)(2,1)S(1)}) custom-call(bf16[256,512]{1,0:T(8,128)(2,1)S(1)} %collective-permute-done.2.delta, bf16[304,512]{1,0:T(8,128)(2,1)S(1)} %collective-permute-done.3.delta.key_msg, ...), custom_call_target="tpu_custom_call", output_to_operand_aliasing={{0}: (2, {})} | custom-call | flops 524288 | bytes 786432 | tf_op jit(solution)/shard_map/pallas_call | solution.py:150
  37.9 15.5 %collective-permute-done.1.delta.key_msg = bf16[304,512]{1,0:T(8,128)(2,1)S(1)} collective-permute-done((bf16[304,512]{1,0:T(8,128)(2,1)S(1)}, bf16[304,512]{1,0:T(8,128)(2,1)S(1)}, u32[]{:S(2)}, u32[]{:S(2)}) %collective-permute-start.1) | collective-permute-done | bytes 311328 | tf_op jit(solution)/shard_map/ppermute | solution.py:266
  53.4 0.6 collective-permute-start.10
  54.0 0.0 copy-start.6
  54.0 0.0 copy-start.5
  54.0 0.8 %shard_map.93 = (bf16[4,2,256,512]{3,2,1,0:T(8,128)(2,1)}, bf16[256,256]{1,0:T(8,128)(2,1)S(1)}, bf16[256,256]{1,0:T(8,128)(2,1)S(1)}) custom-call(bf16[304,512]{1,0:T(8,128)(2,1)S(1)} %collective-permute-done.1.delta.key_msg, bf16[304,512]{1,0:T(8,128)(2,1)S(1)} %collective-permute-done.1.delta.key_msg, ...), custom_call_target="tpu_custom_call", output_to_operand_aliasing={{0}: (2, {})} | custom-call | flops 524288 | bytes 786432 | tf_op jit(solution)/shard_map/pallas_call | solution.py:150
  54.8 4.2 %collective-permute-done.delta = bf16[256,512]{1,0:T(8,128)(2,1)S(1)} collective-permute-done((bf16[256,512]{1,0:T(8,128)(2,1)S(1)}, bf16[256,512]{1,0:T(8,128)(2,1)S(1)}, u32[]{:S(2)}, u32[]{:S(2)}) %collective-permute-start) | collective-permute-done | bytes 262176 | tf_op jit(solution)/shard_map/ppermute | solution.py:267
  59.0 0.5 collective-permute-start.9
  59.5 0.8 %shard_map.94 = (bf16[4,2,256,512]{3,2,1,0:T(8,128)(2,1)}, bf16[256,256]{1,0:T(8,128)(2,1)S(1)}, bf16[256,256]{1,0:T(8,128)(2,1)S(1)}) custom-call(bf16[256,512]{1,0:T(8,128)(2,1)S(1)} %collective-permute-done.delta, bf16[304,512]{1,0:T(8,128)(2,1)S(1)} %collective-permute-done.1.delta.key_msg, ...), custom_call_target="tpu_custom_call", output_to_operand_aliasing={{0}: (2, {})} | custom-call | flops 524288 | bytes 786432 | tf_op jit(solution)/shard_map/pallas_call | solution.py:150
  60.3 0.0 collective-permute-done.13.value_other
  60.3 0.1 collective-permute-start.8
  60.4 0.0 collective-permute-done.12.key_other
  60.4 0.5 collective-permute-start.7
  60.9 0.0 collective-permute-done.11.value_other
  60.9 0.1 collective-permute-start.6
  61.0 0.0 copy-done.6
  61.1 0.0 copy-done.5
  61.1 1.3 %shard_map.95.refs_0_ = bf16[4,4,2048]{2,1,0:T(4,128)(2,1)} custom-call(bf16[4,2,64,128]{3,2,1,0:T(8,128)(2,1)S(1)} %pad_bitcast_fusion.query, bf16[4,2,16,256]{3,2,1,0:T(8,128)(2,1)S(1)} %pad.9.new_kv, bf16[304,512]{1,0:T(8,128)(2,1)S(1)} %get-tuple-element.41.delta.key_msg, bf16[256,256]{1,0:T(8,128)(2,1)S(1)} %get-tuple-element.62.key_mine, ...), custom_call_target="tpu_custom_call" | custom-call | flops 33554432 | bytes 524288 | tf_op jit(solution)/shard_map/pallas_call | solution.py:226
  62.4 0.0 collective-permute-done.10.key_other
  62.4 1.3 %shard_map.96.refs_0_ = bf16[4,4,2048]{2,1,0:T(4,128)(2,1)} custom-call(bf16[4,2,64,128]{3,2,1,0:T(8,128)(2,1)S(1)} %pad_bitcast_fusion.query, bf16[4,2,16,256]{3,2,1,0:T(8,128)(2,1)S(1)} %pad.9.new_kv, bf16[304,512]{1,0:T(8,128)(2,1)S(1)} %collective-permute-done.5.delta.key_msg, ...), custom_call_target="tpu_custom_call", output_to_operand_aliasing={{}: (7, {})} | custom-call | flops 33554432 | bytes 524288 | tf_op jit(solution)/shard_map/pallas_call | solution.py:226
  63.8 0.0 collective-permute-done.9.value_other
  63.8 0.0 collective-permute-done.8.key_other
  63.8 1.3 %shard_map.97.refs_0_ = bf16[4,4,2048]{2,1,0:T(4,128)(2,1)} custom-call(bf16[4,2,64,128]{3,2,1,0:T(8,128)(2,1)S(1)} %pad_bitcast_fusion.query, bf16[4,2,16,256]{3,2,1,0:T(8,128)(2,1)S(1)} %pad.9.new_kv, bf16[304,512]{1,0:T(8,128)(2,1)S(1)} %collective-permute-done.3.delta.key_msg, ...), custom_call_target="tpu_custom_call", output_to_operand_aliasing={{}: (7, {})} | custom-call | flops 33554432 | bytes 524288 | tf_op jit(solution)/shard_map/pallas_call | solution.py:226
  65.1 0.0 collective-permute-done.7.value_other
  65.1 0.0 collective-permute-done.6.key_other
  65.1 1.3 %shard_map.98 = bf16[4,4,2048]{2,1,0:T(4,128)(2,1)} custom-call(bf16[4,2,64,128]{3,2,1,0:T(8,128)(2,1)S(1)} %pad_bitcast_fusion.query, bf16[4,2,16,256]{3,2,1,0:T(8,128)(2,1)S(1)} %pad.9.new_kv, bf16[304,512]{1,0:T(8,128)(2,1)S(1)} %collective-permute-done.1.delta.key_msg, ...), custom_call_target="tpu_custom_call", output_to_operand_aliasing={{}: (7, {})} | custom-call | flops 33554432 | bytes 524288 | tf_op jit(solution)/shard_map/pallas_call | solution.py:226
  (3 shorter events, 0.1 us)
Async XLA Ops:
  0.6 1.6 %copy-start = (bf16[4,2,256,512]{3,2,1,0:T(8,128)(2,1)S(1)}, bf16[4,2,256,512]{3,2,1,0:T(8,128)(2,1)}, u32[]{:S(2)}) copy-start(bf16[4,2,256,512]{3,2,1,0:T(8,128)(2,1)} %deltas.1) | copy-start | bytes 6291460
  2.2 0.9 %copy-start.1 = (bf16[4,2,16,512]{3,2,1,0:T(8,128)(2,1)S(1)}, bf16[4,2,16,512]{3,2,1,0:T(8,128)(2,1)}, u32[]{:S(2)}) copy-start(bf16[4,2,16,512]{3,2,1,0:T(8,128)(2,1)} %anchors.1) | copy-start | bytes 393220
  3.1 0.7 %copy-start.2 = (bf16[4,2,512]{2,1,0:T(2,128)(2,1)S(1)}, bf16[4,2,512]{2,1,0:T(2,128)(2,1)}, u32[]{:S(2)}) copy-start(bf16[4,2,512]{2,1,0:T(2,128)(2,1)} %scale.1) | copy-start | bytes 24580
  3.8 0.7 copy-start.3
  4.5 0.7 copy-start.4
  6.2 9.2 %collective-permute-start.5 = (bf16[304,512]{1,0:T(8,128)(2,1)S(1)}, bf16[304,512]{1,0:T(8,128)(2,1)S(1)}, u32[]{:S(2)}, u32[]{:S(2)}) collective-permute-start(bf16[304,512]{1,0:T(8,128)(2,1)S(1)} %get-tuple-element.39), channel_id=1, source_target_pairs={{0,8},{4,0},{8,12},{12,4},{1,9},{5,1},{9,13},{13,5},{2,10},{6,2},{... | collective-permute-start | bytes 933896 | tf_op jit(solution)/shard_map/ppermute | solution.py:266
  6.3 29.9 %collective-permute-start.3 = (bf16[304,512]{1,0:T(8,128)(2,1)S(1)}, bf16[304,512]{1,0:T(8,128)(2,1)S(1)}, u32[]{:S(2)}, u32[]{:S(2)}) collective-permute-start(bf16[304,512]{1,0:T(8,128)(2,1)S(1)} %get-tuple-element.37), channel_id=1, source_target_pairs={{0,4},{4,12},{8,0},{12,8},{1,5},{5,13},{9,1},{13,9},{2,6},{6,14},{... | collective-permute-start | bytes 933896 | tf_op jit(solution)/shard_map/ppermute | solution.py:266
  8.7 19.1 %collective-permute-start.4 = (bf16[256,512]{1,0:T(8,128)(2,1)S(1)}, bf16[256,512]{1,0:T(8,128)(2,1)S(1)}, u32[]{:S(2)}, u32[]{:S(2)}) collective-permute-start(bf16[256,512]{1,0:T(8,128)(2,1)S(1)} %get-tuple-element.38), channel_id=1, source_target_pairs={{0,8},{4,0},{8,12},{12,4},{1,9},{5,1},{9,13},{13,5},{2,10},{6,2},{... | collective-permute-start | bytes 786440 | tf_op jit(solution)/shard_map/ppermute | solution.py:267
  8.8 25.3 %collective-permute-start.2 = (bf16[256,512]{1,0:T(8,128)(2,1)S(1)}, bf16[256,512]{1,0:T(8,128)(2,1)S(1)}, u32[]{:S(2)}, u32[]{:S(2)}) collective-permute-start(bf16[256,512]{1,0:T(8,128)(2,1)S(1)} %get-tuple-element.36), channel_id=1, source_target_pairs={{0,4},{4,12},{8,0},{12,8},{1,5},{5,13},{9,1},{13,9},{2,6},{6,14},{... | collective-permute-start | bytes 786440 | tf_op jit(solution)/shard_map/ppermute | solution.py:267
  11.0 42.4 %collective-permute-start.1 = (bf16[304,512]{1,0:T(8,128)(2,1)S(1)}, bf16[304,512]{1,0:T(8,128)(2,1)S(1)}, u32[]{:S(2)}, u32[]{:S(2)}) collective-permute-start(bf16[304,512]{1,0:T(8,128)(2,1)S(1)} %get-tuple-element.35), channel_id=1, source_target_pairs={{0,12},{4,8},{8,4},{12,0},{1,13},{5,9},{9,5},{13,1},{2,14},{6,10},... | collective-permute-start | bytes 933896 | tf_op jit(solution)/shard_map/ppermute | solution.py:266
  15.5 43.5 %collective-permute-start = (bf16[256,512]{1,0:T(8,128)(2,1)S(1)}, bf16[256,512]{1,0:T(8,128)(2,1)S(1)}, u32[]{:S(2)}, u32[]{:S(2)}) collective-permute-start(bf16[256,512]{1,0:T(8,128)(2,1)S(1)} %get-tuple-element.34), channel_id=1, source_target_pairs={{0,12},{4,8},{8,4},{12,0},{1,13},{5,9},{9,5},{13,1},{2,14},{6,10},... | collective-permute-start | bytes 786440 | tf_op jit(solution)/shard_map/ppermute | solution.py:267
  27.8 32.5 %collective-permute-start.13 = (bf16[256,256]{1,0:T(8,128)(2,1)}, bf16[256,256]{1,0:T(8,128)(2,1)S(1)}, u32[]{:S(2)}, u32[]{:S(2)}) collective-permute-start(bf16[256,256]{1,0:T(8,128)(2,1)} %get-tuple-element.65), channel_id=1, source_target_pairs={{0,1},{1,0},{2,3},{3,2},{4,5},{5,4},{6,7},{7,6},{8,9},{9,8},{10,11... | collective-permute-start | bytes 393224 | tf_op jit(solution)/shard_map/ppermute | solution.py:277
  34.0 26.4 %collective-permute-start.12 = (bf16[256,256]{1,0:T(8,128)(2,1)S(1)}, bf16[256,256]{1,0:T(8,128)(2,1)S(1)}, u32[]{:S(2)}, u32[]{:S(2)}) collective-permute-start(bf16[256,256]{1,0:T(8,128)(2,1)S(1)} %get-tuple-element.63), channel_id=1, source_target_pairs={{0,1},{1,0},{2,3},{3,2},{4,5},{5,4},{6,7},{7,6},{8,9},{9,8},{10,11... | collective-permute-start | bytes 393224 | tf_op jit(solution)/shard_map/ppermute | solution.py:277
  36.2 24.7 %collective-permute-start.11 = (bf16[256,256]{1,0:T(8,128)(2,1)}, bf16[256,256]{1,0:T(8,128)(2,1)S(1)}, u32[]{:S(2)}, u32[]{:S(2)}) collective-permute-start(bf16[256,256]{1,0:T(8,128)(2,1)} %get-tuple-element.61), channel_id=1, source_target_pairs={{0,1},{1,0},{2,3},{3,2},{4,5},{5,4},{6,7},{7,6},{8,9},{9,8},{10,11... | collective-permute-start | bytes 393224 | tf_op jit(solution)/shard_map/ppermute | solution.py:277
  53.4 9.1 %collective-permute-start.10 = (bf16[256,256]{1,0:T(8,128)(2,1)S(1)}, bf16[256,256]{1,0:T(8,128)(2,1)S(1)}, u32[]{:S(2)}, u32[]{:S(2)}) collective-permute-start(bf16[256,256]{1,0:T(8,128)(2,1)S(1)} %get-tuple-element.59), channel_id=1, source_target_pairs={{0,1},{1,0},{2,3},{3,2},{4,5},{5,4},{6,7},{7,6},{8,9},{9,8},{10,11... | collective-permute-start | bytes 393224 | tf_op jit(solution)/shard_map/ppermute | solution.py:277
  54.0 7.1 %copy-start.6 = (bf16[4,2,4,512]{3,2,1,0:T(4,128)(2,1)S(1)}, bf16[4,2,4,512]{3,2,1,0:T(4,128)(2,1)}, u32[]{:S(2)}) copy-start(bf16[4,2,4,512]{3,2,1,0:T(4,128)(2,1)} %param.13) | copy-start | bytes 98308
  54.0 7.1 %copy-start.5 = (bf16[4,4,2048]{2,1,0:T(4,128)(2,1)S(1)}, bf16[4,4,2048]{2,1,0:T(4,128)(2,1)}, u32[]{:S(2)}) copy-start(bf16[4,4,2048]{2,1,0:T(4,128)(2,1)} %param.12) | copy-start | bytes 196612
  59.0 4.8 %collective-permute-start.9 = (bf16[256,256]{1,0:T(8,128)(2,1)S(1)}, bf16[256,256]{1,0:T(8,128)(2,1)S(1)}, u32[]{:S(2)}, u32[]{:S(2)}) collective-permute-start(bf16[256,256]{1,0:T(8,128)(2,1)S(1)} %get-tuple-element.57), channel_id=1, source_target_pairs={{0,1},{1,0},{2,3},{3,2},{4,5},{5,4},{6,7},{7,6},{8,9},{9,8},{10,11... | collective-permute-start | bytes 393224 | tf_op jit(solution)/shard_map/ppermute | solution.py:277
  60.3 3.4 %collective-permute-start.8 = (bf16[256,256]{1,0:T(8,128)(2,1)S(1)}, bf16[256,256]{1,0:T(8,128)(2,1)S(1)}, u32[]{:S(2)}, u32[]{:S(2)}) collective-permute-start(bf16[256,256]{1,0:T(8,128)(2,1)S(1)} %get-tuple-element.55), channel_id=1, source_target_pairs={{0,1},{1,0},{2,3},{3,2},{4,5},{5,4},{6,7},{7,6},{8,9},{9,8},{10,11... | collective-permute-start | bytes 393224 | tf_op jit(solution)/shard_map/ppermute | solution.py:277
  60.4 4.7 %collective-permute-start.7 = (bf16[256,256]{1,0:T(8,128)(2,1)S(1)}, bf16[256,256]{1,0:T(8,128)(2,1)S(1)}, u32[]{:S(2)}, u32[]{:S(2)}) collective-permute-start(bf16[256,256]{1,0:T(8,128)(2,1)S(1)} %get-tuple-element.53), channel_id=1, source_target_pairs={{0,1},{1,0},{2,3},{3,2},{4,5},{5,4},{6,7},{7,6},{8,9},{9,8},{10,11... | collective-permute-start | bytes 393224 | tf_op jit(solution)/shard_map/ppermute | solution.py:277
  60.9 4.2 %collective-permute-start.6 = (bf16[256,256]{1,0:T(8,128)(2,1)S(1)}, bf16[256,256]{1,0:T(8,128)(2,1)S(1)}, u32[]{:S(2)}, u32[]{:S(2)}) collective-permute-start(bf16[256,256]{1,0:T(8,128)(2,1)S(1)} %get-tuple-element.51), channel_id=1, source_target_pairs={{0,1},{1,0},{2,3},{3,2},{4,5},{5,4},{6,7},{7,6},{8,9},{9,8},{10,11... | collective-permute-start | bytes 393224 | tf_op jit(solution)/shard_map/ppermute | solution.py:277

commit v3 on v0

v3 whole, which is shorter than its diff:
```python
import functools
import math

import jax
import jax.numpy as jnp
from jax import lax
from jax.experimental import pallas as pl
from jax.experimental.pallas import tpu as pltpu
from jax.sharding import PartitionSpec as P

HEAD_DIM = 128
Q_PER_KV = 8
TILE = 16
PAD_STEPS = 8
BF = jnp.bfloat16
F32 = jnp.float32
LOW = -1e30
NT = (((1,), (1,)), ((), ()))

IN_VMEM = pl.BlockSpec(memory_space=pltpu.VMEM)
IN_SMEM = pl.BlockSpec(memory_space=pltpu.SMEM)
IN_HBM = pl.BlockSpec(memory_space=pltpu.HBM)
LIMIT = pltpu.CompilerParams(vmem_limit_bytes=16 * 1024 * 1024)


def vmem(x):
    return pltpu.with_memory_space_constraint(x, pltpu.VMEM)


def hbm(x):
    return pltpu.with_memory_space_constraint(x, pltpu.HBM)


def far(n, k):
    ring = (0, 2, 3, 1) if n == 4 else tuple(range(n))
    return tuple(ring[(ring.index(z) + k) % n] for z in range(n))


def pick(values, at):
    out = jnp.int32(values[0])
    for i, value in enumerate(values[1:], 1):
        out = jnp.where(at == i, jnp.int32(value), out)
    return out


class Sizes:
    def __init__(self, deltas, anchors, new_query, n):
        self.n = n
        self.count, _, self.span, self.channels = deltas.shape
        self.rows = anchors.shape[2]
        self.repeat = self.span // self.rows
        self.steps = new_query.shape[1]
        self.heads = self.channels // HEAD_DIM
        self.q_local = new_query.shape[2] // HEAD_DIM
        self.mine = max(1, self.q_local // Q_PER_KV)
        self.group = self.q_local // self.mine
        self.wide = self.group * PAD_STEPS

    def anchor_at(self, which, parts):
        return len(parts) * self.heads * self.span + which * self.heads * self.rows

    def side_at(self, parts):
        return len(parts) * self.heads * self.span + 2 * self.heads * self.rows

    def message_rows(self, parts):
        if 0 in parts:
            return self.side_at(parts) + TILE
        return len(parts) * self.heads * self.span

    def source_row(self, k):
        return pick(far(self.n, self.n - k), lax.axis_index("pool"))


def side_block(size, scale, length):
    row = lax.broadcasted_iota(jnp.int32, (TILE, HEAD_DIM), 0)
    scale = scale.astype(F32)
    out = jnp.where(row == 2 * size.heads, length.astype(F32), jnp.float32(0.0))
    for which in range(2):
        for h in range(size.heads):
            piece = scale[which:which + 1, h * HEAD_DIM:(h + 1) * HEAD_DIM]
            out = jnp.where(row == which * size.heads + h, piece, out)
    return out.astype(BF)


def pack_kernel(size, plan, route, lengths, deltas, anchors, scale, *rest):
    outs, sems = rest[:-1], rest[-1]
    z = lax.axis_index("pool")
    copies = []
    for m, (k, parts) in enumerate(plan):
        msg = outs[m]
        dest = pick(far(size.n, k), z)
        index = jnp.int32(0)
        for j in range(size.count):
            index = jnp.where(route[j] == dest, jnp.int32(j), index)
        moves = []
        for p, which in enumerate(parts):
            for h in range(size.heads):
                lanes = pl.ds(h * HEAD_DIM, HEAD_DIM)
                at = (p * size.heads + h) * size.span
                moves.append((deltas.at[index, which, :, lanes], msg.at[pl.ds(at, size.span)]))
        if 0 in parts:
            for which in range(2):
                for h in range(size.heads):
                    lanes = pl.ds(h * HEAD_DIM, HEAD_DIM)
                    at = size.anchor_at(which, parts) + h * size.rows
                    moves.append((anchors.at[index, which, :, lanes], msg.at[pl.ds(at, size.rows)]))
        for i, (src, dst) in enumerate(moves):
            copy = pltpu.make_async_copy(src, dst, sems.at[m, i])
            copy.start()
            copies.append(copy)
        if 0 in parts:
            msg[pl.ds(size.side_at(parts), TILE), :] = side_block(size, scale[index], lengths[index])
    for copy in copies:
        copy.wait()


def pack(size, plan, route, lengths, deltas, anchors, scale):
    shapes = [pltpu.VMEM((size.message_rows(parts), HEAD_DIM), BF) for _, parts in plan]
    return pl.pallas_call(
        functools.partial(pack_kernel, size, plan),
        out_shape=shapes,
        in_specs=[IN_SMEM, IN_SMEM, IN_HBM, IN_HBM, IN_VMEM],
        out_specs=[IN_VMEM] * len(shapes),
        scratch_shapes=[pltpu.SemaphoreType.DMA((len(plan), 4 * size.heads))],
        compiler_params=LIMIT,
        cost_estimate=pl.CostEstimate(
            flops=0, bytes_accessed=2 * len(plan) * size.span * size.channels * 2, transcendentals=0
        ),
    )(hbm(route), hbm(lengths), hbm(deltas), hbm(anchors), hbm(scale))


def row_copies(size, k, parts, cache, mine, theirs, sems):
    sub = lax.axis_index("sub")
    row = size.source_row(k)
    rest = size.heads - size.mine
    copies = []
    for o, (out, first) in enumerate(((mine, sub * rest), (theirs, (1 - sub) * rest))):
        if o and not rest:
            break
        for p, which in enumerate(parts):
            for j in range(size.mine):
                lanes = pl.ds(pl.multiple_of((first + j) * HEAD_DIM, HEAD_DIM), HEAD_DIM)
                at = (p * size.mine + j) * size.span
                copies.append(pltpu.make_async_copy(
                    out.at[pl.ds(at, size.span)],
                    cache.at[row, which, :, lanes],
                    sems.at[o, p * size.mine + j],
                ))
    return copies


def rebuild_kernel(size, k, parts, all_parts, store, chained, *refs):
    if parts == all_parts:
        message = tables = refs[0]
        refs = refs[1:]
    else:
        message, tables = refs[0], refs[1]
        refs = refs[2:]
    refs = refs[2 * chained:]
    cache, _, mine, theirs = refs[:4]
    sub = lax.axis_index("sub")
    rest = size.heads - size.mine
    side_at = size.side_at(all_parts)
    side = tables[side_at:side_at + TILE, :].astype(F32)
    length = side[2 * size.heads:2 * size.heads + 1, :]
    base = sub * size.span
    copies = row_copies(size, k, parts, cache, mine, theirs, refs[4]) if store else []
    at_copy = 0
    for o, out in enumerate((theirs, mine)):
        first = (1 - sub) * rest if o == 0 else sub * rest
        other = sub == 0 if o == 0 else sub != 0
        for p, which in enumerate(parts):
            for j in range(size.mine):
                h = which * size.heads + j
                scale = jnp.where(other, side[h + rest:h + rest + 1, :], side[h:h + 1, :])
                table = pl.multiple_of(
                    size.anchor_at(which, all_parts) + (first + j) * size.rows, TILE
                )
                anchor = tables[pl.ds(table, size.rows), :].astype(F32)
                source = (p * size.heads + first + j) * size.span
                to = (p * size.mine + j) * size.span
                for i in range(size.rows):
                    at = pl.multiple_of(source + i * size.repeat, TILE)
                    value = anchor[i:i + 1, :] + scale * message[pl.ds(at, size.repeat), :].astype(F32)
                    keep = (base + i * size.repeat).astype(F32) < length
                    value = jnp.where(keep, value, jnp.float32(0.0)).astype(BF)
                    out[to + i * size.repeat:to + (i + 1) * size.repeat, :] = value
    for copy in copies:
        copy.start()
    for copy in copies:
        copy.wait()


def rebuild(size, k, parts, all_parts, message, tables, state, store=True):
    args = [vmem(message)] + ([vmem(tables)] if tables is not None else [])
    in_specs = [IN_VMEM] * len(args)
    aliases = {}
    if state is not None:
        aliases = {len(args): 0, len(args) + 1: 1}
        args += list(state)
        in_specs += [IN_HBM, IN_HBM]
    given = (len(parts) * size.mine * size.span, HEAD_DIM)
    scratch = [pltpu.SemaphoreType.DMA((2, len(parts) * size.mine))] if store else []
    out = pl.pallas_call(
        functools.partial(rebuild_kernel, size, k, parts, all_parts, store, state is not None),
        in_specs=in_specs,
        out_specs=[IN_HBM, IN_HBM, IN_VMEM, IN_VMEM],
        out_shape=[
            pltpu.HBM((size.count, 2, size.span, size.channels), BF),
            pltpu.HBM((size.count, size.steps, size.q_local * HEAD_DIM), BF),
            pltpu.VMEM(given, BF),
            pltpu.VMEM(given, BF),
        ],
        scratch_shapes=scratch,
        input_output_aliases=aliases,
        compiler_params=LIMIT,
        cost_estimate=pl.CostEstimate(
            flops=4 * len(parts) * size.span * size.channels,
            bytes_accessed=6 * len(parts) * size.span * size.channels,
            transcendentals=0,
        ),
    )(*args)
    return tuple(out[:2]), out[2], out[3]


def weigh(size, j, q, new_key, key_mine, key_other, live_mine, live_other, causal):
    factor = 1.0 / math.sqrt(HEAD_DIM)
    s0 = lax.dot_general(q, key_mine, NT, preferred_element_type=F32) * factor
    s1 = lax.dot_general(q, key_other, NT, preferred_element_type=F32) * factor
    s2 = lax.dot_general(q, new_key, NT, preferred_element_type=F32) * factor
    s0 = jnp.where(live_mine, s0, jnp.float32(LOW))
    s1 = jnp.where(live_other, s1, jnp.float32(LOW))
    s2 = jnp.where(causal, s2, jnp.float32(LOW))
    top = jnp.maximum(
        jnp.max(jnp.maximum(s0, s1), axis=1, keepdims=True), jnp.max(s2, axis=1, keepdims=True)
    )
    w0 = jnp.where(live_mine, jnp.exp(s0 - top), jnp.float32(0.0))
    w1 = jnp.where(live_other, jnp.exp(s1 - top), jnp.float32(0.0))
    w2 = jnp.where(causal, jnp.exp(s2 - top), jnp.float32(0.0))
    total = jnp.sum(w0 + w1, axis=1, keepdims=True) + jnp.sum(w2, axis=1, keepdims=True)
    return w0.astype(BF), w1.astype(BF), w2.astype(BF), total


def masks(size, tables, parts, fresh):
    sub = lax.axis_index("sub")
    at = size.side_at(parts)
    side = tables[at:at + TILE, :].astype(F32)
    length = side[2 * size.heads:2 * size.heads + 1, 0:1]
    spot = lax.broadcasted_iota(jnp.int32, (1, size.span), 1)
    live_mine = (spot + sub * size.span).astype(F32) < length
    live_other = (spot + (1 - sub) * size.span).astype(F32) < length
    step = lax.broadcasted_iota(jnp.int32, (size.wide, fresh), 0) % PAD_STEPS
    token = lax.broadcasted_iota(jnp.int32, (size.wide, fresh), 1)
    return live_mine, live_other, (token <= step) & (token < size.steps)


def place_heads(size, made, j, result):
    for g in range(size.group):
        at = (j * size.group + g) * HEAD_DIM
        made[:, at:at + HEAD_DIM] = result[g * PAD_STEPS:g * PAD_STEPS + size.steps, :]


def attend_kernel(size, k, parts, query, new_kv, tables, mine, other, *refs):
    _, attended, made, sem = refs[2:]
    row = size.source_row(k)
    live_mine, live_other, causal = masks(size, tables, parts, new_kv.shape[2])
    for j in range(size.mine):
        lanes = slice(j * HEAD_DIM, (j + 1) * HEAD_DIM)
        keys = slice(j * size.span, (j + 1) * size.span)
        values = slice((size.mine + j) * size.span, (size.mine + j + 1) * size.span)
        w0, w1, w2, total = weigh(
            size, j, query[row, j], new_kv[row, 0, :, lanes], mine[keys, :], other[keys, :],
            live_mine, live_other, causal,
        )
        acc = jnp.dot(w0, mine[values, :], preferred_element_type=F32)
        acc = acc + jnp.dot(w1, other[values, :], preferred_element_type=F32)
        acc = acc + jnp.dot(w2, new_kv[row, 1, :, lanes], preferred_element_type=F32)
        place_heads(size, made, j, (acc / total).astype(BF))
    copy = pltpu.make_async_copy(made, attended.at[row], sem)
    copy.start()
    copy.wait()


def weights_kernel(size, k, parts, query, new_kv, tables, mine, other, *refs):
    weights, share, totals = refs[4:]
    row = size.source_row(k)
    live_mine, live_other, causal = masks(size, tables, parts, new_kv.shape[2])
    for j in range(size.mine):
        lanes = slice(j * HEAD_DIM, (j + 1) * HEAD_DIM)
        keys = slice(j * size.span, (j + 1) * size.span)
        w0, w1, w2, total = weigh(
            size, j, query[row, j], new_kv[row, 0, :, lanes], mine[keys, :], other[keys, :],
            live_mine, live_other, causal,
        )
        weights[j, :, :size.span] = w0
        weights[j, :, size.span:] = w1
        share[j] = jnp.dot(w2, new_kv[row, 1, :, lanes], preferred_element_type=F32)
        totals[j] = jnp.broadcast_to(total, totals.shape[1:])


def finish_kernel(size, k, parts, weights, share, totals, mine, other, theirs, *refs):
    cache, attended, made, sem, sems = refs[2:]
    row = size.source_row(k)
    copies = row_copies(size, k, parts, cache, mine, theirs, sems)
    for copy in copies:
        copy.start()
    for j in range(size.mine):
        values = slice(j * size.span, (j + 1) * size.span)
        acc = jnp.dot(weights[j, :, :size.span], mine[values, :], preferred_element_type=F32)
        acc = acc + jnp.dot(weights[j, :, size.span:], other[values, :], preferred_element_type=F32)
        place_heads(size, made, j, ((acc + share[j]) / totals[j]).astype(BF))
    copy = pltpu.make_async_copy(made, attended.at[row], sem)
    copy.start()
    for each in copies:
        each.wait()
    copy.wait()


def chained_call(size, kernel, args, state, shapes, scratch, flops):
    args = [vmem(x) for x in args]
    many = len(args)
    out = pl.pallas_call(
        kernel,
        in_specs=[IN_VMEM] * many + [IN_HBM, IN_HBM],
        out_specs=[IN_HBM, IN_HBM] + [IN_VMEM] * len(shapes),
        out_shape=[pltpu.HBM(x.shape, x.dtype) for x in state] + shapes,
        scratch_shapes=scratch,
        input_output_aliases={many: 0, many + 1: 1},
        compiler_params=LIMIT,
        cost_estimate=pl.CostEstimate(
            flops=flops,
            bytes_accessed=8 * size.span * size.channels,
            transcendentals=2 * size.mine * size.wide * size.span,
        ),
    )(*args, *state)
    return tuple(out[:2]), out[2:]


def body(deltas, anchors, chan_scale, lengths, route, new_query, new_kv):
    n = lax.axis_size("pool")
    size = Sizes(deltas, anchors, new_query, n)
    sub = lax.axis_index("sub")
    both, last = (0, 1), n - 1
    plan = [(k, both) for k in range(1, last)] + [(last, (0,)), (last, (1,)), (0, both)]

    query = new_query.reshape(size.count, size.steps, size.mine, size.group, HEAD_DIM)
    query = jnp.pad(query.transpose(0, 2, 3, 1, 4), ((0, 0),) * 3 + ((0, PAD_STEPS - size.steps), (0, 0)))
    query = query.reshape(size.count, size.mine, size.wide, HEAD_DIM)
    width = size.mine * HEAD_DIM
    fresh = new_kv if width == size.channels else jnp.where(
        sub == 0, new_kv[..., :width], new_kv[..., size.channels - width:]
    )
    fresh = jnp.pad(fresh, ((0, 0), (0, 0), (0, TILE - size.steps), (0, 0)))

    packed = dict(zip(plan, pack(size, plan, route, lengths, deltas, anchors, chan_scale)))
    message = {}
    for k, parts in plan:
        message[k, parts] = packed[k, parts]
        if k:
            message[k, parts] = lax.ppermute(packed[k, parts], "pool", list(enumerate(far(n, k))))

    def swapped(x):
        return lax.ppermute(x, "sub", [(0, 1), (1, 0)])

    flops = 8 * size.mine * size.wide * size.span * HEAD_DIM
    result = pltpu.VMEM((size.steps, size.q_local * HEAD_DIM), BF)
    one = pltpu.SemaphoreType.DMA

    def attend(k, mine, other, state):
        state, _ = chained_call(
            size, functools.partial(attend_kernel, size, k, both),
            (query, fresh, message[k, both], mine, other), state, [], [result, one], flops,
        )
        return state

    state, mine, theirs = rebuild(size, 0, both, both, message[0, both], None, None)
    held = (0, mine, swapped(theirs))
    for k in range(1, last):
        state, mine, theirs = rebuild(size, k, both, both, message[k, both], None, state)
        state = attend(*held, state)
        held = (k, mine, swapped(theirs))
    state = attend(*held, state)

    tables = message[last, (0,)]
    state, mine, theirs = rebuild(size, last, (0,), (0,), tables, None, state)
    state, (weights, share, totals) = chained_call(
        size, functools.partial(weights_kernel, size, last, (0,)),
        (query, fresh, tables, mine, swapped(theirs)), state,
        [
            pltpu.VMEM((size.mine, size.wide, 2 * size.span), BF),
            pltpu.VMEM((size.mine, size.wide, HEAD_DIM), F32),
            pltpu.VMEM((size.mine, size.wide, HEAD_DIM), F32),
        ],
        [], flops // 2,
    )
    state, mine, theirs = rebuild(size, last, (1,), (0,), message[last, (1,)], tables, state, store=False)
    state, _ = chained_call(
        size, functools.partial(finish_kernel, size, last, (1,)),
        (weights, share, totals, mine, swapped(theirs), theirs), state, [],
        [result, one, pltpu.SemaphoreType.DMA((2, size.mine))], flops // 2,
    )
    return state


def solution(mesh):
    placed = (
        P(("parts", "pool"), None, "sub", "tp"),
        P(("parts", "pool"), None, "sub", "tp"),
        P(("parts", "pool"), None, "tp"),
        P(("parts", "pool")),
        P(("parts", "pool")),
        P(("parts", "pool"), None, ("tp", "sub")),
        P(("parts", "pool"), None, None, "tp"),
    )
    return jax.shard_map(
        body,
        mesh=mesh,
        in_specs=placed,
        out_specs=(
            P(("parts", "pool"), None, "sub", "tp"),
            P(("parts", "pool"), None, ("tp", "sub")),
        ),
        check_vma=False,
    )
```

time: 165 us -> 62.1 us (0.38)
  the two profiles are of different devices: /device:TPU:9 before, /device:TPU:0 now
where the time goes in v3:
time: 62.1 us; the launch traced here: 61.9 us
  waiting for transfers between devices  28.2 us (45%)
  starting transfers between devices  18.1 us (29%)
  Pallas kernels  14 us (23%)
  between operations  0.84 us (1%)
  local copies, waits for them, and re-layouts  0.74 us (1%)
    ppermute x4, waiting for transfers between devices, body(): lax.ppermute(packed[k, parts], 'pool', list(enumerate(far(n, k))))  25.6 us
    ppermute x4, starting transfers between devices, body(): lax.ppermute(packed[k, parts], 'pool', list(enumerate(far(n, k))))  17.7 us
    pallas_call x5, Pallas kernels, chained_call(): pl.pallas_call(kernel, in_specs=[IN_VMEM] * many + [IN_HBM, IN_HBM], out_...  5.42 us
    pallas_call x5, Pallas kernels, rebuild(): pl.pallas_call(functools.partial(rebuild_kernel, size, k, parts, all_part...  4.47 us
    pallas_call x1, Pallas kernels, pack(): pl.pallas_call(functools.partial(pack_kernel, size, plan), out_shape=shap...  4.09 us
    ppermute x5, waiting for transfers between devices, swapped(): return lax.ppermute(x, 'sub', [(0, 1), (1, 0)])  2.67 us
  transfers between devices with their start and end apart: 9, of which 6 were waited for; matrix products, arithmetic and copies ran while one was open for 0% of the time, Pallas kernels for 14%

profile of v3, /device:TPU:0, one launch (start us, length us, event | category | flops | bytes accessed | tf_op | source)
XLA Modules:
  0.0 61.9 jit_solution(14624865173837665465)
XLA Ops:
  0.6 0.0 copy-start.3
  0.6 0.0 copy-start.2
  0.7 4.1 %shard_map.86 = (bf16[2192,128]{1,0:T(8,128)(2,1)}, bf16[2192,128]{1,0:T(8,128)(2,1)S(1)}, bf16[1168,128]{1,0:T(8,128)(2,1)S(1)}, bf16[1024,128]{1,0:T(8,128)(2,1)S(1)}, bf16[2192,128]{1,0:T(8,128)(2,1)S(1)}) custom-call(s32[4]{0:T(128)} %route.1, s32[4]{0:T(128)} %lengths.1, bf16[4,2,256,512]{3,2,1,0:T(8,128)(2,1)} %deltas.1, ...), custom_call_target="tpu_custom_call" | custom-call | bytes 2621440 | tf_op jit(solution)/shard_map/pallas_call | solution.py:119
  4.7 0.0 copy-start
  4.8 0.7 %copy-done = bf16[1024,128]{1,0:T(8,128)(2,1)} copy-done((bf16[1024,128]{1,0:T(8,128)(2,1)}, bf16[1024,128]{1,0:T(8,128)(2,1)S(1)}, u32[]{:S(2)}) %copy-start) | copy-done | bytes 262168
  5.4 4.0 %collective-permute-start.3 = (bf16[2192,128]{1,0:T(8,128)(2,1)}, bf16[2192,128]{1,0:T(8,128)(2,1)S(1)}, u32[]{:S(2)}, u32[]{:S(2)}) collective-permute-start(bf16[2192,128]{1,0:T(8,128)(2,1)} %get-tuple-element.43), channel_id=1, source_target_pairs={{0,8},{4,0},{8,12},{12,4},{1,9},{5,1},{9,13},{13,5},{2,10},{6,2},{... | collective-permute-start | bytes 1683464 | tf_op jit(solution)/shard_map/ppermute | solution.py:360
  9.5 1.3 %collective-permute-start.1 = (bf16[2192,128]{1,0:T(8,128)(2,1)S(1)}, bf16[2192,128]{1,0:T(8,128)(2,1)S(1)}, u32[]{:S(2)}, u32[]{:S(2)}) collective-permute-start(bf16[2192,128]{1,0:T(8,128)(2,1)S(1)} %get-tuple-element.39), channel_id=1, source_target_pairs={{0,12},{4,8},{8,4},{12,0},{1,13},{5,9},{9,5},{13,1},{2,14},{6,10},... | collective-permute-start | bytes 1683464 | tf_op jit(solution)/shard_map/ppermute | solution.py:360
  10.8 0.8 %collective-permute-start = (bf16[1168,128]{1,0:T(8,128)(2,1)S(1)}, bf16[1168,128]{1,0:T(8,128)(2,1)S(1)}, u32[]{:S(2)}, u32[]{:S(2)}) collective-permute-start(bf16[1168,128]{1,0:T(8,128)(2,1)S(1)} %get-tuple-element.38), channel_id=1, source_target_pairs={{0,4},{4,12},{8,0},{12,8},{1,5},{5,13},{9,1},{13,9},{2,6},{6,14},{... | collective-permute-start | bytes 897032 | tf_op jit(solution)/shard_map/ppermute | solution.py:360
  11.6 1.7 %shard_map.87 = (bf16[4,2,256,512]{3,2,1,0:T(8,128)(2,1)}, bf16[4,4,2048]{2,1,0:T(4,128)(2,1)}, bf16[1024,128]{1,0:T(8,128)(2,1)S(1)}, bf16[1024,128]{1,0:T(8,128)(2,1)}) custom-call(bf16[2192,128]{1,0:T(8,128)(2,1)S(1)} %get-tuple-element.40.refs_0_.tables), custom_call_target="tpu_custom_call" | custom-call | flops 1048576 | bytes 1572864 | tf_op jit(solution)/shard_map/pallas_call | solution.py:204
  13.3 0.1 collective-permute-start.2
  13.4 0.0 copy-done.3
  13.4 0.0 copy-done.2
  13.5 9.5 %collective-permute-done.3.refs_0_.tables = bf16[2192,128]{1,0:T(8,128)(2,1)S(1)} collective-permute-done((bf16[2192,128]{1,0:T(8,128)(2,1)}, bf16[2192,128]{1,0:T(8,128)(2,1)S(1)}, u32[]{:S(2)}, u32[]{:S(2)}) %collective-permute-start.3) | collective-permute-done | bytes 561184 | tf_op jit(solution)/shard_map/ppermute | solution.py:360
  23.0 1.0 %shard_map.88 = (bf16[4,2,256,512]{3,2,1,0:T(8,128)(2,1)}, bf16[4,4,2048]{2,1,0:T(4,128)(2,1)}, bf16[1024,128]{1,0:T(8,128)(2,1)S(1)}, bf16[1024,128]{1,0:T(8,128)(2,1)S(1)}) custom-call(bf16[2192,128]{1,0:T(8,128)(2,1)S(1)} %collective-permute-done.3.refs_0_.tables, ...), custom_call_target="tpu_custom_call", output_to_operand_aliasing={{0}: (1, {}), {1}: (2, {})} | custom-call | flops 1048576 | bytes 1572864 | tf_op jit(solution)/shard_map/pallas_call | solution.py:204
  23.9 0.1 collective-permute-start.5
  24.0 0.0 collective-permute-done.2.other
  24.0 1.3 %shard_map.89 = (bf16[4,2,256,512]{3,2,1,0:T(8,128)(2,1)}, bf16[4,4,2048]{2,1,0:T(4,128)(2,1)}) custom-call(bf16[4,2,64,128]{3,2,1,0:T(8,128)(2,1)S(1)} %pad_bitcast_fusion.query, bf16[4,2,16,256]{3,2,1,0:T(8,128)(2,1)S(1)} %pad.9.new_kv, bf16[2192,128]{1,0:T(8,128)(2,1)S(1)} %get-tuple-element.40.refs_0_.tables, ...), custom_call_target="tpu_custom_call", output_to_operand_aliasing={{0}: (5, {}), {1}: (6, {})} | custom-call | flops 33554432 | bytes 1048576 | tf_op jit(solution)/shard_map/pallas_call | solution.py:322
  25.3 0.0 copy-start.1
  25.3 11.3 %collective-permute-done.1.refs_0_.tables = bf16[2192,128]{1,0:T(8,128)(2,1)S(1)} collective-permute-done((bf16[2192,128]{1,0:T(8,128)(2,1)S(1)}, bf16[2192,128]{1,0:T(8,128)(2,1)S(1)}, u32[]{:S(2)}, u32[]{:S(2)}) %collective-permute-start.1) | collective-permute-done | bytes 561184 | tf_op jit(solution)/shard_map/ppermute | solution.py:360
  36.7 1.0 %shard_map.90 = (bf16[4,2,256,512]{3,2,1,0:T(8,128)(2,1)}, bf16[4,4,2048]{2,1,0:T(4,128)(2,1)}, bf16[1024,128]{1,0:T(8,128)(2,1)S(1)}, bf16[1024,128]{1,0:T(8,128)(2,1)S(1)}) custom-call(bf16[2192,128]{1,0:T(8,128)(2,1)S(1)} %collective-permute-done.1.refs_0_.tables, ...), custom_call_target="tpu_custom_call", output_to_operand_aliasing={{0}: (1, {}), {1}: (2, {})} | custom-call | flops 1048576 | bytes 1572864 | tf_op jit(solution)/shard_map/pallas_call | solution.py:204
  37.6 0.1 collective-permute-start.4
  37.7 0.0 copy-done.1
  37.7 11.5 %collective-permute-start.7 = (bf16[1024,128]{1,0:T(8,128)(2,1)S(1)}, bf16[1024,128]{1,0:T(8,128)(2,1)S(1)}, u32[]{:S(2)}, u32[]{:S(2)}) collective-permute-start(bf16[1024,128]{1,0:T(8,128)(2,1)S(1)} %copy-done.1), channel_id=1, source_target_pairs={{0,4},{4,12},{8,0},{12,8},{1,5},{5,13},{9,1},{13,9},{2,6},{6,14},{... | collective-permute-start | bytes 786440 | tf_op jit(solution)/shard_map/ppermute | solution.py:360
  49.3 0.0 collective-permute-done.5.other
  49.3 1.3 %shard_map.91 = (bf16[4,2,256,512]{3,2,1,0:T(8,128)(2,1)}, bf16[4,4,2048]{2,1,0:T(4,128)(2,1)}) custom-call(bf16[4,2,64,128]{3,2,1,0:T(8,128)(2,1)S(1)} %pad_bitcast_fusion.query, bf16[4,2,16,256]{3,2,1,0:T(8,128)(2,1)S(1)} %pad.9.new_kv, bf16[2192,128]{1,0:T(8,128)(2,1)S(1)} %collective-permute-done.3.refs_0_.tables, ...), custom_call_target="tpu_custom_call", output_to_operand_aliasing={{0}: (5, {}), {1}: (6, {})} | custom-call | flops 33554432 | bytes 1048576 | tf_op jit(solution)/shard_map/pallas_call | solution.py:322
  50.6 0.0 collective-permute-done.4.other
  50.6 1.3 %shard_map.92 = (bf16[4,2,256,512]{3,2,1,0:T(8,128)(2,1)}, bf16[4,4,2048]{2,1,0:T(4,128)(2,1)}) custom-call(bf16[4,2,64,128]{3,2,1,0:T(8,128)(2,1)S(1)} %pad_bitcast_fusion.query, bf16[4,2,16,256]{3,2,1,0:T(8,128)(2,1)S(1)} %pad.9.new_kv, bf16[2192,128]{1,0:T(8,128)(2,1)S(1)} %collective-permute-done.1.refs_0_.tables, ...), custom_call_target="tpu_custom_call", output_to_operand_aliasing={{0}: (5, {}), {1}: (6, {})} | custom-call | flops 33554432 | bytes 1048576 | tf_op jit(solution)/shard_map/pallas_call | solution.py:322
  51.9 2.1 %collective-permute-done.refs_0_.tables.refs_1_ = bf16[1168,128]{1,0:T(8,128)(2,1)S(1)} collective-permute-done((bf16[1168,128]{1,0:T(8,128)(2,1)S(1)}, bf16[1168,128]{1,0:T(8,128)(2,1)S(1)}, u32[]{:S(2)}, u32[]{:S(2)}) %collective-permute-start) | collective-permute-done | bytes 299040 | tf_op jit(solution)/shard_map/ppermute | solution.py:360
  54.0 0.8 %shard_map.93 = (bf16[4,2,256,512]{3,2,1,0:T(8,128)(2,1)}, bf16[4,4,2048]{2,1,0:T(4,128)(2,1)}, bf16[512,128]{1,0:T(8,128)(2,1)S(1)}, bf16[512,128]{1,0:T(8,128)(2,1)S(1)}) custom-call(bf16[1168,128]{1,0:T(8,128)(2,1)S(1)} %collective-permute-done.refs_0_.tables.refs_1_, ...), custom_call_target="tpu_custom_call", output_to_operand_aliasing={{0}: (1, {}), {1}: (2, {})} | custom-call | flops 524288 | bytes 786432 | tf_op jit(solution)/shard_map/pallas_call | solution.py:204
  54.8 0.1 collective-permute-start.6
  54.9 1.3 %collective-permute-done.6.other = bf16[512,128]{1,0:T(8,128)(2,1)S(1)} collective-permute-done((bf16[512,128]{1,0:T(8,128)(2,1)S(1)}, bf16[512,128]{1,0:T(8,128)(2,1)S(1)}, u32[]{:S(2)}, u32[]{:S(2)}) %collective-permute-start.6) | collective-permute-done | bytes 131104 | tf_op jit(solution)/shard_map/ppermute | solution.py:363
  56.2 0.6 %shard_map.94 = (bf16[4,2,256,512]{3,2,1,0:T(8,128)(2,1)}, bf16[4,4,2048]{2,1,0:T(4,128)(2,1)}, bf16[2,64,512]{2,1,0:T(8,128)(2,1)S(1)}, f32[2,64,128]{2,1,0:T(8,128)S(1)}, f32[2,64,128]{2,1,0:T(8,128)S(1)}) custom-call(bf16[4,2,64,128]{3,2,1,0:T(8,128)(2,1)S(1)} %pad_bitcast_fusion.query, ...), custom_call_target="tpu_custom_call", output_to_operand_aliasing={{0}: (5, {}), {1}: (6, {})} | custom-call | flops 16777216 | bytes 1048576 | tf_op jit(solution)/shard_map/pallas_call | solution.py:322
  56.9 2.7 %collective-permute-done.7.refs_0_ = bf16[1024,128]{1,0:T(8,128)(2,1)S(1)} collective-permute-done((bf16[1024,128]{1,0:T(8,128)(2,1)S(1)}, bf16[1024,128]{1,0:T(8,128)(2,1)S(1)}, u32[]{:S(2)}, u32[]{:S(2)}) %collective-permute-start.7) | collective-permute-done | bytes 262176 | tf_op jit(solution)/shard_map/ppermute | solution.py:360
  59.5 0.1 shard_map.95
  59.6 0.1 collective-permute-start.8
  59.7 1.3 %collective-permute-done.8.other = bf16[512,128]{1,0:T(8,128)(2,1)S(1)} collective-permute-done((bf16[512,128]{1,0:T(8,128)(2,1)S(1)}, bf16[512,128]{1,0:T(8,128)(2,1)S(1)}, u32[]{:S(2)}, u32[]{:S(2)}) %collective-permute-start.8) | collective-permute-done | bytes 131104 | tf_op jit(solution)/shard_map/ppermute | solution.py:363
  61.1 0.8 %shard_map.96 = (bf16[4,2,256,512]{3,2,1,0:T(8,128)(2,1)}, bf16[4,4,2048]{2,1,0:T(4,128)(2,1)}) custom-call(bf16[2,64,512]{2,1,0:T(8,128)(2,1)S(1)} %get-tuple-element.64.weights, f32[2,64,128]{2,1,0:T(8,128)S(1)} %get-tuple-element.65.share, f32[2,64,128]{2,1,0:T(8,128)S(1)} %get-tuple-element.66.totals, ...), custom_call_target="tpu_custom_call", output_to_operand_aliasing={{0}: (6, {}), {1}: (7, {})} | custom-call | flops 16777216 | bytes 1048576 | tf_op jit(solution)/shard_map/pallas_call | solution.py:322
  (3 shorter events, 0.1 us)
Async XLA Ops:
  0.6 12.7 %copy-start.3 = (bf16[4,2,4,512]{3,2,1,0:T(4,128)(2,1)S(1)}, bf16[4,2,4,512]{3,2,1,0:T(4,128)(2,1)}, u32[]{:S(2)}) copy-start(bf16[4,2,4,512]{3,2,1,0:T(4,128)(2,1)} %param.13) | copy-start | bytes 98308
  0.6 12.8 %copy-start.2 = (bf16[4,4,2048]{2,1,0:T(4,128)(2,1)S(1)}, bf16[4,4,2048]{2,1,0:T(4,128)(2,1)}, u32[]{:S(2)}) copy-start(bf16[4,4,2048]{2,1,0:T(4,128)(2,1)} %param.12) | copy-start | bytes 196612
  4.7 0.7 %copy-start = (bf16[1024,128]{1,0:T(8,128)(2,1)}, bf16[1024,128]{1,0:T(8,128)(2,1)S(1)}, u32[]{:S(2)}) copy-start(bf16[1024,128]{1,0:T(8,128)(2,1)S(1)} %get-tuple-element.67) | copy-start | bytes 786436
  5.4 17.5 %collective-permute-start.3 = (bf16[2192,128]{1,0:T(8,128)(2,1)}, bf16[2192,128]{1,0:T(8,128)(2,1)S(1)}, u32[]{:S(2)}, u32[]{:S(2)}) collective-permute-start(bf16[2192,128]{1,0:T(8,128)(2,1)} %get-tuple-element.43), channel_id=1, source_target_pairs={{0,8},{4,0},{8,12},{12,4},{1,9},{5,1},{9,13},{13,5},{2,10},{6,2},{... | collective-permute-start | bytes 1683464 | tf_op jit(solution)/shard_map/ppermute | solution.py:360
  9.5 27.2 %collective-permute-start.1 = (bf16[2192,128]{1,0:T(8,128)(2,1)S(1)}, bf16[2192,128]{1,0:T(8,128)(2,1)S(1)}, u32[]{:S(2)}, u32[]{:S(2)}) collective-permute-start(bf16[2192,128]{1,0:T(8,128)(2,1)S(1)} %get-tuple-element.39), channel_id=1, source_target_pairs={{0,12},{4,8},{8,4},{12,0},{1,13},{5,9},{9,5},{13,1},{2,14},{6,10},... | collective-permute-start | bytes 1683464 | tf_op jit(solution)/shard_map/ppermute | solution.py:360
  10.8 43.2 %collective-permute-start = (bf16[1168,128]{1,0:T(8,128)(2,1)S(1)}, bf16[1168,128]{1,0:T(8,128)(2,1)S(1)}, u32[]{:S(2)}, u32[]{:S(2)}) collective-permute-start(bf16[1168,128]{1,0:T(8,128)(2,1)S(1)} %get-tuple-element.38), channel_id=1, source_target_pairs={{0,4},{4,12},{8,0},{12,8},{1,5},{5,13},{9,1},{13,9},{2,6},{6,14},{... | collective-permute-start | bytes 897032 | tf_op jit(solution)/shard_map/ppermute | solution.py:360
  13.3 10.7 %collective-permute-start.2 = (bf16[1024,128]{1,0:T(8,128)(2,1)}, bf16[1024,128]{1,0:T(8,128)(2,1)S(1)}, u32[]{:S(2)}, u32[]{:S(2)}) collective-permute-start(bf16[1024,128]{1,0:T(8,128)(2,1)} %get-tuple-element.42), channel_id=1, source_target_pairs={{0,1},{1,0},{2,3},{3,2},{4,5},{5,4},{6,7},{7,6},{8,9},{9,8},{10,11... | collective-permute-start | bytes 786440 | tf_op jit(solution)/shard_map/ppermute | solution.py:363
  23.9 25.4 %collective-permute-start.5 = (bf16[1024,128]{1,0:T(8,128)(2,1)S(1)}, bf16[1024,128]{1,0:T(8,128)(2,1)S(1)}, u32[]{:S(2)}, u32[]{:S(2)}) collective-permute-start(bf16[1024,128]{1,0:T(8,128)(2,1)S(1)} %get-tuple-element.53), channel_id=1, source_target_pairs={{0,1},{1,0},{2,3},{3,2},{4,5},{5,4},{6,7},{7,6},{8,9},{9,8},{10,11... | collective-permute-start | bytes 786440 | tf_op jit(solution)/shard_map/ppermute | solution.py:363
  25.3 12.4 %copy-start.1 = (bf16[1024,128]{1,0:T(8,128)(2,1)S(1)}, bf16[1024,128]{1,0:T(8,128)(2,1)}, u32[]{:S(2)}) copy-start(bf16[1024,128]{1,0:T(8,128)(2,1)} %copy-done) | copy-start | bytes 786436
  37.6 13.0 %collective-permute-start.4 = (bf16[1024,128]{1,0:T(8,128)(2,1)S(1)}, bf16[1024,128]{1,0:T(8,128)(2,1)S(1)}, u32[]{:S(2)}, u32[]{:S(2)}) collective-permute-start(bf16[1024,128]{1,0:T(8,128)(2,1)S(1)} %get-tuple-element.51), channel_id=1, source_target_pairs={{0,1},{1,0},{2,3},{3,2},{4,5},{5,4},{6,7},{7,6},{8,9},{9,8},{10,11... | collective-permute-start | bytes 786440 | tf_op jit(solution)/shard_map/ppermute | solution.py:363
  37.7 21.8 %collective-permute-start.7 = (bf16[1024,128]{1,0:T(8,128)(2,1)S(1)}, bf16[1024,128]{1,0:T(8,128)(2,1)S(1)}, u32[]{:S(2)}, u32[]{:S(2)}) collective-permute-start(bf16[1024,128]{1,0:T(8,128)(2,1)S(1)} %copy-done.1), channel_id=1, source_target_pairs={{0,4},{4,12},{8,0},{12,8},{1,5},{5,13},{9,1},{13,9},{2,6},{6,14},{... | collective-permute-start | bytes 786440 | tf_op jit(solution)/shard_map/ppermute | solution.py:360
  54.8 1.4 %collective-permute-start.6 = (bf16[512,128]{1,0:T(8,128)(2,1)S(1)}, bf16[512,128]{1,0:T(8,128)(2,1)S(1)}, u32[]{:S(2)}, u32[]{:S(2)}) collective-permute-start(bf16[512,128]{1,0:T(8,128)(2,1)S(1)} %get-tuple-element.61), channel_id=1, source_target_pairs={{0,1},{1,0},{2,3},{3,2},{4,5},{5,4},{6,7},{7,6},{8,9},{9,8},{10,11... | collective-permute-start | bytes 393224 | tf_op jit(solution)/shard_map/ppermute | solution.py:363
  59.6 1.4 %collective-permute-start.8 = (bf16[512,128]{1,0:T(8,128)(2,1)S(1)}, bf16[512,128]{1,0:T(8,128)(2,1)S(1)}, u32[]{:S(2)}, u32[]{:S(2)}) collective-permute-start(bf16[512,128]{1,0:T(8,128)(2,1)S(1)} %get-tuple-element.71.theirs), channel_id=1, source_target_pairs={{0,1},{1,0},{2,3},{3,2},{4,5},{5,4},{6,7},{7,6},{8,9},{9,8},{10,11... | collective-permute-start | bytes 393224 | tf_op jit(solution)/shard_map/ppermute | solution.py:363

commit v4 on v3

--- a/solution.py
+++ b/solution.py
@@ -57,15 +57,13 @@
         self.wide = self.group * PAD_STEPS
 
     def anchor_at(self, which, parts):
-        return len(parts) * self.heads * self.span + which * self.heads * self.rows
+        return (len(parts) * self.span + parts.index(which) * self.rows) * self.heads
 
     def side_at(self, parts):
-        return len(parts) * self.heads * self.span + 2 * self.heads * self.rows
+        return len(parts) * self.heads * (self.span + self.rows)
 
     def message_rows(self, parts):
-        if 0 in parts:
-            return self.side_at(parts) + TILE
-        return len(parts) * self.heads * self.span
+        return self.side_at(parts) + (TILE if 0 in parts else 0)
 
     def source_row(self, k):
         return pick(far(self.n, self.n - k), lax.axis_index("pool"))
@@ -83,50 +81,88 @@
 
 
 def pack_kernel(size, plan, route, lengths, deltas, anchors, scale, *rest):
-    outs, sems = rest[:-1], rest[-1]
+    outs, (held, tables, sems) = rest[:-3], rest[-3:]
     z = lax.axis_index("pool")
-    copies = []
+    work = []
     for m, (k, parts) in enumerate(plan):
-        msg = outs[m]
         dest = pick(far(size.n, k), z)
         index = jnp.int32(0)
         for j in range(size.count):
             index = jnp.where(route[j] == dest, jnp.int32(j), index)
-        moves = []
-        for p, which in enumerate(parts):
-            for h in range(size.heads):
-                lanes = pl.ds(h * HEAD_DIM, HEAD_DIM)
-                at = (p * size.heads + h) * size.span
-                moves.append((deltas.at[index, which, :, lanes], msg.at[pl.ds(at, size.span)]))
+        for which in parts:
+            slot = len(work)
+            copies = (
+                pltpu.make_async_copy(deltas.at[index, which], held.at[slot], sems.at[0, slot]),
+                pltpu.make_async_copy(anchors.at[index, which], tables.at[slot], sems.at[1, slot]),
+            )
+            for copy in copies:
+                copy.start()
+            work.append((outs[m], parts, which, slot, copies))
         if 0 in parts:
-            for which in range(2):
-                for h in range(size.heads):
-                    lanes = pl.ds(h * HEAD_DIM, HEAD_DIM)
-                    at = size.anchor_at(which, parts) + h * size.rows
-                    moves.append((anchors.at[index, which, :, lanes], msg.at[pl.ds(at, size.rows)]))
-        for i, (src, dst) in enumerate(moves):
-            copy = pltpu.make_async_copy(src, dst, sems.at[m, i])
-            copy.start()
-            copies.append(copy)
-        if 0 in parts:
-            msg[pl.ds(size.side_at(parts), TILE), :] = side_block(size, scale[index], lengths[index])
-    for copy in copies:
-        copy.wait()
+            outs[m][pl.ds(size.side_at(parts), TILE), :] = side_block(size, scale[index], lengths[index])
+    for msg, parts, which, slot, copies in work:
+        for copy in copies:
+            copy.wait()
+        for h in range(size.heads):
+            lanes = slice(h * HEAD_DIM, (h + 1) * HEAD_DIM)
+            at = (parts.index(which) * size.heads + h) * size.span
+            msg[at:at + size.span, :] = held[slot, :, lanes]
+            at = size.anchor_at(which, parts) + h * size.rows
+            msg[at:at + size.rows, :] = tables[slot, :, lanes]
 
 
 def pack(size, plan, route, lengths, deltas, anchors, scale):
     shapes = [pltpu.VMEM((size.message_rows(parts), HEAD_DIM), BF) for _, parts in plan]
+    slots = sum(len(parts) for _, parts in plan)
     return pl.pallas_call(
         functools.partial(pack_kernel, size, plan),
         out_shape=shapes,
         in_specs=[IN_SMEM, IN_SMEM, IN_HBM, IN_HBM, IN_VMEM],
         out_specs=[IN_VMEM] * len(shapes),
-        scratch_shapes=[pltpu.SemaphoreType.DMA((len(plan), 4 * size.heads))],
+        scratch_shapes=[
+            pltpu.VMEM((slots, size.span, size.channels), BF),
+            pltpu.VMEM((slots, size.rows, size.channels), BF),
+            pltpu.SemaphoreType.DMA((2, slots)),
+        ],
         compiler_params=LIMIT,
         cost_estimate=pl.CostEstimate(
-            flops=0, bytes_accessed=2 * len(plan) * size.span * size.channels * 2, transcendentals=0
+            flops=0, bytes_accessed=2 * slots * size.span * size.channels, transcendentals=0
         ),
     )(hbm(route), hbm(lengths), hbm(deltas), hbm(anchors), hbm(scale))
+
+
+def arrange_kernel(size, new_query, new_kv, query, fresh, wide, tall):
+    sub = lax.axis_index("sub")
+    rest = size.heads - size.mine
+    wide[...] = jnp.zeros_like(wide)
+    tall[...] = jnp.zeros_like(tall)
+    for r in range(size.count):
+        for j in range(size.mine):
+            for g in range(size.group):
+                at = (j * size.group + g) * HEAD_DIM
+                piece = new_query[r, :, at:at + HEAD_DIM].astype(F32)
+                wide[g * PAD_STEPS:g * PAD_STEPS + size.steps, :] = piece
+            query[r, j] = wide[...].astype(BF)
+            for which in range(2):
+                own, other = (
+                    new_kv[r, which, :, h * HEAD_DIM:(h + 1) * HEAD_DIM].astype(F32) for h in (j, j + rest)
+                )
+                tall[:size.steps, :] = jnp.where(sub == 0, own, other)
+                fresh[r, which, j] = tall[...].astype(BF)
+
+
+def arrange(size, new_query, new_kv):
+    return pl.pallas_call(
+        functools.partial(arrange_kernel, size),
+        in_specs=[IN_VMEM, IN_VMEM],
+        out_specs=[IN_VMEM, IN_VMEM],
+        out_shape=[
+            pltpu.VMEM((size.count, size.mine, size.wide, HEAD_DIM), BF),
+            pltpu.VMEM((size.count, 2, size.mine, TILE, HEAD_DIM), BF),
+        ],
+        scratch_shapes=[pltpu.VMEM((size.wide, HEAD_DIM), F32), pltpu.VMEM((TILE, HEAD_DIM), F32)],
+        compiler_params=LIMIT,
+    )(hbm(new_query), hbm(new_kv))
 
 
 def row_copies(size, k, parts, cache, mine, theirs, sems):
@@ -149,18 +185,14 @@
     return copies
 
 
-def rebuild_kernel(size, k, parts, all_parts, store, chained, *refs):
-    if parts == all_parts:
-        message = tables = refs[0]
-        refs = refs[1:]
-    else:
-        message, tables = refs[0], refs[1]
-        refs = refs[2:]
+def rebuild_kernel(size, k, parts, store, chained, *refs):
+    message, tables = refs[0], refs[0 if 0 in parts else 1]
+    refs = refs[1 if 0 in parts else 2:]
     refs = refs[2 * chained:]
     cache, _, mine, theirs = refs[:4]
     sub = lax.axis_index("sub")
     rest = size.heads - size.mine
-    side_at = size.side_at(all_parts)
+    side_at = size.side_at(parts if 0 in parts else (0,))
     side = tables[side_at:side_at + TILE, :].astype(F32)
     length = side[2 * size.heads:2 * size.heads + 1, :]
     base = sub * size.span
@@ -174,9 +206,9 @@
                 h = which * size.heads + j
                 scale = jnp.where(other, side[h + rest:h + rest + 1, :], side[h:h + 1, :])
                 table = pl.multiple_of(
-                    size.anchor_at(which, all_parts) + (first + j) * size.rows, TILE
+                    size.anchor_at(which, parts) + (first + j) * size.rows, TILE
                 )
-                anchor = tables[pl.ds(table, size.rows), :].astype(F32)
+                anchor = message[pl.ds(table, size.rows), :].astype(F32)
                 source = (p * size.heads + first + j) * size.span
                 to = (p * size.mine + j) * size.span
                 for i in range(size.rows):
@@ -191,7 +223,7 @@
         copy.wait()
 
 
-def rebuild(size, k, parts, all_parts, message, tables, state, store=True):
+def rebuild(size, k, parts, message, tables, state, store=True):
     args = [vmem(message)] + ([vmem(tables)] if tables is not None else [])
     in_specs = [IN_VMEM] * len(args)
     aliases = {}
@@ -202,7 +234,7 @@
     given = (len(parts) * size.mine * size.span, HEAD_DIM)
     scratch = [pltpu.SemaphoreType.DMA((2, len(parts) * size.mine))] if store else []
     out = pl.pallas_call(
-        functools.partial(rebuild_kernel, size, k, parts, all_parts, store, state is not None),
+        functools.partial(rebuild_kernel, size, k, parts, store, state is not None),
         in_specs=in_specs,
         out_specs=[IN_HBM, IN_HBM, IN_VMEM, IN_VMEM],
         out_shape=[
@@ -263,18 +295,17 @@
 def attend_kernel(size, k, parts, query, new_kv, tables, mine, other, *refs):
     _, attended, made, sem = refs[2:]
     row = size.source_row(k)
-    live_mine, live_other, causal = masks(size, tables, parts, new_kv.shape[2])
+    live_mine, live_other, causal = masks(size, tables, parts, new_kv.shape[3])
     for j in range(size.mine):
-        lanes = slice(j * HEAD_DIM, (j + 1) * HEAD_DIM)
         keys = slice(j * size.span, (j + 1) * size.span)
         values = slice((size.mine + j) * size.span, (size.mine + j + 1) * size.span)
         w0, w1, w2, total = weigh(
-            size, j, query[row, j], new_kv[row, 0, :, lanes], mine[keys, :], other[keys, :],
+            size, j, query[row, j], new_kv[row, 0, j], mine[keys, :], other[keys, :],
             live_mine, live_other, causal,
         )
         acc = jnp.dot(w0, mine[values, :], preferred_element_type=F32)
         acc = acc + jnp.dot(w1, other[values, :], preferred_element_type=F32)
-        acc = acc + jnp.dot(w2, new_kv[row, 1, :, lanes], preferred_element_type=F32)
+        acc = acc + jnp.dot(w2, new_kv[row, 1, j], preferred_element_type=F32)
         place_heads(size, made, j, (acc / total).astype(BF))
     copy = pltpu.make_async_copy(made, attended.at[row], sem)
     copy.start()
@@ -284,17 +315,16 @@
 def weights_kernel(size, k, parts, query, new_kv, tables, mine, other, *refs):
     weights, share, totals = refs[4:]
     row = size.source_row(k)
-    live_mine, live_other, causal = masks(size, tables, parts, new_kv.shape[2])
+    live_mine, live_other, causal = masks(size, tables, parts, new_kv.shape[3])
     for j in range(size.mine):
-        lanes = slice(j * HEAD_DIM, (j + 1) * HEAD_DIM)
         keys = slice(j * size.span, (j + 1) * size.span)
         w0, w1, w2, total = weigh(
-            size, j, query[row, j], new_kv[row, 0, :, lanes], mine[keys, :], other[keys, :],
+            size, j, query[row, j], new_kv[row, 0, j], mine[keys, :], other[keys, :],
             live_mine, live_other, causal,
         )
         weights[j, :, :size.span] = w0
         weights[j, :, size.span:] = w1
-        share[j] = jnp.dot(w2, new_kv[row, 1, :, lanes], preferred_element_type=F32)
+        share[j] = jnp.dot(w2, new_kv[row, 1, j], preferred_element_type=F32)
         totals[j] = jnp.broadcast_to(total, totals.shape[1:])
 
 
@@ -339,25 +369,15 @@
 def body(deltas, anchors, chan_scale, lengths, route, new_query, new_kv):
     n = lax.axis_size("pool")
     size = Sizes(deltas, anchors, new_query, n)
-    sub = lax.axis_index("sub")
     both, last = (0, 1), n - 1
     plan = [(k, both) for k in range(1, last)] + [(last, (0,)), (last, (1,)), (0, both)]
-
-    query = new_query.reshape(size.count, size.steps, size.mine, size.group, HEAD_DIM)
-    query = jnp.pad(query.transpose(0, 2, 3, 1, 4), ((0, 0),) * 3 + ((0, PAD_STEPS - size.steps), (0, 0)))
-    query = query.reshape(size.count, size.mine, size.wide, HEAD_DIM)
-    width = size.mine * HEAD_DIM
-    fresh = new_kv if width == size.channels else jnp.where(
-        sub == 0, new_kv[..., :width], new_kv[..., size.channels - width:]
-    )
-    fresh = jnp.pad(fresh, ((0, 0), (0, 0), (0, TILE - size.steps), (0, 0)))
-
-    packed = dict(zip(plan, pack(size, plan, route, lengths, deltas, anchors, chan_scale)))
+    query, fresh = arrange(size, new_query, new_kv)
     message = {}
-    for k, parts in plan:
-        message[k, parts] = packed[k, parts]
-        if k:
-            message[k, parts] = lax.ppermute(packed[k, parts], "pool", list(enumerate(far(n, k))))
+    for part in (plan[:1], plan[1:]):
+        for (k, parts), msg in zip(part, pack(size, part, route, lengths, deltas, anchors, chan_scale)):
+            if k:
+                msg = lax.ppermute(msg, "pool", list(enumerate(far(n, k))))
+            message[k, parts] = msg
 
     def swapped(x):
         return lax.ppermute(x, "sub", [(0, 1), (1, 0)])
@@ -373,19 +393,23 @@
         )
         return state
 
-    state, mine, theirs = rebuild(size, 0, both, both, message[0, both], None, None)
-    held = (0, mine, swapped(theirs))
-    for k in range(1, last):
-        state, mine, theirs = rebuild(size, k, both, both, message[k, both], None, state)
-        state = attend(*held, state)
-        held = (k, mine, swapped(theirs))
-    state = attend(*held, state)
-
-    tables = message[last, (0,)]
-    state, mine, theirs = rebuild(size, last, (0,), (0,), tables, None, state)
+    def take(k, parts, state, store=True):
+        tables = None if 0 in parts else message[last, (0,)]
+        state, mine, theirs = rebuild(size, k, parts, message[k, parts], tables, state, store)
+        return state, mine, theirs, swapped(theirs)
+
+    state, held = None, []
+    for k in range(last):
+        state, mine, _, other = take(k, both, state)
+        held.append((k, mine, other))
+        if 0 < k < last - 1:
+            state = attend(*held.pop(0), state)
+    state, mine, _, other = take(last, (0,), state)
+    for each in held:
+        state = attend(*each, state)
     state, (weights, share, totals) = chained_call(
         size, functools.partial(weights_kernel, size, last, (0,)),
-        (query, fresh, tables, mine, swapped(theirs)), state,
+        (query, fresh, message[last, (0,)], mine, other), state,
         [
             pltpu.VMEM((size.mine, size.wide, 2 * size.span), BF),
             pltpu.VMEM((size.mine, size.wide, HEAD_DIM), F32),
@@ -393,10 +417,10 @@
         ],
         [], flops // 2,
     )
-    state, mine, theirs = rebuild(size, last, (1,), (0,), message[last, (1,)], tables, state, store=False)
+    state, mine, theirs, other = take(last, (1,), state, store=False)
     state, _ = chained_call(
         size, functools.partial(finish_kernel, size, last, (1,)),
-        (weights, share, totals, mine, swapped(theirs), theirs), state, [],
+        (weights, share, totals, mine, other, theirs), state, [],
         [result, one, pltpu.SemaphoreType.DMA((2, size.mine))], flops // 2,
     )
     return state

time: 62.1 us -> 59.1 us (0.952)
  starting transfers between devices: 18.1 us -> 8.96 us
  waiting for transfers between devices: 28.2 us -> 34.8 us
  local copies, waits for them, and re-layouts: 0.74 us -> 0 us
    ppermute x4, starting transfers between devices: 17.7 us -> 8.59 us  [body(): msg = lax.ppermute(msg, 'pool', list(enumerate(far(n, k))))]
    ppermute x4, waiting for transfers between devices: 25.6 us -> 33.4 us  [body(): msg = lax.ppermute(msg, 'pool', list(enumerate(far(n, k))))]
    ppermute x5, waiting for transfers between devices: 2.67 us -> 1.34 us  [swapped(): return lax.ppermute(x, 'sub', [(0, 1), (1, 0)])]
    unnamed x8 -> x0, local copies, waits for them, and re-layouts: 0.7 us -> none
    pallas_call x5 -> x6, Pallas kernels: 4.47 us -> 4.71 us  [the longest x5 3.77 us: rebuild(): pl.pallas_call(functools.partial(rebuild_kernel, size, k, parts, store, s...]
    pallas_call x1 -> x2, Pallas kernels: 4.09 us -> 4.15 us  [pack(): pl.pallas_call(functools.partial(pack_kernel, size, plan), out_shape=shap...]
  transfers between devices with their start and end apart: 9 -> 9, of which waited for: 6 -> 5; matrix products, arithmetic and copies ran while one was open for 0% -> 0% of each run, Pallas kernels for 14% -> 20%
where the time goes in v4:
time: 59.1 us; the launch traced here: 58.8 us
  waiting for transfers between devices  34.8 us (59%)
  Pallas kernels  14.3 us (24%)
  starting transfers between devices  8.96 us (15%)
  between operations  0.77 us (1%)
    ppermute x4, waiting for transfers between devices, body(): msg = lax.ppermute(msg, 'pool', list(enumerate(far(n, k))))  33.4 us
    ppermute x4, starting transfers between devices, body(): msg = lax.ppermute(msg, 'pool', list(enumerate(far(n, k))))  8.59 us
    pallas_call x5, Pallas kernels, chained_call(): pl.pallas_call(kernel, in_specs=[IN_VMEM] * many + [IN_HBM, IN_HBM], out_...  5.44 us
    pallas_call x2, Pallas kernels, pack(): pl.pallas_call(functools.partial(pack_kernel, size, plan), out_shape=shap...  4.15 us
    pallas_call x5, Pallas kernels, rebuild(): pl.pallas_call(functools.partial(rebuild_kernel, size, k, parts, store, s...  3.77 us
    ppermute x5, waiting for transfers between devices, swapped(): return lax.ppermute(x, 'sub', [(0, 1), (1, 0)])  1.34 us
  transfers between devices with their start and end apart: 9, of which 5 were waited for; matrix products, arithmetic and copies ran while one was open for 0% of the time, Pallas kernels for 20%

profile of v4, /device:TPU:0, one launch (start us, length us, event | category | flops | bytes accessed | tf_op | source)
XLA Modules:
  0.0 58.8 jit_solution(17245031423157502140)
XLA Ops:
  0.6 1.9 %shard_map.89 = bf16[2192,128]{1,0:T(8,128)(2,1)S(1)} custom-call(s32[4]{0:T(128)} %route.3, s32[4]{0:T(128)} %lengths.3, bf16[4,2,256,512]{3,2,1,0:T(8,128)(2,1)} %deltas.3, bf16[4,2,16,512]{3,2,1,0:T(8,128)(2,1)} %anchors.3, bf16[4,2,512]{2,1,0:T(2,128)(2,1)} %scale.3), custom_call_target="tpu_custom_call" | custom-call | bytes 524288 | tf_op jit(solution)/shard_map/pallas_call | solution.py:117
  2.5 4.1 %collective-permute-start.3 = (bf16[2192,128]{1,0:T(8,128)(2,1)S(1)}, bf16[2192,128]{1,0:T(8,128)(2,1)S(1)}, u32[]{:S(2)}, u32[]{:S(2)}) collective-permute-start(bf16[2192,128]{1,0:T(8,128)(2,1)S(1)} %shard_map.89), channel_id=1, source_target_pairs={{0,8},{4,0},{8,12},{12,4},{1,9},{5,1},{9,13},{13,5},{2,10},{6,2},{... | collective-permute-start | bytes 1683464 | tf_op jit(solution)/shard_map/ppermute | solution.py:379
  6.6 2.3 %shard_map.87 = (bf16[2192,128]{1,0:T(8,128)(2,1)S(1)}, bf16[1104,128]{1,0:T(8,128)(2,1)S(1)}, bf16[1088,128]{1,0:T(8,128)(2,1)S(1)}, bf16[2192,128]{1,0:T(8,128)(2,1)S(1)}) custom-call(s32[4]{0:T(128)} %route.3, s32[4]{0:T(128)} %lengths.3, bf16[4,2,256,512]{3,2,1,0:T(8,128)(2,1)} %deltas.3, bf16[4,2,16,512]{3,2,1,0:T(8,128)(2,1)} %anchors.3, ...), custom_call_target="tpu_custom_call" | custom-call | bytes 1572864 | tf_op jit(solution)/shard_map/pallas_call | solution.py:117
  8.9 1.4 %collective-permute-start.1 = (bf16[2192,128]{1,0:T(8,128)(2,1)S(1)}, bf16[2192,128]{1,0:T(8,128)(2,1)S(1)}, u32[]{:S(2)}, u32[]{:S(2)}) collective-permute-start(bf16[2192,128]{1,0:T(8,128)(2,1)S(1)} %get-tuple-element.42), channel_id=1, source_target_pairs={{0,12},{4,8},{8,4},{12,0},{1,13},{5,9},{9,5},{13,1},{2,14},{6,10},... | collective-permute-start | bytes 1683464 | tf_op jit(solution)/shard_map/ppermute | solution.py:379
  10.3 1.0 %shard_map.88 = (bf16[4,2,256,512]{3,2,1,0:T(8,128)(2,1)}, bf16[4,4,2048]{2,1,0:T(4,128)(2,1)}, bf16[1024,128]{1,0:T(8,128)(2,1)S(1)}, bf16[1024,128]{1,0:T(8,128)(2,1)S(1)}) custom-call(bf16[2192,128]{1,0:T(8,128)(2,1)S(1)} %get-tuple-element.43.refs_0_.tables), custom_call_target="tpu_custom_call" | custom-call | flops 1048576 | bytes 1572864 | tf_op jit(solution)/shard_map/pallas_call | solution.py:236
  11.3 0.1 collective-permute-start.2
  11.3 0.8 %collective-permute-start = (bf16[1104,128]{1,0:T(8,128)(2,1)S(1)}, bf16[1104,128]{1,0:T(8,128)(2,1)S(1)}, u32[]{:S(2)}, u32[]{:S(2)}) collective-permute-start(bf16[1104,128]{1,0:T(8,128)(2,1)S(1)} %get-tuple-element.41), channel_id=1, source_target_pairs={{0,4},{4,12},{8,0},{12,8},{1,5},{5,13},{9,1},{13,9},{2,6},{6,14},{... | collective-permute-start | bytes 847880 | tf_op jit(solution)/shard_map/ppermute | solution.py:379
  12.2 2.2 %collective-permute-start.7 = (bf16[1088,128]{1,0:T(8,128)(2,1)S(1)}, bf16[1088,128]{1,0:T(8,128)(2,1)S(1)}, u32[]{:S(2)}, u32[]{:S(2)}) collective-permute-start(bf16[1088,128]{1,0:T(8,128)(2,1)S(1)} %get-tuple-element.69), channel_id=1, source_target_pairs={{0,4},{4,12},{8,0},{12,8},{1,5},{5,13},{9,1},{13,9},{2,6},{6,14},{... | collective-permute-start | bytes 835592 | tf_op jit(solution)/shard_map/ppermute | solution.py:379
  14.4 0.9 %shard_map.86 = (bf16[4,2,64,128]{3,2,1,0:T(8,128)(2,1)S(1)}, bf16[4,2,2,16,128]{4,3,2,1,0:T(8,128)(2,1)S(1)}) custom-call(bf16[4,4,2048]{2,1,0:T(4,128)(2,1)} %new_query.1, bf16[4,2,4,512]{3,2,1,0:T(4,128)(2,1)} %new_kv.1), custom_call_target="tpu_custom_call" | custom-call | tf_op jit(solution)/shard_map/pallas_call | solution.py:155
  15.4 4.4 %collective-permute-done.3.refs_0_.tables = bf16[2192,128]{1,0:T(8,128)(2,1)S(1)} collective-permute-done((bf16[2192,128]{1,0:T(8,128)(2,1)S(1)}, bf16[2192,128]{1,0:T(8,128)(2,1)S(1)}, u32[]{:S(2)}, u32[]{:S(2)}) %collective-permute-start.3) | collective-permute-done | bytes 561184 | tf_op jit(solution)/shard_map/ppermute | solution.py:379
  19.7 1.0 %shard_map.90 = (bf16[4,2,256,512]{3,2,1,0:T(8,128)(2,1)}, bf16[4,4,2048]{2,1,0:T(4,128)(2,1)}, bf16[1024,128]{1,0:T(8,128)(2,1)S(1)}, bf16[1024,128]{1,0:T(8,128)(2,1)S(1)}) custom-call(bf16[2192,128]{1,0:T(8,128)(2,1)S(1)} %collective-permute-done.3.refs_0_.tables, ...), custom_call_target="tpu_custom_call", output_to_operand_aliasing={{0}: (1, {}), {1}: (2, {})} | custom-call | flops 1048576 | bytes 1572864 | tf_op jit(solution)/shard_map/pallas_call | solution.py:236
  20.7 0.1 collective-permute-start.6
  20.8 0.0 collective-permute-done.2.other
  20.8 1.3 %shard_map.91 = (bf16[4,2,256,512]{3,2,1,0:T(8,128)(2,1)}, bf16[4,4,2048]{2,1,0:T(4,128)(2,1)}) custom-call(bf16[4,2,64,128]{3,2,1,0:T(8,128)(2,1)S(1)} %get-tuple-element.39.query, bf16[4,2,2,16,128]{4,3,2,1,0:T(8,128)(2,1)S(1)} %get-tuple-element.40.new_kv, ...), custom_call_target="tpu_custom_call", output_to_operand_aliasing={{0}: (5, {}), {1}: (6, {})} | custom-call | flops 33554432 | bytes 1048576 | tf_op jit(solution)/shard_map/pallas_call | solution.py:352
  22.1 11.5 %collective-permute-done.1.refs_0_.tables = bf16[2192,128]{1,0:T(8,128)(2,1)S(1)} collective-permute-done((bf16[2192,128]{1,0:T(8,128)(2,1)S(1)}, bf16[2192,128]{1,0:T(8,128)(2,1)S(1)}, u32[]{:S(2)}, u32[]{:S(2)}) %collective-permute-start.1) | collective-permute-done | bytes 561184 | tf_op jit(solution)/shard_map/ppermute | solution.py:379
  33.6 1.0 %shard_map.92 = (bf16[4,2,256,512]{3,2,1,0:T(8,128)(2,1)}, bf16[4,4,2048]{2,1,0:T(4,128)(2,1)}, bf16[1024,128]{1,0:T(8,128)(2,1)S(1)}, bf16[1024,128]{1,0:T(8,128)(2,1)S(1)}) custom-call(bf16[2192,128]{1,0:T(8,128)(2,1)S(1)} %collective-permute-done.1.refs_0_.tables, ...), custom_call_target="tpu_custom_call", output_to_operand_aliasing={{0}: (1, {}), {1}: (2, {})} | custom-call | flops 1048576 | bytes 1572864 | tf_op jit(solution)/shard_map/pallas_call | solution.py:236
  34.5 0.1 collective-permute-start.5
  34.6 15.9 %collective-permute-done.refs_0_.tables.refs_1_ = bf16[1104,128]{1,0:T(8,128)(2,1)S(1)} collective-permute-done((bf16[1104,128]{1,0:T(8,128)(2,1)S(1)}, bf16[1104,128]{1,0:T(8,128)(2,1)S(1)}, u32[]{:S(2)}, u32[]{:S(2)}) %collective-permute-start) | collective-permute-done | bytes 282656 | tf_op jit(solution)/shard_map/ppermute | solution.py:379
  50.6 0.8 %shard_map.93 = (bf16[4,2,256,512]{3,2,1,0:T(8,128)(2,1)}, bf16[4,4,2048]{2,1,0:T(4,128)(2,1)}, bf16[512,128]{1,0:T(8,128)(2,1)S(1)}, bf16[512,128]{1,0:T(8,128)(2,1)S(1)}) custom-call(bf16[1104,128]{1,0:T(8,128)(2,1)S(1)} %collective-permute-done.refs_0_.tables.refs_1_, ...), custom_call_target="tpu_custom_call", output_to_operand_aliasing={{0}: (1, {}), {1}: (2, {})} | custom-call | flops 524288 | bytes 786432 | tf_op jit(solution)/shard_map/pallas_call | solution.py:236
  51.4 0.1 collective-permute-start.4
  51.4 0.0 collective-permute-done.6.other
  51.5 1.3 %shard_map.94 = (bf16[4,2,256,512]{3,2,1,0:T(8,128)(2,1)}, bf16[4,4,2048]{2,1,0:T(4,128)(2,1)}) custom-call(bf16[4,2,64,128]{3,2,1,0:T(8,128)(2,1)S(1)} %get-tuple-element.39.query, bf16[4,2,2,16,128]{4,3,2,1,0:T(8,128)(2,1)S(1)} %get-tuple-element.40.new_kv, ...), custom_call_target="tpu_custom_call", output_to_operand_aliasing={{0}: (5, {}), {1}: (6, {})} | custom-call | flops 33554432 | bytes 1048576 | tf_op jit(solution)/shard_map/pallas_call | solution.py:352
  52.8 0.0 collective-permute-done.5.other
  52.8 1.3 %shard_map.95 = (bf16[4,2,256,512]{3,2,1,0:T(8,128)(2,1)}, bf16[4,4,2048]{2,1,0:T(4,128)(2,1)}) custom-call(bf16[4,2,64,128]{3,2,1,0:T(8,128)(2,1)S(1)} %get-tuple-element.39.query, bf16[4,2,2,16,128]{4,3,2,1,0:T(8,128)(2,1)S(1)} %get-tuple-element.40.new_kv, ...), custom_call_target="tpu_custom_call", output_to_operand_aliasing={{0}: (5, {}), {1}: (6, {})} | custom-call | flops 33554432 | bytes 1048576 | tf_op jit(solution)/shard_map/pallas_call | solution.py:352
  54.1 0.0 collective-permute-done.4.other
  54.1 0.7 %shard_map.96 = (bf16[4,2,256,512]{3,2,1,0:T(8,128)(2,1)}, bf16[4,4,2048]{2,1,0:T(4,128)(2,1)}, bf16[2,64,512]{2,1,0:T(8,128)(2,1)S(1)}, f32[2,64,128]{2,1,0:T(8,128)S(1)}, f32[2,64,128]{2,1,0:T(8,128)S(1)}) custom-call(bf16[4,2,64,128]{3,2,1,0:T(8,128)(2,1)S(1)} %get-tuple-element.39.query, ...), custom_call_target="tpu_custom_call", output_to_operand_aliasing={{0}: (5, {}), {1}: (6, {})} | custom-call | flops 16777216 | bytes 1048576 | tf_op jit(solution)/shard_map/pallas_call | solution.py:352
  54.8 1.7 %collective-permute-done.7.refs_0_ = bf16[1088,128]{1,0:T(8,128)(2,1)S(1)} collective-permute-done((bf16[1088,128]{1,0:T(8,128)(2,1)S(1)}, bf16[1088,128]{1,0:T(8,128)(2,1)S(1)}, u32[]{:S(2)}, u32[]{:S(2)}) %collective-permute-start.7) | collective-permute-done | bytes 278560 | tf_op jit(solution)/shard_map/ppermute | solution.py:379
  56.4 0.1 shard_map.97
  56.5 0.1 collective-permute-start.8
  56.6 1.3 %collective-permute-done.8.other = bf16[512,128]{1,0:T(8,128)(2,1)S(1)} collective-permute-done((bf16[512,128]{1,0:T(8,128)(2,1)S(1)}, bf16[512,128]{1,0:T(8,128)(2,1)S(1)}, u32[]{:S(2)}, u32[]{:S(2)}) %collective-permute-start.8) | collective-permute-done | bytes 131104 | tf_op jit(solution)/shard_map/ppermute | solution.py:383
  58.0 0.8 %shard_map.98 = (bf16[4,2,256,512]{3,2,1,0:T(8,128)(2,1)}, bf16[4,4,2048]{2,1,0:T(4,128)(2,1)}) custom-call(bf16[2,64,512]{2,1,0:T(8,128)(2,1)S(1)} %get-tuple-element.66.weights, f32[2,64,128]{2,1,0:T(8,128)S(1)} %get-tuple-element.67.share, f32[2,64,128]{2,1,0:T(8,128)S(1)} %get-tuple-element.68.totals, ...), custom_call_target="tpu_custom_call", output_to_operand_aliasing={{0}: (6, {}), {1}: (7, {})} | custom-call | flops 16777216 | bytes 1048576 | tf_op jit(solution)/shard_map/pallas_call | solution.py:352
Async XLA Ops:
  2.5 17.3 %collective-permute-start.3 = (bf16[2192,128]{1,0:T(8,128)(2,1)S(1)}, bf16[2192,128]{1,0:T(8,128)(2,1)S(1)}, u32[]{:S(2)}, u32[]{:S(2)}) collective-permute-start(bf16[2192,128]{1,0:T(8,128)(2,1)S(1)} %shard_map.89), channel_id=1, source_target_pairs={{0,8},{4,0},{8,12},{12,4},{1,9},{5,1},{9,13},{13,5},{2,10},{6,2},{... | collective-permute-start | bytes 1683464 | tf_op jit(solution)/shard_map/ppermute | solution.py:379
  8.9 24.7 %collective-permute-start.1 = (bf16[2192,128]{1,0:T(8,128)(2,1)S(1)}, bf16[2192,128]{1,0:T(8,128)(2,1)S(1)}, u32[]{:S(2)}, u32[]{:S(2)}) collective-permute-start(bf16[2192,128]{1,0:T(8,128)(2,1)S(1)} %get-tuple-element.42), channel_id=1, source_target_pairs={{0,12},{4,8},{8,4},{12,0},{1,13},{5,9},{9,5},{13,1},{2,14},{6,10},... | collective-permute-start | bytes 1683464 | tf_op jit(solution)/shard_map/ppermute | solution.py:379
  11.3 9.5 %collective-permute-start.2 = (bf16[1024,128]{1,0:T(8,128)(2,1)S(1)}, bf16[1024,128]{1,0:T(8,128)(2,1)S(1)}, u32[]{:S(2)}, u32[]{:S(2)}) collective-permute-start(bf16[1024,128]{1,0:T(8,128)(2,1)S(1)} %get-tuple-element.45), channel_id=1, source_target_pairs={{0,1},{1,0},{2,3},{3,2},{4,5},{5,4},{6,7},{7,6},{8,9},{9,8},{10,11... | collective-permute-start | bytes 786440 | tf_op jit(solution)/shard_map/ppermute | solution.py:383
  11.3 39.2 %collective-permute-start = (bf16[1104,128]{1,0:T(8,128)(2,1)S(1)}, bf16[1104,128]{1,0:T(8,128)(2,1)S(1)}, u32[]{:S(2)}, u32[]{:S(2)}) collective-permute-start(bf16[1104,128]{1,0:T(8,128)(2,1)S(1)} %get-tuple-element.41), channel_id=1, source_target_pairs={{0,4},{4,12},{8,0},{12,8},{1,5},{5,13},{9,1},{13,9},{2,6},{6,14},{... | collective-permute-start | bytes 847880 | tf_op jit(solution)/shard_map/ppermute | solution.py:379
  12.2 44.2 %collective-permute-start.7 = (bf16[1088,128]{1,0:T(8,128)(2,1)S(1)}, bf16[1088,128]{1,0:T(8,128)(2,1)S(1)}, u32[]{:S(2)}, u32[]{:S(2)}) collective-permute-start(bf16[1088,128]{1,0:T(8,128)(2,1)S(1)} %get-tuple-element.69), channel_id=1, source_target_pairs={{0,4},{4,12},{8,0},{12,8},{1,5},{5,13},{9,1},{13,9},{2,6},{6,14},{... | collective-permute-start | bytes 835592 | tf_op jit(solution)/shard_map/ppermute | solution.py:379
  20.7 30.7 %collective-permute-start.6 = (bf16[1024,128]{1,0:T(8,128)(2,1)S(1)}, bf16[1024,128]{1,0:T(8,128)(2,1)S(1)}, u32[]{:S(2)}, u32[]{:S(2)}) collective-permute-start(bf16[1024,128]{1,0:T(8,128)(2,1)S(1)} %get-tuple-element.59), channel_id=1, source_target_pairs={{0,1},{1,0},{2,3},{3,2},{4,5},{5,4},{6,7},{7,6},{8,9},{9,8},{10,11... | collective-permute-start | bytes 786440 | tf_op jit(solution)/shard_map/ppermute | solution.py:383
  34.5 18.2 %collective-permute-start.5 = (bf16[1024,128]{1,0:T(8,128)(2,1)S(1)}, bf16[1024,128]{1,0:T(8,128)(2,1)S(1)}, u32[]{:S(2)}, u32[]{:S(2)}) collective-permute-start(bf16[1024,128]{1,0:T(8,128)(2,1)S(1)} %get-tuple-element.57), channel_id=1, source_target_pairs={{0,1},{1,0},{2,3},{3,2},{4,5},{5,4},{6,7},{7,6},{8,9},{9,8},{10,11... | collective-permute-start | bytes 786440 | tf_op jit(solution)/shard_map/ppermute | solution.py:383
  51.4 2.8 %collective-permute-start.4 = (bf16[512,128]{1,0:T(8,128)(2,1)S(1)}, bf16[512,128]{1,0:T(8,128)(2,1)S(1)}, u32[]{:S(2)}, u32[]{:S(2)}) collective-permute-start(bf16[512,128]{1,0:T(8,128)(2,1)S(1)} %get-tuple-element.55), channel_id=1, source_target_pairs={{0,1},{1,0},{2,3},{3,2},{4,5},{5,4},{6,7},{7,6},{8,9},{9,8},{10,11... | collective-permute-start | bytes 393224 | tf_op jit(solution)/shard_map/ppermute | solution.py:383
  56.5 1.4 %collective-permute-start.8 = (bf16[512,128]{1,0:T(8,128)(2,1)S(1)}, bf16[512,128]{1,0:T(8,128)(2,1)S(1)}, u32[]{:S(2)}, u32[]{:S(2)}) collective-permute-start(bf16[512,128]{1,0:T(8,128)(2,1)S(1)} %get-tuple-element.73.theirs), channel_id=1, source_target_pairs={{0,1},{1,0},{2,3},{3,2},{4,5},{5,4},{6,7},{7,6},{8,9},{9,8},{10,11... | collective-permute-start | bytes 393224 | tf_op jit(solution)/shard_map/ppermute | solution.py:383

commit v5 on v4

--- a/solution.py
+++ b/solution.py
@@ -11,7 +11,6 @@
 HEAD_DIM = 128
 Q_PER_KV = 8
 TILE = 16
-PAD_STEPS = 8
 BF = jnp.bfloat16
 F32 = jnp.float32
 LOW = -1e30
@@ -54,7 +53,7 @@
         self.q_local = new_query.shape[2] // HEAD_DIM
         self.mine = max(1, self.q_local // Q_PER_KV)
         self.group = self.q_local // self.mine
-        self.wide = self.group * PAD_STEPS
+        self.wide = self.group * self.steps
 
     def anchor_at(self, which, parts):
         return (len(parts) * self.span + parts.index(which) * self.rows) * self.heads
@@ -134,14 +133,13 @@
 def arrange_kernel(size, new_query, new_kv, query, fresh, wide, tall):
     sub = lax.axis_index("sub")
     rest = size.heads - size.mine
-    wide[...] = jnp.zeros_like(wide)
     tall[...] = jnp.zeros_like(tall)
     for r in range(size.count):
         for j in range(size.mine):
             for g in range(size.group):
                 at = (j * size.group + g) * HEAD_DIM
                 piece = new_query[r, :, at:at + HEAD_DIM].astype(F32)
-                wide[g * PAD_STEPS:g * PAD_STEPS + size.steps, :] = piece
+                wide[g * size.steps:(g + 1) * size.steps, :] = piece
             query[r, j] = wide[...].astype(BF)
             for which in range(2):
                 own, other = (
@@ -185,19 +183,17 @@
     return copies
 
 
-def rebuild_kernel(size, k, parts, store, chained, *refs):
+def rebuild_kernel(size, parts, chained, *refs):
     message, tables = refs[0], refs[0 if 0 in parts else 1]
     refs = refs[1 if 0 in parts else 2:]
     refs = refs[2 * chained:]
-    cache, _, mine, theirs = refs[:4]
+    _, _, mine, theirs = refs
     sub = lax.axis_index("sub")
     rest = size.heads - size.mine
     side_at = size.side_at(parts if 0 in parts else (0,))
     side = tables[side_at:side_at + TILE, :].astype(F32)
     length = side[2 * size.heads:2 * size.heads + 1, :]
     base = sub * size.span
-    copies = row_copies(size, k, parts, cache, mine, theirs, refs[4]) if store else []
-    at_copy = 0
     for o, out in enumerate((theirs, mine)):
         first = (1 - sub) * rest if o == 0 else sub * rest
         other = sub == 0 if o == 0 else sub != 0
@@ -217,13 +213,9 @@
                     keep = (base + i * size.repeat).astype(F32) < length
                     value = jnp.where(keep, value, jnp.float32(0.0)).astype(BF)
                     out[to + i * size.repeat:to + (i + 1) * size.repeat, :] = value
-    for copy in copies:
-        copy.start()
-    for copy in copies:
-        copy.wait()
-
-
-def rebuild(size, k, parts, message, tables, state, store=True):
+
+
+def rebuild(size, parts, message, tables, state):
     args = [vmem(message)] + ([vmem(tables)] if tables is not None else [])
     in_specs = [IN_VMEM] * len(args)
     aliases = {}
@@ -232,9 +224,8 @@
         args += list(state)
         in_specs += [IN_HBM, IN_HBM]
     given = (len(parts) * size.mine * size.span, HEAD_DIM)
-    scratch = [pltpu.SemaphoreType.DMA((2, len(parts) * size.mine))] if store else []
     out = pl.pallas_call(
-        functools.partial(rebuild_kernel, size, k, parts, store, state is not None),
+        functools.partial(rebuild_kernel, size, parts, state is not None),
         in_specs=in_specs,
         out_specs=[IN_HBM, IN_HBM, IN_VMEM, IN_VMEM],
         out_shape=[
@@ -243,7 +234,6 @@
             pltpu.VMEM(given, BF),
             pltpu.VMEM(given, BF),
         ],
-        scratch_shapes=scratch,
         input_output_aliases=aliases,
         compiler_params=LIMIT,
         cost_estimate=pl.CostEstimate(
@@ -281,21 +271,35 @@
     spot = lax.broadcasted_iota(jnp.int32, (1, size.span), 1)
     live_mine = (spot + sub * size.span).astype(F32) < length
     live_other = (spot + (1 - sub) * size.span).astype(F32) < length
-    step = lax.broadcasted_iota(jnp.int32, (size.wide, fresh), 0) % PAD_STEPS
+    step = lax.broadcasted_iota(jnp.int32, (size.wide, fresh), 0) % size.steps
     token = lax.broadcasted_iota(jnp.int32, (size.wide, fresh), 1)
     return live_mine, live_other, (token <= step) & (token < size.steps)
 
 
-def place_heads(size, made, j, result):
-    for g in range(size.group):
-        at = (j * size.group + g) * HEAD_DIM
-        made[:, at:at + HEAD_DIM] = result[g * PAD_STEPS:g * PAD_STEPS + size.steps, :]
-
-
-def attend_kernel(size, k, parts, query, new_kv, tables, mine, other, *refs):
-    _, attended, made, sem = refs[2:]
+def start_store(size, k, parts, cache, mine, theirs, sems):
+    copies = row_copies(size, k, parts, cache, mine, theirs, sems)
+    for copy in copies:
+        copy.start()
+    return copies
+
+
+def store_heads(size, k, flat, made, attended, sem, copies):
+    for j in range(size.mine):
+        for g in range(size.group):
+            at = (j * size.group + g) * HEAD_DIM
+            made[:, at:at + HEAD_DIM] = flat[j, g * size.steps:(g + 1) * size.steps, :].astype(BF)
+    copy = pltpu.make_async_copy(made, attended.at[size.source_row(k)], sem)
+    copy.start()
+    for each in copies:
+        each.wait()
+    copy.wait()
+
+
+def attend_kernel(size, k, query, new_kv, tables, mine, other, theirs, *refs):
+    cache, attended, made, flat, sem, sems = refs[2:]
     row = size.source_row(k)
-    live_mine, live_other, causal = masks(size, tables, parts, new_kv.shape[3])
+    copies = start_store(size, k, (0, 1), cache, mine, theirs, sems)
+    live_mine, live_other, causal = masks(size, tables, (0, 1), new_kv.shape[3])
     for j in range(size.mine):
         keys = slice(j * size.span, (j + 1) * size.span)
         values = slice((size.mine + j) * size.span, (size.mine + j + 1) * size.span)
@@ -306,16 +310,15 @@
         acc = jnp.dot(w0, mine[values, :], preferred_element_type=F32)
         acc = acc + jnp.dot(w1, other[values, :], preferred_element_type=F32)
         acc = acc + jnp.dot(w2, new_kv[row, 1, j], preferred_element_type=F32)
-        place_heads(size, made, j, (acc / total).astype(BF))
-    copy = pltpu.make_async_copy(made, attended.at[row], sem)
-    copy.start()
-    copy.wait()
-
-
-def weights_kernel(size, k, parts, query, new_kv, tables, mine, other, *refs):
-    weights, share, totals = refs[4:]
+        flat[j] = acc / total
+    store_heads(size, k, flat, made, attended, sem, copies)
+
+
+def weights_kernel(size, k, query, new_kv, tables, mine, other, theirs, *refs):
+    cache, _, weights, share, totals, sems = refs[2:]
     row = size.source_row(k)
-    live_mine, live_other, causal = masks(size, tables, parts, new_kv.shape[3])
+    copies = start_store(size, k, (0,), cache, mine, theirs, sems)
+    live_mine, live_other, causal = masks(size, tables, (0,), new_kv.shape[3])
     for j in range(size.mine):
         keys = slice(j * size.span, (j + 1) * size.span)
         w0, w1, w2, total = weigh(
@@ -326,24 +329,31 @@
         weights[j, :, size.span:] = w1
         share[j] = jnp.dot(w2, new_kv[row, 1, j], preferred_element_type=F32)
         totals[j] = jnp.broadcast_to(total, totals.shape[1:])
-
-
-def finish_kernel(size, k, parts, weights, share, totals, mine, other, theirs, *refs):
-    cache, attended, made, sem, sems = refs[2:]
-    row = size.source_row(k)
-    copies = row_copies(size, k, parts, cache, mine, theirs, sems)
     for copy in copies:
-        copy.start()
+        copy.wait()
+
+
+def half_kernel(size, k, weights, share, mine, theirs, *refs):
+    cache, _, half, sems = refs[2:]
+    copies = start_store(size, k, (1,), cache, mine, theirs, sems)
     for j in range(size.mine):
         values = slice(j * size.span, (j + 1) * size.span)
-        acc = jnp.dot(weights[j, :, :size.span], mine[values, :], preferred_element_type=F32)
-        acc = acc + jnp.dot(weights[j, :, size.span:], other[values, :], preferred_element_type=F32)
-        place_heads(size, made, j, ((acc + share[j]) / totals[j]).astype(BF))
-    copy = pltpu.make_async_copy(made, attended.at[row], sem)
-    copy.start()
-    for each in copies:
-        each.wait()
-    copy.wait()
+        half[j] = share[j] + jnp.dot(
+            weights[j, :, :size.span], mine[values, :], preferred_element_type=F32
+        )
+    for copy in copies:
+        copy.wait()
+
+
+def finish_kernel(size, k, weights, half, totals, other, *refs):
+    _, attended, made, flat, sem = refs[2:]
+    for j in range(size.mine):
+        values = slice(j * size.span, (j + 1) * size.span)
+        acc = half[j] + jnp.dot(
+            weights[j, :, size.span:], other[values, :], preferred_element_type=F32
+        )
+        flat[j] = acc / totals[j]
+    store_heads(size, k, flat, made, attended, sem, ())
 
 
 def chained_call(size, kernel, args, state, shapes, scratch, flops):
@@ -383,45 +393,48 @@
         return lax.ppermute(x, "sub", [(0, 1), (1, 0)])
 
     flops = 8 * size.mine * size.wide * size.span * HEAD_DIM
-    result = pltpu.VMEM((size.steps, size.q_local * HEAD_DIM), BF)
-    one = pltpu.SemaphoreType.DMA
-
-    def attend(k, mine, other, state):
+    rows = [
+        pltpu.VMEM((size.steps, size.q_local * HEAD_DIM), BF),
+        pltpu.VMEM((size.mine, size.wide, HEAD_DIM), F32),
+        pltpu.SemaphoreType.DMA,
+    ]
+    sems = pltpu.SemaphoreType.DMA((2, 2 * size.mine))
+    wide = pltpu.VMEM((size.mine, size.wide, HEAD_DIM), F32)
+
+    def attend(k, mine, other, theirs, state):
         state, _ = chained_call(
-            size, functools.partial(attend_kernel, size, k, both),
-            (query, fresh, message[k, both], mine, other), state, [], [result, one], flops,
+            size, functools.partial(attend_kernel, size, k),
+            (query, fresh, message[k, both], mine, other, theirs), state, [], rows + [sems], flops,
         )
         return state
 
-    def take(k, parts, state, store=True):
+    def take(k, parts, state):
         tables = None if 0 in parts else message[last, (0,)]
-        state, mine, theirs = rebuild(size, k, parts, message[k, parts], tables, state, store)
-        return state, mine, theirs, swapped(theirs)
+        state, mine, theirs = rebuild(size, parts, message[k, parts], tables, state)
+        return state, mine, swapped(theirs), theirs
 
     state, held = None, []
     for k in range(last):
-        state, mine, _, other = take(k, both, state)
-        held.append((k, mine, other))
+        state, *each = take(k, both, state)
+        held.append((k, *each))
         if 0 < k < last - 1:
             state = attend(*held.pop(0), state)
-    state, mine, _, other = take(last, (0,), state)
+    state, *keys = take(last, (0,), state)
     for each in held:
         state = attend(*each, state)
     state, (weights, share, totals) = chained_call(
-        size, functools.partial(weights_kernel, size, last, (0,)),
-        (query, fresh, message[last, (0,)], mine, other), state,
-        [
-            pltpu.VMEM((size.mine, size.wide, 2 * size.span), BF),
-            pltpu.VMEM((size.mine, size.wide, HEAD_DIM), F32),
-            pltpu.VMEM((size.mine, size.wide, HEAD_DIM), F32),
-        ],
-        [], flops // 2,
-    )
-    state, mine, theirs, other = take(last, (1,), state, store=False)
+        size, functools.partial(weights_kernel, size, last),
+        (query, fresh, message[last, (0,)], *keys), state,
+        [pltpu.VMEM((size.mine, size.wide, 2 * size.span), BF), wide, wide], [sems], flops // 2,
+    )
+    state, mine, other, theirs = take(last, (1,), state)
+    state, (half,) = chained_call(
+        size, functools.partial(half_kernel, size, last),
+        (weights, share, mine, theirs), state, [wide], [sems], flops // 4,
+    )
     state, _ = chained_call(
-        size, functools.partial(finish_kernel, size, last, (1,)),
-        (weights, share, totals, mine, other, theirs), state, [],
-        [result, one, pltpu.SemaphoreType.DMA((2, size.mine))], flops // 2,
+        size, functools.partial(finish_kernel, size, last),
+        (weights, half, totals, other), state, [], rows, flops // 4,
     )
     return state
 

time: 59.1 us -> 59.1 us (level)
  Pallas kernels: 14.3 us -> 12.7 us
  waiting for transfers between devices: 34.8 us -> 36.3 us
    pallas_call x5, Pallas kernels: 3.77 us -> 0.78 us  [rebuild(): pl.pallas_call(functools.partial(rebuild_kernel, size, parts, state is no...]
    ppermute x4, waiting for transfers between devices: 33.4 us -> 35.7 us  [body(): msg = lax.ppermute(msg, 'pool', list(enumerate(far(n, k))))]
    pallas_call x5 -> x6, Pallas kernels: 5.44 us -> 6.83 us  [chained_call(): pl.pallas_call(kernel, in_specs=[IN_VMEM] * many + [IN_HBM, IN_HBM], out_...]
    ppermute x5, waiting for transfers between devices: 1.34 us -> 0.55 us  [swapped(): return lax.ppermute(x, 'sub', [(0, 1), (1, 0)])]
  transfers between devices with their start and end apart: 9 -> 9, of which waited for: 5 -> 5; matrix products, arithmetic and copies ran while one was open for 0% -> 0% of each run, Pallas kernels for 20% -> 17%
where the time goes in v5:
time: 59.1 us; the launch traced here: 58.7 us
  waiting for transfers between devices  36.3 us (61%)
  Pallas kernels  12.7 us (21%)
  starting transfers between devices  8.96 us (15%)
  between operations  0.77 us (1%)
    ppermute x4, waiting for transfers between devices, body(): msg = lax.ppermute(msg, 'pool', list(enumerate(far(n, k))))  35.7 us
    ppermute x4, starting transfers between devices, body(): msg = lax.ppermute(msg, 'pool', list(enumerate(far(n, k))))  8.59 us
    pallas_call x6, Pallas kernels, chained_call(): pl.pallas_call(kernel, in_specs=[IN_VMEM] * many + [IN_HBM, IN_HBM], out_...  6.83 us
    pallas_call x2, Pallas kernels, pack(): pl.pallas_call(functools.partial(pack_kernel, size, plan), out_shape=shap...  4.15 us
  transfers between devices with their start and end apart: 9, of which 5 were waited for; matrix products, arithmetic and copies ran while one was open for 0% of the time, Pallas kernels for 17%

profile of v5, /device:TPU:0, one launch (start us, length us, event | category | flops | bytes accessed | tf_op | source)
XLA Modules:
  0.0 58.7 jit_solution(11588865278559401113)
XLA Ops:
  0.6 1.9 %shard_map.89 = bf16[2192,128]{1,0:T(8,128)(2,1)S(1)} custom-call(s32[4]{0:T(128)} %route.3, s32[4]{0:T(128)} %lengths.3, bf16[4,2,256,512]{3,2,1,0:T(8,128)(2,1)} %deltas.3, bf16[4,2,16,512]{3,2,1,0:T(8,128)(2,1)} %anchors.3, bf16[4,2,512]{2,1,0:T(2,128)(2,1)} %scale.3), custom_call_target="tpu_custom_call" | custom-call | bytes 524288 | tf_op jit(solution)/shard_map/pallas_call | solution.py:116
  2.5 4.1 %collective-permute-start.3 = (bf16[2192,128]{1,0:T(8,128)(2,1)S(1)}, bf16[2192,128]{1,0:T(8,128)(2,1)S(1)}, u32[]{:S(2)}, u32[]{:S(2)}) collective-permute-start(bf16[2192,128]{1,0:T(8,128)(2,1)S(1)} %shard_map.89), channel_id=1, source_target_pairs={{0,8},{4,0},{8,12},{12,4},{1,9},{5,1},{9,13},{13,5},{2,10},{6,2},{... | collective-permute-start | bytes 1683464 | tf_op jit(solution)/shard_map/ppermute | solution.py:389
  6.6 2.3 %shard_map.87 = (bf16[2192,128]{1,0:T(8,128)(2,1)S(1)}, bf16[1104,128]{1,0:T(8,128)(2,1)S(1)}, bf16[1088,128]{1,0:T(8,128)(2,1)S(1)}, bf16[2192,128]{1,0:T(8,128)(2,1)S(1)}) custom-call(s32[4]{0:T(128)} %route.3, s32[4]{0:T(128)} %lengths.3, bf16[4,2,256,512]{3,2,1,0:T(8,128)(2,1)} %deltas.3, bf16[4,2,16,512]{3,2,1,0:T(8,128)(2,1)} %anchors.3, ...), custom_call_target="tpu_custom_call" | custom-call | bytes 1572864 | tf_op jit(solution)/shard_map/pallas_call | solution.py:116
  8.9 1.4 %collective-permute-start.1 = (bf16[2192,128]{1,0:T(8,128)(2,1)S(1)}, bf16[2192,128]{1,0:T(8,128)(2,1)S(1)}, u32[]{:S(2)}, u32[]{:S(2)}) collective-permute-start(bf16[2192,128]{1,0:T(8,128)(2,1)S(1)} %get-tuple-element.45), channel_id=1, source_target_pairs={{0,12},{4,8},{8,4},{12,0},{1,13},{5,9},{9,5},{13,1},{2,14},{6,10},... | collective-permute-start | bytes 1683464 | tf_op jit(solution)/shard_map/ppermute | solution.py:389
  10.3 0.2 shard_map.88
  10.5 0.1 collective-permute-start.2
  10.6 0.8 %collective-permute-start = (bf16[1104,128]{1,0:T(8,128)(2,1)S(1)}, bf16[1104,128]{1,0:T(8,128)(2,1)S(1)}, u32[]{:S(2)}, u32[]{:S(2)}) collective-permute-start(bf16[1104,128]{1,0:T(8,128)(2,1)S(1)} %get-tuple-element.44), channel_id=1, source_target_pairs={{0,4},{4,12},{8,0},{12,8},{1,5},{5,13},{9,1},{13,9},{2,6},{6,14},{... | collective-permute-start | bytes 847880 | tf_op jit(solution)/shard_map/ppermute | solution.py:389
  11.4 2.2 %collective-permute-start.7 = (bf16[1088,128]{1,0:T(8,128)(2,1)S(1)}, bf16[1088,128]{1,0:T(8,128)(2,1)S(1)}, u32[]{:S(2)}, u32[]{:S(2)}) collective-permute-start(bf16[1088,128]{1,0:T(8,128)(2,1)S(1)} %get-tuple-element.71), channel_id=1, source_target_pairs={{0,4},{4,12},{8,0},{12,8},{1,5},{5,13},{9,1},{13,9},{2,6},{6,14},{... | collective-permute-start | bytes 835592 | tf_op jit(solution)/shard_map/ppermute | solution.py:389
  13.7 0.9 %shard_map.86 = (bf16[4,2,32,128]{3,2,1,0:T(8,128)(2,1)S(1)}, bf16[4,2,2,16,128]{4,3,2,1,0:T(8,128)(2,1)S(1)}) custom-call(bf16[4,4,2048]{2,1,0:T(4,128)(2,1)} %new_query.1, bf16[4,2,4,512]{3,2,1,0:T(4,128)(2,1)} %new_kv.1), custom_call_target="tpu_custom_call" | custom-call | tf_op jit(solution)/shard_map/pallas_call | solution.py:153
  14.6 5.1 %collective-permute-done.3.refs_0_.tables = bf16[2192,128]{1,0:T(8,128)(2,1)S(1)} collective-permute-done((bf16[2192,128]{1,0:T(8,128)(2,1)S(1)}, bf16[2192,128]{1,0:T(8,128)(2,1)S(1)}, u32[]{:S(2)}, u32[]{:S(2)}) %collective-permute-start.3) | collective-permute-done | bytes 561184 | tf_op jit(solution)/shard_map/ppermute | solution.py:389
  19.7 0.2 shard_map.90
  19.9 0.1 collective-permute-start.6
  20.0 0.0 collective-permute-done.2.other
  20.0 1.3 %shard_map.91 = (bf16[4,2,256,512]{3,2,1,0:T(8,128)(2,1)}, bf16[4,4,2048]{2,1,0:T(4,128)(2,1)}) custom-call(bf16[4,2,32,128]{3,2,1,0:T(8,128)(2,1)S(1)} %get-tuple-element.42.query, bf16[4,2,2,16,128]{4,3,2,1,0:T(8,128)(2,1)S(1)} %get-tuple-element.43.new_kv, ...), custom_call_target="tpu_custom_call", output_to_operand_aliasing={{0}: (6, {}), {1}: (7, {})} | custom-call | flops 16777216 | bytes 1048576 | tf_op jit(solution)/shard_map/pallas_call | solution.py:362
  21.4 12.2 %collective-permute-done.1.refs_0_.tables = bf16[2192,128]{1,0:T(8,128)(2,1)S(1)} collective-permute-done((bf16[2192,128]{1,0:T(8,128)(2,1)S(1)}, bf16[2192,128]{1,0:T(8,128)(2,1)S(1)}, u32[]{:S(2)}, u32[]{:S(2)}) %collective-permute-start.1) | collective-permute-done | bytes 561184 | tf_op jit(solution)/shard_map/ppermute | solution.py:389
  33.6 0.2 shard_map.92
  33.8 0.1 collective-permute-start.5
  33.8 16.7 %collective-permute-done.refs_0_.tables.refs_1_ = bf16[1104,128]{1,0:T(8,128)(2,1)S(1)} collective-permute-done((bf16[1104,128]{1,0:T(8,128)(2,1)S(1)}, bf16[1104,128]{1,0:T(8,128)(2,1)S(1)}, u32[]{:S(2)}, u32[]{:S(2)}) %collective-permute-start) | collective-permute-done | bytes 282656 | tf_op jit(solution)/shard_map/ppermute | solution.py:389
  50.6 0.1 shard_map.93
  50.7 0.1 collective-permute-start.4
  50.7 0.0 collective-permute-done.6.other
  50.8 1.3 %shard_map.94 = (bf16[4,2,256,512]{3,2,1,0:T(8,128)(2,1)}, bf16[4,4,2048]{2,1,0:T(4,128)(2,1)}) custom-call(bf16[4,2,32,128]{3,2,1,0:T(8,128)(2,1)S(1)} %get-tuple-element.42.query, bf16[4,2,2,16,128]{4,3,2,1,0:T(8,128)(2,1)S(1)} %get-tuple-element.43.new_kv, ...), custom_call_target="tpu_custom_call", output_to_operand_aliasing={{0}: (6, {}), {1}: (7, {})} | custom-call | flops 16777216 | bytes 1048576 | tf_op jit(solution)/shard_map/pallas_call | solution.py:362
  52.1 0.0 collective-permute-done.5.other
  52.1 1.3 %shard_map.95 = (bf16[4,2,256,512]{3,2,1,0:T(8,128)(2,1)}, bf16[4,4,2048]{2,1,0:T(4,128)(2,1)}) custom-call(bf16[4,2,32,128]{3,2,1,0:T(8,128)(2,1)S(1)} %get-tuple-element.42.query, bf16[4,2,2,16,128]{4,3,2,1,0:T(8,128)(2,1)S(1)} %get-tuple-element.43.new_kv, ...), custom_call_target="tpu_custom_call", output_to_operand_aliasing={{0}: (6, {}), {1}: (7, {})} | custom-call | flops 16777216 | bytes 1048576 | tf_op jit(solution)/shard_map/pallas_call | solution.py:362
  53.5 0.0 collective-permute-done.4.other
  53.5 1.3 %shard_map.96 = (bf16[4,2,256,512]{3,2,1,0:T(8,128)(2,1)}, bf16[4,4,2048]{2,1,0:T(4,128)(2,1)}, bf16[2,32,512]{2,1,0:T(8,128)(2,1)S(1)}, f32[2,32,128]{2,1,0:T(8,128)S(1)}, f32[2,32,128]{2,1,0:T(8,128)S(1)}) custom-call(bf16[4,2,32,128]{3,2,1,0:T(8,128)(2,1)S(1)} %get-tuple-element.42.query, ...), custom_call_target="tpu_custom_call", output_to_operand_aliasing={{0}: (6, {}), {1}: (7, {})} | custom-call | flops 8388608 | bytes 1048576 | tf_op jit(solution)/shard_map/pallas_call | solution.py:362
  54.8 1.7 %collective-permute-done.7.refs_0_ = bf16[1088,128]{1,0:T(8,128)(2,1)S(1)} collective-permute-done((bf16[1088,128]{1,0:T(8,128)(2,1)S(1)}, bf16[1088,128]{1,0:T(8,128)(2,1)S(1)}, u32[]{:S(2)}, u32[]{:S(2)}) %collective-permute-start.7) | collective-permute-done | bytes 278560 | tf_op jit(solution)/shard_map/ppermute | solution.py:389
  56.4 0.1 shard_map.97
  56.5 0.1 collective-permute-start.8
  56.6 0.8 %shard_map.98 = (bf16[4,2,256,512]{3,2,1,0:T(8,128)(2,1)}, bf16[4,4,2048]{2,1,0:T(4,128)(2,1)}, f32[2,32,128]{2,1,0:T(8,128)S(1)}) custom-call(bf16[2,32,512]{2,1,0:T(8,128)(2,1)S(1)} %get-tuple-element.69.weights, f32[2,32,128]{2,1,0:T(8,128)S(1)} %get-tuple-element.70.share, ...), custom_call_target="tpu_custom_call", output_to_operand_aliasing={{0}: (4, {}), {1}: (5, {})} | custom-call | flops 4194304 | bytes 1048576 | tf_op jit(solution)/shard_map/pallas_call | solution.py:362
  57.4 0.5 collective-permute-done.8.other
  58.0 0.8 %shard_map.99 = (bf16[4,2,256,512]{3,2,1,0:T(8,128)(2,1)}, bf16[4,4,2048]{2,1,0:T(4,128)(2,1)}) custom-call(bf16[2,32,512]{2,1,0:T(8,128)(2,1)S(1)} %get-tuple-element.69.weights, f32[2,32,128]{2,1,0:T(8,128)S(1)} %get-tuple-element.78.half, f32[2,32,128]{2,1,0:T(8,128)S(1)} %get-tuple-element.79.totals, ...), custom_call_target="tpu_custom_call", output_to_operand_aliasing={{0}: (4, {}), {1}: (5, {})} | custom-call | flops 4194304 | bytes 1048576 | tf_op jit(solution)/shard_map/pallas_call | solution.py:362
Async XLA Ops:
  2.5 17.3 %collective-permute-start.3 = (bf16[2192,128]{1,0:T(8,128)(2,1)S(1)}, bf16[2192,128]{1,0:T(8,128)(2,1)S(1)}, u32[]{:S(2)}, u32[]{:S(2)}) collective-permute-start(bf16[2192,128]{1,0:T(8,128)(2,1)S(1)} %shard_map.89), channel_id=1, source_target_pairs={{0,8},{4,0},{8,12},{12,4},{1,9},{5,1},{9,13},{13,5},{2,10},{6,2},{... | collective-permute-start | bytes 1683464 | tf_op jit(solution)/shard_map/ppermute | solution.py:389
  8.9 24.7 %collective-permute-start.1 = (bf16[2192,128]{1,0:T(8,128)(2,1)S(1)}, bf16[2192,128]{1,0:T(8,128)(2,1)S(1)}, u32[]{:S(2)}, u32[]{:S(2)}) collective-permute-start(bf16[2192,128]{1,0:T(8,128)(2,1)S(1)} %get-tuple-element.45), channel_id=1, source_target_pairs={{0,12},{4,8},{8,4},{12,0},{1,13},{5,9},{9,5},{13,1},{2,14},{6,10},... | collective-permute-start | bytes 1683464 | tf_op jit(solution)/shard_map/ppermute | solution.py:389
  10.5 9.5 %collective-permute-start.2 = (bf16[1024,128]{1,0:T(8,128)(2,1)S(1)}, bf16[1024,128]{1,0:T(8,128)(2,1)S(1)}, u32[]{:S(2)}, u32[]{:S(2)}) collective-permute-start(bf16[1024,128]{1,0:T(8,128)(2,1)S(1)} %get-tuple-element.48.theirs), channel_id=1, source_target_pairs={{0,1},{1,0},{2,3},{3,2},{4,5},{5,4},{6,7},{7,6},{8,9},{9,8},{10,11... | collective-permute-start | bytes 786440 | tf_op jit(solution)/shard_map/ppermute | solution.py:393
  10.6 40.0 %collective-permute-start = (bf16[1104,128]{1,0:T(8,128)(2,1)S(1)}, bf16[1104,128]{1,0:T(8,128)(2,1)S(1)}, u32[]{:S(2)}, u32[]{:S(2)}) collective-permute-start(bf16[1104,128]{1,0:T(8,128)(2,1)S(1)} %get-tuple-element.44), channel_id=1, source_target_pairs={{0,4},{4,12},{8,0},{12,8},{1,5},{5,13},{9,1},{13,9},{2,6},{6,14},{... | collective-permute-start | bytes 847880 | tf_op jit(solution)/shard_map/ppermute | solution.py:389
  11.4 45.0 %collective-permute-start.7 = (bf16[1088,128]{1,0:T(8,128)(2,1)S(1)}, bf16[1088,128]{1,0:T(8,128)(2,1)S(1)}, u32[]{:S(2)}, u32[]{:S(2)}) collective-permute-start(bf16[1088,128]{1,0:T(8,128)(2,1)S(1)} %get-tuple-element.71), channel_id=1, source_target_pairs={{0,4},{4,12},{8,0},{12,8},{1,5},{5,13},{9,1},{13,9},{2,6},{6,14},{... | collective-permute-start | bytes 835592 | tf_op jit(solution)/shard_map/ppermute | solution.py:389
  19.9 30.8 %collective-permute-start.6 = (bf16[1024,128]{1,0:T(8,128)(2,1)S(1)}, bf16[1024,128]{1,0:T(8,128)(2,1)S(1)}, u32[]{:S(2)}, u32[]{:S(2)}) collective-permute-start(bf16[1024,128]{1,0:T(8,128)(2,1)S(1)} %get-tuple-element.62.theirs), channel_id=1, source_target_pairs={{0,1},{1,0},{2,3},{3,2},{4,5},{5,4},{6,7},{7,6},{8,9},{9,8},{10,11... | collective-permute-start | bytes 786440 | tf_op jit(solution)/shard_map/ppermute | solution.py:393
  33.8 18.3 %collective-permute-start.5 = (bf16[1024,128]{1,0:T(8,128)(2,1)S(1)}, bf16[1024,128]{1,0:T(8,128)(2,1)S(1)}, u32[]{:S(2)}, u32[]{:S(2)}) collective-permute-start(bf16[1024,128]{1,0:T(8,128)(2,1)S(1)} %get-tuple-element.60.theirs), channel_id=1, source_target_pairs={{0,1},{1,0},{2,3},{3,2},{4,5},{5,4},{6,7},{7,6},{8,9},{9,8},{10,11... | collective-permute-start | bytes 786440 | tf_op jit(solution)/shard_map/ppermute | solution.py:393
  50.7 2.8 %collective-permute-start.4 = (bf16[512,128]{1,0:T(8,128)(2,1)S(1)}, bf16[512,128]{1,0:T(8,128)(2,1)S(1)}, u32[]{:S(2)}, u32[]{:S(2)}) collective-permute-start(bf16[512,128]{1,0:T(8,128)(2,1)S(1)} %get-tuple-element.58.theirs), channel_id=1, source_target_pairs={{0,1},{1,0},{2,3},{3,2},{4,5},{5,4},{6,7},{7,6},{8,9},{9,8},{10,11... | collective-permute-start | bytes 393224 | tf_op jit(solution)/shard_map/ppermute | solution.py:393
  56.5 1.4 %collective-permute-start.8 = (bf16[512,128]{1,0:T(8,128)(2,1)S(1)}, bf16[512,128]{1,0:T(8,128)(2,1)S(1)}, u32[]{:S(2)}, u32[]{:S(2)}) collective-permute-start(bf16[512,128]{1,0:T(8,128)(2,1)S(1)} %get-tuple-element.75.theirs), channel_id=1, source_target_pairs={{0,1},{1,0},{2,3},{3,2},{4,5},{5,4},{6,7},{7,6},{8,9},{9,8},{10,11... | collective-permute-start | bytes 393224 | tf_op jit(solution)/shard_map/ppermute | solution.py:393

commit v6 on v5

--- a/solution.py
+++ b/solution.py
@@ -383,11 +383,8 @@
     plan = [(k, both) for k in range(1, last)] + [(last, (0,)), (last, (1,)), (0, both)]
     query, fresh = arrange(size, new_query, new_kv)
     message = {}
-    for part in (plan[:1], plan[1:]):
-        for (k, parts), msg in zip(part, pack(size, part, route, lengths, deltas, anchors, chan_scale)):
-            if k:
-                msg = lax.ppermute(msg, "pool", list(enumerate(far(n, k))))
-            message[k, parts] = msg
+    for (k, parts), msg in zip(plan, pack(size, plan, route, lengths, deltas, anchors, chan_scale)):
+        message[k, parts] = lax.ppermute(msg, "pool", list(enumerate(far(n, k)))) if k else msg
 
     def swapped(x):
         return lax.ppermute(x, "sub", [(0, 1), (1, 0)])

time: 59.1 us -> 59.6 us (level)
  waiting for transfers between devices: 36.3 us -> 38.7 us
  Pallas kernels: 12.7 us -> 11.1 us
    ppermute x4, waiting for transfers between devices: 35.7 us -> 38.1 us  [body(): lax.ppermute(msg, 'pool', list(enumerate(far(n, k))))]
    pallas_call x2 -> x1, Pallas kernels: 4.15 us -> 2.5 us  [pack(): pl.pallas_call(functools.partial(pack_kernel, size, plan), out_shape=shap...]
  transfers between devices with their start and end apart: 9 -> 9, of which waited for: 5 -> 5; matrix products, arithmetic and copies ran while one was open for 0% -> 0% of each run, Pallas kernels for 17% -> 13%
where the time goes in v6:
time: 59.6 us; the launch traced here: 59.4 us
  waiting for transfers between devices  38.7 us (65%)
  Pallas kernels  11.1 us (19%)
  starting transfers between devices  8.9 us (15%)
  between operations  0.76 us (1%)
    ppermute x4, waiting for transfers between devices, body(): lax.ppermute(msg, 'pool', list(enumerate(far(n, k))))  38.1 us
    ppermute x4, starting transfers between devices, body(): lax.ppermute(msg, 'pool', list(enumerate(far(n, k))))  8.53 us
    pallas_call x6, Pallas kernels, chained_call(): pl.pallas_call(kernel, in_specs=[IN_VMEM] * many + [IN_HBM, IN_HBM], out_...  6.83 us
    pallas_call x1, Pallas kernels, pack(): pl.pallas_call(functools.partial(pack_kernel, size, plan), out_shape=shap...  2.5 us
  transfers between devices with their start and end apart: 9, of which 5 were waited for; matrix products, arithmetic and copies ran while one was open for 0% of the time, Pallas kernels for 13%

profile of v6, /device:TPU:0, one launch (start us, length us, event | category | flops | bytes accessed | tf_op | source)
XLA Modules:
  0.0 59.4 jit_solution(4621076202813100760)
XLA Ops:
  0.6 2.5 %shard_map.87 = (bf16[2192,128]{1,0:T(8,128)(2,1)S(1)}, bf16[2192,128]{1,0:T(8,128)(2,1)S(1)}, bf16[1104,128]{1,0:T(8,128)(2,1)S(1)}, bf16[1088,128]{1,0:T(8,128)(2,1)S(1)}, bf16[2192,128]{1,0:T(8,128)(2,1)S(1)}) custom-call(s32[4]{0:T(128)} %route.1, s32[4]{0:T(128)} %lengths.1, bf16[4,2,256,512]{3,2,1,0:T(8,128)(2,1)} %deltas.1, ...), custom_call_target="tpu_custom_call" | custom-call | bytes 2097152 | tf_op jit(solution)/shard_map/pallas_call | solution.py:116
  3.1 4.1 %collective-permute-start.3 = (bf16[2192,128]{1,0:T(8,128)(2,1)S(1)}, bf16[2192,128]{1,0:T(8,128)(2,1)S(1)}, u32[]{:S(2)}, u32[]{:S(2)}) collective-permute-start(bf16[2192,128]{1,0:T(8,128)(2,1)S(1)} %get-tuple-element.50), channel_id=1, source_target_pairs={{0,8},{4,0},{8,12},{12,4},{1,9},{5,1},{9,13},{13,5},{2,10},{6,2},{... | collective-permute-start | bytes 1683464 | tf_op jit(solution)/shard_map/ppermute | solution.py:387
  7.2 1.3 %collective-permute-start.1 = (bf16[2192,128]{1,0:T(8,128)(2,1)S(1)}, bf16[2192,128]{1,0:T(8,128)(2,1)S(1)}, u32[]{:S(2)}, u32[]{:S(2)}) collective-permute-start(bf16[2192,128]{1,0:T(8,128)(2,1)S(1)} %get-tuple-element.46), channel_id=1, source_target_pairs={{0,12},{4,8},{8,4},{12,0},{1,13},{5,9},{9,5},{13,1},{2,14},{6,10},... | collective-permute-start | bytes 1683464 | tf_op jit(solution)/shard_map/ppermute | solution.py:387
  8.6 0.2 shard_map.88
  8.8 0.1 collective-permute-start.2
  8.9 0.8 %collective-permute-start = (bf16[1104,128]{1,0:T(8,128)(2,1)S(1)}, bf16[1104,128]{1,0:T(8,128)(2,1)S(1)}, u32[]{:S(2)}, u32[]{:S(2)}) collective-permute-start(bf16[1104,128]{1,0:T(8,128)(2,1)S(1)} %get-tuple-element.45), channel_id=1, source_target_pairs={{0,4},{4,12},{8,0},{12,8},{1,5},{5,13},{9,1},{13,9},{2,6},{6,14},{... | collective-permute-start | bytes 847880 | tf_op jit(solution)/shard_map/ppermute | solution.py:387
  9.7 2.2 %collective-permute-start.7 = (bf16[1088,128]{1,0:T(8,128)(2,1)S(1)}, bf16[1088,128]{1,0:T(8,128)(2,1)S(1)}, u32[]{:S(2)}, u32[]{:S(2)}) collective-permute-start(bf16[1088,128]{1,0:T(8,128)(2,1)S(1)} %get-tuple-element.73), channel_id=1, source_target_pairs={{0,4},{4,12},{8,0},{12,8},{1,5},{5,13},{9,1},{13,9},{2,6},{6,14},{... | collective-permute-start | bytes 835592 | tf_op jit(solution)/shard_map/ppermute | solution.py:387
  11.9 0.9 %shard_map.86 = (bf16[4,2,32,128]{3,2,1,0:T(8,128)(2,1)S(1)}, bf16[4,2,2,16,128]{4,3,2,1,0:T(8,128)(2,1)S(1)}) custom-call(bf16[4,4,2048]{2,1,0:T(4,128)(2,1)} %new_query.1, bf16[4,2,4,512]{3,2,1,0:T(4,128)(2,1)} %new_kv.1), custom_call_target="tpu_custom_call" | custom-call | tf_op jit(solution)/shard_map/pallas_call | solution.py:153
  12.9 7.5 %collective-permute-done.3.refs_0_.tables = bf16[2192,128]{1,0:T(8,128)(2,1)S(1)} collective-permute-done((bf16[2192,128]{1,0:T(8,128)(2,1)S(1)}, bf16[2192,128]{1,0:T(8,128)(2,1)S(1)}, u32[]{:S(2)}, u32[]{:S(2)}) %collective-permute-start.3) | collective-permute-done | bytes 561184 | tf_op jit(solution)/shard_map/ppermute | solution.py:387
  20.4 0.2 shard_map.89
  20.6 0.1 collective-permute-start.6
  20.7 0.0 collective-permute-done.2.other
  20.7 1.3 %shard_map.90 = (bf16[4,2,256,512]{3,2,1,0:T(8,128)(2,1)}, bf16[4,4,2048]{2,1,0:T(4,128)(2,1)}) custom-call(bf16[4,2,32,128]{3,2,1,0:T(8,128)(2,1)S(1)} %get-tuple-element.43.query, bf16[4,2,2,16,128]{4,3,2,1,0:T(8,128)(2,1)S(1)} %get-tuple-element.44.new_kv, ...), custom_call_target="tpu_custom_call", output_to_operand_aliasing={{0}: (6, {}), {1}: (7, {})} | custom-call | flops 16777216 | bytes 1048576 | tf_op jit(solution)/shard_map/pallas_call | solution.py:362
  22.0 12.2 %collective-permute-done.1.refs_0_.tables = bf16[2192,128]{1,0:T(8,128)(2,1)S(1)} collective-permute-done((bf16[2192,128]{1,0:T(8,128)(2,1)S(1)}, bf16[2192,128]{1,0:T(8,128)(2,1)S(1)}, u32[]{:S(2)}, u32[]{:S(2)}) %collective-permute-start.1) | collective-permute-done | bytes 561184 | tf_op jit(solution)/shard_map/ppermute | solution.py:387
  34.2 0.2 shard_map.91
  34.4 0.1 collective-permute-start.5
  34.5 16.7 %collective-permute-done.refs_0_.tables.refs_1_ = bf16[1104,128]{1,0:T(8,128)(2,1)S(1)} collective-permute-done((bf16[1104,128]{1,0:T(8,128)(2,1)S(1)}, bf16[1104,128]{1,0:T(8,128)(2,1)S(1)}, u32[]{:S(2)}, u32[]{:S(2)}) %collective-permute-start) | collective-permute-done | bytes 282656 | tf_op jit(solution)/shard_map/ppermute | solution.py:387
  51.2 0.1 shard_map.92
  51.3 0.1 collective-permute-start.4
  51.4 0.0 collective-permute-done.6.other
  51.4 1.3 %shard_map.93 = (bf16[4,2,256,512]{3,2,1,0:T(8,128)(2,1)}, bf16[4,4,2048]{2,1,0:T(4,128)(2,1)}) custom-call(bf16[4,2,32,128]{3,2,1,0:T(8,128)(2,1)S(1)} %get-tuple-element.43.query, bf16[4,2,2,16,128]{4,3,2,1,0:T(8,128)(2,1)S(1)} %get-tuple-element.44.new_kv, ...), custom_call_target="tpu_custom_call", output_to_operand_aliasing={{0}: (6, {}), {1}: (7, {})} | custom-call | flops 16777216 | bytes 1048576 | tf_op jit(solution)/shard_map/pallas_call | solution.py:362
  52.8 0.0 collective-permute-done.5.other
  52.8 1.3 %shard_map.94 = (bf16[4,2,256,512]{3,2,1,0:T(8,128)(2,1)}, bf16[4,4,2048]{2,1,0:T(4,128)(2,1)}) custom-call(bf16[4,2,32,128]{3,2,1,0:T(8,128)(2,1)S(1)} %get-tuple-element.43.query, bf16[4,2,2,16,128]{4,3,2,1,0:T(8,128)(2,1)S(1)} %get-tuple-element.44.new_kv, ...), custom_call_target="tpu_custom_call", output_to_operand_aliasing={{0}: (6, {}), {1}: (7, {})} | custom-call | flops 16777216 | bytes 1048576 | tf_op jit(solution)/shard_map/pallas_call | solution.py:362
  54.1 0.0 collective-permute-done.4.other
  54.1 1.3 %shard_map.95 = (bf16[4,2,256,512]{3,2,1,0:T(8,128)(2,1)}, bf16[4,4,2048]{2,1,0:T(4,128)(2,1)}, bf16[2,32,512]{2,1,0:T(8,128)(2,1)S(1)}, f32[2,32,128]{2,1,0:T(8,128)S(1)}, f32[2,32,128]{2,1,0:T(8,128)S(1)}) custom-call(bf16[4,2,32,128]{3,2,1,0:T(8,128)(2,1)S(1)} %get-tuple-element.43.query, ...), custom_call_target="tpu_custom_call", output_to_operand_aliasing={{0}: (6, {}), {1}: (7, {})} | custom-call | flops 8388608 | bytes 1048576 | tf_op jit(solution)/shard_map/pallas_call | solution.py:362
  55.4 1.7 %collective-permute-done.7.refs_0_ = bf16[1088,128]{1,0:T(8,128)(2,1)S(1)} collective-permute-done((bf16[1088,128]{1,0:T(8,128)(2,1)S(1)}, bf16[1088,128]{1,0:T(8,128)(2,1)S(1)}, u32[]{:S(2)}, u32[]{:S(2)}) %collective-permute-start.7) | collective-permute-done | bytes 278560 | tf_op jit(solution)/shard_map/ppermute | solution.py:387
  57.1 0.1 shard_map.96
  57.2 0.1 collective-permute-start.8
  57.3 0.8 %shard_map.97 = (bf16[4,2,256,512]{3,2,1,0:T(8,128)(2,1)}, bf16[4,4,2048]{2,1,0:T(4,128)(2,1)}, f32[2,32,128]{2,1,0:T(8,128)S(1)}) custom-call(bf16[2,32,512]{2,1,0:T(8,128)(2,1)S(1)} %get-tuple-element.71.weights, f32[2,32,128]{2,1,0:T(8,128)S(1)} %get-tuple-element.72.share, ...), custom_call_target="tpu_custom_call", output_to_operand_aliasing={{0}: (4, {}), {1}: (5, {})} | custom-call | flops 4194304 | bytes 1048576 | tf_op jit(solution)/shard_map/pallas_call | solution.py:362
  58.1 0.5 collective-permute-done.8.other
  58.6 0.8 %shard_map.98 = (bf16[4,2,256,512]{3,2,1,0:T(8,128)(2,1)}, bf16[4,4,2048]{2,1,0:T(4,128)(2,1)}) custom-call(bf16[2,32,512]{2,1,0:T(8,128)(2,1)S(1)} %get-tuple-element.71.weights, f32[2,32,128]{2,1,0:T(8,128)S(1)} %get-tuple-element.80.half, f32[2,32,128]{2,1,0:T(8,128)S(1)} %get-tuple-element.81.totals, ...), custom_call_target="tpu_custom_call", output_to_operand_aliasing={{0}: (4, {}), {1}: (5, {})} | custom-call | flops 4194304 | bytes 1048576 | tf_op jit(solution)/shard_map/pallas_call | solution.py:362
Async XLA Ops:
  3.1 17.3 %collective-permute-start.3 = (bf16[2192,128]{1,0:T(8,128)(2,1)S(1)}, bf16[2192,128]{1,0:T(8,128)(2,1)S(1)}, u32[]{:S(2)}, u32[]{:S(2)}) collective-permute-start(bf16[2192,128]{1,0:T(8,128)(2,1)S(1)} %get-tuple-element.50), channel_id=1, source_target_pairs={{0,8},{4,0},{8,12},{12,4},{1,9},{5,1},{9,13},{13,5},{2,10},{6,2},{... | collective-permute-start | bytes 1683464 | tf_op jit(solution)/shard_map/ppermute | solution.py:387
  7.2 27.0 %collective-permute-start.1 = (bf16[2192,128]{1,0:T(8,128)(2,1)S(1)}, bf16[2192,128]{1,0:T(8,128)(2,1)S(1)}, u32[]{:S(2)}, u32[]{:S(2)}) collective-permute-start(bf16[2192,128]{1,0:T(8,128)(2,1)S(1)} %get-tuple-element.46), channel_id=1, source_target_pairs={{0,12},{4,8},{8,4},{12,0},{1,13},{5,9},{9,5},{13,1},{2,14},{6,10},... | collective-permute-start | bytes 1683464 | tf_op jit(solution)/shard_map/ppermute | solution.py:387
  8.8 11.9 %collective-permute-start.2 = (bf16[1024,128]{1,0:T(8,128)(2,1)S(1)}, bf16[1024,128]{1,0:T(8,128)(2,1)S(1)}, u32[]{:S(2)}, u32[]{:S(2)}) collective-permute-start(bf16[1024,128]{1,0:T(8,128)(2,1)S(1)} %get-tuple-element.49.theirs), channel_id=1, source_target_pairs={{0,1},{1,0},{2,3},{3,2},{4,5},{5,4},{6,7},{7,6},{8,9},{9,8},{10,11... | collective-permute-start | bytes 786440 | tf_op jit(solution)/shard_map/ppermute | solution.py:390
  8.9 42.4 %collective-permute-start = (bf16[1104,128]{1,0:T(8,128)(2,1)S(1)}, bf16[1104,128]{1,0:T(8,128)(2,1)S(1)}, u32[]{:S(2)}, u32[]{:S(2)}) collective-permute-start(bf16[1104,128]{1,0:T(8,128)(2,1)S(1)} %get-tuple-element.45), channel_id=1, source_target_pairs={{0,4},{4,12},{8,0},{12,8},{1,5},{5,13},{9,1},{13,9},{2,6},{6,14},{... | collective-permute-start | bytes 847880 | tf_op jit(solution)/shard_map/ppermute | solution.py:387
  9.7 47.4 %collective-permute-start.7 = (bf16[1088,128]{1,0:T(8,128)(2,1)S(1)}, bf16[1088,128]{1,0:T(8,128)(2,1)S(1)}, u32[]{:S(2)}, u32[]{:S(2)}) collective-permute-start(bf16[1088,128]{1,0:T(8,128)(2,1)S(1)} %get-tuple-element.73), channel_id=1, source_target_pairs={{0,4},{4,12},{8,0},{12,8},{1,5},{5,13},{9,1},{13,9},{2,6},{6,14},{... | collective-permute-start | bytes 835592 | tf_op jit(solution)/shard_map/ppermute | solution.py:387
  20.6 30.8 %collective-permute-start.6 = (bf16[1024,128]{1,0:T(8,128)(2,1)S(1)}, bf16[1024,128]{1,0:T(8,128)(2,1)S(1)}, u32[]{:S(2)}, u32[]{:S(2)}) collective-permute-start(bf16[1024,128]{1,0:T(8,128)(2,1)S(1)} %get-tuple-element.64.theirs), channel_id=1, source_target_pairs={{0,1},{1,0},{2,3},{3,2},{4,5},{5,4},{6,7},{7,6},{8,9},{9,8},{10,11... | collective-permute-start | bytes 786440 | tf_op jit(solution)/shard_map/ppermute | solution.py:390
  34.4 18.3 %collective-permute-start.5 = (bf16[1024,128]{1,0:T(8,128)(2,1)S(1)}, bf16[1024,128]{1,0:T(8,128)(2,1)S(1)}, u32[]{:S(2)}, u32[]{:S(2)}) collective-permute-start(bf16[1024,128]{1,0:T(8,128)(2,1)S(1)} %get-tuple-element.62.theirs), channel_id=1, source_target_pairs={{0,1},{1,0},{2,3},{3,2},{4,5},{5,4},{6,7},{7,6},{8,9},{9,8},{10,11... | collective-permute-start | bytes 786440 | tf_op jit(solution)/shard_map/ppermute | solution.py:390
  51.3 2.8 %collective-permute-start.4 = (bf16[512,128]{1,0:T(8,128)(2,1)S(1)}, bf16[512,128]{1,0:T(8,128)(2,1)S(1)}, u32[]{:S(2)}, u32[]{:S(2)}) collective-permute-start(bf16[512,128]{1,0:T(8,128)(2,1)S(1)} %get-tuple-element.60.theirs), channel_id=1, source_target_pairs={{0,1},{1,0},{2,3},{3,2},{4,5},{5,4},{6,7},{7,6},{8,9},{9,8},{10,11... | collective-permute-start | bytes 393224 | tf_op jit(solution)/shard_map/ppermute | solution.py:390
  57.2 1.4 %collective-permute-start.8 = (bf16[512,128]{1,0:T(8,128)(2,1)S(1)}, bf16[512,128]{1,0:T(8,128)(2,1)S(1)}, u32[]{:S(2)}, u32[]{:S(2)}) collective-permute-start(bf16[512,128]{1,0:T(8,128)(2,1)S(1)} %get-tuple-element.77.theirs), channel_id=1, source_target_pairs={{0,1},{1,0},{2,3},{3,2},{4,5},{5,4},{6,7},{7,6},{8,9},{9,8},{10,11... | collective-permute-start | bytes 393224 | tf_op jit(solution)/shard_map/ppermute | solution.py:390

commit v7 on v5

--- a/solution.py
+++ b/solution.py
@@ -379,8 +379,10 @@
 def body(deltas, anchors, chan_scale, lengths, route, new_query, new_kv):
     n = lax.axis_size("pool")
     size = Sizes(deltas, anchors, new_query, n)
-    both, last = (0, 1), n - 1
-    plan = [(k, both) for k in range(1, last)] + [(last, (0,)), (last, (1,)), (0, both)]
+    both = (0, 1)
+    order = sorted(range(1, n), key=lambda k: (min(k, n - k), k))
+    last = order[-1]
+    plan = [(k, both) for k in order[:-1]] + [(last, (0,)), (last, (1,)), (0, both)]
     query, fresh = arrange(size, new_query, new_kv)
     message = {}
     for part in (plan[:1], plan[1:]):
@@ -414,10 +416,10 @@
         return state, mine, swapped(theirs), theirs
 
     state, held = None, []
-    for k in range(last):
+    for k in [0] + order[:-1]:
         state, *each = take(k, both, state)
         held.append((k, *each))
-        if 0 < k < last - 1:
+        if k and k != order[-2]:
             state = attend(*held.pop(0), state)
     state, *keys = take(last, (0,), state)
     for each in held:

time: 59.1 us -> 56.9 us (0.963)
  the two profiles are of different devices: /device:TPU:0 before, /device:TPU:9 now
where the time goes in v7:
time: 56.9 us; the launch traced here: 56.6 us
  waiting for transfers between devices  31.7 us (56%)
  Pallas kernels  12.7 us (22%)
  starting transfers between devices  11.5 us (20%)
  between operations  0.73 us (1%)
    ppermute x4, waiting for transfers between devices, body(): msg = lax.ppermute(msg, 'pool', list(enumerate(far(n, k))))  31.5 us
    ppermute x5, starting transfers between devices, swapped(): return lax.ppermute(x, 'sub', [(0, 1), (1, 0)])  7.53 us
    pallas_call x6, Pallas kernels, chained_call(): pl.pallas_call(kernel, in_specs=[IN_VMEM] * many + [IN_HBM, IN_HBM], out_...  6.82 us
    pallas_call x2, Pallas kernels, pack(): pl.pallas_call(functools.partial(pack_kernel, size, plan), out_shape=shap...  4.16 us
    ppermute x4, starting transfers between devices, body(): msg = lax.ppermute(msg, 'pool', list(enumerate(far(n, k))))  3.94 us
  transfers between devices with their start and end apart: 9, of which 5 were waited for; matrix products, arithmetic and copies ran while one was open for 0% of the time, Pallas kernels for 18%

profile of v7, /device:TPU:9, one launch (start us, length us, event | category | flops | bytes accessed | tf_op | source)
XLA Modules:
  0.0 56.6 jit_solution(14140040197387118883)
XLA Ops:
  0.6 1.9 %shard_map.89 = bf16[2192,128]{1,0:T(8,128)(2,1)S(1)} custom-call(s32[4]{0:T(128)} %route.3, s32[4]{0:T(128)} %lengths.3, bf16[4,2,256,512]{3,2,1,0:T(8,128)(2,1)} %deltas.3, bf16[4,2,16,512]{3,2,1,0:T(8,128)(2,1)} %anchors.3, bf16[4,2,512]{2,1,0:T(2,128)(2,1)} %scale.3), custom_call_target="tpu_custom_call" | custom-call | bytes 524288 | tf_op jit(solution)/shard_map/pallas_call | solution.py:116
  2.5 0.1 collective-permute-start.3
  2.6 2.3 %shard_map.87 = (bf16[2192,128]{1,0:T(8,128)(2,1)S(1)}, bf16[1104,128]{1,0:T(8,128)(2,1)S(1)}, bf16[1088,128]{1,0:T(8,128)(2,1)S(1)}, bf16[2192,128]{1,0:T(8,128)(2,1)S(1)}) custom-call(s32[4]{0:T(128)} %route.3, s32[4]{0:T(128)} %lengths.3, bf16[4,2,256,512]{3,2,1,0:T(8,128)(2,1)} %deltas.3, bf16[4,2,16,512]{3,2,1,0:T(8,128)(2,1)} %anchors.3, ...), custom_call_target="tpu_custom_call" | custom-call | bytes 1572864 | tf_op jit(solution)/shard_map/pallas_call | solution.py:116
  4.9 2.4 %collective-permute-start.1 = (bf16[2192,128]{1,0:T(8,128)(2,1)S(1)}, bf16[2192,128]{1,0:T(8,128)(2,1)S(1)}, u32[]{:S(2)}, u32[]{:S(2)}) collective-permute-start(bf16[2192,128]{1,0:T(8,128)(2,1)S(1)} %get-tuple-element.45), channel_id=1, source_target_pairs={{0,4},{4,12},{8,0},{12,8},{1,5},{5,13},{9,1},{13,9},{2,6},{6,14},{... | collective-permute-start | bytes 1683464 | tf_op jit(solution)/shard_map/ppermute | solution.py:391
  7.3 0.2 shard_map.88
  7.5 1.3 %collective-permute-start.2 = (bf16[1024,128]{1,0:T(8,128)(2,1)S(1)}, bf16[1024,128]{1,0:T(8,128)(2,1)S(1)}, u32[]{:S(2)}, u32[]{:S(2)}) collective-permute-start(bf16[1024,128]{1,0:T(8,128)(2,1)S(1)} %get-tuple-element.48.theirs), channel_id=1, source_target_pairs={{0,1},{1,0},{2,3},{3,2},{4,5},{5,4},{6,7},{7,6},{8,9},{9,8},{10,11... | collective-permute-start | bytes 786440 | tf_op jit(solution)/shard_map/ppermute | solution.py:395
  8.8 1.3 %collective-permute-start = (bf16[1104,128]{1,0:T(8,128)(2,1)S(1)}, bf16[1104,128]{1,0:T(8,128)(2,1)S(1)}, u32[]{:S(2)}, u32[]{:S(2)}) collective-permute-start(bf16[1104,128]{1,0:T(8,128)(2,1)S(1)} %get-tuple-element.44), channel_id=1, source_target_pairs={{0,12},{4,8},{8,4},{12,0},{1,13},{5,9},{9,5},{13,1},{2,14},{6,10},... | collective-permute-start | bytes 847880 | tf_op jit(solution)/shard_map/ppermute | solution.py:391
  10.1 0.2 collective-permute-start.7
  10.2 0.9 %shard_map.86 = (bf16[4,2,32,128]{3,2,1,0:T(8,128)(2,1)S(1)}, bf16[4,2,2,16,128]{4,3,2,1,0:T(8,128)(2,1)S(1)}) custom-call(bf16[4,4,2048]{2,1,0:T(4,128)(2,1)} %new_query.1, bf16[4,2,4,512]{3,2,1,0:T(4,128)(2,1)} %new_kv.1), custom_call_target="tpu_custom_call" | custom-call | tf_op jit(solution)/shard_map/pallas_call | solution.py:153
  11.2 5.9 %collective-permute-done.3.refs_0_.tables = bf16[2192,128]{1,0:T(8,128)(2,1)S(1)} collective-permute-done((bf16[2192,128]{1,0:T(8,128)(2,1)S(1)}, bf16[2192,128]{1,0:T(8,128)(2,1)S(1)}, u32[]{:S(2)}, u32[]{:S(2)}) %collective-permute-start.3) | collective-permute-done | bytes 561184 | tf_op jit(solution)/shard_map/ppermute | solution.py:391
  17.1 0.2 shard_map.90
  17.3 2.8 %collective-permute-start.6 = (bf16[1024,128]{1,0:T(8,128)(2,1)S(1)}, bf16[1024,128]{1,0:T(8,128)(2,1)S(1)}, u32[]{:S(2)}, u32[]{:S(2)}) collective-permute-start(bf16[1024,128]{1,0:T(8,128)(2,1)S(1)} %get-tuple-element.62.theirs), channel_id=1, source_target_pairs={{0,1},{1,0},{2,3},{3,2},{4,5},{5,4},{6,7},{7,6},{8,9},{9,8},{10,11... | collective-permute-start | bytes 786440 | tf_op jit(solution)/shard_map/ppermute | solution.py:395
  20.0 0.0 collective-permute-done.2.other
  20.0 1.3 %shard_map.91 = (bf16[4,2,256,512]{3,2,1,0:T(8,128)(2,1)}, bf16[4,4,2048]{2,1,0:T(4,128)(2,1)}) custom-call(bf16[4,2,32,128]{3,2,1,0:T(8,128)(2,1)S(1)} %get-tuple-element.42.query, bf16[4,2,2,16,128]{4,3,2,1,0:T(8,128)(2,1)S(1)} %get-tuple-element.43.new_kv, ...), custom_call_target="tpu_custom_call", output_to_operand_aliasing={{0}: (6, {}), {1}: (7, {})} | custom-call | flops 16777216 | bytes 1048576 | tf_op jit(solution)/shard_map/pallas_call | solution.py:362
  21.4 8.3 %collective-permute-done.1.refs_0_.tables = bf16[2192,128]{1,0:T(8,128)(2,1)S(1)} collective-permute-done((bf16[2192,128]{1,0:T(8,128)(2,1)S(1)}, bf16[2192,128]{1,0:T(8,128)(2,1)S(1)}, u32[]{:S(2)}, u32[]{:S(2)}) %collective-permute-start.1) | collective-permute-done | bytes 561184 | tf_op jit(solution)/shard_map/ppermute | solution.py:391
  29.7 0.2 shard_map.92
  29.9 2.3 %collective-permute-start.5 = (bf16[1024,128]{1,0:T(8,128)(2,1)S(1)}, bf16[1024,128]{1,0:T(8,128)(2,1)S(1)}, u32[]{:S(2)}, u32[]{:S(2)}) collective-permute-start(bf16[1024,128]{1,0:T(8,128)(2,1)S(1)} %get-tuple-element.60.theirs), channel_id=1, source_target_pairs={{0,1},{1,0},{2,3},{3,2},{4,5},{5,4},{6,7},{7,6},{8,9},{9,8},{10,11... | collective-permute-start | bytes 786440 | tf_op jit(solution)/shard_map/ppermute | solution.py:395
  32.2 16.0 %collective-permute-done.refs_0_.tables.refs_1_ = bf16[1104,128]{1,0:T(8,128)(2,1)S(1)} collective-permute-done((bf16[1104,128]{1,0:T(8,128)(2,1)S(1)}, bf16[1104,128]{1,0:T(8,128)(2,1)S(1)}, u32[]{:S(2)}, u32[]{:S(2)}) %collective-permute-start) | collective-permute-done | bytes 282656 | tf_op jit(solution)/shard_map/ppermute | solution.py:391
  48.2 0.1 shard_map.93
  48.3 0.7 %collective-permute-start.4 = (bf16[512,128]{1,0:T(8,128)(2,1)S(1)}, bf16[512,128]{1,0:T(8,128)(2,1)S(1)}, u32[]{:S(2)}, u32[]{:S(2)}) collective-permute-start(bf16[512,128]{1,0:T(8,128)(2,1)S(1)} %get-tuple-element.58.theirs), channel_id=1, source_target_pairs={{0,1},{1,0},{2,3},{3,2},{4,5},{5,4},{6,7},{7,6},{8,9},{9,8},{10,11... | collective-permute-start | bytes 393224 | tf_op jit(solution)/shard_map/ppermute | solution.py:395
  48.9 0.0 collective-permute-done.6.other
  49.0 1.3 %shard_map.94 = (bf16[4,2,256,512]{3,2,1,0:T(8,128)(2,1)}, bf16[4,4,2048]{2,1,0:T(4,128)(2,1)}) custom-call(bf16[4,2,32,128]{3,2,1,0:T(8,128)(2,1)S(1)} %get-tuple-element.42.query, bf16[4,2,2,16,128]{4,3,2,1,0:T(8,128)(2,1)S(1)} %get-tuple-element.43.new_kv, ...), custom_call_target="tpu_custom_call", output_to_operand_aliasing={{0}: (6, {}), {1}: (7, {})} | custom-call | flops 16777216 | bytes 1048576 | tf_op jit(solution)/shard_map/pallas_call | solution.py:362
  50.3 0.0 collective-permute-done.5.other
  50.3 1.3 %shard_map.95 = (bf16[4,2,256,512]{3,2,1,0:T(8,128)(2,1)}, bf16[4,4,2048]{2,1,0:T(4,128)(2,1)}) custom-call(bf16[4,2,32,128]{3,2,1,0:T(8,128)(2,1)S(1)} %get-tuple-element.42.query, bf16[4,2,2,16,128]{4,3,2,1,0:T(8,128)(2,1)S(1)} %get-tuple-element.43.new_kv, ...), custom_call_target="tpu_custom_call", output_to_operand_aliasing={{0}: (6, {}), {1}: (7, {})} | custom-call | flops 16777216 | bytes 1048576 | tf_op jit(solution)/shard_map/pallas_call | solution.py:362
  51.7 0.0 collective-permute-done.4.other
  51.7 1.3 %shard_map.96 = (bf16[4,2,256,512]{3,2,1,0:T(8,128)(2,1)}, bf16[4,4,2048]{2,1,0:T(4,128)(2,1)}, bf16[2,32,512]{2,1,0:T(8,128)(2,1)S(1)}, f32[2,32,128]{2,1,0:T(8,128)S(1)}, f32[2,32,128]{2,1,0:T(8,128)S(1)}) custom-call(bf16[4,2,32,128]{3,2,1,0:T(8,128)(2,1)S(1)} %get-tuple-element.42.query, ...), custom_call_target="tpu_custom_call", output_to_operand_aliasing={{0}: (6, {}), {1}: (7, {})} | custom-call | flops 8388608 | bytes 1048576 | tf_op jit(solution)/shard_map/pallas_call | solution.py:362
  52.9 1.2 %collective-permute-done.7.refs_0_ = bf16[1088,128]{1,0:T(8,128)(2,1)S(1)} collective-permute-done((bf16[1088,128]{1,0:T(8,128)(2,1)S(1)}, bf16[1088,128]{1,0:T(8,128)(2,1)S(1)}, u32[]{:S(2)}, u32[]{:S(2)}) %collective-permute-start.7) | collective-permute-done | bytes 278560 | tf_op jit(solution)/shard_map/ppermute | solution.py:391
  54.2 0.1 shard_map.97
  54.3 0.6 collective-permute-start.8
  54.8 0.8 %shard_map.98 = (bf16[4,2,256,512]{3,2,1,0:T(8,128)(2,1)}, bf16[4,4,2048]{2,1,0:T(4,128)(2,1)}, f32[2,32,128]{2,1,0:T(8,128)S(1)}) custom-call(bf16[2,32,512]{2,1,0:T(8,128)(2,1)S(1)} %get-tuple-element.69.weights, f32[2,32,128]{2,1,0:T(8,128)S(1)} %get-tuple-element.70.share, ...), custom_call_target="tpu_custom_call", output_to_operand_aliasing={{0}: (4, {}), {1}: (5, {})} | custom-call | flops 4194304 | bytes 1048576 | tf_op jit(solution)/shard_map/pallas_call | solution.py:362
  55.6 0.2 collective-permute-done.8.other
  55.8 0.8 %shard_map.99 = (bf16[4,2,256,512]{3,2,1,0:T(8,128)(2,1)}, bf16[4,4,2048]{2,1,0:T(4,128)(2,1)}) custom-call(bf16[2,32,512]{2,1,0:T(8,128)(2,1)S(1)} %get-tuple-element.69.weights, f32[2,32,128]{2,1,0:T(8,128)S(1)} %get-tuple-element.78.half, f32[2,32,128]{2,1,0:T(8,128)S(1)} %get-tuple-element.79.totals, ...), custom_call_target="tpu_custom_call", output_to_operand_aliasing={{0}: (4, {}), {1}: (5, {})} | custom-call | flops 4194304 | bytes 1048576 | tf_op jit(solution)/shard_map/pallas_call | solution.py:362
Async XLA Ops:
  2.5 14.6 %collective-permute-start.3 = (bf16[2192,128]{1,0:T(8,128)(2,1)S(1)}, bf16[2192,128]{1,0:T(8,128)(2,1)S(1)}, u32[]{:S(2)}, u32[]{:S(2)}) collective-permute-start(bf16[2192,128]{1,0:T(8,128)(2,1)S(1)} %shard_map.89), channel_id=1, source_target_pairs={{0,8},{4,0},{8,12},{12,4},{1,9},{5,1},{9,13},{13,5},{2,10},{6,2},{... | collective-permute-start | bytes 1683464 | tf_op jit(solution)/shard_map/ppermute | solution.py:391
  4.9 24.8 %collective-permute-start.1 = (bf16[2192,128]{1,0:T(8,128)(2,1)S(1)}, bf16[2192,128]{1,0:T(8,128)(2,1)S(1)}, u32[]{:S(2)}, u32[]{:S(2)}) collective-permute-start(bf16[2192,128]{1,0:T(8,128)(2,1)S(1)} %get-tuple-element.45), channel_id=1, source_target_pairs={{0,4},{4,12},{8,0},{12,8},{1,5},{5,13},{9,1},{13,9},{2,6},{6,14},{... | collective-permute-start | bytes 1683464 | tf_op jit(solution)/shard_map/ppermute | solution.py:391
  7.5 12.6 %collective-permute-start.2 = (bf16[1024,128]{1,0:T(8,128)(2,1)S(1)}, bf16[1024,128]{1,0:T(8,128)(2,1)S(1)}, u32[]{:S(2)}, u32[]{:S(2)}) collective-permute-start(bf16[1024,128]{1,0:T(8,128)(2,1)S(1)} %get-tuple-element.48.theirs), channel_id=1, source_target_pairs={{0,1},{1,0},{2,3},{3,2},{4,5},{5,4},{6,7},{7,6},{8,9},{9,8},{10,11... | collective-permute-start | bytes 786440 | tf_op jit(solution)/shard_map/ppermute | solution.py:395
  8.8 39.4 %collective-permute-start = (bf16[1104,128]{1,0:T(8,128)(2,1)S(1)}, bf16[1104,128]{1,0:T(8,128)(2,1)S(1)}, u32[]{:S(2)}, u32[]{:S(2)}) collective-permute-start(bf16[1104,128]{1,0:T(8,128)(2,1)S(1)} %get-tuple-element.44), channel_id=1, source_target_pairs={{0,12},{4,8},{8,4},{12,0},{1,13},{5,9},{9,5},{13,1},{2,14},{6,10},... | collective-permute-start | bytes 847880 | tf_op jit(solution)/shard_map/ppermute | solution.py:391
  10.1 44.1 %collective-permute-start.7 = (bf16[1088,128]{1,0:T(8,128)(2,1)S(1)}, bf16[1088,128]{1,0:T(8,128)(2,1)S(1)}, u32[]{:S(2)}, u32[]{:S(2)}) collective-permute-start(bf16[1088,128]{1,0:T(8,128)(2,1)S(1)} %get-tuple-element.71), channel_id=1, source_target_pairs={{0,12},{4,8},{8,4},{12,0},{1,13},{5,9},{9,5},{13,1},{2,14},{6,10},... | collective-permute-start | bytes 835592 | tf_op jit(solution)/shard_map/ppermute | solution.py:391
  17.3 31.7 %collective-permute-start.6 = (bf16[1024,128]{1,0:T(8,128)(2,1)S(1)}, bf16[1024,128]{1,0:T(8,128)(2,1)S(1)}, u32[]{:S(2)}, u32[]{:S(2)}) collective-permute-start(bf16[1024,128]{1,0:T(8,128)(2,1)S(1)} %get-tuple-element.62.theirs), channel_id=1, source_target_pairs={{0,1},{1,0},{2,3},{3,2},{4,5},{5,4},{6,7},{7,6},{8,9},{9,8},{10,11... | collective-permute-start | bytes 786440 | tf_op jit(solution)/shard_map/ppermute | solution.py:395
  29.9 20.4 %collective-permute-start.5 = (bf16[1024,128]{1,0:T(8,128)(2,1)S(1)}, bf16[1024,128]{1,0:T(8,128)(2,1)S(1)}, u32[]{:S(2)}, u32[]{:S(2)}) collective-permute-start(bf16[1024,128]{1,0:T(8,128)(2,1)S(1)} %get-tuple-element.60.theirs), channel_id=1, source_target_pairs={{0,1},{1,0},{2,3},{3,2},{4,5},{5,4},{6,7},{7,6},{8,9},{9,8},{10,11... | collective-permute-start | bytes 786440 | tf_op jit(solution)/shard_map/ppermute | solution.py:395
  48.3 3.4 %collective-permute-start.4 = (bf16[512,128]{1,0:T(8,128)(2,1)S(1)}, bf16[512,128]{1,0:T(8,128)(2,1)S(1)}, u32[]{:S(2)}, u32[]{:S(2)}) collective-permute-start(bf16[512,128]{1,0:T(8,128)(2,1)S(1)} %get-tuple-element.58.theirs), channel_id=1, source_target_pairs={{0,1},{1,0},{2,3},{3,2},{4,5},{5,4},{6,7},{7,6},{8,9},{9,8},{10,11... | collective-permute-start | bytes 393224 | tf_op jit(solution)/shard_map/ppermute | solution.py:395
  54.3 1.5 %collective-permute-start.8 = (bf16[512,128]{1,0:T(8,128)(2,1)S(1)}, bf16[512,128]{1,0:T(8,128)(2,1)S(1)}, u32[]{:S(2)}, u32[]{:S(2)}) collective-permute-start(bf16[512,128]{1,0:T(8,128)(2,1)S(1)} %get-tuple-element.75.theirs), channel_id=1, source_target_pairs={{0,1},{1,0},{2,3},{3,2},{4,5},{5,4},{6,7},{7,6},{8,9},{9,8},{10,11... | collective-permute-start | bytes 393224 | tf_op jit(solution)/shard_map/ppermute | solution.py:395

commit v8 on v7

--- a/solution.py
+++ b/solution.py
@@ -11,6 +11,7 @@
 HEAD_DIM = 128
 Q_PER_KV = 8
 TILE = 16
+CHUNKS = 4
 BF = jnp.bfloat16
 F32 = jnp.float32
 LOW = -1e30
@@ -80,34 +81,56 @@
 
 
 def pack_kernel(size, plan, route, lengths, deltas, anchors, scale, *rest):
-    outs, (held, tables, sems) = rest[:-3], rest[-3:]
+    outs, (to, long, scales, held, tables, sems, few) = rest[:-7], rest[-7:]
+    first = [
+        pltpu.make_async_copy(source, target, few.at[i])
+        for i, (source, target) in enumerate(((route, to), (lengths, long), (scale, scales)))
+    ]
+    for copy in first:
+        copy.start()
     z = lax.axis_index("pool")
-    work = []
+    step = size.span // CHUNKS
+    first[0].wait()
+    work, indices = [], []
     for m, (k, parts) in enumerate(plan):
         dest = pick(far(size.n, k), z)
         index = jnp.int32(0)
         for j in range(size.count):
-            index = jnp.where(route[j] == dest, jnp.int32(j), index)
+            index = jnp.where(to[j] == dest, jnp.int32(j), index)
+        indices.append(index)
         for which in parts:
             slot = len(work)
-            copies = (
-                pltpu.make_async_copy(deltas.at[index, which], held.at[slot], sems.at[0, slot]),
-                pltpu.make_async_copy(anchors.at[index, which], tables.at[slot], sems.at[1, slot]),
+            copies = [
+                pltpu.make_async_copy(
+                    deltas.at[index, which, pl.ds(c * step, step)],
+                    held.at[slot, pl.ds(c * step, step)],
+                    sems.at[slot, c],
+                )
+                for c in range(CHUNKS)
+            ]
+            copies.append(
+                pltpu.make_async_copy(anchors.at[index, which], tables.at[slot], sems.at[slot, CHUNKS])
             )
             for copy in copies:
                 copy.start()
             work.append((outs[m], parts, which, slot, copies))
+    for copy in first[1:]:
+        copy.wait()
+    for m, (k, parts) in enumerate(plan):
         if 0 in parts:
-            outs[m][pl.ds(size.side_at(parts), TILE), :] = side_block(size, scale[index], lengths[index])
+            side = side_block(size, scales[indices[m]], long[indices[m]])
+            outs[m][pl.ds(size.side_at(parts), TILE), :] = side
     for msg, parts, which, slot, copies in work:
-        for copy in copies:
+        for c, copy in enumerate(copies):
             copy.wait()
-        for h in range(size.heads):
-            lanes = slice(h * HEAD_DIM, (h + 1) * HEAD_DIM)
-            at = (parts.index(which) * size.heads + h) * size.span
-            msg[at:at + size.span, :] = held[slot, :, lanes]
-            at = size.anchor_at(which, parts) + h * size.rows
-            msg[at:at + size.rows, :] = tables[slot, :, lanes]
+            for h in range(size.heads):
+                lanes = slice(h * HEAD_DIM, (h + 1) * HEAD_DIM)
+                if c < CHUNKS:
+                    at = (parts.index(which) * size.heads + h) * size.span + c * step
+                    msg[at:at + step, :] = held[slot, c * step:(c + 1) * step, lanes]
+                else:
+                    at = size.anchor_at(which, parts) + h * size.rows
+                    msg[at:at + size.rows, :] = tables[slot, :, lanes]
 
 
 def pack(size, plan, route, lengths, deltas, anchors, scale):
@@ -116,12 +139,16 @@
     return pl.pallas_call(
         functools.partial(pack_kernel, size, plan),
         out_shape=shapes,
-        in_specs=[IN_SMEM, IN_SMEM, IN_HBM, IN_HBM, IN_VMEM],
+        in_specs=[IN_HBM] * 5,
         out_specs=[IN_VMEM] * len(shapes),
         scratch_shapes=[
+            pltpu.SMEM(route.shape, jnp.int32),
+            pltpu.SMEM(lengths.shape, jnp.int32),
+            pltpu.VMEM(scale.shape, BF),
             pltpu.VMEM((slots, size.span, size.channels), BF),
             pltpu.VMEM((slots, size.rows, size.channels), BF),
-            pltpu.SemaphoreType.DMA((2, slots)),
+            pltpu.SemaphoreType.DMA((slots, CHUNKS + 1)),
+            pltpu.SemaphoreType.DMA((3,)),
         ],
         compiler_params=LIMIT,
         cost_estimate=pl.CostEstimate(

time: 56.9 us -> 57 us (level)
  no operation moved by 1% of the time
where the time goes in v8:
time: 57 us; the launch traced here: 56.6 us
  waiting for transfers between devices  31.6 us (55%)
  Pallas kernels  12.8 us (22%)
  starting transfers between devices  11.5 us (20%)
  between operations  0.73 us (1%)
    ppermute x4, waiting for transfers between devices, body(): msg = lax.ppermute(msg, 'pool', list(enumerate(far(n, k))))  31.4 us
    ppermute x5, starting transfers between devices, swapped(): return lax.ppermute(x, 'sub', [(0, 1), (1, 0)])  7.53 us
    pallas_call x6, Pallas kernels, chained_call(): pl.pallas_call(kernel, in_specs=[IN_VMEM] * many + [IN_HBM, IN_HBM], out_...  6.82 us
    pallas_call x2, Pallas kernels, pack(): pl.pallas_call(functools.partial(pack_kernel, size, plan), out_shape=shap...  4.29 us
    ppermute x4, starting transfers between devices, body(): msg = lax.ppermute(msg, 'pool', list(enumerate(far(n, k))))  3.94 us
  transfers between devices with their start and end apart: 9, of which 5 were waited for; matrix products, arithmetic and copies ran while one was open for 0% of the time, Pallas kernels for 18%

profile of v8, /device:TPU:9, one launch (start us, length us, event | category | flops | bytes accessed | tf_op | source)
XLA Modules:
  0.0 56.6 jit_solution(15157719261416982266)
XLA Ops:
  0.6 1.9 %shard_map.89 = bf16[2192,128]{1,0:T(8,128)(2,1)S(1)} custom-call(s32[4]{0:T(128)} %route.3, s32[4]{0:T(128)} %lengths.3, bf16[4,2,256,512]{3,2,1,0:T(8,128)(2,1)} %deltas.3, bf16[4,2,16,512]{3,2,1,0:T(8,128)(2,1)} %anchors.3, bf16[4,2,512]{2,1,0:T(2,128)(2,1)} %scale.3), custom_call_target="tpu_custom_call" | custom-call | bytes 524288 | tf_op jit(solution)/shard_map/pallas_call | solution.py:139
  2.5 0.1 collective-permute-start.3
  2.6 2.4 %shard_map.87 = (bf16[2192,128]{1,0:T(8,128)(2,1)S(1)}, bf16[1104,128]{1,0:T(8,128)(2,1)S(1)}, bf16[1088,128]{1,0:T(8,128)(2,1)S(1)}, bf16[2192,128]{1,0:T(8,128)(2,1)S(1)}) custom-call(s32[4]{0:T(128)} %route.3, s32[4]{0:T(128)} %lengths.3, bf16[4,2,256,512]{3,2,1,0:T(8,128)(2,1)} %deltas.3, bf16[4,2,16,512]{3,2,1,0:T(8,128)(2,1)} %anchors.3, ...), custom_call_target="tpu_custom_call" | custom-call | bytes 1572864 | tf_op jit(solution)/shard_map/pallas_call | solution.py:139
  5.0 2.4 %collective-permute-start.1 = (bf16[2192,128]{1,0:T(8,128)(2,1)S(1)}, bf16[2192,128]{1,0:T(8,128)(2,1)S(1)}, u32[]{:S(2)}, u32[]{:S(2)}) collective-permute-start(bf16[2192,128]{1,0:T(8,128)(2,1)S(1)} %get-tuple-element.45), channel_id=1, source_target_pairs={{0,4},{4,12},{8,0},{12,8},{1,5},{5,13},{9,1},{13,9},{2,6},{6,14},{... | collective-permute-start | bytes 1683464 | tf_op jit(solution)/shard_map/ppermute | solution.py:418
  7.4 0.2 shard_map.88
  7.6 1.3 %collective-permute-start.2 = (bf16[1024,128]{1,0:T(8,128)(2,1)S(1)}, bf16[1024,128]{1,0:T(8,128)(2,1)S(1)}, u32[]{:S(2)}, u32[]{:S(2)}) collective-permute-start(bf16[1024,128]{1,0:T(8,128)(2,1)S(1)} %get-tuple-element.48.theirs), channel_id=1, source_target_pairs={{0,1},{1,0},{2,3},{3,2},{4,5},{5,4},{6,7},{7,6},{8,9},{9,8},{10,11... | collective-permute-start | bytes 786440 | tf_op jit(solution)/shard_map/ppermute | solution.py:422
  8.9 1.3 %collective-permute-start = (bf16[1104,128]{1,0:T(8,128)(2,1)S(1)}, bf16[1104,128]{1,0:T(8,128)(2,1)S(1)}, u32[]{:S(2)}, u32[]{:S(2)}) collective-permute-start(bf16[1104,128]{1,0:T(8,128)(2,1)S(1)} %get-tuple-element.44), channel_id=1, source_target_pairs={{0,12},{4,8},{8,4},{12,0},{1,13},{5,9},{9,5},{13,1},{2,14},{6,10},... | collective-permute-start | bytes 847880 | tf_op jit(solution)/shard_map/ppermute | solution.py:418
  10.2 0.2 collective-permute-start.7
  10.4 0.9 %shard_map.86 = (bf16[4,2,32,128]{3,2,1,0:T(8,128)(2,1)S(1)}, bf16[4,2,2,16,128]{4,3,2,1,0:T(8,128)(2,1)S(1)}) custom-call(bf16[4,4,2048]{2,1,0:T(4,128)(2,1)} %new_query.1, bf16[4,2,4,512]{3,2,1,0:T(4,128)(2,1)} %new_kv.1), custom_call_target="tpu_custom_call" | custom-call | tf_op jit(solution)/shard_map/pallas_call | solution.py:180
  11.3 5.8 %collective-permute-done.3.refs_0_.tables = bf16[2192,128]{1,0:T(8,128)(2,1)S(1)} collective-permute-done((bf16[2192,128]{1,0:T(8,128)(2,1)S(1)}, bf16[2192,128]{1,0:T(8,128)(2,1)S(1)}, u32[]{:S(2)}, u32[]{:S(2)}) %collective-permute-start.3) | collective-permute-done | bytes 561184 | tf_op jit(solution)/shard_map/ppermute | solution.py:418
  17.1 0.2 shard_map.90
  17.3 2.8 %collective-permute-start.6 = (bf16[1024,128]{1,0:T(8,128)(2,1)S(1)}, bf16[1024,128]{1,0:T(8,128)(2,1)S(1)}, u32[]{:S(2)}, u32[]{:S(2)}) collective-permute-start(bf16[1024,128]{1,0:T(8,128)(2,1)S(1)} %get-tuple-element.62.theirs), channel_id=1, source_target_pairs={{0,1},{1,0},{2,3},{3,2},{4,5},{5,4},{6,7},{7,6},{8,9},{9,8},{10,11... | collective-permute-start | bytes 786440 | tf_op jit(solution)/shard_map/ppermute | solution.py:422
  20.0 0.0 collective-permute-done.2.other
  20.1 1.3 %shard_map.91 = (bf16[4,2,256,512]{3,2,1,0:T(8,128)(2,1)}, bf16[4,4,2048]{2,1,0:T(4,128)(2,1)}) custom-call(bf16[4,2,32,128]{3,2,1,0:T(8,128)(2,1)S(1)} %get-tuple-element.42.query, bf16[4,2,2,16,128]{4,3,2,1,0:T(8,128)(2,1)S(1)} %get-tuple-element.43.new_kv, ...), custom_call_target="tpu_custom_call", output_to_operand_aliasing={{0}: (6, {}), {1}: (7, {})} | custom-call | flops 16777216 | bytes 1048576 | tf_op jit(solution)/shard_map/pallas_call | solution.py:389
  21.4 8.3 %collective-permute-done.1.refs_0_.tables = bf16[2192,128]{1,0:T(8,128)(2,1)S(1)} collective-permute-done((bf16[2192,128]{1,0:T(8,128)(2,1)S(1)}, bf16[2192,128]{1,0:T(8,128)(2,1)S(1)}, u32[]{:S(2)}, u32[]{:S(2)}) %collective-permute-start.1) | collective-permute-done | bytes 561184 | tf_op jit(solution)/shard_map/ppermute | solution.py:418
  29.7 0.2 shard_map.92
  29.9 2.3 %collective-permute-start.5 = (bf16[1024,128]{1,0:T(8,128)(2,1)S(1)}, bf16[1024,128]{1,0:T(8,128)(2,1)S(1)}, u32[]{:S(2)}, u32[]{:S(2)}) collective-permute-start(bf16[1024,128]{1,0:T(8,128)(2,1)S(1)} %get-tuple-element.60.theirs), channel_id=1, source_target_pairs={{0,1},{1,0},{2,3},{3,2},{4,5},{5,4},{6,7},{7,6},{8,9},{9,8},{10,11... | collective-permute-start | bytes 786440 | tf_op jit(solution)/shard_map/ppermute | solution.py:422
  32.2 16.0 %collective-permute-done.refs_0_.tables.refs_1_ = bf16[1104,128]{1,0:T(8,128)(2,1)S(1)} collective-permute-done((bf16[1104,128]{1,0:T(8,128)(2,1)S(1)}, bf16[1104,128]{1,0:T(8,128)(2,1)S(1)}, u32[]{:S(2)}, u32[]{:S(2)}) %collective-permute-start) | collective-permute-done | bytes 282656 | tf_op jit(solution)/shard_map/ppermute | solution.py:418
  48.2 0.1 shard_map.93
  48.3 0.7 %collective-permute-start.4 = (bf16[512,128]{1,0:T(8,128)(2,1)S(1)}, bf16[512,128]{1,0:T(8,128)(2,1)S(1)}, u32[]{:S(2)}, u32[]{:S(2)}) collective-permute-start(bf16[512,128]{1,0:T(8,128)(2,1)S(1)} %get-tuple-element.58.theirs), channel_id=1, source_target_pairs={{0,1},{1,0},{2,3},{3,2},{4,5},{5,4},{6,7},{7,6},{8,9},{9,8},{10,11... | collective-permute-start | bytes 393224 | tf_op jit(solution)/shard_map/ppermute | solution.py:422
  49.0 0.0 collective-permute-done.6.other
  49.0 1.3 %shard_map.94 = (bf16[4,2,256,512]{3,2,1,0:T(8,128)(2,1)}, bf16[4,4,2048]{2,1,0:T(4,128)(2,1)}) custom-call(bf16[4,2,32,128]{3,2,1,0:T(8,128)(2,1)S(1)} %get-tuple-element.42.query, bf16[4,2,2,16,128]{4,3,2,1,0:T(8,128)(2,1)S(1)} %get-tuple-element.43.new_kv, ...), custom_call_target="tpu_custom_call", output_to_operand_aliasing={{0}: (6, {}), {1}: (7, {})} | custom-call | flops 16777216 | bytes 1048576 | tf_op jit(solution)/shard_map/pallas_call | solution.py:389
  50.3 0.0 collective-permute-done.5.other
  50.3 1.3 %shard_map.95 = (bf16[4,2,256,512]{3,2,1,0:T(8,128)(2,1)}, bf16[4,4,2048]{2,1,0:T(4,128)(2,1)}) custom-call(bf16[4,2,32,128]{3,2,1,0:T(8,128)(2,1)S(1)} %get-tuple-element.42.query, bf16[4,2,2,16,128]{4,3,2,1,0:T(8,128)(2,1)S(1)} %get-tuple-element.43.new_kv, ...), custom_call_target="tpu_custom_call", output_to_operand_aliasing={{0}: (6, {}), {1}: (7, {})} | custom-call | flops 16777216 | bytes 1048576 | tf_op jit(solution)/shard_map/pallas_call | solution.py:389
  51.7 0.0 collective-permute-done.4.other
  51.7 1.3 %shard_map.96 = (bf16[4,2,256,512]{3,2,1,0:T(8,128)(2,1)}, bf16[4,4,2048]{2,1,0:T(4,128)(2,1)}, bf16[2,32,512]{2,1,0:T(8,128)(2,1)S(1)}, f32[2,32,128]{2,1,0:T(8,128)S(1)}, f32[2,32,128]{2,1,0:T(8,128)S(1)}) custom-call(bf16[4,2,32,128]{3,2,1,0:T(8,128)(2,1)S(1)} %get-tuple-element.42.query, ...), custom_call_target="tpu_custom_call", output_to_operand_aliasing={{0}: (6, {}), {1}: (7, {})} | custom-call | flops 8388608 | bytes 1048576 | tf_op jit(solution)/shard_map/pallas_call | solution.py:389
  53.0 1.2 %collective-permute-done.7.refs_0_ = bf16[1088,128]{1,0:T(8,128)(2,1)S(1)} collective-permute-done((bf16[1088,128]{1,0:T(8,128)(2,1)S(1)}, bf16[1088,128]{1,0:T(8,128)(2,1)S(1)}, u32[]{:S(2)}, u32[]{:S(2)}) %collective-permute-start.7) | collective-permute-done | bytes 278560 | tf_op jit(solution)/shard_map/ppermute | solution.py:418
  54.2 0.1 shard_map.97
  54.3 0.6 collective-permute-start.8
  54.8 0.8 %shard_map.98 = (bf16[4,2,256,512]{3,2,1,0:T(8,128)(2,1)}, bf16[4,4,2048]{2,1,0:T(4,128)(2,1)}, f32[2,32,128]{2,1,0:T(8,128)S(1)}) custom-call(bf16[2,32,512]{2,1,0:T(8,128)(2,1)S(1)} %get-tuple-element.69.weights, f32[2,32,128]{2,1,0:T(8,128)S(1)} %get-tuple-element.70.share, ...), custom_call_target="tpu_custom_call", output_to_operand_aliasing={{0}: (4, {}), {1}: (5, {})} | custom-call | flops 4194304 | bytes 1048576 | tf_op jit(solution)/shard_map/pallas_call | solution.py:389
  55.6 0.2 collective-permute-done.8.other
  55.8 0.8 %shard_map.99 = (bf16[4,2,256,512]{3,2,1,0:T(8,128)(2,1)}, bf16[4,4,2048]{2,1,0:T(4,128)(2,1)}) custom-call(bf16[2,32,512]{2,1,0:T(8,128)(2,1)S(1)} %get-tuple-element.69.weights, f32[2,32,128]{2,1,0:T(8,128)S(1)} %get-tuple-element.78.half, f32[2,32,128]{2,1,0:T(8,128)S(1)} %get-tuple-element.79.totals, ...), custom_call_target="tpu_custom_call", output_to_operand_aliasing={{0}: (4, {}), {1}: (5, {})} | custom-call | flops 4194304 | bytes 1048576 | tf_op jit(solution)/shard_map/pallas_call | solution.py:389
Async XLA Ops:
  2.5 14.6 %collective-permute-start.3 = (bf16[2192,128]{1,0:T(8,128)(2,1)S(1)}, bf16[2192,128]{1,0:T(8,128)(2,1)S(1)}, u32[]{:S(2)}, u32[]{:S(2)}) collective-permute-start(bf16[2192,128]{1,0:T(8,128)(2,1)S(1)} %shard_map.89), channel_id=1, source_target_pairs={{0,8},{4,0},{8,12},{12,4},{1,9},{5,1},{9,13},{13,5},{2,10},{6,2},{... | collective-permute-start | bytes 1683464 | tf_op jit(solution)/shard_map/ppermute | solution.py:418
  5.0 24.7 %collective-permute-start.1 = (bf16[2192,128]{1,0:T(8,128)(2,1)S(1)}, bf16[2192,128]{1,0:T(8,128)(2,1)S(1)}, u32[]{:S(2)}, u32[]{:S(2)}) collective-permute-start(bf16[2192,128]{1,0:T(8,128)(2,1)S(1)} %get-tuple-element.45), channel_id=1, source_target_pairs={{0,4},{4,12},{8,0},{12,8},{1,5},{5,13},{9,1},{13,9},{2,6},{6,14},{... | collective-permute-start | bytes 1683464 | tf_op jit(solution)/shard_map/ppermute | solution.py:418
  7.6 12.5 %collective-permute-start.2 = (bf16[1024,128]{1,0:T(8,128)(2,1)S(1)}, bf16[1024,128]{1,0:T(8,128)(2,1)S(1)}, u32[]{:S(2)}, u32[]{:S(2)}) collective-permute-start(bf16[1024,128]{1,0:T(8,128)(2,1)S(1)} %get-tuple-element.48.theirs), channel_id=1, source_target_pairs={{0,1},{1,0},{2,3},{3,2},{4,5},{5,4},{6,7},{7,6},{8,9},{9,8},{10,11... | collective-permute-start | bytes 786440 | tf_op jit(solution)/shard_map/ppermute | solution.py:422
  8.9 39.3 %collective-permute-start = (bf16[1104,128]{1,0:T(8,128)(2,1)S(1)}, bf16[1104,128]{1,0:T(8,128)(2,1)S(1)}, u32[]{:S(2)}, u32[]{:S(2)}) collective-permute-start(bf16[1104,128]{1,0:T(8,128)(2,1)S(1)} %get-tuple-element.44), channel_id=1, source_target_pairs={{0,12},{4,8},{8,4},{12,0},{1,13},{5,9},{9,5},{13,1},{2,14},{6,10},... | collective-permute-start | bytes 847880 | tf_op jit(solution)/shard_map/ppermute | solution.py:418
  10.2 44.0 %collective-permute-start.7 = (bf16[1088,128]{1,0:T(8,128)(2,1)S(1)}, bf16[1088,128]{1,0:T(8,128)(2,1)S(1)}, u32[]{:S(2)}, u32[]{:S(2)}) collective-permute-start(bf16[1088,128]{1,0:T(8,128)(2,1)S(1)} %get-tuple-element.71), channel_id=1, source_target_pairs={{0,12},{4,8},{8,4},{12,0},{1,13},{5,9},{9,5},{13,1},{2,14},{6,10},... | collective-permute-start | bytes 835592 | tf_op jit(solution)/shard_map/ppermute | solution.py:418
  17.3 31.7 %collective-permute-start.6 = (bf16[1024,128]{1,0:T(8,128)(2,1)S(1)}, bf16[1024,128]{1,0:T(8,128)(2,1)S(1)}, u32[]{:S(2)}, u32[]{:S(2)}) collective-permute-start(bf16[1024,128]{1,0:T(8,128)(2,1)S(1)} %get-tuple-element.62.theirs), channel_id=1, source_target_pairs={{0,1},{1,0},{2,3},{3,2},{4,5},{5,4},{6,7},{7,6},{8,9},{9,8},{10,11... | collective-permute-start | bytes 786440 | tf_op jit(solution)/shard_map/ppermute | solution.py:422
  29.9 20.4 %collective-permute-start.5 = (bf16[1024,128]{1,0:T(8,128)(2,1)S(1)}, bf16[1024,128]{1,0:T(8,128)(2,1)S(1)}, u32[]{:S(2)}, u32[]{:S(2)}) collective-permute-start(bf16[1024,128]{1,0:T(8,128)(2,1)S(1)} %get-tuple-element.60.theirs), channel_id=1, source_target_pairs={{0,1},{1,0},{2,3},{3,2},{4,5},{5,4},{6,7},{7,6},{8,9},{9,8},{10,11... | collective-permute-start | bytes 786440 | tf_op jit(solution)/shard_map/ppermute | solution.py:422
  48.3 3.4 %collective-permute-start.4 = (bf16[512,128]{1,0:T(8,128)(2,1)S(1)}, bf16[512,128]{1,0:T(8,128)(2,1)S(1)}, u32[]{:S(2)}, u32[]{:S(2)}) collective-permute-start(bf16[512,128]{1,0:T(8,128)(2,1)S(1)} %get-tuple-element.58.theirs), channel_id=1, source_target_pairs={{0,1},{1,0},{2,3},{3,2},{4,5},{5,4},{6,7},{7,6},{8,9},{9,8},{10,11... | collective-permute-start | bytes 393224 | tf_op jit(solution)/shard_map/ppermute | solution.py:422
  54.3 1.5 %collective-permute-start.8 = (bf16[512,128]{1,0:T(8,128)(2,1)S(1)}, bf16[512,128]{1,0:T(8,128)(2,1)S(1)}, u32[]{:S(2)}, u32[]{:S(2)}) collective-permute-start(bf16[512,128]{1,0:T(8,128)(2,1)S(1)} %get-tuple-element.75.theirs), channel_id=1, source_target_pairs={{0,1},{1,0},{2,3},{3,2},{4,5},{5,4},{6,7},{7,6},{8,9},{9,8},{10,11... | collective-permute-start | bytes 393224 | tf_op jit(solution)/shard_map/ppermute | solution.py:422

commit v9 on v7

--- a/solution.py
+++ b/solution.py
@@ -183,11 +183,7 @@
     return copies
 
 
-def rebuild_kernel(size, parts, chained, *refs):
-    message, tables = refs[0], refs[0 if 0 in parts else 1]
-    refs = refs[1 if 0 in parts else 2:]
-    refs = refs[2 * chained:]
-    _, _, mine, theirs = refs
+def rebuild_heads(size, parts, message, tables, mine, theirs):
     sub = lax.axis_index("sub")
     rest = size.heads - size.mine
     side_at = size.side_at(parts if 0 in parts else (0,))
@@ -215,8 +211,13 @@
                     out[to + i * size.repeat:to + (i + 1) * size.repeat, :] = value
 
 
-def rebuild(size, parts, message, tables, state):
-    args = [vmem(message)] + ([vmem(tables)] if tables is not None else [])
+def rebuild_kernel(size, parts, chained, message, *refs):
+    _, _, mine, theirs = refs[2 * chained:]
+    rebuild_heads(size, parts, message, message, mine, theirs)
+
+
+def rebuild(size, parts, message, state):
+    args = [vmem(message)]
     in_specs = [IN_VMEM] * len(args)
     aliases = {}
     if state is not None:
@@ -315,7 +316,7 @@
 
 
 def weights_kernel(size, k, query, new_kv, tables, mine, other, theirs, *refs):
-    cache, _, weights, share, totals, sems = refs[2:]
+    cache, _, weights, lent, share, totals, sems = refs[2:]
     row = size.source_row(k)
     copies = start_store(size, k, (0,), cache, mine, theirs, sems)
     live_mine, live_other, causal = masks(size, tables, (0,), new_kv.shape[3])
@@ -325,34 +326,33 @@
             size, j, query[row, j], new_kv[row, 0, j], mine[keys, :], other[keys, :],
             live_mine, live_other, causal,
         )
-        weights[j, :, :size.span] = w0
-        weights[j, :, size.span:] = w1
+        weights[j] = w0
+        lent[j] = w1
         share[j] = jnp.dot(w2, new_kv[row, 1, j], preferred_element_type=F32)
         totals[j] = jnp.broadcast_to(total, totals.shape[1:])
     for copy in copies:
         copy.wait()
 
 
-def half_kernel(size, k, weights, share, mine, theirs, *refs):
-    cache, _, half, sems = refs[2:]
-    copies = start_store(size, k, (1,), cache, mine, theirs, sems)
+def values_kernel(size, weights, share, lent, message, tables, *refs):
+    _, _, mine, theirs, kept, given = refs[2:]
+    rebuild_heads(size, (1,), message, tables, mine, theirs)
     for j in range(size.mine):
         values = slice(j * size.span, (j + 1) * size.span)
-        half[j] = share[j] + jnp.dot(
-            weights[j, :, :size.span], mine[values, :], preferred_element_type=F32
-        )
-    for copy in copies:
+        kept[j] = share[j] + jnp.dot(weights[j], mine[values, :], preferred_element_type=F32)
+        given[j] = jnp.dot(lent[j], theirs[values, :], preferred_element_type=F32)
+
+
+def store_kernel(size, k, mine, theirs, *refs):
+    cache, _, sems = refs[2:]
+    for copy in start_store(size, k, (1,), cache, mine, theirs, sems):
         copy.wait()
 
 
-def finish_kernel(size, k, weights, half, totals, other, *refs):
+def finish_kernel(size, k, kept, got, totals, *refs):
     _, attended, made, flat, sem = refs[2:]
     for j in range(size.mine):
-        values = slice(j * size.span, (j + 1) * size.span)
-        acc = half[j] + jnp.dot(
-            weights[j, :, size.span:], other[values, :], preferred_element_type=F32
-        )
-        flat[j] = acc / totals[j]
+        flat[j] = (kept[j] + got[j]) / totals[j]
     store_heads(size, k, flat, made, attended, sem, ())
 
 
@@ -411,32 +411,34 @@
         return state
 
     def take(k, parts, state):
-        tables = None if 0 in parts else message[last, (0,)]
-        state, mine, theirs = rebuild(size, parts, message[k, parts], tables, state)
+        state, mine, theirs = rebuild(size, parts, message[k, parts], state)
         return state, mine, swapped(theirs), theirs
 
     state, held = None, []
     for k in [0] + order[:-1]:
         state, *each = take(k, both, state)
         held.append((k, *each))
-        if k and k != order[-2]:
+        if k:
             state = attend(*held.pop(0), state)
+    state = attend(*held.pop(0), state)
     state, *keys = take(last, (0,), state)
-    for each in held:
-        state = attend(*each, state)
-    state, (weights, share, totals) = chained_call(
+    half = pltpu.VMEM((size.mine, size.wide, size.span), BF)
+    state, (weights, lent, share, totals) = chained_call(
         size, functools.partial(weights_kernel, size, last),
-        (query, fresh, message[last, (0,)], *keys), state,
-        [pltpu.VMEM((size.mine, size.wide, 2 * size.span), BF), wide, wide], [sems], flops // 2,
-    )
-    state, mine, other, theirs = take(last, (1,), state)
-    state, (half,) = chained_call(
-        size, functools.partial(half_kernel, size, last),
-        (weights, share, mine, theirs), state, [wide], [sems], flops // 4,
-    )
+        (query, fresh, message[last, (0,)], *keys), state, [half, half, wide, wide], [sems], flops // 2,
+    )
+    given = pltpu.VMEM((size.mine * size.span, HEAD_DIM), BF)
+    state, (mine, theirs, kept, given) = chained_call(
+        size, functools.partial(values_kernel, size),
+        (weights, share, swapped(lent), message[last, (1,)], message[last, (0,)]), state,
+        [given, given, wide, wide], [], flops // 2,
+    )
+    got = swapped(given)
     state, _ = chained_call(
-        size, functools.partial(finish_kernel, size, last),
-        (weights, half, totals, other), state, [], rows, flops // 4,
+        size, functools.partial(store_kernel, size, last), (mine, theirs), state, [], [sems], 0
+    )
+    state, _ = chained_call(
+        size, functools.partial(finish_kernel, size, last), (kept, got, totals), state, [], rows, 0
     )
     return state
 

time: 56.9 us -> 56.8 us (level)
  waiting for transfers between devices: 31.7 us -> 31.1 us
    ppermute x4, waiting for transfers between devices: 31.5 us -> 30.1 us  [body(): msg = lax.ppermute(msg, 'pool', list(enumerate(far(n, k))))]
    ppermute x5 -> x6, waiting for transfers between devices: 0.21 us -> 1.09 us  [swapped(): return lax.ppermute(x, 'sub', [(0, 1), (1, 0)])]
    ppermute x5 -> x6, starting transfers between devices: 7.53 us -> 7.93 us  [swapped(): return lax.ppermute(x, 'sub', [(0, 1), (1, 0)])]
    pallas_call x6 -> x7, Pallas kernels: 6.82 us -> 6.93 us  [chained_call(): pl.pallas_call(kernel, in_specs=[IN_VMEM] * many + [IN_HBM, IN_HBM], out_...]
  transfers between devices with their start and end apart: 9 -> 10, of which waited for: 5 -> 6; matrix products, arithmetic and copies ran while one was open for 0% -> 0% of each run, Pallas kernels for 18% -> 18%
where the time goes in v9:
time: 56.8 us; the launch traced here: 56.4 us
  waiting for transfers between devices  31.1 us (55%)
  Pallas kernels  12.7 us (22%)
  starting transfers between devices  11.9 us (21%)
  between operations  0.72 us (1%)
    ppermute x4, waiting for transfers between devices, body(): msg = lax.ppermute(msg, 'pool', list(enumerate(far(n, k))))  30.1 us
    ppermute x6, starting transfers between devices, swapped(): return lax.ppermute(x, 'sub', [(0, 1), (1, 0)])  7.93 us
    pallas_call x7, Pallas kernels, chained_call(): pl.pallas_call(kernel, in_specs=[IN_VMEM] * many + [IN_HBM, IN_HBM], out_...  6.93 us
    pallas_call x2, Pallas kernels, pack(): pl.pallas_call(functools.partial(pack_kernel, size, plan), out_shape=shap...  4.16 us
    ppermute x4, starting transfers between devices, body(): msg = lax.ppermute(msg, 'pool', list(enumerate(far(n, k))))  3.95 us
  transfers between devices with their start and end apart: 10, of which 6 were waited for; matrix products, arithmetic and copies ran while one was open for 0% of the time, Pallas kernels for 18%

profile of v9, /device:TPU:9, one launch (start us, length us, event | category | flops | bytes accessed | tf_op | source)
XLA Modules:
  0.0 56.4 jit_solution(15846964717650366298)
XLA Ops:
  0.6 1.9 %shard_map.89 = bf16[2192,128]{1,0:T(8,128)(2,1)S(1)} custom-call(s32[4]{0:T(128)} %route.3, s32[4]{0:T(128)} %lengths.3, bf16[4,2,256,512]{3,2,1,0:T(8,128)(2,1)} %deltas.3, bf16[4,2,16,512]{3,2,1,0:T(8,128)(2,1)} %anchors.3, bf16[4,2,512]{2,1,0:T(2,128)(2,1)} %scale.3), custom_call_target="tpu_custom_call" | custom-call | bytes 524288 | tf_op jit(solution)/shard_map/pallas_call | solution.py:116
  2.5 0.1 collective-permute-start.3
  2.6 2.3 %shard_map.87 = (bf16[2192,128]{1,0:T(8,128)(2,1)S(1)}, bf16[1104,128]{1,0:T(8,128)(2,1)S(1)}, bf16[1088,128]{1,0:T(8,128)(2,1)S(1)}, bf16[2192,128]{1,0:T(8,128)(2,1)S(1)}) custom-call(s32[4]{0:T(128)} %route.3, s32[4]{0:T(128)} %lengths.3, bf16[4,2,256,512]{3,2,1,0:T(8,128)(2,1)} %deltas.3, bf16[4,2,16,512]{3,2,1,0:T(8,128)(2,1)} %anchors.3, ...), custom_call_target="tpu_custom_call" | custom-call | bytes 1572864 | tf_op jit(solution)/shard_map/pallas_call | solution.py:116
  4.9 2.4 %collective-permute-start.1 = (bf16[2192,128]{1,0:T(8,128)(2,1)S(1)}, bf16[2192,128]{1,0:T(8,128)(2,1)S(1)}, u32[]{:S(2)}, u32[]{:S(2)}) collective-permute-start(bf16[2192,128]{1,0:T(8,128)(2,1)S(1)} %get-tuple-element.47), channel_id=1, source_target_pairs={{0,4},{4,12},{8,0},{12,8},{1,5},{5,13},{9,1},{13,9},{2,6},{6,14},{... | collective-permute-start | bytes 1683464 | tf_op jit(solution)/shard_map/ppermute | solution.py:391
  7.3 0.2 shard_map.88
  7.5 1.3 %collective-permute-start.2 = (bf16[1024,128]{1,0:T(8,128)(2,1)S(1)}, bf16[1024,128]{1,0:T(8,128)(2,1)S(1)}, u32[]{:S(2)}, u32[]{:S(2)}) collective-permute-start(bf16[1024,128]{1,0:T(8,128)(2,1)S(1)} %get-tuple-element.50.theirs), channel_id=1, source_target_pairs={{0,1},{1,0},{2,3},{3,2},{4,5},{5,4},{6,7},{7,6},{8,9},{9,8},{10,11... | collective-permute-start | bytes 786440 | tf_op jit(solution)/shard_map/ppermute | solution.py:395
  8.8 1.3 %collective-permute-start = (bf16[1104,128]{1,0:T(8,128)(2,1)S(1)}, bf16[1104,128]{1,0:T(8,128)(2,1)S(1)}, u32[]{:S(2)}, u32[]{:S(2)}) collective-permute-start(bf16[1104,128]{1,0:T(8,128)(2,1)S(1)} %get-tuple-element.46), channel_id=1, source_target_pairs={{0,12},{4,8},{8,4},{12,0},{1,13},{5,9},{9,5},{13,1},{2,14},{6,10},... | collective-permute-start | bytes 847880 | tf_op jit(solution)/shard_map/ppermute | solution.py:391
  10.1 0.9 %shard_map.86 = (bf16[4,2,32,128]{3,2,1,0:T(8,128)(2,1)S(1)}, bf16[4,2,2,16,128]{4,3,2,1,0:T(8,128)(2,1)S(1)}) custom-call(bf16[4,4,2048]{2,1,0:T(4,128)(2,1)} %new_query.1, bf16[4,2,4,512]{3,2,1,0:T(4,128)(2,1)} %new_kv.1), custom_call_target="tpu_custom_call" | custom-call | tf_op jit(solution)/shard_map/pallas_call | solution.py:153
  11.0 6.1 %collective-permute-done.3.message.tables = bf16[2192,128]{1,0:T(8,128)(2,1)S(1)} collective-permute-done((bf16[2192,128]{1,0:T(8,128)(2,1)S(1)}, bf16[2192,128]{1,0:T(8,128)(2,1)S(1)}, u32[]{:S(2)}, u32[]{:S(2)}) %collective-permute-start.3) | collective-permute-done | bytes 561184 | tf_op jit(solution)/shard_map/ppermute | solution.py:391
  17.1 0.2 shard_map.90
  17.3 2.8 %collective-permute-start.5 = (bf16[1024,128]{1,0:T(8,128)(2,1)S(1)}, bf16[1024,128]{1,0:T(8,128)(2,1)S(1)}, u32[]{:S(2)}, u32[]{:S(2)}) collective-permute-start(bf16[1024,128]{1,0:T(8,128)(2,1)S(1)} %get-tuple-element.60.theirs), channel_id=1, source_target_pairs={{0,1},{1,0},{2,3},{3,2},{4,5},{5,4},{6,7},{7,6},{8,9},{9,8},{10,11... | collective-permute-start | bytes 786440 | tf_op jit(solution)/shard_map/ppermute | solution.py:395
  20.0 0.0 collective-permute-done.2.other
  20.0 1.3 %shard_map.91 = (bf16[4,2,256,512]{3,2,1,0:T(8,128)(2,1)}, bf16[4,4,2048]{2,1,0:T(4,128)(2,1)}) custom-call(bf16[4,2,32,128]{3,2,1,0:T(8,128)(2,1)S(1)} %get-tuple-element.44.query, bf16[4,2,2,16,128]{4,3,2,1,0:T(8,128)(2,1)S(1)} %get-tuple-element.45.new_kv, ...), custom_call_target="tpu_custom_call", output_to_operand_aliasing={{0}: (6, {}), {1}: (7, {})} | custom-call | flops 16777216 | bytes 1048576 | tf_op jit(solution)/shard_map/pallas_call | solution.py:362
  21.4 8.3 %collective-permute-done.1.message.tables = bf16[2192,128]{1,0:T(8,128)(2,1)S(1)} collective-permute-done((bf16[2192,128]{1,0:T(8,128)(2,1)S(1)}, bf16[2192,128]{1,0:T(8,128)(2,1)S(1)}, u32[]{:S(2)}, u32[]{:S(2)}) %collective-permute-start.1) | collective-permute-done | bytes 561184 | tf_op jit(solution)/shard_map/ppermute | solution.py:391
  29.7 0.2 shard_map.92
  29.9 2.3 %collective-permute-start.4 = (bf16[1024,128]{1,0:T(8,128)(2,1)S(1)}, bf16[1024,128]{1,0:T(8,128)(2,1)S(1)}, u32[]{:S(2)}, u32[]{:S(2)}) collective-permute-start(bf16[1024,128]{1,0:T(8,128)(2,1)S(1)} %get-tuple-element.58.theirs), channel_id=1, source_target_pairs={{0,1},{1,0},{2,3},{3,2},{4,5},{5,4},{6,7},{7,6},{8,9},{9,8},{10,11... | collective-permute-start | bytes 786440 | tf_op jit(solution)/shard_map/ppermute | solution.py:395
  32.2 0.2 collective-permute-start.8
  32.3 0.0 collective-permute-done.5.other
  32.3 1.3 %shard_map.93 = (bf16[4,2,256,512]{3,2,1,0:T(8,128)(2,1)}, bf16[4,4,2048]{2,1,0:T(4,128)(2,1)}) custom-call(bf16[4,2,32,128]{3,2,1,0:T(8,128)(2,1)S(1)} %get-tuple-element.44.query, bf16[4,2,2,16,128]{4,3,2,1,0:T(8,128)(2,1)S(1)} %get-tuple-element.45.new_kv, ...), custom_call_target="tpu_custom_call", output_to_operand_aliasing={{0}: (6, {}), {1}: (7, {})} | custom-call | flops 16777216 | bytes 1048576 | tf_op jit(solution)/shard_map/pallas_call | solution.py:362
  33.7 0.0 collective-permute-done.4.other
  33.7 1.3 %shard_map.94 = (bf16[4,2,256,512]{3,2,1,0:T(8,128)(2,1)}, bf16[4,4,2048]{2,1,0:T(4,128)(2,1)}) custom-call(bf16[4,2,32,128]{3,2,1,0:T(8,128)(2,1)S(1)} %get-tuple-element.44.query, bf16[4,2,2,16,128]{4,3,2,1,0:T(8,128)(2,1)S(1)} %get-tuple-element.45.new_kv, ...), custom_call_target="tpu_custom_call", output_to_operand_aliasing={{0}: (6, {}), {1}: (7, {})} | custom-call | flops 16777216 | bytes 1048576 | tf_op jit(solution)/shard_map/pallas_call | solution.py:362
  35.0 13.1 %collective-permute-done.message.tables = bf16[1104,128]{1,0:T(8,128)(2,1)S(1)} collective-permute-done((bf16[1104,128]{1,0:T(8,128)(2,1)S(1)}, bf16[1104,128]{1,0:T(8,128)(2,1)S(1)}, u32[]{:S(2)}, u32[]{:S(2)}) %collective-permute-start) | collective-permute-done | bytes 282656 | tf_op jit(solution)/shard_map/ppermute | solution.py:391
  48.2 0.1 shard_map.95
  48.3 0.7 %collective-permute-start.6 = (bf16[512,128]{1,0:T(8,128)(2,1)S(1)}, bf16[512,128]{1,0:T(8,128)(2,1)S(1)}, u32[]{:S(2)}, u32[]{:S(2)}) collective-permute-start(bf16[512,128]{1,0:T(8,128)(2,1)S(1)} %get-tuple-element.68.theirs), channel_id=1, source_target_pairs={{0,1},{1,0},{2,3},{3,2},{4,5},{5,4},{6,7},{7,6},{8,9},{9,8},{10,11... | collective-permute-start | bytes 393224 | tf_op jit(solution)/shard_map/ppermute | solution.py:395
  48.9 1.0 %collective-permute-done.6.other = bf16[512,128]{1,0:T(8,128)(2,1)S(1)} collective-permute-done((bf16[512,128]{1,0:T(8,128)(2,1)S(1)}, bf16[512,128]{1,0:T(8,128)(2,1)S(1)}, u32[]{:S(2)}, u32[]{:S(2)}) %collective-permute-start.6) | collective-permute-done | bytes 131104 | tf_op jit(solution)/shard_map/ppermute | solution.py:395
  49.9 1.3 %shard_map.96 = (bf16[4,2,256,512]{3,2,1,0:T(8,128)(2,1)}, bf16[4,4,2048]{2,1,0:T(4,128)(2,1)}, bf16[2,32,256]{2,1,0:T(8,128)(2,1)S(1)}, bf16[2,32,256]{2,1,0:T(...) custom-call(bf16[4,2,32,128]{3,2,1,0:T(8,128)(2,1)S(1)} %get-tuple-e, ...), custom_call_target="tpu_custom_call", output_to_operand_aliasing={{0}: (6, {}), {1}: (7, {})} | custom-call | flops 8388608 | bytes 1048576 | tf_op jit(solution)/shard_map/pallas_call | solution.py:362
  51.2 0.4 collective-permute-start.7
  51.6 2.5 %collective-permute-done.8.message = bf16[1088,128]{1,0:T(8,128)(2,1)S(1)} collective-permute-done((bf16[1088,128]{1,0:T(8,128)(2,1)S(1)}, bf16[1088,128]{1,0:T(8,128)(2,1)S(1)}, u32[]{:S(2)}, u32[]{:S(2)}) %collective-permute-start.8) | collective-permute-done | bytes 278560 | tf_op jit(solution)/shard_map/ppermute | solution.py:391
  54.2 0.0 collective-permute-done.7.lent
  54.2 0.3 shard_map.97
  54.4 0.5 collective-permute-start.9
  55.0 0.8 %shard_map.98 = (bf16[4,2,256,512]{3,2,1,0:T(8,128)(2,1)}, bf16[4,4,2048]{2,1,0:T(4,128)(2,1)}) custom-call(bf16[512,128]{1,0:T(8,128)(2,1)S(1)} %get-tuple-element.80.mine, bf16[512,128]{1,0:T(8,128)(2,1)S(1)} %get-tuple-element.81.theirs, bf16[4,2,256,512]{3,2,1,0:T(8,128)(2,1)} %get-tuple-element.82.refs_0_, ...), custom_call_target="tpu_custom_call", output_to_operand_aliasing={{0}: (2, {}), {1}: (3, {})} | custom-call | bytes 1048576 | tf_op jit(solution)/shard_map/pallas_call | solution.py:362
  55.7 0.1 collective-permute-done.9.got
  55.8 0.6 %shard_map.99 = (bf16[4,2,256,512]{3,2,1,0:T(8,128)(2,1)}, bf16[4,4,2048]{2,1,0:T(4,128)(2,1)}) custom-call(f32[2,32,128]{2,1,0:T(8,128)S(1)} %get-tuple-element.77.kept, f32[2,32,128]{2,1,0:T(8,128)S(1)} %collective-permute-done.9.got, f32[2,32,128]{2,1,0:T(8,128)S(1)} %get-tuple-element.79.totals, ...), custom_call_target="tpu_custom_call", output_to_operand_aliasing={{0}: (3, {}), {1}: (4, {})} | custom-call | bytes 1048576 | tf_op jit(solution)/shard_map/pallas_call | solution.py:362
Async XLA Ops:
  2.5 14.6 %collective-permute-start.3 = (bf16[2192,128]{1,0:T(8,128)(2,1)S(1)}, bf16[2192,128]{1,0:T(8,128)(2,1)S(1)}, u32[]{:S(2)}, u32[]{:S(2)}) collective-permute-start(bf16[2192,128]{1,0:T(8,128)(2,1)S(1)} %shard_map.89), channel_id=1, source_target_pairs={{0,8},{4,0},{8,12},{12,4},{1,9},{5,1},{9,13},{13,5},{2,10},{6,2},{... | collective-permute-start | bytes 1683464 | tf_op jit(solution)/shard_map/ppermute | solution.py:391
  4.9 24.8 %collective-permute-start.1 = (bf16[2192,128]{1,0:T(8,128)(2,1)S(1)}, bf16[2192,128]{1,0:T(8,128)(2,1)S(1)}, u32[]{:S(2)}, u32[]{:S(2)}) collective-permute-start(bf16[2192,128]{1,0:T(8,128)(2,1)S(1)} %get-tuple-element.47), channel_id=1, source_target_pairs={{0,4},{4,12},{8,0},{12,8},{1,5},{5,13},{9,1},{13,9},{2,6},{6,14},{... | collective-permute-start | bytes 1683464 | tf_op jit(solution)/shard_map/ppermute | solution.py:391
  7.5 12.6 %collective-permute-start.2 = (bf16[1024,128]{1,0:T(8,128)(2,1)S(1)}, bf16[1024,128]{1,0:T(8,128)(2,1)S(1)}, u32[]{:S(2)}, u32[]{:S(2)}) collective-permute-start(bf16[1024,128]{1,0:T(8,128)(2,1)S(1)} %get-tuple-element.50.theirs), channel_id=1, source_target_pairs={{0,1},{1,0},{2,3},{3,2},{4,5},{5,4},{6,7},{7,6},{8,9},{9,8},{10,11... | collective-permute-start | bytes 786440 | tf_op jit(solution)/shard_map/ppermute | solution.py:395
  8.8 39.4 %collective-permute-start = (bf16[1104,128]{1,0:T(8,128)(2,1)S(1)}, bf16[1104,128]{1,0:T(8,128)(2,1)S(1)}, u32[]{:S(2)}, u32[]{:S(2)}) collective-permute-start(bf16[1104,128]{1,0:T(8,128)(2,1)S(1)} %get-tuple-element.46), channel_id=1, source_target_pairs={{0,12},{4,8},{8,4},{12,0},{1,13},{5,9},{9,5},{13,1},{2,14},{6,10},... | collective-permute-start | bytes 847880 | tf_op jit(solution)/shard_map/ppermute | solution.py:391
  17.3 15.1 %collective-permute-start.5 = (bf16[1024,128]{1,0:T(8,128)(2,1)S(1)}, bf16[1024,128]{1,0:T(8,128)(2,1)S(1)}, u32[]{:S(2)}, u32[]{:S(2)}) collective-permute-start(bf16[1024,128]{1,0:T(8,128)(2,1)S(1)} %get-tuple-element.60.theirs), channel_id=1, source_target_pairs={{0,1},{1,0},{2,3},{3,2},{4,5},{5,4},{6,7},{7,6},{8,9},{9,8},{10,11... | collective-permute-start | bytes 786440 | tf_op jit(solution)/shard_map/ppermute | solution.py:395
  29.9 3.8 %collective-permute-start.4 = (bf16[1024,128]{1,0:T(8,128)(2,1)S(1)}, bf16[1024,128]{1,0:T(8,128)(2,1)S(1)}, u32[]{:S(2)}, u32[]{:S(2)}) collective-permute-start(bf16[1024,128]{1,0:T(8,128)(2,1)S(1)} %get-tuple-element.58.theirs), channel_id=1, source_target_pairs={{0,1},{1,0},{2,3},{3,2},{4,5},{5,4},{6,7},{7,6},{8,9},{9,8},{10,11... | collective-permute-start | bytes 786440 | tf_op jit(solution)/shard_map/ppermute | solution.py:395
  32.2 22.0 %collective-permute-start.8 = (bf16[1088,128]{1,0:T(8,128)(2,1)S(1)}, bf16[1088,128]{1,0:T(8,128)(2,1)S(1)}, u32[]{:S(2)}, u32[]{:S(2)}) collective-permute-start(bf16[1088,128]{1,0:T(8,128)(2,1)S(1)} %get-tuple-element.74), channel_id=1, source_target_pairs={{0,12},{4,8},{8,4},{12,0},{1,13},{5,9},{9,5},{13,1},{2,14},{6,10},... | collective-permute-start | bytes 835592 | tf_op jit(solution)/shard_map/ppermute | solution.py:391
  48.3 1.6 %collective-permute-start.6 = (bf16[512,128]{1,0:T(8,128)(2,1)S(1)}, bf16[512,128]{1,0:T(8,128)(2,1)S(1)}, u32[]{:S(2)}, u32[]{:S(2)}) collective-permute-start(bf16[512,128]{1,0:T(8,128)(2,1)S(1)} %get-tuple-element.68.theirs), channel_id=1, source_target_pairs={{0,1},{1,0},{2,3},{3,2},{4,5},{5,4},{6,7},{7,6},{8,9},{9,8},{10,11... | collective-permute-start | bytes 393224 | tf_op jit(solution)/shard_map/ppermute | solution.py:395
  51.2 2.9 %collective-permute-start.7 = (bf16[2,32,256]{2,1,0:T(8,128)(2,1)S(1)}, bf16[2,32,256]{2,1,0:T(8,128)(2,1)S(1)}, u32[]{:S(2)}, u32[]{:S(2)}) collective-permute-start(bf16[2,32,256]{2,1,0:T(8,128)(2,1)S(1)} %get-tuple-element.73), channel_id=1, source_target_pairs={{0,1},{1,0},{2,3},{3,2},{4,5},{5,4},{6,7},{7,6},{8,9},{9,8},{10,11... | collective-permute-start | bytes 98312 | tf_op jit(solution)/shard_map/ppermute | solution.py:395
  54.4 1.4 %collective-permute-start.9 = (f32[2,32,128]{2,1,0:T(8,128)S(1)}, f32[2,32,128]{2,1,0:T(8,128)S(1)}, u32[]{:S(2)}, u32[]{:S(2)}) collective-permute-start(f32[2,32,128]{2,1,0:T(8,128)S(1)} %get-tuple-element.78), channel_id=1, source_target_pairs={{0,1},{1,0},{2,3},{3,2},{4,5},{5,4},{6,7},{7,6},{8,9},{9,8},{10,11... | collective-permute-start | bytes 98312 | tf_op jit(solution)/shard_map/ppermute | solution.py:395

commit v10 on v9

--- a/solution.py
+++ b/solution.py
@@ -31,8 +31,7 @@
 
 
 def far(n, k):
-    ring = (0, 2, 3, 1) if n == 4 else tuple(range(n))
-    return tuple(ring[(ring.index(z) + k) % n] for z in range(n))
+    return tuple(z ^ k for z in range(n))
 
 
 def pick(values, at):
@@ -65,7 +64,7 @@
         return self.side_at(parts) + (TILE if 0 in parts else 0)
 
     def source_row(self, k):
-        return pick(far(self.n, self.n - k), lax.axis_index("pool"))
+        return pick(far(self.n, k), lax.axis_index("pool"))
 
 
 def side_block(size, scale, length):
@@ -380,7 +379,7 @@
     n = lax.axis_size("pool")
     size = Sizes(deltas, anchors, new_query, n)
     both = (0, 1)
-    order = sorted(range(1, n), key=lambda k: (min(k, n - k), k))
+    order = [2, 1] + list(range(3, n))
     last = order[-1]
     plan = [(k, both) for k in order[:-1]] + [(last, (0,)), (last, (1,)), (0, both)]
     query, fresh = arrange(size, new_query, new_kv)

time: 56.8 us -> 56.8 us (level)
  the two profiles are of different devices: /device:TPU:9 before, /device:TPU:21 now
where the time goes in v10:
time: 56.8 us; the launch traced here: 56.5 us
  waiting for transfers between devices  27.5 us (48%)
  starting transfers between devices  15.6 us (27%)
  Pallas kernels  12.7 us (22%)
  between operations  0.73 us (1%)
    ppermute x4, waiting for transfers between devices, body(): msg = lax.ppermute(msg, 'pool', list(enumerate(far(n, k))))  26.4 us
    ppermute x6, starting transfers between devices, swapped(): return lax.ppermute(x, 'sub', [(0, 1), (1, 0)])  12.5 us
    pallas_call x7, Pallas kernels, chained_call(): pl.pallas_call(kernel, in_specs=[IN_VMEM] * many + [IN_HBM, IN_HBM], out_...  6.93 us
    pallas_call x2, Pallas kernels, pack(): pl.pallas_call(functools.partial(pack_kernel, size, plan), out_shape=shap...  4.15 us
    ppermute x4, starting transfers between devices, body(): msg = lax.ppermute(msg, 'pool', list(enumerate(far(n, k))))  3.09 us
  transfers between devices with their start and end apart: 10, of which 5 were waited for; matrix products, arithmetic and copies ran while one was open for 0% of the time, Pallas kernels for 18%

profile of v10, /device:TPU:21, one launch (start us, length us, event | category | flops | bytes accessed | tf_op | source)
XLA Modules:
  0.0 56.5 jit_solution(13426463220873013016)
XLA Ops:
  0.6 1.9 %shard_map.89 = bf16[2192,128]{1,0:T(8,128)(2,1)S(1)} custom-call(s32[4]{0:T(128)} %route.3, s32[4]{0:T(128)} %lengths.3, bf16[4,2,256,512]{3,2,1,0:T(8,128)(2,1)} %deltas.3, bf16[4,2,16,512]{3,2,1,0:T(8,128)(2,1)} %anchors.3, bf16[4,2,512]{2,1,0:T(2,128)(2,1)} %scale.3), custom_call_target="tpu_custom_call" | custom-call | bytes 524288 | tf_op jit(solution)/shard_map/pallas_call | solution.py:115
  2.5 0.1 collective-permute-start.3
  2.6 2.3 %shard_map.87 = (bf16[2192,128]{1,0:T(8,128)(2,1)S(1)}, bf16[1104,128]{1,0:T(8,128)(2,1)S(1)}, bf16[1088,128]{1,0:T(8,128)(2,1)S(1)}, bf16[2192,128]{1,0:T(8,128)(2,1)S(1)}) custom-call(s32[4]{0:T(128)} %route.3, s32[4]{0:T(128)} %lengths.3, bf16[4,2,256,512]{3,2,1,0:T(8,128)(2,1)} %deltas.3, bf16[4,2,16,512]{3,2,1,0:T(8,128)(2,1)} %anchors.3, ...), custom_call_target="tpu_custom_call" | custom-call | bytes 1572864 | tf_op jit(solution)/shard_map/pallas_call | solution.py:115
  4.9 1.4 %collective-permute-start.1 = (bf16[2192,128]{1,0:T(8,128)(2,1)S(1)}, bf16[2192,128]{1,0:T(8,128)(2,1)S(1)}, u32[]{:S(2)}, u32[]{:S(2)}) collective-permute-start(bf16[2192,128]{1,0:T(8,128)(2,1)S(1)} %get-tuple-element.47), channel_id=1, source_target_pairs={{0,4},{4,0},{8,12},{12,8},{1,5},{5,1},{9,13},{13,9},{2,6},{6,2},{1... | collective-permute-start | bytes 1683464 | tf_op jit(solution)/shard_map/ppermute | solution.py:390
  6.3 0.2 shard_map.88
  6.5 1.3 %collective-permute-start.2 = (bf16[1024,128]{1,0:T(8,128)(2,1)S(1)}, bf16[1024,128]{1,0:T(8,128)(2,1)S(1)}, u32[]{:S(2)}, u32[]{:S(2)}) collective-permute-start(bf16[1024,128]{1,0:T(8,128)(2,1)S(1)} %get-tuple-element.50.theirs), channel_id=1, source_target_pairs={{0,1},{1,0},{2,3},{3,2},{4,5},{5,4},{6,7},{7,6},{8,9},{9,8},{10,11... | collective-permute-start | bytes 786440 | tf_op jit(solution)/shard_map/ppermute | solution.py:394
  7.8 1.3 %collective-permute-start = (bf16[1104,128]{1,0:T(8,128)(2,1)S(1)}, bf16[1104,128]{1,0:T(8,128)(2,1)S(1)}, u32[]{:S(2)}, u32[]{:S(2)}) collective-permute-start(bf16[1104,128]{1,0:T(8,128)(2,1)S(1)} %get-tuple-element.46), channel_id=1, source_target_pairs={{0,12},{4,8},{8,4},{12,0},{1,13},{5,9},{9,5},{13,1},{2,14},{6,10},... | collective-permute-start | bytes 847880 | tf_op jit(solution)/shard_map/ppermute | solution.py:390
  9.1 0.9 %shard_map.86 = (bf16[4,2,32,128]{3,2,1,0:T(8,128)(2,1)S(1)}, bf16[4,2,2,16,128]{4,3,2,1,0:T(8,128)(2,1)S(1)}) custom-call(bf16[4,4,2048]{2,1,0:T(4,128)(2,1)} %new_query.1, bf16[4,2,4,512]{3,2,1,0:T(4,128)(2,1)} %new_kv.1), custom_call_target="tpu_custom_call" | custom-call | tf_op jit(solution)/shard_map/pallas_call | solution.py:152
  10.0 16.1 %collective-permute-done.3.message.tables = bf16[2192,128]{1,0:T(8,128)(2,1)S(1)} collective-permute-done((bf16[2192,128]{1,0:T(8,128)(2,1)S(1)}, bf16[2192,128]{1,0:T(8,128)(2,1)S(1)}, u32[]{:S(2)}, u32[]{:S(2)}) %collective-permute-start.3) | collective-permute-done | bytes 561184 | tf_op jit(solution)/shard_map/ppermute | solution.py:390
  26.1 0.2 shard_map.90
  26.3 3.4 %collective-permute-start.5 = (bf16[1024,128]{1,0:T(8,128)(2,1)S(1)}, bf16[1024,128]{1,0:T(8,128)(2,1)S(1)}, u32[]{:S(2)}, u32[]{:S(2)}) collective-permute-start(bf16[1024,128]{1,0:T(8,128)(2,1)S(1)} %get-tuple-element.60.theirs), channel_id=1, source_target_pairs={{0,1},{1,0},{2,3},{3,2},{4,5},{5,4},{6,7},{7,6},{8,9},{9,8},{10,11... | collective-permute-start | bytes 786440 | tf_op jit(solution)/shard_map/ppermute | solution.py:394
  29.7 0.0 collective-permute-done.2.other
  29.7 1.3 %shard_map.91 = (bf16[4,2,256,512]{3,2,1,0:T(8,128)(2,1)}, bf16[4,4,2048]{2,1,0:T(4,128)(2,1)}) custom-call(bf16[4,2,32,128]{3,2,1,0:T(8,128)(2,1)S(1)} %get-tuple-element.44.query, bf16[4,2,2,16,128]{4,3,2,1,0:T(8,128)(2,1)S(1)} %get-tuple-element.45.new_kv, ...), custom_call_target="tpu_custom_call", output_to_operand_aliasing={{0}: (6, {}), {1}: (7, {})} | custom-call | flops 16777216 | bytes 1048576 | tf_op jit(solution)/shard_map/pallas_call | solution.py:361
  31.1 0.0 collective-permute-done.1.message.tables
  31.1 0.2 shard_map.92
  31.3 6.2 %collective-permute-start.4 = (bf16[1024,128]{1,0:T(8,128)(2,1)S(1)}, bf16[1024,128]{1,0:T(8,128)(2,1)S(1)}, u32[]{:S(2)}, u32[]{:S(2)}) collective-permute-start(bf16[1024,128]{1,0:T(8,128)(2,1)S(1)} %get-tuple-element.58.theirs), channel_id=1, source_target_pairs={{0,1},{1,0},{2,3},{3,2},{4,5},{5,4},{6,7},{7,6},{8,9},{9,8},{10,11... | collective-permute-start | bytes 786440 | tf_op jit(solution)/shard_map/ppermute | solution.py:394
  37.4 0.3 collective-permute-start.8
  37.7 0.0 collective-permute-done.5.other
  37.7 1.3 %shard_map.93 = (bf16[4,2,256,512]{3,2,1,0:T(8,128)(2,1)}, bf16[4,4,2048]{2,1,0:T(4,128)(2,1)}) custom-call(bf16[4,2,32,128]{3,2,1,0:T(8,128)(2,1)S(1)} %get-tuple-element.44.query, bf16[4,2,2,16,128]{4,3,2,1,0:T(8,128)(2,1)S(1)} %get-tuple-element.45.new_kv, ...), custom_call_target="tpu_custom_call", output_to_operand_aliasing={{0}: (6, {}), {1}: (7, {})} | custom-call | flops 16777216 | bytes 1048576 | tf_op jit(solution)/shard_map/pallas_call | solution.py:361
  39.1 0.0 collective-permute-done.4.other
  39.1 1.3 %shard_map.94 = (bf16[4,2,256,512]{3,2,1,0:T(8,128)(2,1)}, bf16[4,4,2048]{2,1,0:T(4,128)(2,1)}) custom-call(bf16[4,2,32,128]{3,2,1,0:T(8,128)(2,1)S(1)} %get-tuple-element.44.query, bf16[4,2,2,16,128]{4,3,2,1,0:T(8,128)(2,1)S(1)} %get-tuple-element.45.new_kv, ...), custom_call_target="tpu_custom_call", output_to_operand_aliasing={{0}: (6, {}), {1}: (7, {})} | custom-call | flops 16777216 | bytes 1048576 | tf_op jit(solution)/shard_map/pallas_call | solution.py:361
  40.4 1.8 %collective-permute-done.message.tables = bf16[1104,128]{1,0:T(8,128)(2,1)S(1)} collective-permute-done((bf16[1104,128]{1,0:T(8,128)(2,1)S(1)}, bf16[1104,128]{1,0:T(8,128)(2,1)S(1)}, u32[]{:S(2)}, u32[]{:S(2)}) %collective-permute-start) | collective-permute-done | bytes 282656 | tf_op jit(solution)/shard_map/ppermute | solution.py:390
  42.3 0.1 shard_map.95
  42.4 0.7 %collective-permute-start.6 = (bf16[512,128]{1,0:T(8,128)(2,1)S(1)}, bf16[512,128]{1,0:T(8,128)(2,1)S(1)}, u32[]{:S(2)}, u32[]{:S(2)}) collective-permute-start(bf16[512,128]{1,0:T(8,128)(2,1)S(1)} %get-tuple-element.68.theirs), channel_id=1, source_target_pairs={{0,1},{1,0},{2,3},{3,2},{4,5},{5,4},{6,7},{7,6},{8,9},{9,8},{10,11... | collective-permute-start | bytes 393224 | tf_op jit(solution)/shard_map/ppermute | solution.py:394
  43.0 1.0 %collective-permute-done.6.other = bf16[512,128]{1,0:T(8,128)(2,1)S(1)} collective-permute-done((bf16[512,128]{1,0:T(8,128)(2,1)S(1)}, bf16[512,128]{1,0:T(8,128)(2,1)S(1)}, u32[]{:S(2)}, u32[]{:S(2)}) %collective-permute-start.6) | collective-permute-done | bytes 131104 | tf_op jit(solution)/shard_map/ppermute | solution.py:394
  44.0 1.3 %shard_map.96 = (bf16[4,2,256,512]{3,2,1,0:T(8,128)(2,1)}, bf16[4,4,2048]{2,1,0:T(4,128)(2,1)}, bf16[2,32,256]{2,1,0:T(8,128)(2,1)S(1)}, bf16[2,32,256]{2,1,0:T(...) custom-call(bf16[4,2,32,128]{3,2,1,0:T(8,128)(2,1)S(1)} %get-tuple-e, ...), custom_call_target="tpu_custom_call", output_to_operand_aliasing={{0}: (6, {}), {1}: (7, {})} | custom-call | flops 8388608 | bytes 1048576 | tf_op jit(solution)/shard_map/pallas_call | solution.py:361
  45.3 0.4 collective-permute-start.7
  45.7 8.5 %collective-permute-done.8.message = bf16[1088,128]{1,0:T(8,128)(2,1)S(1)} collective-permute-done((bf16[1088,128]{1,0:T(8,128)(2,1)S(1)}, bf16[1088,128]{1,0:T(8,128)(2,1)S(1)}, u32[]{:S(2)}, u32[]{:S(2)}) %collective-permute-start.8) | collective-permute-done | bytes 278560 | tf_op jit(solution)/shard_map/ppermute | solution.py:390
  54.2 0.0 collective-permute-done.7.lent
  54.2 0.3 shard_map.97
  54.5 0.5 collective-permute-start.9
  55.0 0.8 %shard_map.98 = (bf16[4,2,256,512]{3,2,1,0:T(8,128)(2,1)}, bf16[4,4,2048]{2,1,0:T(4,128)(2,1)}) custom-call(bf16[512,128]{1,0:T(8,128)(2,1)S(1)} %get-tuple-element.80.mine, bf16[512,128]{1,0:T(8,128)(2,1)S(1)} %get-tuple-element.81.theirs, bf16[4,2,256,512]{3,2,1,0:T(8,128)(2,1)} %get-tuple-element.82.refs_0_, ...), custom_call_target="tpu_custom_call", output_to_operand_aliasing={{0}: (2, {}), {1}: (3, {})} | custom-call | bytes 1048576 | tf_op jit(solution)/shard_map/pallas_call | solution.py:361
  55.8 0.1 collective-permute-done.9.got
  55.9 0.6 %shard_map.99 = (bf16[4,2,256,512]{3,2,1,0:T(8,128)(2,1)}, bf16[4,4,2048]{2,1,0:T(4,128)(2,1)}) custom-call(f32[2,32,128]{2,1,0:T(8,128)S(1)} %get-tuple-element.77.kept, f32[2,32,128]{2,1,0:T(8,128)S(1)} %collective-permute-done.9.got, f32[2,32,128]{2,1,0:T(8,128)S(1)} %get-tuple-element.79.totals, ...), custom_call_target="tpu_custom_call", output_to_operand_aliasing={{0}: (3, {}), {1}: (4, {})} | custom-call | bytes 1048576 | tf_op jit(solution)/shard_map/pallas_call | solution.py:361
Async XLA Ops:
  2.5 23.6 %collective-permute-start.3 = (bf16[2192,128]{1,0:T(8,128)(2,1)S(1)}, bf16[2192,128]{1,0:T(8,128)(2,1)S(1)}, u32[]{:S(2)}, u32[]{:S(2)}) collective-permute-start(bf16[2192,128]{1,0:T(8,128)(2,1)S(1)} %shard_map.89), channel_id=1, source_target_pairs={{0,8},{4,12},{8,0},{12,4},{1,9},{5,13},{9,1},{13,5},{2,10},{6,14},... | collective-permute-start | bytes 1683464 | tf_op jit(solution)/shard_map/ppermute | solution.py:390
  4.9 26.1 %collective-permute-start.1 = (bf16[2192,128]{1,0:T(8,128)(2,1)S(1)}, bf16[2192,128]{1,0:T(8,128)(2,1)S(1)}, u32[]{:S(2)}, u32[]{:S(2)}) collective-permute-start(bf16[2192,128]{1,0:T(8,128)(2,1)S(1)} %get-tuple-element.47), channel_id=1, source_target_pairs={{0,4},{4,0},{8,12},{12,8},{1,5},{5,1},{9,13},{13,9},{2,6},{6,2},{1... | collective-permute-start | bytes 1683464 | tf_op jit(solution)/shard_map/ppermute | solution.py:390
  6.5 23.2 %collective-permute-start.2 = (bf16[1024,128]{1,0:T(8,128)(2,1)S(1)}, bf16[1024,128]{1,0:T(8,128)(2,1)S(1)}, u32[]{:S(2)}, u32[]{:S(2)}) collective-permute-start(bf16[1024,128]{1,0:T(8,128)(2,1)S(1)} %get-tuple-element.50.theirs), channel_id=1, source_target_pairs={{0,1},{1,0},{2,3},{3,2},{4,5},{5,4},{6,7},{7,6},{8,9},{9,8},{10,11... | collective-permute-start | bytes 786440 | tf_op jit(solution)/shard_map/ppermute | solution.py:394
  7.8 34.5 %collective-permute-start = (bf16[1104,128]{1,0:T(8,128)(2,1)S(1)}, bf16[1104,128]{1,0:T(8,128)(2,1)S(1)}, u32[]{:S(2)}, u32[]{:S(2)}) collective-permute-start(bf16[1104,128]{1,0:T(8,128)(2,1)S(1)} %get-tuple-element.46), channel_id=1, source_target_pairs={{0,12},{4,8},{8,4},{12,0},{1,13},{5,9},{9,5},{13,1},{2,14},{6,10},... | collective-permute-start | bytes 847880 | tf_op jit(solution)/shard_map/ppermute | solution.py:390
  26.3 11.5 %collective-permute-start.5 = (bf16[1024,128]{1,0:T(8,128)(2,1)S(1)}, bf16[1024,128]{1,0:T(8,128)(2,1)S(1)}, u32[]{:S(2)}, u32[]{:S(2)}) collective-permute-start(bf16[1024,128]{1,0:T(8,128)(2,1)S(1)} %get-tuple-element.60.theirs), channel_id=1, source_target_pairs={{0,1},{1,0},{2,3},{3,2},{4,5},{5,4},{6,7},{7,6},{8,9},{9,8},{10,11... | collective-permute-start | bytes 786440 | tf_op jit(solution)/shard_map/ppermute | solution.py:394
  31.3 7.8 %collective-permute-start.4 = (bf16[1024,128]{1,0:T(8,128)(2,1)S(1)}, bf16[1024,128]{1,0:T(8,128)(2,1)S(1)}, u32[]{:S(2)}, u32[]{:S(2)}) collective-permute-start(bf16[1024,128]{1,0:T(8,128)(2,1)S(1)} %get-tuple-element.58.theirs), channel_id=1, source_target_pairs={{0,1},{1,0},{2,3},{3,2},{4,5},{5,4},{6,7},{7,6},{8,9},{9,8},{10,11... | collective-permute-start | bytes 786440 | tf_op jit(solution)/shard_map/ppermute | solution.py:394
  37.4 16.8 %collective-permute-start.8 = (bf16[1088,128]{1,0:T(8,128)(2,1)S(1)}, bf16[1088,128]{1,0:T(8,128)(2,1)S(1)}, u32[]{:S(2)}, u32[]{:S(2)}) collective-permute-start(bf16[1088,128]{1,0:T(8,128)(2,1)S(1)} %get-tuple-element.74), channel_id=1, source_target_pairs={{0,12},{4,8},{8,4},{12,0},{1,13},{5,9},{9,5},{13,1},{2,14},{6,10},... | collective-permute-start | bytes 835592 | tf_op jit(solution)/shard_map/ppermute | solution.py:390
  42.4 1.6 %collective-permute-start.6 = (bf16[512,128]{1,0:T(8,128)(2,1)S(1)}, bf16[512,128]{1,0:T(8,128)(2,1)S(1)}, u32[]{:S(2)}, u32[]{:S(2)}) collective-permute-start(bf16[512,128]{1,0:T(8,128)(2,1)S(1)} %get-tuple-element.68.theirs), channel_id=1, source_target_pairs={{0,1},{1,0},{2,3},{3,2},{4,5},{5,4},{6,7},{7,6},{8,9},{9,8},{10,11... | collective-permute-start | bytes 393224 | tf_op jit(solution)/shard_map/ppermute | solution.py:394
  45.3 8.9 %collective-permute-start.7 = (bf16[2,32,256]{2,1,0:T(8,128)(2,1)S(1)}, bf16[2,32,256]{2,1,0:T(8,128)(2,1)S(1)}, u32[]{:S(2)}, u32[]{:S(2)}) collective-permute-start(bf16[2,32,256]{2,1,0:T(8,128)(2,1)S(1)} %get-tuple-element.73), channel_id=1, source_target_pairs={{0,1},{1,0},{2,3},{3,2},{4,5},{5,4},{6,7},{7,6},{8,9},{9,8},{10,11... | collective-permute-start | bytes 98312 | tf_op jit(solution)/shard_map/ppermute | solution.py:394
  54.5 1.4 %collective-permute-start.9 = (f32[2,32,128]{2,1,0:T(8,128)S(1)}, f32[2,32,128]{2,1,0:T(8,128)S(1)}, u32[]{:S(2)}, u32[]{:S(2)}) collective-permute-start(f32[2,32,128]{2,1,0:T(8,128)S(1)} %get-tuple-element.78), channel_id=1, source_target_pairs={{0,1},{1,0},{2,3},{3,2},{4,5},{5,4},{6,7},{7,6},{8,9},{9,8},{10,11... | collective-permute-start | bytes 98312 | tf_op jit(solution)/shard_map/ppermute | solution.py:394

commit v11 on v10

--- a/solution.py
+++ b/solution.py
@@ -162,7 +162,7 @@
     )(hbm(new_query), hbm(new_kv))
 
 
-def row_copies(size, k, parts, cache, mine, theirs, sems):
+def row_copies(size, k, parts, cache, mine, theirs, sems, base=0):
     sub = lax.axis_index("sub")
     row = size.source_row(k)
     rest = size.heads - size.mine
@@ -177,7 +177,7 @@
                 copies.append(pltpu.make_async_copy(
                     out.at[pl.ds(at, size.span)],
                     cache.at[row, which, :, lanes],
-                    sems.at[o, p * size.mine + j],
+                    sems.at[o, base + p * size.mine + j],
                 ))
     return copies
 
@@ -210,30 +210,30 @@
                     out[to + i * size.repeat:to + (i + 1) * size.repeat, :] = value
 
 
-def rebuild_kernel(size, parts, chained, message, *refs):
-    _, _, mine, theirs = refs[2 * chained:]
-    rebuild_heads(size, parts, message, message, mine, theirs)
-
-
-def rebuild(size, parts, message, state):
-    args = [vmem(message)]
+def rebuild_kernel(size, parts, skip, message, tables, *refs):
+    mine, theirs = refs[skip + 2:skip + 4]
+    rebuild_heads(size, parts, message, tables, mine, theirs)
+
+
+def rebuild(size, parts, message, tables, state, gate):
+    args = [vmem(x) for x in (message, tables, *gate)]
+    aliases = {2 + i: 4 + i for i in range(len(gate))}
     in_specs = [IN_VMEM] * len(args)
-    aliases = {}
     if state is not None:
-        aliases = {len(args): 0, len(args) + 1: 1}
+        aliases |= {len(args): 0, len(args) + 1: 1}
         args += list(state)
         in_specs += [IN_HBM, IN_HBM]
     given = (len(parts) * size.mine * size.span, HEAD_DIM)
     out = pl.pallas_call(
-        functools.partial(rebuild_kernel, size, parts, state is not None),
+        functools.partial(rebuild_kernel, size, parts, len(args) - 2),
         in_specs=in_specs,
-        out_specs=[IN_HBM, IN_HBM, IN_VMEM, IN_VMEM],
+        out_specs=[IN_HBM, IN_HBM] + [IN_VMEM] * (2 + len(gate)),
         out_shape=[
             pltpu.HBM((size.count, 2, size.span, size.channels), BF),
             pltpu.HBM((size.count, size.steps, size.q_local * HEAD_DIM), BF),
             pltpu.VMEM(given, BF),
             pltpu.VMEM(given, BF),
-        ],
+        ] + [pltpu.VMEM(x.shape, BF) for x in gate],
         input_output_aliases=aliases,
         compiler_params=LIMIT,
         cost_estimate=pl.CostEstimate(
@@ -242,7 +242,7 @@
             transcendentals=0,
         ),
     )(*args)
-    return tuple(out[:2]), out[2], out[3]
+    return tuple(out[:2]), out[2], out[3], out[4:]
 
 
 def weigh(size, j, q, new_key, key_mine, key_other, live_mine, live_other, causal):
@@ -276,8 +276,8 @@
     return live_mine, live_other, (token <= step) & (token < size.steps)
 
 
-def start_store(size, k, parts, cache, mine, theirs, sems):
-    copies = row_copies(size, k, parts, cache, mine, theirs, sems)
+def start_store(size, k, parts, cache, mine, theirs, sems, base=0):
+    copies = row_copies(size, k, parts, cache, mine, theirs, sems, base)
     for copy in copies:
         copy.start()
     return copies
@@ -295,20 +295,24 @@
     copy.wait()
 
 
-def attend_kernel(size, k, query, new_kv, tables, mine, other, theirs, *refs):
-    cache, attended, made, flat, sem, sems = refs[2:]
+def attend_kernel(size, k, parts, query, new_kv, tables, mine, other, theirs, *refs):
+    own, rest, away = (mine, other, theirs) if len(parts) == 2 else refs[:3]
+    shift = size.mine if len(parts) == 2 else 0
+    cache, attended, made, flat, sem, sems = refs[-6:]
     row = size.source_row(k)
-    copies = start_store(size, k, (0, 1), cache, mine, theirs, sems)
-    live_mine, live_other, causal = masks(size, tables, (0, 1), new_kv.shape[3])
+    copies = start_store(size, k, parts, cache, mine, theirs, sems)
+    if len(parts) == 1:
+        copies += start_store(size, k, (1,), cache, own, away, sems, size.mine)
+    live_mine, live_other, causal = masks(size, tables, parts, new_kv.shape[3])
     for j in range(size.mine):
         keys = slice(j * size.span, (j + 1) * size.span)
-        values = slice((size.mine + j) * size.span, (size.mine + j + 1) * size.span)
+        values = slice((shift + j) * size.span, (shift + j + 1) * size.span)
         w0, w1, w2, total = weigh(
             size, j, query[row, j], new_kv[row, 0, j], mine[keys, :], other[keys, :],
             live_mine, live_other, causal,
         )
-        acc = jnp.dot(w0, mine[values, :], preferred_element_type=F32)
-        acc = acc + jnp.dot(w1, other[values, :], preferred_element_type=F32)
+        acc = jnp.dot(w0, own[values, :], preferred_element_type=F32)
+        acc = acc + jnp.dot(w1, rest[values, :], preferred_element_type=F32)
         acc = acc + jnp.dot(w2, new_kv[row, 1, j], preferred_element_type=F32)
         flat[j] = acc / total
     store_heads(size, k, flat, made, attended, sem, copies)
@@ -381,14 +385,19 @@
     both = (0, 1)
     order = [2, 1] + list(range(3, n))
     last = order[-1]
-    plan = [(k, both) for k in order[:-1]] + [(last, (0,)), (last, (1,)), (0, both)]
+    halves = [(k, (p,)) for k in order[1:-1] for p in both]
+    plan = [(order[0], both), (last, (0,))] + halves + [(last, (1,)), (0, both)]
     query, fresh = arrange(size, new_query, new_kv)
-    message = {}
+    message, packed = {}, {}
+
+    def send(k, parts):
+        message[k, parts] = lax.ppermute(packed[k, parts], "pool", list(enumerate(far(n, k))))
+
     for part in (plan[:1], plan[1:]):
         for (k, parts), msg in zip(part, pack(size, part, route, lengths, deltas, anchors, chan_scale)):
-            if k:
-                msg = lax.ppermute(msg, "pool", list(enumerate(far(n, k))))
-            message[k, parts] = msg
+            packed[k, parts] = msg
+            if k and (k, parts) not in halves:
+                send(k, parts)
 
     def swapped(x):
         return lax.ppermute(x, "sub", [(0, 1), (1, 0)])
@@ -402,30 +411,38 @@
     sems = pltpu.SemaphoreType.DMA((2, 2 * size.mine))
     wide = pltpu.VMEM((size.mine, size.wide, HEAD_DIM), F32)
 
-    def attend(k, mine, other, theirs, state):
+    def attend(k, parts, arrays, state):
+        tables = (message if k else packed)[k, parts]
         state, _ = chained_call(
-            size, functools.partial(attend_kernel, size, k),
-            (query, fresh, message[k, both], mine, other, theirs), state, [], rows + [sems], flops,
+            size, functools.partial(attend_kernel, size, k, parts),
+            (query, fresh, tables, *arrays), state, [], rows + [sems], flops,
         )
         return state
 
-    def take(k, parts, state):
-        state, mine, theirs = rebuild(size, parts, message[k, parts], state)
-        return state, mine, swapped(theirs), theirs
-
-    state, held = None, []
-    for k in [0] + order[:-1]:
-        state, *each = take(k, both, state)
-        held.append((k, *each))
-        if k:
-            state = attend(*held.pop(0), state)
-    state = attend(*held.pop(0), state)
-    state, *keys = take(last, (0,), state)
+    def take(k, parts, state, gate=()):
+        msg, tables = (
+            (message if k else packed)[k, p] for p in (parts, parts if 0 in parts else (0,))
+        )
+        state, mine, theirs, gate = rebuild(size, parts, msg, tables, state, gate)
+        return state, mine, swapped(theirs), theirs, gate
+
+    state, *own, _ = take(0, both, None)
+    state = attend(0, both, own, state)
+    state, *first, gate = take(order[0], both, state, [packed[x] for x in halves])
+    for (k, parts), msg in zip(halves, gate):
+        packed[k, parts] = msg
+        send(k, parts)
+    state, *keys, _ = take(last, (0,), state)
+    state = attend(order[0], both, first, state)
     half = pltpu.VMEM((size.mine, size.wide, size.span), BF)
     state, (weights, lent, share, totals) = chained_call(
         size, functools.partial(weights_kernel, size, last),
         (query, fresh, message[last, (0,)], *keys), state, [half, half, wide, wide], [sems], flops // 2,
     )
+    for k in order[1:-1]:
+        state, *each, _ = take(k, (0,), state)
+        state, *more, _ = take(k, (1,), state)
+        state = attend(k, (0,), (*each, *more), state)
     given = pltpu.VMEM((size.mine * size.span, HEAD_DIM), BF)
     state, (mine, theirs, kept, given) = chained_call(
         size, functools.partial(values_kernel, size),

time: 56.8 us -> 62.8 us (1.11)
  the two profiles are of different devices: /device:TPU:21 before, /device:TPU:25 now
where the time goes in v11:
time: 62.8 us; the launch traced here: 62.5 us
  waiting for transfers between devices  34.7 us (55%)
  starting transfers between devices  14.3 us (23%)
  Pallas kernels  12.7 us (20%)
  between operations  0.75 us (1%)
    ppermute x5, waiting for transfers between devices, send(): lax.ppermute(packed[k, parts], 'pool', list(enumerate(far(n, k))))  33.6 us
    ppermute x7, starting transfers between devices, swapped(): return lax.ppermute(x, 'sub', [(0, 1), (1, 0)])  9.7 us
    pallas_call x7, Pallas kernels, chained_call(): pl.pallas_call(kernel, in_specs=[IN_VMEM] * many + [IN_HBM, IN_HBM], out_...  6.94 us
    ppermute x5, starting transfers between devices, send(): lax.ppermute(packed[k, parts], 'pool', list(enumerate(far(n, k))))  4.59 us
    pallas_call x2, Pallas kernels, pack(): pl.pallas_call(functools.partial(pack_kernel, size, plan), out_shape=shap...  4.15 us
  transfers between devices with their start and end apart: 12, of which 6 were waited for; matrix products, arithmetic and copies ran while one was open for 0% of the time, Pallas kernels for 16%

profile of v11, /device:TPU:25, one launch (start us, length us, event | category | flops | bytes accessed | tf_op | source)
XLA Modules:
  0.0 62.5 jit_solution(4097920589967276630)
XLA Ops:
  0.6 1.9 %shard_map.88 = bf16[2192,128]{1,0:T(8,128)(2,1)S(1)} custom-call(s32[4]{0:T(128)} %route.3, s32[4]{0:T(128)} %lengths.3, bf16[4,2,256,512]{3,2,1,0:T(8,128)(2,1)} %deltas.3, bf16[4,2,16,512]{3,2,1,0:T(8,128)(2,1)} %anchors.3, bf16[4,2,512]{2,1,0:T(2,128)(2,1)} %scale.3), custom_call_target="tpu_custom_call" | custom-call | bytes 524288 | tf_op jit(solution)/shard_map/pallas_call | solution.py:115
  2.5 0.1 collective-permute-start.1
  2.6 2.3 %shard_map.87 = (bf16[1104,128]{1,0:T(8,128)(2,1)S(1)}, bf16[1104,128]{1,0:T(8,128)(2,1)S(1)}, bf16[1088,128]{1,0:T(8,128)(2,1)S(1)}, bf16[1088,128]{1,0:T(8,128)(2,1)S(1)}, bf16[2192,128]{1,0:T(8,128)(2,1)S(1)}) custom-call(s32[4]{0:T(128)} %route.3, s32[4]{0:T(128)} %lengths.3, bf16[4,2,256,512]{3,2,1,0:T(8,128)(2,1)} %deltas.3, ...), custom_call_target="tpu_custom_call" | custom-call | bytes 1572864 | tf_op jit(solution)/shard_map/pallas_call | solution.py:115
  4.9 0.2 shard_map.89
  5.1 1.0 %collective-permute-start.2 = (bf16[1024,128]{1,0:T(8,128)(2,1)S(1)}, bf16[1024,128]{1,0:T(8,128)(2,1)S(1)}, u32[]{:S(2)}, u32[]{:S(2)}) collective-permute-start(bf16[1024,128]{1,0:T(8,128)(2,1)S(1)} %get-tuple-element.58.theirs), channel_id=1, source_target_pairs={{0,1},{1,0},{2,3},{3,2},{4,5},{5,4},{6,7},{7,6},{8,9},{9,8},{10,11... | collective-permute-start | bytes 786440 | tf_op jit(solution)/shard_map/ppermute | solution.py:403
  6.1 2.2 %collective-permute-start = (bf16[1104,128]{1,0:T(8,128)(2,1)S(1)}, bf16[1104,128]{1,0:T(8,128)(2,1)S(1)}, u32[]{:S(2)}, u32[]{:S(2)}) collective-permute-start(bf16[1104,128]{1,0:T(8,128)(2,1)S(1)} %get-tuple-element.53), channel_id=1, source_target_pairs={{0,12},{4,8},{8,4},{12,0},{1,13},{5,9},{9,5},{13,1},{2,14},{6,10},... | collective-permute-start | bytes 847880 | tf_op jit(solution)/shard_map/ppermute | solution.py:394
  8.4 0.9 %shard_map.86 = (bf16[4,2,32,128]{3,2,1,0:T(8,128)(2,1)S(1)}, bf16[4,2,2,16,128]{4,3,2,1,0:T(8,128)(2,1)S(1)}) custom-call(bf16[4,4,2048]{2,1,0:T(4,128)(2,1)} %new_query.1, bf16[4,2,4,512]{3,2,1,0:T(4,128)(2,1)} %new_kv.1), custom_call_target="tpu_custom_call" | custom-call | tf_op jit(solution)/shard_map/pallas_call | solution.py:152
  9.3 0.0 collective-permute-done.2.other
  9.3 1.3 %shard_map.90 = (bf16[4,2,256,512]{3,2,1,0:T(8,128)(2,1)}, bf16[4,4,2048]{2,1,0:T(4,128)(2,1)}) custom-call(bf16[4,2,32,128]{3,2,1,0:T(8,128)(2,1)S(1)} %get-tuple-element.51.query, bf16[4,2,2,16,128]{4,3,2,1,0:T(8,128)(2,1)S(1)} %get-tuple-element.52.new_kv, ...), custom_call_target="tpu_custom_call", output_to_operand_aliasing={{0}: (6, {}), {1}: (7, {})} | custom-call | flops 16777216 | bytes 1048576 | tf_op jit(solution)/shard_map/pallas_call | solution.py:365
  10.6 25.4 %collective-permute-done.1.message.tables = bf16[2192,128]{1,0:T(8,128)(2,1)S(1)} collective-permute-done((bf16[2192,128]{1,0:T(8,128)(2,1)S(1)}, bf16[2192,128]{1,0:T(8,128)(2,1)S(1)}, u32[]{:S(2)}, u32[]{:S(2)}) %collective-permute-start.1) | collective-permute-done | bytes 561184 | tf_op jit(solution)/shard_map/ppermute | solution.py:394
  36.1 0.2 shard_map.91
  36.3 0.1 collective-permute-start.7
  36.3 1.5 %collective-permute-start.9 = (bf16[1088,128]{1,0:T(8,128)(2,1)S(1)}, bf16[1088,128]{1,0:T(8,128)(2,1)S(1)}, u32[]{:S(2)}, u32[]{:S(2)}) collective-permute-start(bf16[1088,128]{1,0:T(8,128)(2,1)S(1)} %get-tuple-element.82), channel_id=1, source_target_pairs={{0,4},{4,0},{8,12},{12,8},{1,5},{5,1},{9,13},{13,9},{2,6},{6,2},{1... | collective-permute-start | bytes 835592 | tf_op jit(solution)/shard_map/ppermute | solution.py:394
  37.8 1.1 %collective-permute-start.4 = (bf16[1024,128]{1,0:T(8,128)(2,1)S(1)}, bf16[1024,128]{1,0:T(8,128)(2,1)S(1)}, u32[]{:S(2)}, u32[]{:S(2)}) collective-permute-start(bf16[1024,128]{1,0:T(8,128)(2,1)S(1)} %get-tuple-element.68.theirs), channel_id=1, source_target_pairs={{0,1},{1,0},{2,3},{3,2},{4,5},{5,4},{6,7},{7,6},{8,9},{9,8},{10,11... | collective-permute-start | bytes 786440 | tf_op jit(solution)/shard_map/ppermute | solution.py:403
  38.9 0.7 %collective-permute-start.6 = (bf16[1088,128]{1,0:T(8,128)(2,1)S(1)}, bf16[1088,128]{1,0:T(8,128)(2,1)S(1)}, u32[]{:S(2)}, u32[]{:S(2)}) collective-permute-start(bf16[1088,128]{1,0:T(8,128)(2,1)S(1)} %get-tuple-element.76), channel_id=1, source_target_pairs={{0,12},{4,8},{8,4},{12,0},{1,13},{5,9},{9,5},{13,1},{2,14},{6,10},... | collective-permute-start | bytes 835592 | tf_op jit(solution)/shard_map/ppermute | solution.py:394
  39.7 0.0 collective-permute-done.message.tables
  39.7 0.1 shard_map.92
  39.8 0.3 collective-permute-start.3
  40.1 0.0 collective-permute-done.4.other
  40.1 1.3 %shard_map.93 = (bf16[4,2,256,512]{3,2,1,0:T(8,128)(2,1)}, bf16[4,4,2048]{2,1,0:T(4,128)(2,1)}) custom-call(bf16[4,2,32,128]{3,2,1,0:T(8,128)(2,1)S(1)} %get-tuple-element.51.query, bf16[4,2,2,16,128]{4,3,2,1,0:T(8,128)(2,1)S(1)} %get-tuple-element.52.new_kv, ...), custom_call_target="tpu_custom_call", output_to_operand_aliasing={{0}: (6, {}), {1}: (7, {})} | custom-call | flops 16777216 | bytes 1048576 | tf_op jit(solution)/shard_map/pallas_call | solution.py:365
  41.5 0.0 collective-permute-done.3.other
  41.5 1.3 %shard_map.94 = (bf16[4,2,256,512]{3,2,1,0:T(8,128)(2,1)}, bf16[4,4,2048]{2,1,0:T(4,128)(2,1)}, bf16[2,32,256]{2,1,0:T(8,128)(2,1)S(1)}, bf16[2,32,256]{2,1,0:T(...) custom-call(bf16[4,2,32,128]{3,2,1,0:T(8,128)(2,1)S(1)} %get-tuple-e, ...), custom_call_target="tpu_custom_call", output_to_operand_aliasing={{0}: (6, {}), {1}: (7, {})} | custom-call | flops 8388608 | bytes 1048576 | tf_op jit(solution)/shard_map/pallas_call | solution.py:365
  42.8 1.3 %collective-permute-done.7.message.tables = bf16[1104,128]{1,0:T(8,128)(2,1)S(1)} collective-permute-done((bf16[1104,128]{1,0:T(8,128)(2,1)S(1)}, bf16[1104,128]{1,0:T(8,128)(2,1)S(1)}, u32[]{:S(2)}, u32[]{:S(2)}) %collective-permute-start.7) | collective-permute-done | bytes 282656 | tf_op jit(solution)/shard_map/ppermute | solution.py:394
  44.0 0.1 shard_map.95
  44.1 6.9 %collective-permute-done.9.message = bf16[1088,128]{1,0:T(8,128)(2,1)S(1)} collective-permute-done((bf16[1088,128]{1,0:T(8,128)(2,1)S(1)}, bf16[1088,128]{1,0:T(8,128)(2,1)S(1)}, u32[]{:S(2)}, u32[]{:S(2)}) %collective-permute-start.9) | collective-permute-done | bytes 278560 | tf_op jit(solution)/shard_map/ppermute | solution.py:394
  51.0 0.1 shard_map.96
  51.1 6.5 %collective-permute-start.10 = (bf16[512,128]{1,0:T(8,128)(2,1)S(1)}, bf16[512,128]{1,0:T(8,128)(2,1)S(1)}, u32[]{:S(2)}, u32[]{:S(2)}) collective-permute-start(bf16[512,128]{1,0:T(8,128)(2,1)S(1)} %get-tuple-element.86.refs_2_), channel_id=1, source_target_pairs={{0,1},{1,0},{2,3},{3,2},{4,5},{5,4},{6,7},{7,6},{8,9},{9,8},{10,11... | collective-permute-start | bytes 393224 | tf_op jit(solution)/shard_map/ppermute | solution.py:403
  57.6 0.1 collective-permute-start.8
  57.7 0.4 collective-permute-start.5
  58.1 0.5 collective-permute-done.10.refs_1_
  58.6 0.4 collective-permute-done.8.other
  58.9 1.3 %shard_map.97 = (bf16[4,2,256,512]{3,2,1,0:T(8,128)(2,1)}, bf16[4,4,2048]{2,1,0:T(4,128)(2,1)}) custom-call(bf16[4,2,32,128]{3,2,1,0:T(8,128)(2,1)S(1)} %get-tuple-element.51.query, bf16[4,2,2,16,128]{4,3,2,1,0:T(8,128)(2,1)S(1)} %get-tuple-element.52.new_kv, ...), custom_call_target="tpu_custom_call", output_to_operand_aliasing={{0}: (9, {}), {1}: (10, {})} | custom-call | flops 16777216 | bytes 1048576 | tf_op jit(solution)/shard_map/pallas_call | solution.py:365
  60.3 0.0 collective-permute-done.6.message
  60.3 0.0 collective-permute-done.5.lent
  60.3 0.3 shard_map.98
  60.6 0.2 collective-permute-start.11
  60.8 0.8 %shard_map.99 = (bf16[4,2,256,512]{3,2,1,0:T(8,128)(2,1)}, bf16[4,4,2048]{2,1,0:T(4,128)(2,1)}) custom-call(bf16[512,128]{1,0:T(8,128)(2,1)S(1)} %get-tuple-element.94.mine, bf16[512,128]{1,0:T(8,128)(2,1)S(1)} %get-tuple-element.95.theirs, bf16[4,2,256,512]{3,2,1,0:T(8,128)(2,1)} %get-tuple-element.96.refs_0_, ...), custom_call_target="tpu_custom_call", output_to_operand_aliasing={{0}: (2, {}), {1}: (3, {})} | custom-call | bytes 1048576 | tf_op jit(solution)/shard_map/pallas_call | solution.py:365
  61.6 0.3 collective-permute-done.11.got
  61.8 0.6 %shard_map.100 = (bf16[4,2,256,512]{3,2,1,0:T(8,128)(2,1)}, bf16[4,4,2048]{2,1,0:T(4,128)(2,1)}) custom-call(f32[2,32,128]{2,1,0:T(8,128)S(1)} %get-tuple-element.91.kept, f32[2,32,128]{2,1,0:T(8,128)S(1)} %collective-permute-done.11.got, f32[2,32,128]{2,1,0:T(8,128)S(1)} %get-tuple-element.93.totals, ...), custom_call_target="tpu_custom_call", output_to_operand_aliasing={{0}: (3, {}), {1}: (4, {})} | custom-call | bytes 1048576 | tf_op jit(solution)/shard_map/pallas_call | solution.py:365
Async XLA Ops:
  2.5 33.6 %collective-permute-start.1 = (bf16[2192,128]{1,0:T(8,128)(2,1)S(1)}, bf16[2192,128]{1,0:T(8,128)(2,1)S(1)}, u32[]{:S(2)}, u32[]{:S(2)}) collective-permute-start(bf16[2192,128]{1,0:T(8,128)(2,1)S(1)} %shard_map.88), channel_id=1, source_target_pairs={{0,8},{4,12},{8,0},{12,4},{1,9},{5,13},{9,1},{13,5},{2,10},{6,14},... | collective-permute-start | bytes 1683464 | tf_op jit(solution)/shard_map/ppermute | solution.py:394
  5.1 4.2 %collective-permute-start.2 = (bf16[1024,128]{1,0:T(8,128)(2,1)S(1)}, bf16[1024,128]{1,0:T(8,128)(2,1)S(1)}, u32[]{:S(2)}, u32[]{:S(2)}) collective-permute-start(bf16[1024,128]{1,0:T(8,128)(2,1)S(1)} %get-tuple-element.58.theirs), channel_id=1, source_target_pairs={{0,1},{1,0},{2,3},{3,2},{4,5},{5,4},{6,7},{7,6},{8,9},{9,8},{10,11... | collective-permute-start | bytes 786440 | tf_op jit(solution)/shard_map/ppermute | solution.py:403
  6.1 33.5 %collective-permute-start = (bf16[1104,128]{1,0:T(8,128)(2,1)S(1)}, bf16[1104,128]{1,0:T(8,128)(2,1)S(1)}, u32[]{:S(2)}, u32[]{:S(2)}) collective-permute-start(bf16[1104,128]{1,0:T(8,128)(2,1)S(1)} %get-tuple-element.53), channel_id=1, source_target_pairs={{0,12},{4,8},{8,4},{12,0},{1,13},{5,9},{9,5},{13,1},{2,14},{6,10},... | collective-permute-start | bytes 847880 | tf_op jit(solution)/shard_map/ppermute | solution.py:394
  36.3 7.8 %collective-permute-start.7 = (bf16[1104,128]{1,0:T(8,128)(2,1)S(1)}, bf16[1104,128]{1,0:T(8,128)(2,1)S(1)}, u32[]{:S(2)}, u32[]{:S(2)}) collective-permute-start(bf16[1104,128]{1,0:T(8,128)(2,1)S(1)} %get-tuple-element.77), channel_id=1, source_target_pairs={{0,4},{4,0},{8,12},{12,8},{1,5},{5,1},{9,13},{13,9},{2,6},{6,2},{1... | collective-permute-start | bytes 847880 | tf_op jit(solution)/shard_map/ppermute | solution.py:394
  36.3 14.7 %collective-permute-start.9 = (bf16[1088,128]{1,0:T(8,128)(2,1)S(1)}, bf16[1088,128]{1,0:T(8,128)(2,1)S(1)}, u32[]{:S(2)}, u32[]{:S(2)}) collective-permute-start(bf16[1088,128]{1,0:T(8,128)(2,1)S(1)} %get-tuple-element.82), channel_id=1, source_target_pairs={{0,4},{4,0},{8,12},{12,8},{1,5},{5,1},{9,13},{13,9},{2,6},{6,2},{1... | collective-permute-start | bytes 835592 | tf_op jit(solution)/shard_map/ppermute | solution.py:394
  37.8 2.4 %collective-permute-start.4 = (bf16[1024,128]{1,0:T(8,128)(2,1)S(1)}, bf16[1024,128]{1,0:T(8,128)(2,1)S(1)}, u32[]{:S(2)}, u32[]{:S(2)}) collective-permute-start(bf16[1024,128]{1,0:T(8,128)(2,1)S(1)} %get-tuple-element.68.theirs), channel_id=1, source_target_pairs={{0,1},{1,0},{2,3},{3,2},{4,5},{5,4},{6,7},{7,6},{8,9},{9,8},{10,11... | collective-permute-start | bytes 786440 | tf_op jit(solution)/shard_map/ppermute | solution.py:403
  38.9 21.3 %collective-permute-start.6 = (bf16[1088,128]{1,0:T(8,128)(2,1)S(1)}, bf16[1088,128]{1,0:T(8,128)(2,1)S(1)}, u32[]{:S(2)}, u32[]{:S(2)}) collective-permute-start(bf16[1088,128]{1,0:T(8,128)(2,1)S(1)} %get-tuple-element.76), channel_id=1, source_target_pairs={{0,12},{4,8},{8,4},{12,0},{1,13},{5,9},{9,5},{13,1},{2,14},{6,10},... | collective-permute-start | bytes 835592 | tf_op jit(solution)/shard_map/ppermute | solution.py:394
  39.8 1.7 %collective-permute-start.3 = (bf16[512,128]{1,0:T(8,128)(2,1)S(1)}, bf16[512,128]{1,0:T(8,128)(2,1)S(1)}, u32[]{:S(2)}, u32[]{:S(2)}) collective-permute-start(bf16[512,128]{1,0:T(8,128)(2,1)S(1)} %get-tuple-element.66.theirs), channel_id=1, source_target_pairs={{0,1},{1,0},{2,3},{3,2},{4,5},{5,4},{6,7},{7,6},{8,9},{9,8},{10,11... | collective-permute-start | bytes 393224 | tf_op jit(solution)/shard_map/ppermute | solution.py:403
  51.1 7.4 %collective-permute-start.10 = (bf16[512,128]{1,0:T(8,128)(2,1)S(1)}, bf16[512,128]{1,0:T(8,128)(2,1)S(1)}, u32[]{:S(2)}, u32[]{:S(2)}) collective-permute-start(bf16[512,128]{1,0:T(8,128)(2,1)S(1)} %get-tuple-element.86.refs_2_), channel_id=1, source_target_pairs={{0,1},{1,0},{2,3},{3,2},{4,5},{5,4},{6,7},{7,6},{8,9},{9,8},{10,11... | collective-permute-start | bytes 393224 | tf_op jit(solution)/shard_map/ppermute | solution.py:403
  57.6 1.3 %collective-permute-start.8 = (bf16[512,128]{1,0:T(8,128)(2,1)S(1)}, bf16[512,128]{1,0:T(8,128)(2,1)S(1)}, u32[]{:S(2)}, u32[]{:S(2)}) collective-permute-start(bf16[512,128]{1,0:T(8,128)(2,1)S(1)} %get-tuple-element.81.theirs), channel_id=1, source_target_pairs={{0,1},{1,0},{2,3},{3,2},{4,5},{5,4},{6,7},{7,6},{8,9},{9,8},{10,11... | collective-permute-start | bytes 393224 | tf_op jit(solution)/shard_map/ppermute | solution.py:403
  57.7 2.6 %collective-permute-start.5 = (bf16[2,32,256]{2,1,0:T(8,128)(2,1)S(1)}, bf16[2,32,256]{2,1,0:T(8,128)(2,1)S(1)}, u32[]{:S(2)}, u32[]{:S(2)}) collective-permute-start(bf16[2,32,256]{2,1,0:T(8,128)(2,1)S(1)} %get-tuple-element.75), channel_id=1, source_target_pairs={{0,1},{1,0},{2,3},{3,2},{4,5},{5,4},{6,7},{7,6},{8,9},{9,8},{10,11... | collective-permute-start | bytes 98312 | tf_op jit(solution)/shard_map/ppermute | solution.py:403
  60.6 1.2 %collective-permute-start.11 = (f32[2,32,128]{2,1,0:T(8,128)S(1)}, f32[2,32,128]{2,1,0:T(8,128)S(1)}, u32[]{:S(2)}, u32[]{:S(2)}) collective-permute-start(f32[2,32,128]{2,1,0:T(8,128)S(1)} %get-tuple-element.92), channel_id=1, source_target_pairs={{0,1},{1,0},{2,3},{3,2},{4,5},{5,4},{6,7},{7,6},{8,9},{9,8},{10,11... | collective-permute-start | bytes 98312 | tf_op jit(solution)/shard_map/ppermute | solution.py:403

commit v12 on v11

--- a/solution.py
+++ b/solution.py
@@ -385,8 +385,9 @@
     both = (0, 1)
     order = [2, 1] + list(range(3, n))
     last = order[-1]
-    halves = [(k, (p,)) for k in order[1:-1] for p in both]
-    plan = [(order[0], both), (last, (0,))] + halves + [(last, (1,)), (0, both)]
+    nears = order[1:-1]
+    plan = [(order[0], both)] + [(k, (0,)) for k in nears] + [(last, (0,))]
+    plan += [(k, (1,)) for k in nears] + [(last, (1,)), (0, both)]
     query, fresh = arrange(size, new_query, new_kv)
     message, packed = {}, {}
 
@@ -396,7 +397,7 @@
     for part in (plan[:1], plan[1:]):
         for (k, parts), msg in zip(part, pack(size, part, route, lengths, deltas, anchors, chan_scale)):
             packed[k, parts] = msg
-            if k and (k, parts) not in halves:
+            if k:
                 send(k, parts)
 
     def swapped(x):
@@ -427,22 +428,23 @@
         return state, mine, swapped(theirs), theirs, gate
 
     state, *own, _ = take(0, both, None)
+    state, *first, _ = take(order[0], both, state)
     state = attend(0, both, own, state)
-    state, *first, gate = take(order[0], both, state, [packed[x] for x in halves])
-    for (k, parts), msg in zip(halves, gate):
-        packed[k, parts] = msg
-        send(k, parts)
+    near = {}
+    for k in nears:
+        state, *near[k], _ = take(k, (0,), state)
     state, *keys, _ = take(last, (0,), state)
     state = attend(order[0], both, first, state)
+    for k in nears:
+        state, *more, _ = take(k, (1,), state)
+        near[k] += more
     half = pltpu.VMEM((size.mine, size.wide, size.span), BF)
     state, (weights, lent, share, totals) = chained_call(
         size, functools.partial(weights_kernel, size, last),
         (query, fresh, message[last, (0,)], *keys), state, [half, half, wide, wide], [sems], flops // 2,
     )
-    for k in order[1:-1]:
-        state, *each, _ = take(k, (0,), state)
-        state, *more, _ = take(k, (1,), state)
-        state = attend(k, (0,), (*each, *more), state)
+    for k in nears:
+        state = attend(k, (0,), near[k], state)
     given = pltpu.VMEM((size.mine * size.span, HEAD_DIM), BF)
     state, (mine, theirs, kept, given) = chained_call(
         size, functools.partial(values_kernel, size),

time: 62.8 us -> 56.8 us (0.904)
  the two profiles are of different devices: /device:TPU:25 before, /device:TPU:9 now
where the time goes in v12:
time: 56.8 us; the launch traced here: 55.8 us
  waiting for transfers between devices  34.2 us (60%)
  Pallas kernels  12.8 us (23%)
  starting transfers between devices  8.09 us (14%)
  between operations  0.75 us (1%)
    ppermute x5, waiting for transfers between devices, send(): lax.ppermute(packed[k, parts], 'pool', list(enumerate(far(n, k))))  34.1 us
    pallas_call x7, Pallas kernels, chained_call(): pl.pallas_call(kernel, in_specs=[IN_VMEM] * many + [IN_HBM, IN_HBM], out_...  6.94 us
    ppermute x7, starting transfers between devices, swapped(): return lax.ppermute(x, 'sub', [(0, 1), (1, 0)])  4.23 us
    pallas_call x2, Pallas kernels, pack(): pl.pallas_call(functools.partial(pack_kernel, size, plan), out_shape=shap...  4.15 us
    ppermute x5, starting transfers between devices, send(): lax.ppermute(packed[k, parts], 'pool', list(enumerate(far(n, k))))  3.86 us
  transfers between devices with their start and end apart: 12, of which 3 were waited for; matrix products, arithmetic and copies ran while one was open for 0% of the time, Pallas kernels for 18%

profile of v12, /device:TPU:9, one launch (start us, length us, event | category | flops | bytes accessed | tf_op | source)
XLA Modules:
  0.0 55.8 jit_solution(5599117255572274843)
XLA Ops:
  0.6 1.9 %shard_map.89 = bf16[2192,128]{1,0:T(8,128)(2,1)S(1)} custom-call(s32[4]{0:T(128)} %route.3, s32[4]{0:T(128)} %lengths.3, bf16[4,2,256,512]{3,2,1,0:T(8,128)(2,1)} %deltas.3, bf16[4,2,16,512]{3,2,1,0:T(8,128)(2,1)} %anchors.3, bf16[4,2,512]{2,1,0:T(2,128)(2,1)} %scale.3), custom_call_target="tpu_custom_call" | custom-call | bytes 524288 | tf_op jit(solution)/shard_map/pallas_call | solution.py:115
  2.5 2.4 %collective-permute-start.3 = (bf16[2192,128]{1,0:T(8,128)(2,1)S(1)}, bf16[2192,128]{1,0:T(8,128)(2,1)S(1)}, u32[]{:S(2)}, u32[]{:S(2)}) collective-permute-start(bf16[2192,128]{1,0:T(8,128)(2,1)S(1)} %shard_map.89), channel_id=1, source_target_pairs={{0,8},{4,12},{8,0},{12,4},{1,9},{5,13},{9,1},{13,5},{2,10},{6,14},... | collective-permute-start | bytes 1683464 | tf_op jit(solution)/shard_map/ppermute | solution.py:395
  4.9 2.3 %shard_map.87 = (bf16[1104,128]{1,0:T(8,128)(2,1)S(1)}, bf16[1104,128]{1,0:T(8,128)(2,1)S(1)}, bf16[1088,128]{1,0:T(8,128)(2,1)S(1)}, bf16[1088,128]{1,0:T(8,128)(2,1)S(1)}, bf16[2192,128]{1,0:T(8,128)(2,1)S(1)}) custom-call(s32[4]{0:T(128)} %route.3, s32[4]{0:T(128)} %lengths.3, bf16[4,2,256,512]{3,2,1,0:T(8,128)(2,1)} %deltas.3, ...), custom_call_target="tpu_custom_call" | custom-call | bytes 1572864 | tf_op jit(solution)/shard_map/pallas_call | solution.py:115
  7.2 0.2 shard_map.88
  7.4 1.0 %collective-permute-start.2 = (bf16[1024,128]{1,0:T(8,128)(2,1)S(1)}, bf16[1024,128]{1,0:T(8,128)(2,1)S(1)}, u32[]{:S(2)}, u32[]{:S(2)}) collective-permute-start(bf16[1024,128]{1,0:T(8,128)(2,1)S(1)} %get-tuple-element.55.theirs), channel_id=1, source_target_pairs={{0,1},{1,0},{2,3},{3,2},{4,5},{5,4},{6,7},{7,6},{8,9},{9,8},{10,11... | collective-permute-start | bytes 786440 | tf_op jit(solution)/shard_map/ppermute | solution.py:404
  8.4 0.2 collective-permute-start.1
  8.6 0.2 collective-permute-start
  8.8 1.1 %collective-permute-start.5 = (bf16[1088,128]{1,0:T(8,128)(2,1)S(1)}, bf16[1088,128]{1,0:T(8,128)(2,1)S(1)}, u32[]{:S(2)}, u32[]{:S(2)}) collective-permute-start(bf16[1088,128]{1,0:T(8,128)(2,1)S(1)} %get-tuple-element.66), channel_id=1, source_target_pairs={{0,4},{4,0},{8,12},{12,8},{1,5},{5,1},{9,13},{13,9},{2,6},{6,2},{1... | collective-permute-start | bytes 835592 | tf_op jit(solution)/shard_map/ppermute | solution.py:395
  9.9 25.4 %collective-permute-done.3.message.tables = bf16[2192,128]{1,0:T(8,128)(2,1)S(1)} collective-permute-done((bf16[2192,128]{1,0:T(8,128)(2,1)S(1)}, bf16[2192,128]{1,0:T(8,128)(2,1)S(1)}, u32[]{:S(2)}, u32[]{:S(2)}) %collective-permute-start.3) | collective-permute-done | bytes 561184 | tf_op jit(solution)/shard_map/ppermute | solution.py:395
  35.3 0.2 shard_map.90
  35.5 0.7 %collective-permute-start.6 = (bf16[1024,128]{1,0:T(8,128)(2,1)S(1)}, bf16[1024,128]{1,0:T(8,128)(2,1)S(1)}, u32[]{:S(2)}, u32[]{:S(2)}) collective-permute-start(bf16[1024,128]{1,0:T(8,128)(2,1)S(1)} %get-tuple-element.68.theirs), channel_id=1, source_target_pairs={{0,1},{1,0},{2,3},{3,2},{4,5},{5,4},{6,7},{7,6},{8,9},{9,8},{10,11... | collective-permute-start | bytes 786440 | tf_op jit(solution)/shard_map/ppermute | solution.py:404
  36.2 0.0 collective-permute-done.2.other
  36.2 0.0 collective-permute-start.8
  36.2 0.9 %shard_map.86 = (bf16[4,2,32,128]{3,2,1,0:T(8,128)(2,1)S(1)}, bf16[4,2,2,16,128]{4,3,2,1,0:T(8,128)(2,1)S(1)}) custom-call(bf16[4,4,2048]{2,1,0:T(4,128)(2,1)} %new_query.1, bf16[4,2,4,512]{3,2,1,0:T(4,128)(2,1)} %new_kv.1), custom_call_target="tpu_custom_call" | custom-call | tf_op jit(solution)/shard_map/pallas_call | solution.py:152
  37.1 1.3 %shard_map.91 = (bf16[4,2,256,512]{3,2,1,0:T(8,128)(2,1)}, bf16[4,4,2048]{2,1,0:T(4,128)(2,1)}) custom-call(bf16[4,2,32,128]{3,2,1,0:T(8,128)(2,1)S(1)} %get-tuple-element.49.query, bf16[4,2,2,16,128]{4,3,2,1,0:T(8,128)(2,1)S(1)} %get-tuple-element.50.new_kv, ...), custom_call_target="tpu_custom_call", output_to_operand_aliasing={{0}: (6, {}), {1}: (7, {})} | custom-call | flops 16777216 | bytes 1048576 | tf_op jit(solution)/shard_map/pallas_call | solution.py:365
  38.5 0.0 collective-permute-done.1.message.tables
  38.5 0.1 shard_map.92
  38.6 8.6 %collective-permute-done.message.tables = bf16[1104,128]{1,0:T(8,128)(2,1)S(1)} collective-permute-done((bf16[1104,128]{1,0:T(8,128)(2,1)S(1)}, bf16[1104,128]{1,0:T(8,128)(2,1)S(1)}, u32[]{:S(2)}, u32[]{:S(2)}) %collective-permute-start) | collective-permute-done | bytes 282656 | tf_op jit(solution)/shard_map/ppermute | solution.py:395
  47.2 0.1 shard_map.93
  47.3 1.4 %collective-permute-start.4 = (bf16[512,128]{1,0:T(8,128)(2,1)S(1)}, bf16[512,128]{1,0:T(8,128)(2,1)S(1)}, u32[]{:S(2)}, u32[]{:S(2)}) collective-permute-start(bf16[512,128]{1,0:T(8,128)(2,1)S(1)} %get-tuple-element.65.theirs), channel_id=1, source_target_pairs={{0,1},{1,0},{2,3},{3,2},{4,5},{5,4},{6,7},{7,6},{8,9},{9,8},{10,11... | collective-permute-start | bytes 393224 | tf_op jit(solution)/shard_map/ppermute | solution.py:404
  48.7 0.1 collective-permute-start.9
  48.8 0.0 collective-permute-done.6.other
  48.8 1.3 %shard_map.94 = (bf16[4,2,256,512]{3,2,1,0:T(8,128)(2,1)}, bf16[4,4,2048]{2,1,0:T(4,128)(2,1)}) custom-call(bf16[4,2,32,128]{3,2,1,0:T(8,128)(2,1)S(1)} %get-tuple-element.49.query, bf16[4,2,2,16,128]{4,3,2,1,0:T(8,128)(2,1)S(1)} %get-tuple-element.50.new_kv, ...), custom_call_target="tpu_custom_call", output_to_operand_aliasing={{0}: (6, {}), {1}: (7, {})} | custom-call | flops 16777216 | bytes 1048576 | tf_op jit(solution)/shard_map/pallas_call | solution.py:365
  50.1 0.0 collective-permute-done.5.message
  50.1 0.1 shard_map.95
  50.2 0.5 collective-permute-start.10
  50.7 0.0 collective-permute-done.4.other
  50.7 1.3 %shard_map.96 = (bf16[4,2,256,512]{3,2,1,0:T(8,128)(2,1)}, bf16[4,4,2048]{2,1,0:T(4,128)(2,1)}, bf16[2,32,256]{2,1,0:T(8,128)(2,1)S(1)}, bf16[2,32,256]{2,1,0:T(...) custom-call(bf16[4,2,32,128]{3,2,1,0:T(8,128)(2,1)S(1)} %get-tuple-e, ...), custom_call_target="tpu_custom_call", output_to_operand_aliasing={{0}: (6, {}), {1}: (7, {})} | custom-call | flops 8388608 | bytes 1048576 | tf_op jit(solution)/shard_map/pallas_call | solution.py:365
  52.0 0.1 collective-permute-start.7
  52.2 0.0 collective-permute-done.9.other
  52.2 0.0 collective-permute-done.10.refs_1_
  52.2 1.3 %shard_map.97 = (bf16[4,2,256,512]{3,2,1,0:T(8,128)(2,1)}, bf16[4,4,2048]{2,1,0:T(4,128)(2,1)}) custom-call(bf16[4,2,32,128]{3,2,1,0:T(8,128)(2,1)S(1)} %get-tuple-element.49.query, bf16[4,2,2,16,128]{4,3,2,1,0:T(8,128)(2,1)S(1)} %get-tuple-element.50.new_kv, ...), custom_call_target="tpu_custom_call", output_to_operand_aliasing={{0}: (9, {}), {1}: (10, {})} | custom-call | flops 16777216 | bytes 1048576 | tf_op jit(solution)/shard_map/pallas_call | solution.py:365
  53.5 0.0 collective-permute-done.8.message
  53.5 0.0 collective-permute-done.7.lent
  53.5 0.3 shard_map.98
  53.8 0.5 collective-permute-start.11
  54.3 0.8 %shard_map.99 = (bf16[4,2,256,512]{3,2,1,0:T(8,128)(2,1)}, bf16[4,4,2048]{2,1,0:T(4,128)(2,1)}) custom-call(bf16[512,128]{1,0:T(8,128)(2,1)S(1)} %get-tuple-element.90.mine, bf16[512,128]{1,0:T(8,128)(2,1)S(1)} %get-tuple-element.91.theirs, bf16[4,2,256,512]{3,2,1,0:T(8,128)(2,1)} %get-tuple-element.92.refs_0_, ...), custom_call_target="tpu_custom_call", output_to_operand_aliasing={{0}: (2, {}), {1}: (3, {})} | custom-call | bytes 1048576 | tf_op jit(solution)/shard_map/pallas_call | solution.py:365
  55.0 0.1 collective-permute-done.11.got
  55.1 0.6 %shard_map.100 = (bf16[4,2,256,512]{3,2,1,0:T(8,128)(2,1)}, bf16[4,4,2048]{2,1,0:T(4,128)(2,1)}) custom-call(f32[2,32,128]{2,1,0:T(8,128)S(1)} %get-tuple-element.87.kept, f32[2,32,128]{2,1,0:T(8,128)S(1)} %collective-permute-done.11.got, f32[2,32,128]{2,1,0:T(8,128)S(1)} %get-tuple-element.89.totals, ...), custom_call_target="tpu_custom_call", output_to_operand_aliasing={{0}: (3, {}), {1}: (4, {})} | custom-call | bytes 1048576 | tf_op jit(solution)/shard_map/pallas_call | solution.py:365
Async XLA Ops:
  2.5 32.8 %collective-permute-start.3 = (bf16[2192,128]{1,0:T(8,128)(2,1)S(1)}, bf16[2192,128]{1,0:T(8,128)(2,1)S(1)}, u32[]{:S(2)}, u32[]{:S(2)}) collective-permute-start(bf16[2192,128]{1,0:T(8,128)(2,1)S(1)} %shard_map.89), channel_id=1, source_target_pairs={{0,8},{4,12},{8,0},{12,4},{1,9},{5,13},{9,1},{13,5},{2,10},{6,14},... | collective-permute-start | bytes 1683464 | tf_op jit(solution)/shard_map/ppermute | solution.py:395
  7.4 28.8 %collective-permute-start.2 = (bf16[1024,128]{1,0:T(8,128)(2,1)S(1)}, bf16[1024,128]{1,0:T(8,128)(2,1)S(1)}, u32[]{:S(2)}, u32[]{:S(2)}) collective-permute-start(bf16[1024,128]{1,0:T(8,128)(2,1)S(1)} %get-tuple-element.55.theirs), channel_id=1, source_target_pairs={{0,1},{1,0},{2,3},{3,2},{4,5},{5,4},{6,7},{7,6},{8,9},{9,8},{10,11... | collective-permute-start | bytes 786440 | tf_op jit(solution)/shard_map/ppermute | solution.py:404
  8.4 30.1 %collective-permute-start.1 = (bf16[1104,128]{1,0:T(8,128)(2,1)S(1)}, bf16[1104,128]{1,0:T(8,128)(2,1)S(1)}, u32[]{:S(2)}, u32[]{:S(2)}) collective-permute-start(bf16[1104,128]{1,0:T(8,128)(2,1)S(1)} %get-tuple-element.52), channel_id=1, source_target_pairs={{0,4},{4,0},{8,12},{12,8},{1,5},{5,1},{9,13},{13,9},{2,6},{6,2},{1... | collective-permute-start | bytes 847880 | tf_op jit(solution)/shard_map/ppermute | solution.py:395
  8.6 38.6 %collective-permute-start = (bf16[1104,128]{1,0:T(8,128)(2,1)S(1)}, bf16[1104,128]{1,0:T(8,128)(2,1)S(1)}, u32[]{:S(2)}, u32[]{:S(2)}) collective-permute-start(bf16[1104,128]{1,0:T(8,128)(2,1)S(1)} %get-tuple-element.51), channel_id=1, source_target_pairs={{0,12},{4,8},{8,4},{12,0},{1,13},{5,9},{9,5},{13,1},{2,14},{6,10},... | collective-permute-start | bytes 847880 | tf_op jit(solution)/shard_map/ppermute | solution.py:395
  8.8 41.3 %collective-permute-start.5 = (bf16[1088,128]{1,0:T(8,128)(2,1)S(1)}, bf16[1088,128]{1,0:T(8,128)(2,1)S(1)}, u32[]{:S(2)}, u32[]{:S(2)}) collective-permute-start(bf16[1088,128]{1,0:T(8,128)(2,1)S(1)} %get-tuple-element.66), channel_id=1, source_target_pairs={{0,4},{4,0},{8,12},{12,8},{1,5},{5,1},{9,13},{13,9},{2,6},{6,2},{1... | collective-permute-start | bytes 835592 | tf_op jit(solution)/shard_map/ppermute | solution.py:395
  35.5 13.3 %collective-permute-start.6 = (bf16[1024,128]{1,0:T(8,128)(2,1)S(1)}, bf16[1024,128]{1,0:T(8,128)(2,1)S(1)}, u32[]{:S(2)}, u32[]{:S(2)}) collective-permute-start(bf16[1024,128]{1,0:T(8,128)(2,1)S(1)} %get-tuple-element.68.theirs), channel_id=1, source_target_pairs={{0,1},{1,0},{2,3},{3,2},{4,5},{5,4},{6,7},{7,6},{8,9},{9,8},{10,11... | collective-permute-start | bytes 786440 | tf_op jit(solution)/shard_map/ppermute | solution.py:404
  36.2 17.3 %collective-permute-start.8 = (bf16[1088,128]{1,0:T(8,128)(2,1)S(1)}, bf16[1088,128]{1,0:T(8,128)(2,1)S(1)}, u32[]{:S(2)}, u32[]{:S(2)}) collective-permute-start(bf16[1088,128]{1,0:T(8,128)(2,1)S(1)} %get-tuple-element.78), channel_id=1, source_target_pairs={{0,12},{4,8},{8,4},{12,0},{1,13},{5,9},{9,5},{13,1},{2,14},{6,10},... | collective-permute-start | bytes 835592 | tf_op jit(solution)/shard_map/ppermute | solution.py:395
  47.3 3.4 %collective-permute-start.4 = (bf16[512,128]{1,0:T(8,128)(2,1)S(1)}, bf16[512,128]{1,0:T(8,128)(2,1)S(1)}, u32[]{:S(2)}, u32[]{:S(2)}) collective-permute-start(bf16[512,128]{1,0:T(8,128)(2,1)S(1)} %get-tuple-element.65.theirs), channel_id=1, source_target_pairs={{0,1},{1,0},{2,3},{3,2},{4,5},{5,4},{6,7},{7,6},{8,9},{9,8},{10,11... | collective-permute-start | bytes 393224 | tf_op jit(solution)/shard_map/ppermute | solution.py:404
  48.7 3.5 %collective-permute-start.9 = (bf16[512,128]{1,0:T(8,128)(2,1)S(1)}, bf16[512,128]{1,0:T(8,128)(2,1)S(1)}, u32[]{:S(2)}, u32[]{:S(2)}) collective-permute-start(bf16[512,128]{1,0:T(8,128)(2,1)S(1)} %get-tuple-element.80.theirs), channel_id=1, source_target_pairs={{0,1},{1,0},{2,3},{3,2},{4,5},{5,4},{6,7},{7,6},{8,9},{9,8},{10,11... | collective-permute-start | bytes 393224 | tf_op jit(solution)/shard_map/ppermute | solution.py:404
  50.2 1.9 %collective-permute-start.10 = (bf16[512,128]{1,0:T(8,128)(2,1)S(1)}, bf16[512,128]{1,0:T(8,128)(2,1)S(1)}, u32[]{:S(2)}, u32[]{:S(2)}) collective-permute-start(bf16[512,128]{1,0:T(8,128)(2,1)S(1)} %get-tuple-element.82.refs_2_), channel_id=1, source_target_pairs={{0,1},{1,0},{2,3},{3,2},{4,5},{5,4},{6,7},{7,6},{8,9},{9,8},{10,11... | collective-permute-start | bytes 393224 | tf_op jit(solution)/shard_map/ppermute | solution.py:404
  52.0 1.5 %collective-permute-start.7 = (bf16[2,32,256]{2,1,0:T(8,128)(2,1)S(1)}, bf16[2,32,256]{2,1,0:T(8,128)(2,1)S(1)}, u32[]{:S(2)}, u32[]{:S(2)}) collective-permute-start(bf16[2,32,256]{2,1,0:T(8,128)(2,1)S(1)} %get-tuple-element.77), channel_id=1, source_target_pairs={{0,1},{1,0},{2,3},{3,2},{4,5},{5,4},{6,7},{7,6},{8,9},{9,8},{10,11... | collective-permute-start | bytes 98312 | tf_op jit(solution)/shard_map/ppermute | solution.py:404
  53.8 1.3 %collective-permute-start.11 = (f32[2,32,128]{2,1,0:T(8,128)S(1)}, f32[2,32,128]{2,1,0:T(8,128)S(1)}, u32[]{:S(2)}, u32[]{:S(2)}) collective-permute-start(f32[2,32,128]{2,1,0:T(8,128)S(1)} %get-tuple-element.88), channel_id=1, source_target_pairs={{0,1},{1,0},{2,3},{3,2},{4,5},{5,4},{6,7},{7,6},{8,9},{9,8},{10,11... | collective-permute-start | bytes 98312 | tf_op jit(solution)/shard_map/ppermute | solution.py:404

commit v13 on v10

--- a/solution.py
+++ b/solution.py
@@ -53,6 +53,7 @@
         self.mine = max(1, self.q_local // Q_PER_KV)
         self.group = self.q_local // self.mine
         self.wide = self.group * self.steps
+        self.rest = self.heads - self.mine
 
     def anchor_at(self, which, parts):
         return (len(parts) * self.span + parts.index(which) * self.rows) * self.heads
@@ -62,6 +63,12 @@
 
     def message_rows(self, parts):
         return self.side_at(parts) + (TILE if 0 in parts else 0)
+
+    def halved(self, parts):
+        return parts == (1,) and self.rest > 0
+
+    def half_rows(self):
+        return self.mine * (self.span + self.rows)
 
     def source_row(self, k):
         return pick(far(self.n, k), lax.axis_index("pool"))
@@ -81,8 +88,10 @@
 def pack_kernel(size, plan, route, lengths, deltas, anchors, scale, *rest):
     outs, (held, tables, sems) = rest[:-3], rest[-3:]
     z = lax.axis_index("pool")
-    work = []
-    for m, (k, parts) in enumerate(plan):
+    sub = lax.axis_index("sub")
+    outs, work = list(outs), []
+    for k, parts in plan:
+        msgs = [outs.pop(0) for _ in range(1 + size.halved(parts))]
         dest = pick(far(size.n, k), z)
         index = jnp.int32(0)
         for j in range(size.count):
@@ -95,22 +104,40 @@
             )
             for copy in copies:
                 copy.start()
-            work.append((outs[m], parts, which, slot, copies))
+            work.append((msgs, parts, which, slot, copies))
         if 0 in parts:
-            outs[m][pl.ds(size.side_at(parts), TILE), :] = side_block(size, scale[index], lengths[index])
-    for msg, parts, which, slot, copies in work:
+            side = side_block(size, scale[index], lengths[index])
+            msgs[0][pl.ds(size.side_at(parts), TILE), :] = side
+    for msgs, parts, which, slot, copies in work:
         for copy in copies:
             copy.wait()
-        for h in range(size.heads):
-            lanes = slice(h * HEAD_DIM, (h + 1) * HEAD_DIM)
-            at = (parts.index(which) * size.heads + h) * size.span
-            msg[at:at + size.span, :] = held[slot, :, lanes]
-            at = size.anchor_at(which, parts) + h * size.rows
-            msg[at:at + size.rows, :] = tables[slot, :, lanes]
+
+        def fill(upper, msgs=msgs, parts=parts, which=which, slot=slot):
+            for h in range(size.heads):
+                lanes = slice(h * HEAD_DIM, (h + 1) * HEAD_DIM)
+                if len(msgs) == 2:
+                    own = (h >= size.rest) == upper
+                    j, msg = h % size.mine, msgs[int(own)]
+                    at, table = j * size.span, size.mine * size.span + j * size.rows
+                else:
+                    msg = msgs[0]
+                    at = (parts.index(which) * size.heads + h) * size.span
+                    table = size.anchor_at(which, parts) + h * size.rows
+                msg[at:at + size.span, :] = held[slot, :, lanes]
+                msg[table:table + size.rows, :] = tables[slot, :, lanes]
+
+        if len(msgs) == 2:
+            pl.when(sub == 0)(functools.partial(fill, False))
+            pl.when(sub != 0)(functools.partial(fill, True))
+        else:
+            fill(False)
 
 
 def pack(size, plan, route, lengths, deltas, anchors, scale):
-    shapes = [pltpu.VMEM((size.message_rows(parts), HEAD_DIM), BF) for _, parts in plan]
+    shapes = []
+    for _, parts in plan:
+        rows = [size.half_rows()] * 2 if size.halved(parts) else [size.message_rows(parts)]
+        shapes += [pltpu.VMEM((r, HEAD_DIM), BF) for r in rows]
     slots = sum(len(parts) for _, parts in plan)
     return pl.pallas_call(
         functools.partial(pack_kernel, size, plan),
@@ -162,24 +189,46 @@
     )(hbm(new_query), hbm(new_kv))
 
 
-def row_copies(size, k, parts, cache, mine, theirs, sems):
+def side_copies(size, k, parts, cache, out, own, sems, base=0):
     sub = lax.axis_index("sub")
     row = size.source_row(k)
-    rest = size.heads - size.mine
+    first = (sub if own else 1 - sub) * size.rest
     copies = []
-    for o, (out, first) in enumerate(((mine, sub * rest), (theirs, (1 - sub) * rest))):
-        if o and not rest:
-            break
-        for p, which in enumerate(parts):
-            for j in range(size.mine):
-                lanes = pl.ds(pl.multiple_of((first + j) * HEAD_DIM, HEAD_DIM), HEAD_DIM)
-                at = (p * size.mine + j) * size.span
-                copies.append(pltpu.make_async_copy(
-                    out.at[pl.ds(at, size.span)],
-                    cache.at[row, which, :, lanes],
-                    sems.at[o, p * size.mine + j],
-                ))
+    for p, which in enumerate(parts):
+        for j in range(size.mine):
+            lanes = pl.ds(pl.multiple_of((first + j) * HEAD_DIM, HEAD_DIM), HEAD_DIM)
+            at = p * size.mine + j
+            source = out[at] if isinstance(out, tuple) else out.at[pl.ds(at * size.span, size.span)]
+            copies.append(
+                pltpu.make_async_copy(source, cache.at[row, which, :, lanes], sems.at[base, at])
+            )
     return copies
+
+
+def row_copies(size, k, parts, cache, mine, theirs, sems):
+    copies = side_copies(size, k, parts, cache, mine, True, sems)
+    if size.rest:
+        copies += side_copies(size, k, parts, cache, theirs, False, sems, 1)
+    return copies
+
+
+def rebuild_half(size, message, tables, out, own):
+    sub = lax.axis_index("sub")
+    side_at = size.side_at((0,))
+    side = tables[side_at:side_at + TILE, :].astype(F32)
+    length = side[2 * size.heads:2 * size.heads + 1, :]
+    base = sub * size.span
+    last = sub != 0 if own else sub == 0
+    for j in range(size.mine):
+        h = size.heads + j
+        scale = jnp.where(last, side[h + size.rest:h + size.rest + 1, :], side[h:h + 1, :])
+        table = size.mine * size.span + j * size.rows
+        anchor = message[table:table + size.rows, :].astype(F32)
+        for i in range(size.rows):
+            part = slice(j * size.span + i * size.repeat, j * size.span + (i + 1) * size.repeat)
+            value = anchor[i:i + 1, :] + scale * message[part, :].astype(F32)
+            keep = (base + i * size.repeat).astype(F32) < length
+            out[part, :] = jnp.where(keep, value, jnp.float32(0.0)).astype(BF)
 
 
 def rebuild_heads(size, parts, message, tables, mine, theirs):
@@ -202,38 +251,41 @@
                 anchor = message[pl.ds(table, size.rows), :].astype(F32)
                 source = (p * size.heads + first + j) * size.span
                 to = (p * size.mine + j) * size.span
+                target = out
+                if isinstance(out, tuple):
+                    target, to = out[p * size.mine + j], 0
                 for i in range(size.rows):
                     at = pl.multiple_of(source + i * size.repeat, TILE)
                     value = anchor[i:i + 1, :] + scale * message[pl.ds(at, size.repeat), :].astype(F32)
                     keep = (base + i * size.repeat).astype(F32) < length
                     value = jnp.where(keep, value, jnp.float32(0.0)).astype(BF)
-                    out[to + i * size.repeat:to + (i + 1) * size.repeat, :] = value
-
-
-def rebuild_kernel(size, parts, chained, message, *refs):
-    _, _, mine, theirs = refs[2 * chained:]
-    rebuild_heads(size, parts, message, message, mine, theirs)
-
-
-def rebuild(size, parts, message, state):
+                    target[to + i * size.repeat:to + (i + 1) * size.repeat, :] = value
+
+
+def rebuild_kernel(size, parts, chained, split, message, *refs):
+    mine, *theirs = refs[2 * chained + 2:]
+    rebuild_heads(size, parts, message, message, mine, tuple(theirs) if split else theirs[0])
+
+
+def rebuild(size, parts, message, state, split=False):
     args = [vmem(message)]
-    in_specs = [IN_VMEM] * len(args)
+    in_specs = [IN_VMEM]
     aliases = {}
     if state is not None:
-        aliases = {len(args): 0, len(args) + 1: 1}
+        aliases = {1: 0, 2: 1}
         args += list(state)
         in_specs += [IN_HBM, IN_HBM]
     given = (len(parts) * size.mine * size.span, HEAD_DIM)
+    many, one = (size.mine, (size.span, HEAD_DIM)) if split else (1, given)
     out = pl.pallas_call(
-        functools.partial(rebuild_kernel, size, parts, state is not None),
+        functools.partial(rebuild_kernel, size, parts, state is not None, split),
         in_specs=in_specs,
-        out_specs=[IN_HBM, IN_HBM, IN_VMEM, IN_VMEM],
+        out_specs=[IN_HBM, IN_HBM, IN_VMEM] + [IN_VMEM] * many,
         out_shape=[
             pltpu.HBM((size.count, 2, size.span, size.channels), BF),
             pltpu.HBM((size.count, size.steps, size.q_local * HEAD_DIM), BF),
             pltpu.VMEM(given, BF),
-            pltpu.VMEM(given, BF),
-        ],
+        ] + [pltpu.VMEM(one, BF)] * many,
         input_output_aliases=aliases,
         compiler_params=LIMIT,
         cost_estimate=pl.CostEstimate(
@@ -242,7 +294,7 @@
             transcendentals=0,
         ),
     )(*args)
-    return tuple(out[:2]), out[2], out[3]
+    return tuple(out[:2]), out[2], (tuple(out[3:]) if split else out[3])
 
 
 def weigh(size, j, q, new_key, key_mine, key_other, live_mine, live_other, causal):
@@ -314,7 +366,10 @@
     store_heads(size, k, flat, made, attended, sem, copies)
 
 
-def weights_kernel(size, k, query, new_kv, tables, mine, other, theirs, *refs):
+def weights_kernel(size, k, split, query, new_kv, tables, mine, *refs):
+    many = size.mine if split else 1
+    other, theirs, refs = refs[:many], refs[many:2 * many], refs[2 * many:]
+    theirs = theirs if split else theirs[0]
     cache, _, weights, lent, share, totals, sems = refs[2:]
     row = size.source_row(k)
     copies = start_store(size, k, (0,), cache, mine, theirs, sems)
@@ -322,7 +377,8 @@
     for j in range(size.mine):
         keys = slice(j * size.span, (j + 1) * size.span)
         w0, w1, w2, total = weigh(
-            size, j, query[row, j], new_kv[row, 0, j], mine[keys, :], other[keys, :],
+            size, j, query[row, j], new_kv[row, 0, j], mine[keys, :],
+            other[j][...] if split else other[0][keys, :],
             live_mine, live_other, causal,
         )
         weights[j] = w0
@@ -331,6 +387,36 @@
         totals[j] = jnp.broadcast_to(total, totals.shape[1:])
     for copy in copies:
         copy.wait()
+
+
+def lend_kernel(size, lent, message, tables, *refs):
+    _, _, theirs, given = refs[2:]
+    rebuild_half(size, message, tables, theirs, False)
+    for j in range(size.mine):
+        values = slice(j * size.span, (j + 1) * size.span)
+        given[j] = jnp.dot(lent[j], theirs[values, :], preferred_element_type=F32)
+
+
+def lent_store_kernel(size, k, theirs, *refs):
+    cache, _, sems = refs[2:]
+    copies = side_copies(size, k, (1,), cache, theirs, False, sems)
+    for copy in copies:
+        copy.start()
+    for copy in copies:
+        copy.wait()
+
+
+def last_kernel(size, k, weights, share, totals, got, message, tables, *refs):
+    cache, attended, mine, made, flat, sem, sems = refs[2:]
+    rebuild_half(size, message, tables, mine, True)
+    copies = side_copies(size, k, (1,), cache, mine, True, sems)
+    for copy in copies:
+        copy.start()
+    for j in range(size.mine):
+        values = slice(j * size.span, (j + 1) * size.span)
+        acc = share[j] + jnp.dot(weights[j], mine[values, :], preferred_element_type=F32)
+        flat[j] = (acc + got[j]) / totals[j]
+    store_heads(size, k, flat, made, attended, sem, copies)
 
 
 def values_kernel(size, weights, share, lent, message, tables, *refs):
@@ -385,10 +471,13 @@
     query, fresh = arrange(size, new_query, new_kv)
     message = {}
     for part in (plan[:1], plan[1:]):
-        for (k, parts), msg in zip(part, pack(size, part, route, lengths, deltas, anchors, chan_scale)):
-            if k:
-                msg = lax.ppermute(msg, "pool", list(enumerate(far(n, k))))
-            message[k, parts] = msg
+        msgs = list(pack(size, part, route, lengths, deltas, anchors, chan_scale))
+        for k, parts in part:
+            for half in range(1 + size.halved(parts)):
+                msg = msgs.pop(0)
+                if k:
+                    msg = lax.ppermute(msg, "pool", list(enumerate(far(n, k))))
+                message[(k, parts, half) if size.halved(parts) else (k, parts)] = msg
 
     def swapped(x):
         return lax.ppermute(x, "sub", [(0, 1), (1, 0)])
@@ -420,19 +509,38 @@
         if k:
             state = attend(*held.pop(0), state)
     state = attend(*held.pop(0), state)
-    state, *keys = take(last, (0,), state)
+    split = size.rest > 0
+    tables = message[last, (0,)]
+    state, mine, theirs = rebuild(size, (0,), tables, state, split)
+    theirs = theirs if split else (theirs,)
     half = pltpu.VMEM((size.mine, size.wide, size.span), BF)
     state, (weights, lent, share, totals) = chained_call(
-        size, functools.partial(weights_kernel, size, last),
-        (query, fresh, message[last, (0,)], *keys), state, [half, half, wide, wide], [sems], flops // 2,
+        size, functools.partial(weights_kernel, size, last, split),
+        (query, fresh, tables, mine, *[swapped(x) for x in theirs], *theirs), state,
+        [half, half, wide, wide], [sems], flops // 2,
     )
     given = pltpu.VMEM((size.mine * size.span, HEAD_DIM), BF)
-    state, (mine, theirs, kept, given) = chained_call(
+    if split:
+        state, (theirs, sums) = chained_call(
+            size, functools.partial(lend_kernel, size),
+            (swapped(lent), message[last, (1,), 0], tables), state, [given, wide], [], flops // 4,
+        )
+        got = swapped(sums)
+        state, _ = chained_call(
+            size, functools.partial(lent_store_kernel, size, last), (theirs,), state, [], [sems], 0
+        )
+        state, _ = chained_call(
+            size, functools.partial(last_kernel, size, last),
+            (weights, share, totals, got, message[last, (1,), 1], tables), state,
+            [], [given] + rows + [sems], flops // 4,
+        )
+        return state
+    state, (mine, theirs, kept, sums) = chained_call(
         size, functools.partial(values_kernel, size),
-        (weights, share, swapped(lent), message[last, (1,)], message[last, (0,)]), state,
+        (weights, share, swapped(lent), message[last, (1,)], tables), state,
         [given, given, wide, wide], [], flops // 2,
     )
-    got = swapped(given)
+    got = swapped(sums)
     state, _ = chained_call(
         size, functools.partial(store_kernel, size, last), (mine, theirs), state, [], [sems], 0
     )

time: 56.8 us -> 55.4 us (0.975)
  the two profiles are of different devices: /device:TPU:21 before, /device:TPU:17 now
where the time goes in v13:
time: 55.4 us; the launch traced here: 55.1 us
  waiting for transfers between devices  25 us (45%)
  starting transfers between devices  16.5 us (30%)
  Pallas kernels  12.9 us (23%)
  between operations  0.74 us (1%)
    ppermute x5, waiting for transfers between devices, body(): msg = lax.ppermute(msg, 'pool', list(enumerate(far(n, k))))  23.8 us
    ppermute x7, starting transfers between devices, swapped(): return lax.ppermute(x, 'sub', [(0, 1), (1, 0)])  12.2 us
    pallas_call x7, Pallas kernels, chained_call(): pl.pallas_call(kernel, in_specs=[IN_VMEM] * many + [IN_HBM, IN_HBM], out_...  7.1 us
    ppermute x5, starting transfers between devices, body(): msg = lax.ppermute(msg, 'pool', list(enumerate(far(n, k))))  4.26 us
    pallas_call x2, Pallas kernels, pack(): pl.pallas_call(functools.partial(pack_kernel, size, plan), out_shape=shap...  4.16 us
    ppermute x7, waiting for transfers between devices, swapped(): return lax.ppermute(x, 'sub', [(0, 1), (1, 0)])  1.19 us
  transfers between devices with their start and end apart: 12, of which 6 were waited for; matrix products, arithmetic and copies ran while one was open for 0% of the time, Pallas kernels for 18%

profile of v13, /device:TPU:17, one launch (start us, length us, event | category | flops | bytes accessed | tf_op | source)
XLA Modules:
  0.0 55.1 jit_solution(9105909868090894690)
XLA Ops:
  0.6 1.9 %shard_map.89 = bf16[2192,128]{1,0:T(8,128)(2,1)S(1)} custom-call(s32[4]{0:T(128)} %route.3, s32[4]{0:T(128)} %lengths.3, bf16[4,2,256,512]{3,2,1,0:T(8,128)(2,1)} %deltas.3, bf16[4,2,16,512]{3,2,1,0:T(8,128)(2,1)} %anchors.3, bf16[4,2,512]{2,1,0:T(2,128)(2,1)} %scale.3), custom_call_target="tpu_custom_call" | custom-call | bytes 524288 | tf_op jit(solution)/shard_map/pallas_call | solution.py:142
  2.5 0.1 collective-permute-start.3
  2.6 2.3 %shard_map.87 = (bf16[2192,128]{1,0:T(8,128)(2,1)S(1)}, bf16[1104,128]{1,0:T(8,128)(2,1)S(1)}, bf16[544,128]{1,0:T(8,128)(2,1)S(1)}, bf16[544,128]{1,0:T(8,128)(2,1)S(1)}, bf16[2192,128]{1,0:T(8,128)(2,1)S(1)}) custom-call(s32[4]{0:T(128)} %route.3, s32[4]{0:T(128)} %lengths.3, bf16[4,2,256,512]{3,2,1,0:T(8,128)(2,1)} %deltas.3, ...), custom_call_target="tpu_custom_call" | custom-call | bytes 1572864 | tf_op jit(solution)/shard_map/pallas_call | solution.py:142
  4.9 1.4 %collective-permute-start.1 = (bf16[2192,128]{1,0:T(8,128)(2,1)S(1)}, bf16[2192,128]{1,0:T(8,128)(2,1)S(1)}, u32[]{:S(2)}, u32[]{:S(2)}) collective-permute-start(bf16[2192,128]{1,0:T(8,128)(2,1)S(1)} %get-tuple-element.47), channel_id=1, source_target_pairs={{0,4},{4,0},{8,12},{12,8},{1,5},{5,1},{9,13},{13,9},{2,6},{6,2},{1... | collective-permute-start | bytes 1683464 | tf_op jit(solution)/shard_map/ppermute | solution.py:479
  6.3 0.2 shard_map.88
  6.5 1.3 %collective-permute-start.2 = (bf16[1024,128]{1,0:T(8,128)(2,1)S(1)}, bf16[1024,128]{1,0:T(8,128)(2,1)S(1)}, u32[]{:S(2)}, u32[]{:S(2)}) collective-permute-start(bf16[1024,128]{1,0:T(8,128)(2,1)S(1)} %get-tuple-element.50.theirs), channel_id=1, source_target_pairs={{0,1},{1,0},{2,3},{3,2},{4,5},{5,4},{6,7},{7,6},{8,9},{9,8},{10,11... | collective-permute-start | bytes 786440 | tf_op jit(solution)/shard_map/ppermute | solution.py:483
  7.8 1.3 %collective-permute-start = (bf16[1104,128]{1,0:T(8,128)(2,1)S(1)}, bf16[1104,128]{1,0:T(8,128)(2,1)S(1)}, u32[]{:S(2)}, u32[]{:S(2)}) collective-permute-start(bf16[1104,128]{1,0:T(8,128)(2,1)S(1)} %get-tuple-element.46), channel_id=1, source_target_pairs={{0,12},{4,8},{8,4},{12,0},{1,13},{5,9},{9,5},{13,1},{2,14},{6,10},... | collective-permute-start | bytes 847880 | tf_op jit(solution)/shard_map/ppermute | solution.py:479
  9.1 0.9 %shard_map.86 = (bf16[4,2,32,128]{3,2,1,0:T(8,128)(2,1)S(1)}, bf16[4,2,2,16,128]{4,3,2,1,0:T(8,128)(2,1)S(1)}) custom-call(bf16[4,4,2048]{2,1,0:T(4,128)(2,1)} %new_query.1, bf16[4,2,4,512]{3,2,1,0:T(4,128)(2,1)} %new_kv.1), custom_call_target="tpu_custom_call" | custom-call | tf_op jit(solution)/shard_map/pallas_call | solution.py:179
  10.0 16.3 %collective-permute-done.3.message.tables = bf16[2192,128]{1,0:T(8,128)(2,1)S(1)} collective-permute-done((bf16[2192,128]{1,0:T(8,128)(2,1)S(1)}, bf16[2192,128]{1,0:T(8,128)(2,1)S(1)}, u32[]{:S(2)}, u32[]{:S(2)}) %collective-permute-start.3) | collective-permute-done | bytes 561184 | tf_op jit(solution)/shard_map/ppermute | solution.py:479
  26.3 0.2 shard_map.90
  26.5 2.5 %collective-permute-start.5 = (bf16[1024,128]{1,0:T(8,128)(2,1)S(1)}, bf16[1024,128]{1,0:T(8,128)(2,1)S(1)}, u32[]{:S(2)}, u32[]{:S(2)}) collective-permute-start(bf16[1024,128]{1,0:T(8,128)(2,1)S(1)} %get-tuple-element.60.theirs), channel_id=1, source_target_pairs={{0,1},{1,0},{2,3},{3,2},{4,5},{5,4},{6,7},{7,6},{8,9},{9,8},{10,11... | collective-permute-start | bytes 786440 | tf_op jit(solution)/shard_map/ppermute | solution.py:483
  29.0 0.0 collective-permute-done.2.other
  29.0 1.3 %shard_map.91 = (bf16[4,2,256,512]{3,2,1,0:T(8,128)(2,1)}, bf16[4,4,2048]{2,1,0:T(4,128)(2,1)}) custom-call(bf16[4,2,32,128]{3,2,1,0:T(8,128)(2,1)S(1)} %get-tuple-element.44.query, bf16[4,2,2,16,128]{4,3,2,1,0:T(8,128)(2,1)S(1)} %get-tuple-element.45.new_kv, ...), custom_call_target="tpu_custom_call", output_to_operand_aliasing={{0}: (6, {}), {1}: (7, {})} | custom-call | flops 16777216 | bytes 1048576 | tf_op jit(solution)/shard_map/pallas_call | solution.py:447
  30.4 0.0 collective-permute-done.1.message.tables
  30.4 0.2 shard_map.92
  30.6 6.9 %collective-permute-start.4 = (bf16[1024,128]{1,0:T(8,128)(2,1)S(1)}, bf16[1024,128]{1,0:T(8,128)(2,1)S(1)}, u32[]{:S(2)}, u32[]{:S(2)}) collective-permute-start(bf16[1024,128]{1,0:T(8,128)(2,1)S(1)} %get-tuple-element.58.theirs), channel_id=1, source_target_pairs={{0,1},{1,0},{2,3},{3,2},{4,5},{5,4},{6,7},{7,6},{8,9},{9,8},{10,11... | collective-permute-start | bytes 786440 | tf_op jit(solution)/shard_map/ppermute | solution.py:483
  37.4 0.2 collective-permute-start.9
  37.7 1.2 %collective-permute-start.11 = (bf16[544,128]{1,0:T(8,128)(2,1)S(1)}, bf16[544,128]{1,0:T(8,128)(2,1)S(1)}, u32[]{:S(2)}, u32[]{:S(2)}) collective-permute-start(bf16[544,128]{1,0:T(8,128)(2,1)S(1)} %get-tuple-element.80), channel_id=1, source_target_pairs={{0,12},{4,8},{8,4},{12,0},{1,13},{5,9},{9,5},{13,1},{2,14},{6,10},... | collective-permute-start | bytes 417800 | tf_op jit(solution)/shard_map/ppermute | solution.py:479
  38.9 0.0 collective-permute-done.5.other
  38.9 1.3 %shard_map.93 = (bf16[4,2,256,512]{3,2,1,0:T(8,128)(2,1)}, bf16[4,4,2048]{2,1,0:T(4,128)(2,1)}) custom-call(bf16[4,2,32,128]{3,2,1,0:T(8,128)(2,1)S(1)} %get-tuple-element.44.query, bf16[4,2,2,16,128]{4,3,2,1,0:T(8,128)(2,1)S(1)} %get-tuple-element.45.new_kv, ...), custom_call_target="tpu_custom_call", output_to_operand_aliasing={{0}: (6, {}), {1}: (7, {})} | custom-call | flops 16777216 | bytes 1048576 | tf_op jit(solution)/shard_map/pallas_call | solution.py:447
  40.3 0.0 collective-permute-done.4.other
  40.3 1.3 %shard_map.94 = (bf16[4,2,256,512]{3,2,1,0:T(8,128)(2,1)}, bf16[4,4,2048]{2,1,0:T(4,128)(2,1)}) custom-call(bf16[4,2,32,128]{3,2,1,0:T(8,128)(2,1)S(1)} %get-tuple-element.44.query, bf16[4,2,2,16,128]{4,3,2,1,0:T(8,128)(2,1)S(1)} %get-tuple-element.45.new_kv, ...), custom_call_target="tpu_custom_call", output_to_operand_aliasing={{0}: (6, {}), {1}: (7, {})} | custom-call | flops 16777216 | bytes 1048576 | tf_op jit(solution)/shard_map/pallas_call | solution.py:447
  41.6 0.6 %collective-permute-done.message.tables = bf16[1104,128]{1,0:T(8,128)(2,1)S(1)} collective-permute-done((bf16[1104,128]{1,0:T(8,128)(2,1)S(1)}, bf16[1104,128]{1,0:T(8,128)(2,1)S(1)}, u32[]{:S(2)}, u32[]{:S(2)}) %collective-permute-start) | collective-permute-done | bytes 282656 | tf_op jit(solution)/shard_map/ppermute | solution.py:479
  42.3 0.1 shard_map.95
  42.4 0.7 %collective-permute-start.6 = (bf16[256,128]{1,0:T(8,128)(2,1)S(1)}, bf16[256,128]{1,0:T(8,128)(2,1)S(1)}, u32[]{:S(2)}, u32[]{:S(2)}) collective-permute-start(bf16[256,128]{1,0:T(8,128)(2,1)S(1)} %get-tuple-element.68.refs_2_), channel_id=1, source_target_pairs={{0,1},{1,0},{2,3},{3,2},{4,5},{5,4},{6,7},{7,6},{8,9},{9,8},{10,11... | collective-permute-start | bytes 196616 | tf_op jit(solution)/shard_map/ppermute | solution.py:483
  43.0 0.1 collective-permute-start.7
  43.1 0.8 %collective-permute-done.6.refs_0_ = bf16[256,128]{1,0:T(8,128)(2,1)S(1)} collective-permute-done((bf16[256,128]{1,0:T(8,128)(2,1)S(1)}, bf16[256,128]{1,0:T(8,128)(2,1)S(1)}, u32[]{:S(2)}, u32[]{:S(2)}) %collective-permute-start.6) | collective-permute-done | bytes 65568 | tf_op jit(solution)/shard_map/ppermute | solution.py:483
  43.9 0.4 collective-permute-done.7.refs_1_
  44.3 1.3 %shard_map.96 = (bf16[4,2,256,512]{3,2,1,0:T(8,128)(2,1)}, bf16[4,4,2048]{2,1,0:T(4,128)(2,1)}, bf16[2,32,256]{2,1,0:T(8,128)(2,1)S(1)}, bf16[2,32,256]{2,1,0:T(...) custom-call(bf16[4,2,32,128]{3,2,1,0:T(8,128)(2,1)S(1)} %get-tuple-e, ...), custom_call_target="tpu_custom_call", output_to_operand_aliasing={{0}: (8, {}), {1}: (9, {})} | custom-call | flops 8388608 | bytes 1048576 | tf_op jit(solution)/shard_map/pallas_call | solution.py:447
  45.6 0.2 collective-permute-start.8
  45.8 5.4 %collective-permute-done.9.message = bf16[544,128]{1,0:T(8,128)(2,1)S(1)} collective-permute-done((bf16[544,128]{1,0:T(8,128)(2,1)S(1)}, bf16[544,128]{1,0:T(8,128)(2,1)S(1)}, u32[]{:S(2)}, u32[]{:S(2)}) %collective-permute-start.9) | collective-permute-done | bytes 139296 | tf_op jit(solution)/shard_map/ppermute | solution.py:479
  51.2 0.0 collective-permute-done.8.lent
  51.2 0.2 shard_map.97
  51.4 0.6 %collective-permute-start.10 = (f32[2,32,128]{2,1,0:T(8,128)S(1)}, f32[2,32,128]{2,1,0:T(8,128)S(1)}, u32[]{:S(2)}, u32[]{:S(2)}) collective-permute-start(f32[2,32,128]{2,1,0:T(8,128)S(1)} %get-tuple-element.79), channel_id=1, source_target_pairs={{0,1},{1,0},{2,3},{3,2},{4,5},{5,4},{6,7},{7,6},{8,9},{9,8},{10,11... | collective-permute-start | bytes 98312 | tf_op jit(solution)/shard_map/ppermute | solution.py:483
  52.0 0.7 %shard_map.98 = (bf16[4,2,256,512]{3,2,1,0:T(8,128)(2,1)}, bf16[4,4,2048]{2,1,0:T(4,128)(2,1)}) custom-call(bf16[512,128]{1,0:T(8,128)(2,1)S(1)} %get-tuple-element.81.theirs, bf16[4,2,256,512]{3,2,1,0:T(8,128)(2,1)} %get-tuple-element.82.refs_0_, bf16[4,4,2048]{2,1,0:T(4,128)(2,1)} %get-tuple-element.83.refs_1_), custom_call_target="tpu_custom_call", output_to_operand_aliasing={{0}: (1, {}), {1}: (2, {})} | custom-call | bytes 1048576 | tf_op jit(solution)/shard_map/pallas_call | solution.py:447
  52.8 1.4 %collective-permute-done.11.message = bf16[544,128]{1,0:T(8,128)(2,1)S(1)} collective-permute-done((bf16[544,128]{1,0:T(8,128)(2,1)S(1)}, bf16[544,128]{1,0:T(8,128)(2,1)S(1)}, u32[]{:S(2)}, u32[]{:S(2)}) %collective-permute-start.11) | collective-permute-done | bytes 139296 | tf_op jit(solution)/shard_map/ppermute | solution.py:479
  54.2 0.0 collective-permute-done.10.got
  54.2 0.9 %shard_map.99 = (bf16[4,2,256,512]{3,2,1,0:T(8,128)(2,1)}, bf16[4,4,2048]{2,1,0:T(4,128)(2,1)}) custom-call(bf16[2,32,256]{2,1,0:T(8,128)(2,1)S(1)} %get-tuple-element.72.weights, f32[2,32,128]{2,1,0:T(8,128)S(1)} %get-tuple-element.73.share, f32[2,32,128]{2,1,0:T(8,128)S(1)} %get-tuple-element.74.totals, ...), custom_call_target="tpu_custom_call", output_to_operand_aliasing={{0}: (6, {}), {1}: (7, {})} | custom-call | flops 4194304 | bytes 1048576 | tf_op jit(solution)/shard_map/pallas_call | solution.py:447
Async XLA Ops:
  2.5 23.8 %collective-permute-start.3 = (bf16[2192,128]{1,0:T(8,128)(2,1)S(1)}, bf16[2192,128]{1,0:T(8,128)(2,1)S(1)}, u32[]{:S(2)}, u32[]{:S(2)}) collective-permute-start(bf16[2192,128]{1,0:T(8,128)(2,1)S(1)} %shard_map.89), channel_id=1, source_target_pairs={{0,8},{4,12},{8,0},{12,4},{1,9},{5,13},{9,1},{13,5},{2,10},{6,14},... | collective-permute-start | bytes 1683464 | tf_op jit(solution)/shard_map/ppermute | solution.py:479
  4.9 25.5 %collective-permute-start.1 = (bf16[2192,128]{1,0:T(8,128)(2,1)S(1)}, bf16[2192,128]{1,0:T(8,128)(2,1)S(1)}, u32[]{:S(2)}, u32[]{:S(2)}) collective-permute-start(bf16[2192,128]{1,0:T(8,128)(2,1)S(1)} %get-tuple-element.47), channel_id=1, source_target_pairs={{0,4},{4,0},{8,12},{12,8},{1,5},{5,1},{9,13},{13,9},{2,6},{6,2},{1... | collective-permute-start | bytes 1683464 | tf_op jit(solution)/shard_map/ppermute | solution.py:479
  6.5 22.6 %collective-permute-start.2 = (bf16[1024,128]{1,0:T(8,128)(2,1)S(1)}, bf16[1024,128]{1,0:T(8,128)(2,1)S(1)}, u32[]{:S(2)}, u32[]{:S(2)}) collective-permute-start(bf16[1024,128]{1,0:T(8,128)(2,1)S(1)} %get-tuple-element.50.theirs), channel_id=1, source_target_pairs={{0,1},{1,0},{2,3},{3,2},{4,5},{5,4},{6,7},{7,6},{8,9},{9,8},{10,11... | collective-permute-start | bytes 786440 | tf_op jit(solution)/shard_map/ppermute | solution.py:483
  7.8 34.5 %collective-permute-start = (bf16[1104,128]{1,0:T(8,128)(2,1)S(1)}, bf16[1104,128]{1,0:T(8,128)(2,1)S(1)}, u32[]{:S(2)}, u32[]{:S(2)}) collective-permute-start(bf16[1104,128]{1,0:T(8,128)(2,1)S(1)} %get-tuple-element.46), channel_id=1, source_target_pairs={{0,12},{4,8},{8,4},{12,0},{1,13},{5,9},{9,5},{13,1},{2,14},{6,10},... | collective-permute-start | bytes 847880 | tf_op jit(solution)/shard_map/ppermute | solution.py:479
  26.5 12.4 %collective-permute-start.5 = (bf16[1024,128]{1,0:T(8,128)(2,1)S(1)}, bf16[1024,128]{1,0:T(8,128)(2,1)S(1)}, u32[]{:S(2)}, u32[]{:S(2)}) collective-permute-start(bf16[1024,128]{1,0:T(8,128)(2,1)S(1)} %get-tuple-element.60.theirs), channel_id=1, source_target_pairs={{0,1},{1,0},{2,3},{3,2},{4,5},{5,4},{6,7},{7,6},{8,9},{9,8},{10,11... | collective-permute-start | bytes 786440 | tf_op jit(solution)/shard_map/ppermute | solution.py:483
  30.6 9.7 %collective-permute-start.4 = (bf16[1024,128]{1,0:T(8,128)(2,1)S(1)}, bf16[1024,128]{1,0:T(8,128)(2,1)S(1)}, u32[]{:S(2)}, u32[]{:S(2)}) collective-permute-start(bf16[1024,128]{1,0:T(8,128)(2,1)S(1)} %get-tuple-element.58.theirs), channel_id=1, source_target_pairs={{0,1},{1,0},{2,3},{3,2},{4,5},{5,4},{6,7},{7,6},{8,9},{9,8},{10,11... | collective-permute-start | bytes 786440 | tf_op jit(solution)/shard_map/ppermute | solution.py:483
  37.4 13.8 %collective-permute-start.9 = (bf16[544,128]{1,0:T(8,128)(2,1)S(1)}, bf16[544,128]{1,0:T(8,128)(2,1)S(1)}, u32[]{:S(2)}, u32[]{:S(2)}) collective-permute-start(bf16[544,128]{1,0:T(8,128)(2,1)S(1)} %get-tuple-element.76), channel_id=1, source_target_pairs={{0,12},{4,8},{8,4},{12,0},{1,13},{5,9},{9,5},{13,1},{2,14},{6,10},... | collective-permute-start | bytes 417800 | tf_op jit(solution)/shard_map/ppermute | solution.py:479
  37.7 16.5 %collective-permute-start.11 = (bf16[544,128]{1,0:T(8,128)(2,1)S(1)}, bf16[544,128]{1,0:T(8,128)(2,1)S(1)}, u32[]{:S(2)}, u32[]{:S(2)}) collective-permute-start(bf16[544,128]{1,0:T(8,128)(2,1)S(1)} %get-tuple-element.80), channel_id=1, source_target_pairs={{0,12},{4,8},{8,4},{12,0},{1,13},{5,9},{9,5},{13,1},{2,14},{6,10},... | collective-permute-start | bytes 417800 | tf_op jit(solution)/shard_map/ppermute | solution.py:479
  42.4 1.6 %collective-permute-start.6 = (bf16[256,128]{1,0:T(8,128)(2,1)S(1)}, bf16[256,128]{1,0:T(8,128)(2,1)S(1)}, u32[]{:S(2)}, u32[]{:S(2)}) collective-permute-start(bf16[256,128]{1,0:T(8,128)(2,1)S(1)} %get-tuple-element.68.refs_2_), channel_id=1, source_target_pairs={{0,1},{1,0},{2,3},{3,2},{4,5},{5,4},{6,7},{7,6},{8,9},{9,8},{10,11... | collective-permute-start | bytes 196616 | tf_op jit(solution)/shard_map/ppermute | solution.py:483
  43.0 1.3 %collective-permute-start.7 = (bf16[256,128]{1,0:T(8,128)(2,1)S(1)}, bf16[256,128]{1,0:T(8,128)(2,1)S(1)}, u32[]{:S(2)}, u32[]{:S(2)}) collective-permute-start(bf16[256,128]{1,0:T(8,128)(2,1)S(1)} %get-tuple-element.69.refs_3_), channel_id=1, source_target_pairs={{0,1},{1,0},{2,3},{3,2},{4,5},{5,4},{6,7},{7,6},{8,9},{9,8},{10,11... | collective-permute-start | bytes 196616 | tf_op jit(solution)/shard_map/ppermute | solution.py:483
  45.6 5.7 %collective-permute-start.8 = (bf16[2,32,256]{2,1,0:T(8,128)(2,1)S(1)}, bf16[2,32,256]{2,1,0:T(8,128)(2,1)S(1)}, u32[]{:S(2)}, u32[]{:S(2)}) collective-permute-start(bf16[2,32,256]{2,1,0:T(8,128)(2,1)S(1)} %get-tuple-element.75), channel_id=1, source_target_pairs={{0,1},{1,0},{2,3},{3,2},{4,5},{5,4},{6,7},{7,6},{8,9},{9,8},{10,11... | collective-permute-start | bytes 98312 | tf_op jit(solution)/shard_map/ppermute | solution.py:483
  51.4 2.8 %collective-permute-start.10 = (f32[2,32,128]{2,1,0:T(8,128)S(1)}, f32[2,32,128]{2,1,0:T(8,128)S(1)}, u32[]{:S(2)}, u32[]{:S(2)}) collective-permute-start(f32[2,32,128]{2,1,0:T(8,128)S(1)} %get-tuple-element.79), channel_id=1, source_target_pairs={{0,1},{1,0},{2,3},{3,2},{4,5},{5,4},{6,7},{7,6},{8,9},{9,8},{10,11... | collective-permute-start | bytes 98312 | tf_op jit(solution)/shard_map/ppermute | solution.py:483

commit v14 on v13

--- a/solution.py
+++ b/solution.py
@@ -31,7 +31,8 @@
 
 
 def far(n, k):
-    return tuple(z ^ k for z in range(n))
+    ring = (0, 2, 1, 3) if n == 4 else tuple(range(n))
+    return tuple(ring[(ring.index(z) + k) % n] for z in range(n))
 
 
 def pick(values, at):
@@ -71,7 +72,7 @@
         return self.mine * (self.span + self.rows)
 
     def source_row(self, k):
-        return pick(far(self.n, k), lax.axis_index("pool"))
+        return pick(far(self.n, self.n - k), lax.axis_index("pool"))
 
 
 def side_block(size, scale, length):
@@ -465,7 +466,7 @@
     n = lax.axis_size("pool")
     size = Sizes(deltas, anchors, new_query, n)
     both = (0, 1)
-    order = [2, 1] + list(range(3, n))
+    order = list(range(n - 1, 0, -1))
     last = order[-1]
     plan = [(k, both) for k in order[:-1]] + [(last, (0,)), (last, (1,)), (0, both)]
     query, fresh = arrange(size, new_query, new_kv)

time: 55.4 us -> 55.4 us (level)
  the two profiles are of different devices: /device:TPU:17 before, /device:TPU:31 now
where the time goes in v14:
time: 55.4 us; the launch traced here: 55.1 us
  waiting for transfers between devices  21.2 us (38%)
  starting transfers between devices  20.3 us (37%)
  Pallas kernels  12.9 us (23%)
  between operations  0.74 us (1%)
    ppermute x5, waiting for transfers between devices, body(): msg = lax.ppermute(msg, 'pool', list(enumerate(far(n, k))))  18.6 us
    ppermute x7, starting transfers between devices, swapped(): return lax.ppermute(x, 'sub', [(0, 1), (1, 0)])  10.6 us
    ppermute x5, starting transfers between devices, body(): msg = lax.ppermute(msg, 'pool', list(enumerate(far(n, k))))  9.73 us
    pallas_call x7, Pallas kernels, chained_call(): pl.pallas_call(kernel, in_specs=[IN_VMEM] * many + [IN_HBM, IN_HBM], out_...  7.1 us
    pallas_call x2, Pallas kernels, pack(): pl.pallas_call(functools.partial(pack_kernel, size, plan), out_shape=shap...  4.15 us
    ppermute x7, waiting for transfers between devices, swapped(): return lax.ppermute(x, 'sub', [(0, 1), (1, 0)])  2.54 us
  transfers between devices with their start and end apart: 12, of which 6 were waited for; matrix products, arithmetic and copies ran while one was open for 0% of the time, Pallas kernels for 18%

profile of v14, /device:TPU:31, one launch (start us, length us, event | category | flops | bytes accessed | tf_op | source)
XLA Modules:
  0.0 55.1 jit_solution(3561195727420571126)
XLA Ops:
  0.6 1.9 %shard_map.89 = bf16[2192,128]{1,0:T(8,128)(2,1)S(1)} custom-call(s32[4]{0:T(128)} %route.3, s32[4]{0:T(128)} %lengths.3, bf16[4,2,256,512]{3,2,1,0:T(8,128)(2,1)} %deltas.3, bf16[4,2,16,512]{3,2,1,0:T(8,128)(2,1)} %anchors.3, bf16[4,2,512]{2,1,0:T(2,128)(2,1)} %scale.3), custom_call_target="tpu_custom_call" | custom-call | bytes 524288 | tf_op jit(solution)/shard_map/pallas_call | solution.py:143
  2.5 0.1 collective-permute-start.3
  2.6 2.3 %shard_map.87 = (bf16[2192,128]{1,0:T(8,128)(2,1)S(1)}, bf16[1104,128]{1,0:T(8,128)(2,1)S(1)}, bf16[544,128]{1,0:T(8,128)(2,1)S(1)}, bf16[544,128]{1,0:T(8,128)(2,1)S(1)}, bf16[2192,128]{1,0:T(8,128)(2,1)S(1)}) custom-call(s32[4]{0:T(128)} %route.3, s32[4]{0:T(128)} %lengths.3, bf16[4,2,256,512]{3,2,1,0:T(8,128)(2,1)} %deltas.3, ...), custom_call_target="tpu_custom_call" | custom-call | bytes 1572864 | tf_op jit(solution)/shard_map/pallas_call | solution.py:143
  4.9 0.2 collective-permute-start.1
  5.1 0.2 shard_map.88
  5.3 1.3 %collective-permute-start.2 = (bf16[1024,128]{1,0:T(8,128)(2,1)S(1)}, bf16[1024,128]{1,0:T(8,128)(2,1)S(1)}, u32[]{:S(2)}, u32[]{:S(2)}) collective-permute-start(bf16[1024,128]{1,0:T(8,128)(2,1)S(1)} %get-tuple-element.50.theirs), channel_id=1, source_target_pairs={{0,1},{1,0},{2,3},{3,2},{4,5},{5,4},{6,7},{7,6},{8,9},{9,8},{10,11... | collective-permute-start | bytes 786440 | tf_op jit(solution)/shard_map/ppermute | solution.py:484
  6.6 2.8 %collective-permute-start = (bf16[1104,128]{1,0:T(8,128)(2,1)S(1)}, bf16[1104,128]{1,0:T(8,128)(2,1)S(1)}, u32[]{:S(2)}, u32[]{:S(2)}) collective-permute-start(bf16[1104,128]{1,0:T(8,128)(2,1)S(1)} %get-tuple-element.46), channel_id=1, source_target_pairs={{0,8},{4,12},{8,4},{12,0},{1,9},{5,13},{9,5},{13,1},{2,10},{6,14},... | collective-permute-start | bytes 847880 | tf_op jit(solution)/shard_map/ppermute | solution.py:480
  9.4 0.9 %shard_map.86 = (bf16[4,2,32,128]{3,2,1,0:T(8,128)(2,1)S(1)}, bf16[4,2,2,16,128]{4,3,2,1,0:T(8,128)(2,1)S(1)}) custom-call(bf16[4,4,2048]{2,1,0:T(4,128)(2,1)} %new_query.1, bf16[4,2,4,512]{3,2,1,0:T(4,128)(2,1)} %new_kv.1), custom_call_target="tpu_custom_call" | custom-call | tf_op jit(solution)/shard_map/pallas_call | solution.py:180
  10.4 7.7 %collective-permute-done.3.message.tables = bf16[2192,128]{1,0:T(8,128)(2,1)S(1)} collective-permute-done((bf16[2192,128]{1,0:T(8,128)(2,1)S(1)}, bf16[2192,128]{1,0:T(8,128)(2,1)S(1)}, u32[]{:S(2)}, u32[]{:S(2)}) %collective-permute-start.3) | collective-permute-done | bytes 561184 | tf_op jit(solution)/shard_map/ppermute | solution.py:480
  18.1 0.2 shard_map.90
  18.3 2.7 %collective-permute-start.5 = (bf16[1024,128]{1,0:T(8,128)(2,1)S(1)}, bf16[1024,128]{1,0:T(8,128)(2,1)S(1)}, u32[]{:S(2)}, u32[]{:S(2)}) collective-permute-start(bf16[1024,128]{1,0:T(8,128)(2,1)S(1)} %get-tuple-element.60.theirs), channel_id=1, source_target_pairs={{0,1},{1,0},{2,3},{3,2},{4,5},{5,4},{6,7},{7,6},{8,9},{9,8},{10,11... | collective-permute-start | bytes 786440 | tf_op jit(solution)/shard_map/ppermute | solution.py:484
  20.9 0.0 collective-permute-done.2.other
  20.9 1.3 %shard_map.91 = (bf16[4,2,256,512]{3,2,1,0:T(8,128)(2,1)}, bf16[4,4,2048]{2,1,0:T(4,128)(2,1)}) custom-call(bf16[4,2,32,128]{3,2,1,0:T(8,128)(2,1)S(1)} %get-tuple-element.44.query, bf16[4,2,2,16,128]{4,3,2,1,0:T(8,128)(2,1)S(1)} %get-tuple-element.45.new_kv, ...), custom_call_target="tpu_custom_call", output_to_operand_aliasing={{0}: (6, {}), {1}: (7, {})} | custom-call | flops 16777216 | bytes 1048576 | tf_op jit(solution)/shard_map/pallas_call | solution.py:448
  22.3 10.9 %collective-permute-done.1.message.tables = bf16[2192,128]{1,0:T(8,128)(2,1)S(1)} collective-permute-done((bf16[2192,128]{1,0:T(8,128)(2,1)S(1)}, bf16[2192,128]{1,0:T(8,128)(2,1)S(1)}, u32[]{:S(2)}, u32[]{:S(2)}) %collective-permute-start.1) | collective-permute-done | bytes 561184 | tf_op jit(solution)/shard_map/ppermute | solution.py:480
  33.2 0.2 shard_map.92
  33.4 0.6 %collective-permute-start.4 = (bf16[1024,128]{1,0:T(8,128)(2,1)S(1)}, bf16[1024,128]{1,0:T(8,128)(2,1)S(1)}, u32[]{:S(2)}, u32[]{:S(2)}) collective-permute-start(bf16[1024,128]{1,0:T(8,128)(2,1)S(1)} %get-tuple-element.58.theirs), channel_id=1, source_target_pairs={{0,1},{1,0},{2,3},{3,2},{4,5},{5,4},{6,7},{7,6},{8,9},{9,8},{10,11... | collective-permute-start | bytes 786440 | tf_op jit(solution)/shard_map/ppermute | solution.py:484
  34.0 6.6 %collective-permute-start.9 = (bf16[544,128]{1,0:T(8,128)(2,1)S(1)}, bf16[544,128]{1,0:T(8,128)(2,1)S(1)}, u32[]{:S(2)}, u32[]{:S(2)}) collective-permute-start(bf16[544,128]{1,0:T(8,128)(2,1)S(1)} %get-tuple-element.76), channel_id=1, source_target_pairs={{0,8},{4,12},{8,4},{12,0},{1,9},{5,13},{9,5},{13,1},{2,10},{6,14},... | collective-permute-start | bytes 417800 | tf_op jit(solution)/shard_map/ppermute | solution.py:480
  40.5 0.0 collective-permute-start.11
  40.6 0.0 collective-permute-done.5.other
  40.6 1.3 %shard_map.93 = (bf16[4,2,256,512]{3,2,1,0:T(8,128)(2,1)}, bf16[4,4,2048]{2,1,0:T(4,128)(2,1)}) custom-call(bf16[4,2,32,128]{3,2,1,0:T(8,128)(2,1)S(1)} %get-tuple-element.44.query, bf16[4,2,2,16,128]{4,3,2,1,0:T(8,128)(2,1)S(1)} %get-tuple-element.45.new_kv, ...), custom_call_target="tpu_custom_call", output_to_operand_aliasing={{0}: (6, {}), {1}: (7, {})} | custom-call | flops 16777216 | bytes 1048576 | tf_op jit(solution)/shard_map/pallas_call | solution.py:448
  41.9 0.0 collective-permute-done.4.other
  41.9 1.3 %shard_map.94 = (bf16[4,2,256,512]{3,2,1,0:T(8,128)(2,1)}, bf16[4,4,2048]{2,1,0:T(4,128)(2,1)}) custom-call(bf16[4,2,32,128]{3,2,1,0:T(8,128)(2,1)S(1)} %get-tuple-element.44.query, bf16[4,2,2,16,128]{4,3,2,1,0:T(8,128)(2,1)S(1)} %get-tuple-element.45.new_kv, ...), custom_call_target="tpu_custom_call", output_to_operand_aliasing={{0}: (6, {}), {1}: (7, {})} | custom-call | flops 16777216 | bytes 1048576 | tf_op jit(solution)/shard_map/pallas_call | solution.py:448
  43.3 0.0 collective-permute-done.message.tables
  43.3 0.1 shard_map.95
  43.4 5.6 %collective-permute-start.6 = (bf16[256,128]{1,0:T(8,128)(2,1)S(1)}, bf16[256,128]{1,0:T(8,128)(2,1)S(1)}, u32[]{:S(2)}, u32[]{:S(2)}) collective-permute-start(bf16[256,128]{1,0:T(8,128)(2,1)S(1)} %get-tuple-element.68.refs_2_), channel_id=1, source_target_pairs={{0,1},{1,0},{2,3},{3,2},{4,5},{5,4},{6,7},{7,6},{8,9},{9,8},{10,11... | collective-permute-start | bytes 196616 | tf_op jit(solution)/shard_map/ppermute | solution.py:484
  49.0 0.1 collective-permute-start.7
  49.1 0.8 %collective-permute-done.6.refs_0_ = bf16[256,128]{1,0:T(8,128)(2,1)S(1)} collective-permute-done((bf16[256,128]{1,0:T(8,128)(2,1)S(1)}, bf16[256,128]{1,0:T(8,128)(2,1)S(1)}, u32[]{:S(2)}, u32[]{:S(2)}) %collective-permute-start.6) | collective-permute-done | bytes 65568 | tf_op jit(solution)/shard_map/ppermute | solution.py:484
  49.9 0.4 collective-permute-done.7.refs_1_
  50.2 1.3 %shard_map.96 = (bf16[4,2,256,512]{3,2,1,0:T(8,128)(2,1)}, bf16[4,4,2048]{2,1,0:T(4,128)(2,1)}, bf16[2,32,256]{2,1,0:T(8,128)(2,1)S(1)}, bf16[2,32,256]{2,1,0:T(...) custom-call(bf16[4,2,32,128]{3,2,1,0:T(8,128)(2,1)S(1)} %get-tuple-e, ...), custom_call_target="tpu_custom_call", output_to_operand_aliasing={{0}: (8, {}), {1}: (9, {})} | custom-call | flops 8388608 | bytes 1048576 | tf_op jit(solution)/shard_map/pallas_call | solution.py:448
  51.5 0.2 collective-permute-start.8
  51.7 0.0 collective-permute-done.9.message
  51.7 1.0 %collective-permute-done.8.lent = bf16[2,32,256]{2,1,0:T(8,128)(2,1)S(1)} collective-permute-done((bf16[2,32,256]{2,1,0:T(8,128)(2,1)S(1)}, bf16[2,32,256]{2,1,0:T(8,128)(2,1)S(1)}, u32[]{:S(2)}, u32[]{:S(2)}) %collective-permute-start.8) | collective-permute-done | bytes 32800 | tf_op jit(solution)/shard_map/ppermute | solution.py:484
  52.8 0.2 shard_map.97
  53.0 0.2 collective-permute-start.10
  53.2 0.7 %shard_map.98 = (bf16[4,2,256,512]{3,2,1,0:T(8,128)(2,1)}, bf16[4,4,2048]{2,1,0:T(4,128)(2,1)}) custom-call(bf16[512,128]{1,0:T(8,128)(2,1)S(1)} %get-tuple-element.81.theirs, bf16[4,2,256,512]{3,2,1,0:T(8,128)(2,1)} %get-tuple-element.82.refs_0_, bf16[4,4,2048]{2,1,0:T(4,128)(2,1)} %get-tuple-element.83.refs_1_), custom_call_target="tpu_custom_call", output_to_operand_aliasing={{0}: (1, {}), {1}: (2, {})} | custom-call | bytes 1048576 | tf_op jit(solution)/shard_map/pallas_call | solution.py:448
  53.9 0.0 collective-permute-done.11.message
  53.9 0.3 collective-permute-done.10.got
  54.2 0.9 %shard_map.99 = (bf16[4,2,256,512]{3,2,1,0:T(8,128)(2,1)}, bf16[4,4,2048]{2,1,0:T(4,128)(2,1)}) custom-call(bf16[2,32,256]{2,1,0:T(8,128)(2,1)S(1)} %get-tuple-element.72.weights, f32[2,32,128]{2,1,0:T(8,128)S(1)} %get-tuple-element.73.share, f32[2,32,128]{2,1,0:T(8,128)S(1)} %get-tuple-element.74.totals, ...), custom_call_target="tpu_custom_call", output_to_operand_aliasing={{0}: (6, {}), {1}: (7, {})} | custom-call | flops 4194304 | bytes 1048576 | tf_op jit(solution)/shard_map/pallas_call | solution.py:448
Async XLA Ops:
  2.5 15.6 %collective-permute-start.3 = (bf16[2192,128]{1,0:T(8,128)(2,1)S(1)}, bf16[2192,128]{1,0:T(8,128)(2,1)S(1)}, u32[]{:S(2)}, u32[]{:S(2)}) collective-permute-start(bf16[2192,128]{1,0:T(8,128)(2,1)S(1)} %shard_map.89), channel_id=1, source_target_pairs={{0,12},{4,8},{8,0},{12,4},{1,13},{5,9},{9,1},{13,5},{2,14},{6,10},... | collective-permute-start | bytes 1683464 | tf_op jit(solution)/shard_map/ppermute | solution.py:480
  4.9 28.3 %collective-permute-start.1 = (bf16[2192,128]{1,0:T(8,128)(2,1)S(1)}, bf16[2192,128]{1,0:T(8,128)(2,1)S(1)}, u32[]{:S(2)}, u32[]{:S(2)}) collective-permute-start(bf16[2192,128]{1,0:T(8,128)(2,1)S(1)} %get-tuple-element.47), channel_id=1, source_target_pairs={{0,4},{4,0},{8,12},{12,8},{1,5},{5,1},{9,13},{13,9},{2,6},{6,2},{1... | collective-permute-start | bytes 1683464 | tf_op jit(solution)/shard_map/ppermute | solution.py:480
  5.3 15.6 %collective-permute-start.2 = (bf16[1024,128]{1,0:T(8,128)(2,1)S(1)}, bf16[1024,128]{1,0:T(8,128)(2,1)S(1)}, u32[]{:S(2)}, u32[]{:S(2)}) collective-permute-start(bf16[1024,128]{1,0:T(8,128)(2,1)S(1)} %get-tuple-element.50.theirs), channel_id=1, source_target_pairs={{0,1},{1,0},{2,3},{3,2},{4,5},{5,4},{6,7},{7,6},{8,9},{9,8},{10,11... | collective-permute-start | bytes 786440 | tf_op jit(solution)/shard_map/ppermute | solution.py:484
  6.6 36.6 %collective-permute-start = (bf16[1104,128]{1,0:T(8,128)(2,1)S(1)}, bf16[1104,128]{1,0:T(8,128)(2,1)S(1)}, u32[]{:S(2)}, u32[]{:S(2)}) collective-permute-start(bf16[1104,128]{1,0:T(8,128)(2,1)S(1)} %get-tuple-element.46), channel_id=1, source_target_pairs={{0,8},{4,12},{8,4},{12,0},{1,9},{5,13},{9,5},{13,1},{2,10},{6,14},... | collective-permute-start | bytes 847880 | tf_op jit(solution)/shard_map/ppermute | solution.py:480
  18.3 22.3 %collective-permute-start.5 = (bf16[1024,128]{1,0:T(8,128)(2,1)S(1)}, bf16[1024,128]{1,0:T(8,128)(2,1)S(1)}, u32[]{:S(2)}, u32[]{:S(2)}) collective-permute-start(bf16[1024,128]{1,0:T(8,128)(2,1)S(1)} %get-tuple-element.60.theirs), channel_id=1, source_target_pairs={{0,1},{1,0},{2,3},{3,2},{4,5},{5,4},{6,7},{7,6},{8,9},{9,8},{10,11... | collective-permute-start | bytes 786440 | tf_op jit(solution)/shard_map/ppermute | solution.py:484
  33.4 8.5 %collective-permute-start.4 = (bf16[1024,128]{1,0:T(8,128)(2,1)S(1)}, bf16[1024,128]{1,0:T(8,128)(2,1)S(1)}, u32[]{:S(2)}, u32[]{:S(2)}) collective-permute-start(bf16[1024,128]{1,0:T(8,128)(2,1)S(1)} %get-tuple-element.58.theirs), channel_id=1, source_target_pairs={{0,1},{1,0},{2,3},{3,2},{4,5},{5,4},{6,7},{7,6},{8,9},{9,8},{10,11... | collective-permute-start | bytes 786440 | tf_op jit(solution)/shard_map/ppermute | solution.py:484
  34.0 17.8 %collective-permute-start.9 = (bf16[544,128]{1,0:T(8,128)(2,1)S(1)}, bf16[544,128]{1,0:T(8,128)(2,1)S(1)}, u32[]{:S(2)}, u32[]{:S(2)}) collective-permute-start(bf16[544,128]{1,0:T(8,128)(2,1)S(1)} %get-tuple-element.76), channel_id=1, source_target_pairs={{0,8},{4,12},{8,4},{12,0},{1,9},{5,13},{9,5},{13,1},{2,10},{6,14},... | collective-permute-start | bytes 417800 | tf_op jit(solution)/shard_map/ppermute | solution.py:480
  40.5 13.4 %collective-permute-start.11 = (bf16[544,128]{1,0:T(8,128)(2,1)S(1)}, bf16[544,128]{1,0:T(8,128)(2,1)S(1)}, u32[]{:S(2)}, u32[]{:S(2)}) collective-permute-start(bf16[544,128]{1,0:T(8,128)(2,1)S(1)} %get-tuple-element.80), channel_id=1, source_target_pairs={{0,8},{4,12},{8,4},{12,0},{1,9},{5,13},{9,5},{13,1},{2,10},{6,14},... | collective-permute-start | bytes 417800 | tf_op jit(solution)/shard_map/ppermute | solution.py:480
  43.4 6.5 %collective-permute-start.6 = (bf16[256,128]{1,0:T(8,128)(2,1)S(1)}, bf16[256,128]{1,0:T(8,128)(2,1)S(1)}, u32[]{:S(2)}, u32[]{:S(2)}) collective-permute-start(bf16[256,128]{1,0:T(8,128)(2,1)S(1)} %get-tuple-element.68.refs_2_), channel_id=1, source_target_pairs={{0,1},{1,0},{2,3},{3,2},{4,5},{5,4},{6,7},{7,6},{8,9},{9,8},{10,11... | collective-permute-start | bytes 196616 | tf_op jit(solution)/shard_map/ppermute | solution.py:484
  49.0 1.3 %collective-permute-start.7 = (bf16[256,128]{1,0:T(8,128)(2,1)S(1)}, bf16[256,128]{1,0:T(8,128)(2,1)S(1)}, u32[]{:S(2)}, u32[]{:S(2)}) collective-permute-start(bf16[256,128]{1,0:T(8,128)(2,1)S(1)} %get-tuple-element.69.refs_3_), channel_id=1, source_target_pairs={{0,1},{1,0},{2,3},{3,2},{4,5},{5,4},{6,7},{7,6},{8,9},{9,8},{10,11... | collective-permute-start | bytes 196616 | tf_op jit(solution)/shard_map/ppermute | solution.py:484
  51.5 1.3 %collective-permute-start.8 = (bf16[2,32,256]{2,1,0:T(8,128)(2,1)S(1)}, bf16[2,32,256]{2,1,0:T(8,128)(2,1)S(1)}, u32[]{:S(2)}, u32[]{:S(2)}) collective-permute-start(bf16[2,32,256]{2,1,0:T(8,128)(2,1)S(1)} %get-tuple-element.75), channel_id=1, source_target_pairs={{0,1},{1,0},{2,3},{3,2},{4,5},{5,4},{6,7},{7,6},{8,9},{9,8},{10,11... | collective-permute-start | bytes 98312 | tf_op jit(solution)/shard_map/ppermute | solution.py:484
  53.0 1.2 %collective-permute-start.10 = (f32[2,32,128]{2,1,0:T(8,128)S(1)}, f32[2,32,128]{2,1,0:T(8,128)S(1)}, u32[]{:S(2)}, u32[]{:S(2)}) collective-permute-start(f32[2,32,128]{2,1,0:T(8,128)S(1)} %get-tuple-element.79), channel_id=1, source_target_pairs={{0,1},{1,0},{2,3},{3,2},{4,5},{5,4},{6,7},{7,6},{8,9},{9,8},{10,11... | collective-permute-start | bytes 98312 | tf_op jit(solution)/shard_map/ppermute | solution.py:484

commit v15 on v14

--- a/solution.py
+++ b/solution.py
@@ -55,6 +55,7 @@
         self.group = self.q_local // self.mine
         self.wide = self.group * self.steps
         self.rest = self.heads - self.mine
+        self.last = 1
 
     def anchor_at(self, which, parts):
         return (len(parts) * self.span + parts.index(which) * self.rows) * self.heads
@@ -65,8 +66,8 @@
     def message_rows(self, parts):
         return self.side_at(parts) + (TILE if 0 in parts else 0)
 
-    def halved(self, parts):
-        return parts == (1,) and self.rest > 0
+    def halved(self, k, parts):
+        return k == self.last and parts == (1,) and self.rest > 0
 
     def half_rows(self):
         return self.mine * (self.span + self.rows)
@@ -92,7 +93,7 @@
     sub = lax.axis_index("sub")
     outs, work = list(outs), []
     for k, parts in plan:
-        msgs = [outs.pop(0) for _ in range(1 + size.halved(parts))]
+        msgs = [outs.pop(0) for _ in range(1 + size.halved(k, parts))]
         dest = pick(far(size.n, k), z)
         index = jnp.int32(0)
         for j in range(size.count):
@@ -136,8 +137,8 @@
 
 def pack(size, plan, route, lengths, deltas, anchors, scale):
     shapes = []
-    for _, parts in plan:
-        rows = [size.half_rows()] * 2 if size.halved(parts) else [size.message_rows(parts)]
+    for k, parts in plan:
+        rows = [size.half_rows()] * 2 if size.halved(k, parts) else [size.message_rows(parts)]
         shapes += [pltpu.VMEM((r, HEAD_DIM), BF) for r in rows]
     slots = sum(len(parts) for _, parts in plan)
     return pl.pallas_call(
@@ -263,23 +264,29 @@
                     target[to + i * size.repeat:to + (i + 1) * size.repeat, :] = value
 
 
-def rebuild_kernel(size, parts, chained, split, message, *refs):
-    mine, *theirs = refs[2 * chained + 2:]
-    rebuild_heads(size, parts, message, message, mine, tuple(theirs) if split else theirs[0])
-
-
-def rebuild(size, parts, message, state, split=False):
-    args = [vmem(message)]
-    in_specs = [IN_VMEM]
+def rebuild_kernel(size, parts, chained, split, pair, message, *refs):
+    mine, *theirs = refs[pair + 2 * chained + 2:]
+    if pair:
+        half = size.mine * size.span
+        for which, source in enumerate((message, refs[0])):
+            rows = pl.ds(which * half, half)
+            rebuild_heads(size, (which,), source, message, mine.at[rows], theirs[0].at[rows])
+    else:
+        rebuild_heads(size, parts, message, message, mine, tuple(theirs) if split else theirs[0])
+
+
+def rebuild(size, parts, messages, state, split=False):
+    args = [vmem(x) for x in messages]
+    in_specs = [IN_VMEM] * len(args)
     aliases = {}
     if state is not None:
-        aliases = {1: 0, 2: 1}
+        aliases = {len(args): 0, len(args) + 1: 1}
         args += list(state)
         in_specs += [IN_HBM, IN_HBM]
     given = (len(parts) * size.mine * size.span, HEAD_DIM)
     many, one = (size.mine, (size.span, HEAD_DIM)) if split else (1, given)
     out = pl.pallas_call(
-        functools.partial(rebuild_kernel, size, parts, state is not None, split),
+        functools.partial(rebuild_kernel, size, parts, state is not None, split, len(messages) - 1),
         in_specs=in_specs,
         out_specs=[IN_HBM, IN_HBM, IN_VMEM] + [IN_VMEM] * many,
         out_shape=[
@@ -348,11 +355,11 @@
     copy.wait()
 
 
-def attend_kernel(size, k, query, new_kv, tables, mine, other, theirs, *refs):
+def attend_kernel(size, k, parts, query, new_kv, tables, mine, other, theirs, *refs):
     cache, attended, made, flat, sem, sems = refs[2:]
     row = size.source_row(k)
     copies = start_store(size, k, (0, 1), cache, mine, theirs, sems)
-    live_mine, live_other, causal = masks(size, tables, (0, 1), new_kv.shape[3])
+    live_mine, live_other, causal = masks(size, tables, parts, new_kv.shape[3])
     for j in range(size.mine):
         keys = slice(j * size.span, (j + 1) * size.span)
         values = slice((size.mine + j) * size.span, (size.mine + j + 1) * size.span)
@@ -468,17 +475,18 @@
     both = (0, 1)
     order = list(range(n - 1, 0, -1))
     last = order[-1]
-    plan = [(k, both) for k in order[:-1]] + [(last, (0,)), (last, (1,)), (0, both)]
+    plan = [(order[0], (1,)), (order[0], (0,))]
+    plan += [(k, (p,)) for k in order[1:] for p in both] + [(0, both)]
     query, fresh = arrange(size, new_query, new_kv)
     message = {}
     for part in (plan[:1], plan[1:]):
         msgs = list(pack(size, part, route, lengths, deltas, anchors, chan_scale))
         for k, parts in part:
-            for half in range(1 + size.halved(parts)):
+            for half in range(1 + size.halved(k, parts)):
                 msg = msgs.pop(0)
                 if k:
                     msg = lax.ppermute(msg, "pool", list(enumerate(far(n, k))))
-                message[(k, parts, half) if size.halved(parts) else (k, parts)] = msg
+                message[(k, parts, half) if size.halved(k, parts) else (k, parts)] = msg
 
     def swapped(x):
         return lax.ppermute(x, "sub", [(0, 1), (1, 0)])
@@ -494,13 +502,16 @@
 
     def attend(k, mine, other, theirs, state):
         state, _ = chained_call(
-            size, functools.partial(attend_kernel, size, k),
-            (query, fresh, message[k, both], mine, other, theirs), state, [], rows + [sems], flops,
+            size, functools.partial(attend_kernel, size, k, both if (k, both) in message else (0,)),
+            (query, fresh, messages_of(k)[0], mine, other, theirs), state, [], rows + [sems], flops,
         )
         return state
 
+    def messages_of(k):
+        return [message[k, p] for p in ([both] if (k, both) in message else [(0,), (1,)])]
+
     def take(k, parts, state):
-        state, mine, theirs = rebuild(size, parts, message[k, parts], state)
+        state, mine, theirs = rebuild(size, parts, messages_of(k), state)
         return state, mine, swapped(theirs), theirs
 
     state, held = None, []
@@ -512,7 +523,7 @@
     state = attend(*held.pop(0), state)
     split = size.rest > 0
     tables = message[last, (0,)]
-    state, mine, theirs = rebuild(size, (0,), tables, state, split)
+    state, mine, theirs = rebuild(size, (0,), [tables], state, split)
     theirs = theirs if split else (theirs,)
     half = pltpu.VMEM((size.mine, size.wide, size.span), BF)
     state, (weights, lent, share, totals) = chained_call(

time: 55.4 us -> 55.3 us (level)
  waiting for transfers between devices: 21.2 us -> 8.81 us
  starting transfers between devices: 20.3 us -> 32.6 us
    ppermute x5 -> x7, waiting for transfers between devices: 18.6 us -> 6.27 us  [body(): msg = lax.ppermute(msg, 'pool', list(enumerate(far(n, k))))]
    ppermute x5 -> x7, starting transfers between devices: 9.73 us -> 21.5 us  [body(): msg = lax.ppermute(msg, 'pool', list(enumerate(far(n, k))))]
  transfers between devices with their start and end apart: 12 -> 14, of which waited for: 6 -> 6; matrix products, arithmetic and copies ran while one was open for 0% -> 0% of each run, Pallas kernels for 18% -> 19%
where the time goes in v15:
time: 55.3 us; the launch traced here: 55 us
  starting transfers between devices  32.6 us (59%)
  Pallas kernels  12.9 us (23%)
  waiting for transfers between devices  8.81 us (16%)
  between operations  0.74 us (1%)
    ppermute x7, starting transfers between devices, body(): msg = lax.ppermute(msg, 'pool', list(enumerate(far(n, k))))  21.5 us
    ppermute x7, starting transfers between devices, swapped(): return lax.ppermute(x, 'sub', [(0, 1), (1, 0)])  11.1 us
    pallas_call x7, Pallas kernels, chained_call(): pl.pallas_call(kernel, in_specs=[IN_VMEM] * many + [IN_HBM, IN_HBM], out_...  7.1 us
    ppermute x7, waiting for transfers between devices, body(): msg = lax.ppermute(msg, 'pool', list(enumerate(far(n, k))))  6.27 us
    pallas_call x2, Pallas kernels, pack(): pl.pallas_call(functools.partial(pack_kernel, size, plan), out_shape=shap...  4.14 us
    ppermute x7, waiting for transfers between devices, swapped(): return lax.ppermute(x, 'sub', [(0, 1), (1, 0)])  2.54 us
  transfers between devices with their start and end apart: 14, of which 6 were waited for; matrix products, arithmetic and copies ran while one was open for 0% of the time, Pallas kernels for 19%

profile of v15, /device:TPU:31, one launch (start us, length us, event | category | flops | bytes accessed | tf_op | source)
XLA Modules:
  0.0 55.0 jit_solution(442222598046519521)
XLA Ops:
  0.6 1.7 %shard_map.89 = bf16[1088,128]{1,0:T(8,128)(2,1)S(1)} custom-call(s32[4]{0:T(128)} %route.3, s32[4]{0:T(128)} %lengths.3, bf16[4,2,256,512]{3,2,1,0:T(8,128)(2,1)} %deltas.3, bf16[4,2,16,512]{3,2,1,0:T(8,128)(2,1)} %anchors.3, bf16[4,2,512]{2,1,0:T(2,128)(2,1)} %scale.3), custom_call_target="tpu_custom_call" | custom-call | bytes 262144 | tf_op jit(solution)/shard_map/pallas_call | solution.py:144
  2.4 0.1 collective-permute-start.5
  2.5 2.4 %shard_map.87 = (bf16[1104,128]{1,0:T(8,128)(2,1)S(1)}, bf16[1104,128]{1,0:T(8,128)(2,1)S(1)}, bf16[1088,128]{1,0:T(8,128)(2,1)S(1)}, bf16[1104,128]{1,0:T(8,128...) custom-call(s32[4]{0:T(128)} %route.3, s32[4]{0:T(128)} %lengths.3, ...), custom_call_target="tpu_custom_call" | custom-call | bytes 1835008 | tf_op jit(solution)/shard_map/pallas_call | solution.py:144
  4.9 1.4 %collective-permute-start.4 = (bf16[1104,128]{1,0:T(8,128)(2,1)S(1)}, bf16[1104,128]{1,0:T(8,128)(2,1)S(1)}, u32[]{:S(2)}, u32[]{:S(2)}) collective-permute-start(bf16[1104,128]{1,0:T(8,128)(2,1)S(1)} %get-tuple-element.54), channel_id=1, source_target_pairs={{0,12},{4,8},{8,0},{12,4},{1,13},{5,9},{9,1},{13,5},{2,14},{6,10},... | collective-permute-start | bytes 847880 | tf_op jit(solution)/shard_map/ppermute | solution.py:488
  6.2 2.2 %collective-permute-start.1 = (bf16[1104,128]{1,0:T(8,128)(2,1)S(1)}, bf16[1104,128]{1,0:T(8,128)(2,1)S(1)}, u32[]{:S(2)}, u32[]{:S(2)}) collective-permute-start(bf16[1104,128]{1,0:T(8,128)(2,1)S(1)} %get-tuple-element.49), channel_id=1, source_target_pairs={{0,4},{4,0},{8,12},{12,8},{1,5},{5,1},{9,13},{13,9},{2,6},{6,2},{1... | collective-permute-start | bytes 847880 | tf_op jit(solution)/shard_map/ppermute | solution.py:488
  8.4 0.0 collective-permute-start.2
  8.5 0.2 shard_map.88
  8.7 1.6 %collective-permute-start.3 = (bf16[1024,128]{1,0:T(8,128)(2,1)S(1)}, bf16[1024,128]{1,0:T(8,128)(2,1)S(1)}, u32[]{:S(2)}, u32[]{:S(2)}) collective-permute-start(bf16[1024,128]{1,0:T(8,128)(2,1)S(1)} %get-tuple-element.53.theirs), channel_id=1, source_target_pairs={{0,1},{1,0},{2,3},{3,2},{4,5},{5,4},{6,7},{7,6},{8,9},{9,8},{10,11... | collective-permute-start | bytes 786440 | tf_op jit(solution)/shard_map/ppermute | solution.py:492
  10.2 1.6 %collective-permute-done.5.refs_0_ = bf16[1088,128]{1,0:T(8,128)(2,1)S(1)} collective-permute-done((bf16[1088,128]{1,0:T(8,128)(2,1)S(1)}, bf16[1088,128]{1,0:T(8,128)(2,1)S(1)}, u32[]{:S(2)}, u32[]{:S(2)}) %collective-permute-start.5) | collective-permute-done | bytes 278560 | tf_op jit(solution)/shard_map/ppermute | solution.py:488
  11.8 11.0 %collective-permute-start = (bf16[1104,128]{1,0:T(8,128)(2,1)S(1)}, bf16[1104,128]{1,0:T(8,128)(2,1)S(1)}, u32[]{:S(2)}, u32[]{:S(2)}) collective-permute-start(bf16[1104,128]{1,0:T(8,128)(2,1)S(1)} %get-tuple-element.48), channel_id=1, source_target_pairs={{0,8},{4,12},{8,4},{12,0},{1,9},{5,13},{9,5},{13,1},{2,10},{6,14},... | collective-permute-start | bytes 847880 | tf_op jit(solution)/shard_map/ppermute | solution.py:488
  22.9 0.9 %shard_map.86 = (bf16[4,2,32,128]{3,2,1,0:T(8,128)(2,1)S(1)}, bf16[4,2,2,16,128]{4,3,2,1,0:T(8,128)(2,1)S(1)}) custom-call(bf16[4,4,2048]{2,1,0:T(4,128)(2,1)} %new_query.1, bf16[4,2,4,512]{3,2,1,0:T(4,128)(2,1)} %new_kv.1), custom_call_target="tpu_custom_call" | custom-call | tf_op jit(solution)/shard_map/pallas_call | solution.py:181
  23.8 0.0 collective-permute-done.4.message.tables
  23.8 0.2 shard_map.90
  24.0 3.1 %collective-permute-start.7 = (bf16[1024,128]{1,0:T(8,128)(2,1)S(1)}, bf16[1024,128]{1,0:T(8,128)(2,1)S(1)}, u32[]{:S(2)}, u32[]{:S(2)}) collective-permute-start(bf16[1024,128]{1,0:T(8,128)(2,1)S(1)} %get-tuple-element.64.theirs), channel_id=1, source_target_pairs={{0,1},{1,0},{2,3},{3,2},{4,5},{5,4},{6,7},{7,6},{8,9},{9,8},{10,11... | collective-permute-start | bytes 786440 | tf_op jit(solution)/shard_map/ppermute | solution.py:492
  27.1 0.0 collective-permute-done.3.other
  27.1 1.3 %shard_map.91 = (bf16[4,2,256,512]{3,2,1,0:T(8,128)(2,1)}, bf16[4,4,2048]{2,1,0:T(4,128)(2,1)}) custom-call(bf16[4,2,32,128]{3,2,1,0:T(8,128)(2,1)S(1)} %get-tuple-element.46.query, bf16[4,2,2,16,128]{4,3,2,1,0:T(8,128)(2,1)S(1)} %get-tuple-element.47.new_kv, ...), custom_call_target="tpu_custom_call", output_to_operand_aliasing={{0}: (6, {}), {1}: (7, {})} | custom-call | flops 16777216 | bytes 1048576 | tf_op jit(solution)/shard_map/pallas_call | solution.py:455
  28.4 4.7 %collective-permute-done.2.refs_0_ = bf16[1088,128]{1,0:T(8,128)(2,1)S(1)} collective-permute-done((bf16[1088,128]{1,0:T(8,128)(2,1)S(1)}, bf16[1088,128]{1,0:T(8,128)(2,1)S(1)}, u32[]{:S(2)}, u32[]{:S(2)}) %collective-permute-start.2) | collective-permute-done | bytes 278560 | tf_op jit(solution)/shard_map/ppermute | solution.py:488
  33.1 0.0 collective-permute-done.1.message.tables
  33.1 0.2 shard_map.92
  33.3 0.6 %collective-permute-start.6 = (bf16[1024,128]{1,0:T(8,128)(2,1)S(1)}, bf16[1024,128]{1,0:T(8,128)(2,1)S(1)}, u32[]{:S(2)}, u32[]{:S(2)}) collective-permute-start(bf16[1024,128]{1,0:T(8,128)(2,1)S(1)} %get-tuple-element.62.theirs), channel_id=1, source_target_pairs={{0,1},{1,0},{2,3},{3,2},{4,5},{5,4},{6,7},{7,6},{8,9},{9,8},{10,11... | collective-permute-start | bytes 786440 | tf_op jit(solution)/shard_map/ppermute | solution.py:492
  33.9 6.7 %collective-permute-start.11 = (bf16[544,128]{1,0:T(8,128)(2,1)S(1)}, bf16[544,128]{1,0:T(8,128)(2,1)S(1)}, u32[]{:S(2)}, u32[]{:S(2)}) collective-permute-start(bf16[544,128]{1,0:T(8,128)(2,1)S(1)} %get-tuple-element.80), channel_id=1, source_target_pairs={{0,8},{4,12},{8,4},{12,0},{1,9},{5,13},{9,5},{13,1},{2,10},{6,14},... | collective-permute-start | bytes 417800 | tf_op jit(solution)/shard_map/ppermute | solution.py:488
  40.6 0.0 collective-permute-start.13
  40.6 0.0 collective-permute-done.7.other
  40.6 1.3 %shard_map.93 = (bf16[4,2,256,512]{3,2,1,0:T(8,128)(2,1)}, bf16[4,4,2048]{2,1,0:T(4,128)(2,1)}) custom-call(bf16[4,2,32,128]{3,2,1,0:T(8,128)(2,1)S(1)} %get-tuple-element.46.query, bf16[4,2,2,16,128]{4,3,2,1,0:T(8,128)(2,1)S(1)} %get-tuple-element.47.new_kv, ...), custom_call_target="tpu_custom_call", output_to_operand_aliasing={{0}: (6, {}), {1}: (7, {})} | custom-call | flops 16777216 | bytes 1048576 | tf_op jit(solution)/shard_map/pallas_call | solution.py:455
  42.0 0.0 collective-permute-done.6.other
  42.0 1.3 %shard_map.94 = (bf16[4,2,256,512]{3,2,1,0:T(8,128)(2,1)}, bf16[4,4,2048]{2,1,0:T(4,128)(2,1)}) custom-call(bf16[4,2,32,128]{3,2,1,0:T(8,128)(2,1)S(1)} %get-tuple-element.46.query, bf16[4,2,2,16,128]{4,3,2,1,0:T(8,128)(2,1)S(1)} %get-tuple-element.47.new_kv, ...), custom_call_target="tpu_custom_call", output_to_operand_aliasing={{0}: (6, {}), {1}: (7, {})} | custom-call | flops 16777216 | bytes 1048576 | tf_op jit(solution)/shard_map/pallas_call | solution.py:455
  43.3 0.0 collective-permute-done.message.tables
  43.3 0.1 shard_map.95
  43.5 5.4 %collective-permute-start.8 = (bf16[256,128]{1,0:T(8,128)(2,1)S(1)}, bf16[256,128]{1,0:T(8,128)(2,1)S(1)}, u32[]{:S(2)}, u32[]{:S(2)}) collective-permute-start(bf16[256,128]{1,0:T(8,128)(2,1)S(1)} %get-tuple-element.72.refs_2_), channel_id=1, source_target_pairs={{0,1},{1,0},{2,3},{3,2},{4,5},{5,4},{6,7},{7,6},{8,9},{9,8},{10,11... | collective-permute-start | bytes 196616 | tf_op jit(solution)/shard_map/ppermute | solution.py:492
  48.9 0.1 collective-permute-start.9
  49.0 0.8 %collective-permute-done.8.refs_0_ = bf16[256,128]{1,0:T(8,128)(2,1)S(1)} collective-permute-done((bf16[256,128]{1,0:T(8,128)(2,1)S(1)}, bf16[256,128]{1,0:T(8,128)(2,1)S(1)}, u32[]{:S(2)}, u32[]{:S(2)}) %collective-permute-start.8) | collective-permute-done | bytes 65568 | tf_op jit(solution)/shard_map/ppermute | solution.py:492
  49.8 0.4 collective-permute-done.9.refs_1_
  50.1 1.3 %shard_map.96 = (bf16[4,2,256,512]{3,2,1,0:T(8,128)(2,1)}, bf16[4,4,2048]{2,1,0:T(4,128)(2,1)}, bf16[2,32,256]{2,1,0:T(8,128)(2,1)S(1)}, bf16[2,32,256]{2,1,0:T(...) custom-call(bf16[4,2,32,128]{3,2,1,0:T(8,128)(2,1)S(1)} %get-tuple-e, ...), custom_call_target="tpu_custom_call", output_to_operand_aliasing={{0}: (8, {}), {1}: (9, {})} | custom-call | flops 8388608 | bytes 1048576 | tf_op jit(solution)/shard_map/pallas_call | solution.py:455
  51.4 0.2 collective-permute-start.10
  51.6 0.0 collective-permute-done.11.message
  51.6 1.0 %collective-permute-done.10.lent = bf16[2,32,256]{2,1,0:T(8,128)(2,1)S(1)} collective-permute-done((bf16[2,32,256]{2,1,0:T(8,128)(2,1)S(1)}, bf16[2,32,256]{2,1,0:T(8,128)(2,1)S(1)}, u32[]{:S(2)}, u32[]{:S(2)}) %collective-permute-start.10) | collective-permute-done | bytes 32800 | tf_op jit(solution)/shard_map/ppermute | solution.py:492
  52.7 0.2 shard_map.97
  52.9 0.2 collective-permute-start.12
  53.1 0.7 %shard_map.98 = (bf16[4,2,256,512]{3,2,1,0:T(8,128)(2,1)}, bf16[4,4,2048]{2,1,0:T(4,128)(2,1)}) custom-call(bf16[512,128]{1,0:T(8,128)(2,1)S(1)} %get-tuple-element.85.theirs, bf16[4,2,256,512]{3,2,1,0:T(8,128)(2,1)} %get-tuple-element.86.refs_0_, bf16[4,4,2048]{2,1,0:T(4,128)(2,1)} %get-tuple-element.87.refs_1_), custom_call_target="tpu_custom_call", output_to_operand_aliasing={{0}: (1, {}), {1}: (2, {})} | custom-call | bytes 1048576 | tf_op jit(solution)/shard_map/pallas_call | solution.py:455
  53.8 0.0 collective-permute-done.13.message
  53.8 0.3 collective-permute-done.12.got
  54.1 0.9 %shard_map.99 = (bf16[4,2,256,512]{3,2,1,0:T(8,128)(2,1)}, bf16[4,4,2048]{2,1,0:T(4,128)(2,1)}) custom-call(bf16[2,32,256]{2,1,0:T(8,128)(2,1)S(1)} %get-tuple-element.76.weights, f32[2,32,128]{2,1,0:T(8,128)S(1)} %get-tuple-element.77.share, f32[2,32,128]{2,1,0:T(8,128)S(1)} %get-tuple-element.78.totals, ...), custom_call_target="tpu_custom_call", output_to_operand_aliasing={{0}: (6, {}), {1}: (7, {})} | custom-call | flops 4194304 | bytes 1048576 | tf_op jit(solution)/shard_map/pallas_call | solution.py:455
Async XLA Ops:
  2.4 9.5 %collective-permute-start.5 = (bf16[1088,128]{1,0:T(8,128)(2,1)S(1)}, bf16[1088,128]{1,0:T(8,128)(2,1)S(1)}, u32[]{:S(2)}, u32[]{:S(2)}) collective-permute-start(bf16[1088,128]{1,0:T(8,128)(2,1)S(1)} %shard_map.89), channel_id=1, source_target_pairs={{0,12},{4,8},{8,0},{12,4},{1,13},{5,9},{9,1},{13,5},{2,14},{6,10},... | collective-permute-start | bytes 835592 | tf_op jit(solution)/shard_map/ppermute | solution.py:488
  4.9 18.9 %collective-permute-start.4 = (bf16[1104,128]{1,0:T(8,128)(2,1)S(1)}, bf16[1104,128]{1,0:T(8,128)(2,1)S(1)}, u32[]{:S(2)}, u32[]{:S(2)}) collective-permute-start(bf16[1104,128]{1,0:T(8,128)(2,1)S(1)} %get-tuple-element.54), channel_id=1, source_target_pairs={{0,12},{4,8},{8,0},{12,4},{1,13},{5,9},{9,1},{13,5},{2,14},{6,10},... | collective-permute-start | bytes 847880 | tf_op jit(solution)/shard_map/ppermute | solution.py:488
  6.2 26.9 %collective-permute-start.1 = (bf16[1104,128]{1,0:T(8,128)(2,1)S(1)}, bf16[1104,128]{1,0:T(8,128)(2,1)S(1)}, u32[]{:S(2)}, u32[]{:S(2)}) collective-permute-start(bf16[1104,128]{1,0:T(8,128)(2,1)S(1)} %get-tuple-element.49), channel_id=1, source_target_pairs={{0,4},{4,0},{8,12},{12,8},{1,5},{5,1},{9,13},{13,9},{2,6},{6,2},{1... | collective-permute-start | bytes 847880 | tf_op jit(solution)/shard_map/ppermute | solution.py:488
  8.4 24.7 %collective-permute-start.2 = (bf16[1088,128]{1,0:T(8,128)(2,1)S(1)}, bf16[1088,128]{1,0:T(8,128)(2,1)S(1)}, u32[]{:S(2)}, u32[]{:S(2)}) collective-permute-start(bf16[1088,128]{1,0:T(8,128)(2,1)S(1)} %get-tuple-element.50), channel_id=1, source_target_pairs={{0,4},{4,0},{8,12},{12,8},{1,5},{5,1},{9,13},{13,9},{2,6},{6,2},{1... | collective-permute-start | bytes 835592 | tf_op jit(solution)/shard_map/ppermute | solution.py:488
  8.7 18.4 %collective-permute-start.3 = (bf16[1024,128]{1,0:T(8,128)(2,1)S(1)}, bf16[1024,128]{1,0:T(8,128)(2,1)S(1)}, u32[]{:S(2)}, u32[]{:S(2)}) collective-permute-start(bf16[1024,128]{1,0:T(8,128)(2,1)S(1)} %get-tuple-element.53.theirs), channel_id=1, source_target_pairs={{0,1},{1,0},{2,3},{3,2},{4,5},{5,4},{6,7},{7,6},{8,9},{9,8},{10,11... | collective-permute-start | bytes 786440 | tf_op jit(solution)/shard_map/ppermute | solution.py:492
  11.8 31.5 %collective-permute-start = (bf16[1104,128]{1,0:T(8,128)(2,1)S(1)}, bf16[1104,128]{1,0:T(8,128)(2,1)S(1)}, u32[]{:S(2)}, u32[]{:S(2)}) collective-permute-start(bf16[1104,128]{1,0:T(8,128)(2,1)S(1)} %get-tuple-element.48), channel_id=1, source_target_pairs={{0,8},{4,12},{8,4},{12,0},{1,9},{5,13},{9,5},{13,1},{2,10},{6,14},... | collective-permute-start | bytes 847880 | tf_op jit(solution)/shard_map/ppermute | solution.py:488
  24.0 16.6 %collective-permute-start.7 = (bf16[1024,128]{1,0:T(8,128)(2,1)S(1)}, bf16[1024,128]{1,0:T(8,128)(2,1)S(1)}, u32[]{:S(2)}, u32[]{:S(2)}) collective-permute-start(bf16[1024,128]{1,0:T(8,128)(2,1)S(1)} %get-tuple-element.64.theirs), channel_id=1, source_target_pairs={{0,1},{1,0},{2,3},{3,2},{4,5},{5,4},{6,7},{7,6},{8,9},{9,8},{10,11... | collective-permute-start | bytes 786440 | tf_op jit(solution)/shard_map/ppermute | solution.py:492
  33.3 8.7 %collective-permute-start.6 = (bf16[1024,128]{1,0:T(8,128)(2,1)S(1)}, bf16[1024,128]{1,0:T(8,128)(2,1)S(1)}, u32[]{:S(2)}, u32[]{:S(2)}) collective-permute-start(bf16[1024,128]{1,0:T(8,128)(2,1)S(1)} %get-tuple-element.62.theirs), channel_id=1, source_target_pairs={{0,1},{1,0},{2,3},{3,2},{4,5},{5,4},{6,7},{7,6},{8,9},{9,8},{10,11... | collective-permute-start | bytes 786440 | tf_op jit(solution)/shard_map/ppermute | solution.py:492
  33.9 17.8 %collective-permute-start.11 = (bf16[544,128]{1,0:T(8,128)(2,1)S(1)}, bf16[544,128]{1,0:T(8,128)(2,1)S(1)}, u32[]{:S(2)}, u32[]{:S(2)}) collective-permute-start(bf16[544,128]{1,0:T(8,128)(2,1)S(1)} %get-tuple-element.80), channel_id=1, source_target_pairs={{0,8},{4,12},{8,4},{12,0},{1,9},{5,13},{9,5},{13,1},{2,10},{6,14},... | collective-permute-start | bytes 417800 | tf_op jit(solution)/shard_map/ppermute | solution.py:488
  40.6 13.2 %collective-permute-start.13 = (bf16[544,128]{1,0:T(8,128)(2,1)S(1)}, bf16[544,128]{1,0:T(8,128)(2,1)S(1)}, u32[]{:S(2)}, u32[]{:S(2)}) collective-permute-start(bf16[544,128]{1,0:T(8,128)(2,1)S(1)} %get-tuple-element.84), channel_id=1, source_target_pairs={{0,8},{4,12},{8,4},{12,0},{1,9},{5,13},{9,5},{13,1},{2,10},{6,14},... | collective-permute-start | bytes 417800 | tf_op jit(solution)/shard_map/ppermute | solution.py:488
  43.5 6.3 %collective-permute-start.8 = (bf16[256,128]{1,0:T(8,128)(2,1)S(1)}, bf16[256,128]{1,0:T(8,128)(2,1)S(1)}, u32[]{:S(2)}, u32[]{:S(2)}) collective-permute-start(bf16[256,128]{1,0:T(8,128)(2,1)S(1)} %get-tuple-element.72.refs_2_), channel_id=1, source_target_pairs={{0,1},{1,0},{2,3},{3,2},{4,5},{5,4},{6,7},{7,6},{8,9},{9,8},{10,11... | collective-permute-start | bytes 196616 | tf_op jit(solution)/shard_map/ppermute | solution.py:492
  48.9 1.3 %collective-permute-start.9 = (bf16[256,128]{1,0:T(8,128)(2,1)S(1)}, bf16[256,128]{1,0:T(8,128)(2,1)S(1)}, u32[]{:S(2)}, u32[]{:S(2)}) collective-permute-start(bf16[256,128]{1,0:T(8,128)(2,1)S(1)} %get-tuple-element.73.refs_3_), channel_id=1, source_target_pairs={{0,1},{1,0},{2,3},{3,2},{4,5},{5,4},{6,7},{7,6},{8,9},{9,8},{10,11... | collective-permute-start | bytes 196616 | tf_op jit(solution)/shard_map/ppermute | solution.py:492
  51.4 1.3 %collective-permute-start.10 = (bf16[2,32,256]{2,1,0:T(8,128)(2,1)S(1)}, bf16[2,32,256]{2,1,0:T(8,128)(2,1)S(1)}, u32[]{:S(2)}, u32[]{:S(2)}) collective-permute-start(bf16[2,32,256]{2,1,0:T(8,128)(2,1)S(1)} %get-tuple-element.79), channel_id=1, source_target_pairs={{0,1},{1,0},{2,3},{3,2},{4,5},{5,4},{6,7},{7,6},{8,9},{9,8},{10,11... | collective-permute-start | bytes 98312 | tf_op jit(solution)/shard_map/ppermute | solution.py:492
  52.9 1.2 %collective-permute-start.12 = (f32[2,32,128]{2,1,0:T(8,128)S(1)}, f32[2,32,128]{2,1,0:T(8,128)S(1)}, u32[]{:S(2)}, u32[]{:S(2)}) collective-permute-start(f32[2,32,128]{2,1,0:T(8,128)S(1)} %get-tuple-element.83), channel_id=1, source_target_pairs={{0,1},{1,0},{2,3},{3,2},{4,5},{5,4},{6,7},{7,6},{8,9},{9,8},{10,11... | collective-permute-start | bytes 98312 | tf_op jit(solution)/shard_map/ppermute | solution.py:492

commit v16 on v15

--- a/solution.py
+++ b/solution.py
@@ -376,11 +376,9 @@
 
 def weights_kernel(size, k, split, query, new_kv, tables, mine, *refs):
     many = size.mine if split else 1
-    other, theirs, refs = refs[:many], refs[many:2 * many], refs[2 * many:]
-    theirs = theirs if split else theirs[0]
-    cache, _, weights, lent, share, totals, sems = refs[2:]
+    other, refs = refs[:many], refs[many:]
+    _, _, weights, lent, share, totals = refs[2:]
     row = size.source_row(k)
-    copies = start_store(size, k, (0,), cache, mine, theirs, sems)
     live_mine, live_other, causal = masks(size, tables, (0,), new_kv.shape[3])
     for j in range(size.mine):
         keys = slice(j * size.span, (j + 1) * size.span)
@@ -393,8 +391,6 @@
         lent[j] = w1
         share[j] = jnp.dot(w2, new_kv[row, 1, j], preferred_element_type=F32)
         totals[j] = jnp.broadcast_to(total, totals.shape[1:])
-    for copy in copies:
-        copy.wait()
 
 
 def lend_kernel(size, lent, message, tables, *refs):
@@ -405,9 +401,11 @@
         given[j] = jnp.dot(lent[j], theirs[values, :], preferred_element_type=F32)
 
 
-def lent_store_kernel(size, k, theirs, *refs):
-    cache, _, sems = refs[2:]
+def lent_store_kernel(size, k, theirs, mine, *refs):
+    keys, refs = tuple(refs[:size.mine]), refs[size.mine:]
+    cache, _, sems, more = refs[2:]
     copies = side_copies(size, k, (1,), cache, theirs, False, sems)
+    copies += row_copies(size, k, (0,), cache, mine, keys, more)
     for copy in copies:
         copy.start()
     for copy in copies:
@@ -436,9 +434,11 @@
         given[j] = jnp.dot(lent[j], theirs[values, :], preferred_element_type=F32)
 
 
-def store_kernel(size, k, mine, theirs, *refs):
-    cache, _, sems = refs[2:]
-    for copy in start_store(size, k, (1,), cache, mine, theirs, sems):
+def store_kernel(size, k, mine, theirs, key_mine, key_theirs, *refs):
+    cache, _, sems, more = refs[2:]
+    copies = start_store(size, k, (1,), cache, mine, theirs, sems)
+    copies += start_store(size, k, (0,), cache, key_mine, key_theirs, more)
+    for copy in copies:
         copy.wait()
 
 
@@ -523,13 +523,13 @@
     state = attend(*held.pop(0), state)
     split = size.rest > 0
     tables = message[last, (0,)]
-    state, mine, theirs = rebuild(size, (0,), [tables], state, split)
-    theirs = theirs if split else (theirs,)
+    state, key_mine, theirs = rebuild(size, (0,), [tables], state, split)
+    keys = theirs if split else (theirs,)
     half = pltpu.VMEM((size.mine, size.wide, size.span), BF)
     state, (weights, lent, share, totals) = chained_call(
         size, functools.partial(weights_kernel, size, last, split),
-        (query, fresh, tables, mine, *[swapped(x) for x in theirs], *theirs), state,
-        [half, half, wide, wide], [sems], flops // 2,
+        (query, fresh, tables, key_mine, *[swapped(x) for x in keys]), state,
+        [half, half, wide, wide], [], flops // 2,
     )
     given = pltpu.VMEM((size.mine * size.span, HEAD_DIM), BF)
     if split:
@@ -539,7 +539,8 @@
         )
         got = swapped(sums)
         state, _ = chained_call(
-            size, functools.partial(lent_store_kernel, size, last), (theirs,), state, [], [sems], 0
+            size, functools.partial(lent_store_kernel, size, last), (theirs, key_mine, *keys), state,
+            [], [sems, sems], 0,
         )
         state, _ = chained_call(
             size, functools.partial(last_kernel, size, last),
@@ -554,7 +555,8 @@
     )
     got = swapped(sums)
     state, _ = chained_call(
-        size, functools.partial(store_kernel, size, last), (mine, theirs), state, [], [sems], 0
+        size, functools.partial(store_kernel, size, last), (mine, theirs, key_mine, *keys), state,
+        [], [sems, sems], 0,
     )
     state, _ = chained_call(
         size, functools.partial(finish_kernel, size, last), (kept, got, totals), state, [], rows, 0

time: 55.3 us -> 54.7 us (0.989)
  the two profiles are of different devices: /device:TPU:31 before, /device:TPU:9 now
where the time goes in v16:
time: 54.7 us; the launch traced here: 53.7 us
  waiting for transfers between devices  23.4 us (43%)
  starting transfers between devices  17.2 us (31%)
  Pallas kernels  12.4 us (23%)
  between operations  0.72 us (1%)
    ppermute x7, waiting for transfers between devices, body(): msg = lax.ppermute(msg, 'pool', list(enumerate(far(n, k))))  21.2 us
    ppermute x7, starting transfers between devices, swapped(): return lax.ppermute(x, 'sub', [(0, 1), (1, 0)])  9.13 us
    ppermute x7, starting transfers between devices, body(): msg = lax.ppermute(msg, 'pool', list(enumerate(far(n, k))))  8.04 us
    pallas_call x7, Pallas kernels, chained_call(): pl.pallas_call(kernel, in_specs=[IN_VMEM] * many + [IN_HBM, IN_HBM], out_...  6.61 us
    pallas_call x2, Pallas kernels, pack(): pl.pallas_call(functools.partial(pack_kernel, size, plan), out_shape=shap...  4.14 us
    ppermute x7, waiting for transfers between devices, swapped(): return lax.ppermute(x, 'sub', [(0, 1), (1, 0)])  2.23 us
  transfers between devices with their start and end apart: 14, of which 7 were waited for; matrix products, arithmetic and copies ran while one was open for 0% of the time, Pallas kernels for 18%

profile of v16, /device:TPU:9, one launch (start us, length us, event | category | flops | bytes accessed | tf_op | source)
XLA Modules:
  0.0 53.7 jit_solution(8316262306935687351)
XLA Ops:
  0.6 1.7 %shard_map.89 = bf16[1088,128]{1,0:T(8,128)(2,1)S(1)} custom-call(s32[4]{0:T(128)} %route.3, s32[4]{0:T(128)} %lengths.3, bf16[4,2,256,512]{3,2,1,0:T(8,128)(2,1)} %deltas.3, bf16[4,2,16,512]{3,2,1,0:T(8,128)(2,1)} %anchors.3, bf16[4,2,512]{2,1,0:T(2,128)(2,1)} %scale.3), custom_call_target="tpu_custom_call" | custom-call | bytes 262144 | tf_op jit(solution)/shard_map/pallas_call | solution.py:144
  2.4 1.3 %collective-permute-start.5 = (bf16[1088,128]{1,0:T(8,128)(2,1)S(1)}, bf16[1088,128]{1,0:T(8,128)(2,1)S(1)}, u32[]{:S(2)}, u32[]{:S(2)}) collective-permute-start(bf16[1088,128]{1,0:T(8,128)(2,1)S(1)} %shard_map.89), channel_id=1, source_target_pairs={{0,12},{4,8},{8,0},{12,4},{1,13},{5,9},{9,1},{13,5},{2,14},{6,10},... | collective-permute-start | bytes 835592 | tf_op jit(solution)/shard_map/ppermute | solution.py:488
  3.7 2.4 %shard_map.87 = (bf16[1104,128]{1,0:T(8,128)(2,1)S(1)}, bf16[1104,128]{1,0:T(8,128)(2,1)S(1)}, bf16[1088,128]{1,0:T(8,128)(2,1)S(1)}, bf16[1104,128]{1,0:T(8,128...) custom-call(s32[4]{0:T(128)} %route.3, s32[4]{0:T(128)} %lengths.3, ...), custom_call_target="tpu_custom_call" | custom-call | bytes 1835008 | tf_op jit(solution)/shard_map/pallas_call | solution.py:144
  6.1 0.1 collective-permute-start.4
  6.2 2.3 %collective-permute-start.1 = (bf16[1104,128]{1,0:T(8,128)(2,1)S(1)}, bf16[1104,128]{1,0:T(8,128)(2,1)S(1)}, u32[]{:S(2)}, u32[]{:S(2)}) collective-permute-start(bf16[1104,128]{1,0:T(8,128)(2,1)S(1)} %get-tuple-element.49), channel_id=1, source_target_pairs={{0,4},{4,0},{8,12},{12,8},{1,5},{5,1},{9,13},{13,9},{2,6},{6,2},{1... | collective-permute-start | bytes 847880 | tf_op jit(solution)/shard_map/ppermute | solution.py:488
  8.5 0.1 collective-permute-start.2
  8.5 0.2 shard_map.88
  8.7 1.5 %collective-permute-start.3 = (bf16[1024,128]{1,0:T(8,128)(2,1)S(1)}, bf16[1024,128]{1,0:T(8,128)(2,1)S(1)}, u32[]{:S(2)}, u32[]{:S(2)}) collective-permute-start(bf16[1024,128]{1,0:T(8,128)(2,1)S(1)} %get-tuple-element.53.theirs), channel_id=1, source_target_pairs={{0,1},{1,0},{2,3},{3,2},{4,5},{5,4},{6,7},{7,6},{8,9},{9,8},{10,11... | collective-permute-start | bytes 786440 | tf_op jit(solution)/shard_map/ppermute | solution.py:492
  10.2 10.8 %collective-permute-done.5.refs_0_ = bf16[1088,128]{1,0:T(8,128)(2,1)S(1)} collective-permute-done((bf16[1088,128]{1,0:T(8,128)(2,1)S(1)}, bf16[1088,128]{1,0:T(8,128)(2,1)S(1)}, u32[]{:S(2)}, u32[]{:S(2)}) %collective-permute-start.5) | collective-permute-done | bytes 278560 | tf_op jit(solution)/shard_map/ppermute | solution.py:488
  21.1 0.0 collective-permute-start
  21.1 0.9 %shard_map.86 = (bf16[4,2,32,128]{3,2,1,0:T(8,128)(2,1)S(1)}, bf16[4,2,2,16,128]{4,3,2,1,0:T(8,128)(2,1)S(1)}) custom-call(bf16[4,4,2048]{2,1,0:T(4,128)(2,1)} %new_query.1, bf16[4,2,4,512]{3,2,1,0:T(4,128)(2,1)} %new_kv.1), custom_call_target="tpu_custom_call" | custom-call | tf_op jit(solution)/shard_map/pallas_call | solution.py:181
  22.0 5.1 %collective-permute-done.4.message.tables = bf16[1104,128]{1,0:T(8,128)(2,1)S(1)} collective-permute-done((bf16[1104,128]{1,0:T(8,128)(2,1)S(1)}, bf16[1104,128]{1,0:T(8,128)(2,1)S(1)}, u32[]{:S(2)}, u32[]{:S(2)}) %collective-permute-start.4) | collective-permute-done | bytes 282656 | tf_op jit(solution)/shard_map/ppermute | solution.py:488
  27.1 0.2 shard_map.90
  27.3 2.7 %collective-permute-start.7 = (bf16[1024,128]{1,0:T(8,128)(2,1)S(1)}, bf16[1024,128]{1,0:T(8,128)(2,1)S(1)}, u32[]{:S(2)}, u32[]{:S(2)}) collective-permute-start(bf16[1024,128]{1,0:T(8,128)(2,1)S(1)} %get-tuple-element.64.theirs), channel_id=1, source_target_pairs={{0,1},{1,0},{2,3},{3,2},{4,5},{5,4},{6,7},{7,6},{8,9},{9,8},{10,11... | collective-permute-start | bytes 786440 | tf_op jit(solution)/shard_map/ppermute | solution.py:492
  30.1 0.0 collective-permute-done.3.other
  30.1 1.3 %shard_map.91 = (bf16[4,2,256,512]{3,2,1,0:T(8,128)(2,1)}, bf16[4,4,2048]{2,1,0:T(4,128)(2,1)}) custom-call(bf16[4,2,32,128]{3,2,1,0:T(8,128)(2,1)S(1)} %get-tuple-element.46.query, bf16[4,2,2,16,128]{4,3,2,1,0:T(8,128)(2,1)S(1)} %get-tuple-element.47.new_kv, ...), custom_call_target="tpu_custom_call", output_to_operand_aliasing={{0}: (6, {}), {1}: (7, {})} | custom-call | flops 16777216 | bytes 1048576 | tf_op jit(solution)/shard_map/pallas_call | solution.py:455
  31.4 4.8 %collective-permute-done.2.refs_0_ = bf16[1088,128]{1,0:T(8,128)(2,1)S(1)} collective-permute-done((bf16[1088,128]{1,0:T(8,128)(2,1)S(1)}, bf16[1088,128]{1,0:T(8,128)(2,1)S(1)}, u32[]{:S(2)}, u32[]{:S(2)}) %collective-permute-start.2) | collective-permute-done | bytes 278560 | tf_op jit(solution)/shard_map/ppermute | solution.py:488
  36.2 0.0 collective-permute-done.1.message.tables
  36.2 0.2 shard_map.92
  36.4 2.2 %collective-permute-start.6 = (bf16[1024,128]{1,0:T(8,128)(2,1)S(1)}, bf16[1024,128]{1,0:T(8,128)(2,1)S(1)}, u32[]{:S(2)}, u32[]{:S(2)}) collective-permute-start(bf16[1024,128]{1,0:T(8,128)(2,1)S(1)} %get-tuple-element.62.theirs), channel_id=1, source_target_pairs={{0,1},{1,0},{2,3},{3,2},{4,5},{5,4},{6,7},{7,6},{8,9},{9,8},{10,11... | collective-permute-start | bytes 786440 | tf_op jit(solution)/shard_map/ppermute | solution.py:492
  38.6 0.0 collective-permute-start.11
  38.6 4.3 %collective-permute-start.13 = (bf16[544,128]{1,0:T(8,128)(2,1)S(1)}, bf16[544,128]{1,0:T(8,128)(2,1)S(1)}, u32[]{:S(2)}, u32[]{:S(2)}) collective-permute-start(bf16[544,128]{1,0:T(8,128)(2,1)S(1)} %get-tuple-element.84), channel_id=1, source_target_pairs={{0,8},{4,12},{8,4},{12,0},{1,9},{5,13},{9,5},{13,1},{2,10},{6,14},... | collective-permute-start | bytes 417800 | tf_op jit(solution)/shard_map/ppermute | solution.py:488
  42.9 0.0 collective-permute-done.7.other
  42.9 1.3 %shard_map.93 = (bf16[4,2,256,512]{3,2,1,0:T(8,128)(2,1)}, bf16[4,4,2048]{2,1,0:T(4,128)(2,1)}) custom-call(bf16[4,2,32,128]{3,2,1,0:T(8,128)(2,1)S(1)} %get-tuple-element.46.query, bf16[4,2,2,16,128]{4,3,2,1,0:T(8,128)(2,1)S(1)} %get-tuple-element.47.new_kv, ...), custom_call_target="tpu_custom_call", output_to_operand_aliasing={{0}: (6, {}), {1}: (7, {})} | custom-call | flops 16777216 | bytes 1048576 | tf_op jit(solution)/shard_map/pallas_call | solution.py:455
  44.2 0.0 collective-permute-done.6.other
  44.2 1.3 %shard_map.94 = (bf16[4,2,256,512]{3,2,1,0:T(8,128)(2,1)}, bf16[4,4,2048]{2,1,0:T(4,128)(2,1)}) custom-call(bf16[4,2,32,128]{3,2,1,0:T(8,128)(2,1)S(1)} %get-tuple-element.46.query, bf16[4,2,2,16,128]{4,3,2,1,0:T(8,128)(2,1)S(1)} %get-tuple-element.47.new_kv, ...), custom_call_target="tpu_custom_call", output_to_operand_aliasing={{0}: (6, {}), {1}: (7, {})} | custom-call | flops 16777216 | bytes 1048576 | tf_op jit(solution)/shard_map/pallas_call | solution.py:455
  45.6 0.0 collective-permute-done.message.tables
  45.6 0.1 shard_map.95
  45.7 2.2 %collective-permute-start.8 = (bf16[256,128]{1,0:T(8,128)(2,1)S(1)}, bf16[256,128]{1,0:T(8,128)(2,1)S(1)}, u32[]{:S(2)}, u32[]{:S(2)}) collective-permute-start(bf16[256,128]{1,0:T(8,128)(2,1)S(1)} %get-tuple-element.72.refs_0_), channel_id=1, source_target_pairs={{0,1},{1,0},{2,3},{3,2},{4,5},{5,4},{6,7},{7,6},{8,9},{9,8},{10,11... | collective-permute-start | bytes 196616 | tf_op jit(solution)/shard_map/ppermute | solution.py:492
  47.9 0.1 collective-permute-start.9
  48.0 0.8 %collective-permute-done.8.refs_0_ = bf16[256,128]{1,0:T(8,128)(2,1)S(1)} collective-permute-done((bf16[256,128]{1,0:T(8,128)(2,1)S(1)}, bf16[256,128]{1,0:T(8,128)(2,1)S(1)}, u32[]{:S(2)}, u32[]{:S(2)}) %collective-permute-start.8) | collective-permute-done | bytes 65568 | tf_op jit(solution)/shard_map/ppermute | solution.py:492
  48.8 0.4 collective-permute-done.9.refs_1_
  49.2 0.6 %shard_map.96 = (bf16[4,2,256,512]{3,2,1,0:T(8,128)(2,1)}, bf16[4,4,2048]{2,1,0:T(4,128)(2,1)}, bf16[2,32,256]{2,1,0:T(8,128)(2,1)S(1)}, bf16[2,32,256]{2,1,0:T(...) custom-call(bf16[4,2,32,128]{3,2,1,0:T(8,128)(2,1)S(1)} %get-tuple-e, ...), custom_call_target="tpu_custom_call", output_to_operand_aliasing={{0}: (6, {}), {1}: (7, {})} | custom-call | flops 8388608 | bytes 1048576 | tf_op jit(solution)/shard_map/pallas_call | solution.py:455
  49.8 0.2 collective-permute-start.10
  50.0 0.0 collective-permute-done.11.message
  50.0 1.0 %collective-permute-done.10.lent = bf16[2,32,256]{2,1,0:T(8,128)(2,1)S(1)} collective-permute-done((bf16[2,32,256]{2,1,0:T(8,128)(2,1)S(1)}, bf16[2,32,256]{2,1,0:T(8,128)(2,1)S(1)}, u32[]{:S(2)}, u32[]{:S(2)}) %collective-permute-start.10) | collective-permute-done | bytes 32800 | tf_op jit(solution)/shard_map/ppermute | solution.py:492
  51.1 0.2 shard_map.97
  51.3 0.2 collective-permute-start.12
  51.4 0.9 %shard_map.98 = (bf16[4,2,256,512]{3,2,1,0:T(8,128)(2,1)}, bf16[4,4,2048]{2,1,0:T(4,128)(2,1)}) custom-call(bf16[512,128]{1,0:T(8,128)(2,1)S(1)} %get-tuple-element.85.theirs, bf16[512,128]{1,0:T(8,128)(2,1)S(1)} %get-tuple-element.71.mine, bf16[256,128]{1,0:T(8,128)(2,1)S(1)} %get-tuple-element.72.refs_0_, ...), custom_call_target="tpu_custom_call", output_to_operand_aliasing={{0}: (4, {}), {1}: (5, {})} | custom-call | bytes 1048576 | tf_op jit(solution)/shard_map/pallas_call | solution.py:455
  52.3 0.4 collective-permute-done.13.message
  52.8 0.0 collective-permute-done.12.got
  52.8 0.9 %shard_map.99 = (bf16[4,2,256,512]{3,2,1,0:T(8,128)(2,1)}, bf16[4,4,2048]{2,1,0:T(4,128)(2,1)}) custom-call(bf16[2,32,256]{2,1,0:T(8,128)(2,1)S(1)} %get-tuple-element.76.weights, f32[2,32,128]{2,1,0:T(8,128)S(1)} %get-tuple-element.77.share, f32[2,32,128]{2,1,0:T(8,128)S(1)} %get-tuple-element.78.totals, ...), custom_call_target="tpu_custom_call", output_to_operand_aliasing={{0}: (6, {}), {1}: (7, {})} | custom-call | flops 4194304 | bytes 1048576 | tf_op jit(solution)/shard_map/pallas_call | solution.py:455
Async XLA Ops:
  2.4 18.7 %collective-permute-start.5 = (bf16[1088,128]{1,0:T(8,128)(2,1)S(1)}, bf16[1088,128]{1,0:T(8,128)(2,1)S(1)}, u32[]{:S(2)}, u32[]{:S(2)}) collective-permute-start(bf16[1088,128]{1,0:T(8,128)(2,1)S(1)} %shard_map.89), channel_id=1, source_target_pairs={{0,12},{4,8},{8,0},{12,4},{1,13},{5,9},{9,1},{13,5},{2,14},{6,10},... | collective-permute-start | bytes 835592 | tf_op jit(solution)/shard_map/ppermute | solution.py:488
  6.1 21.0 %collective-permute-start.4 = (bf16[1104,128]{1,0:T(8,128)(2,1)S(1)}, bf16[1104,128]{1,0:T(8,128)(2,1)S(1)}, u32[]{:S(2)}, u32[]{:S(2)}) collective-permute-start(bf16[1104,128]{1,0:T(8,128)(2,1)S(1)} %get-tuple-element.54), channel_id=1, source_target_pairs={{0,12},{4,8},{8,0},{12,4},{1,13},{5,9},{9,1},{13,5},{2,14},{6,10},... | collective-permute-start | bytes 847880 | tf_op jit(solution)/shard_map/ppermute | solution.py:488
  6.2 30.0 %collective-permute-start.1 = (bf16[1104,128]{1,0:T(8,128)(2,1)S(1)}, bf16[1104,128]{1,0:T(8,128)(2,1)S(1)}, u32[]{:S(2)}, u32[]{:S(2)}) collective-permute-start(bf16[1104,128]{1,0:T(8,128)(2,1)S(1)} %get-tuple-element.49), channel_id=1, source_target_pairs={{0,4},{4,0},{8,12},{12,8},{1,5},{5,1},{9,13},{13,9},{2,6},{6,2},{1... | collective-permute-start | bytes 847880 | tf_op jit(solution)/shard_map/ppermute | solution.py:488
  8.5 27.7 %collective-permute-start.2 = (bf16[1088,128]{1,0:T(8,128)(2,1)S(1)}, bf16[1088,128]{1,0:T(8,128)(2,1)S(1)}, u32[]{:S(2)}, u32[]{:S(2)}) collective-permute-start(bf16[1088,128]{1,0:T(8,128)(2,1)S(1)} %get-tuple-element.50), channel_id=1, source_target_pairs={{0,4},{4,0},{8,12},{12,8},{1,5},{5,1},{9,13},{13,9},{2,6},{6,2},{1... | collective-permute-start | bytes 835592 | tf_op jit(solution)/shard_map/ppermute | solution.py:488
  8.7 21.3 %collective-permute-start.3 = (bf16[1024,128]{1,0:T(8,128)(2,1)S(1)}, bf16[1024,128]{1,0:T(8,128)(2,1)S(1)}, u32[]{:S(2)}, u32[]{:S(2)}) collective-permute-start(bf16[1024,128]{1,0:T(8,128)(2,1)S(1)} %get-tuple-element.53.theirs), channel_id=1, source_target_pairs={{0,1},{1,0},{2,3},{3,2},{4,5},{5,4},{6,7},{7,6},{8,9},{9,8},{10,11... | collective-permute-start | bytes 786440 | tf_op jit(solution)/shard_map/ppermute | solution.py:492
  21.1 24.5 %collective-permute-start = (bf16[1104,128]{1,0:T(8,128)(2,1)S(1)}, bf16[1104,128]{1,0:T(8,128)(2,1)S(1)}, u32[]{:S(2)}, u32[]{:S(2)}) collective-permute-start(bf16[1104,128]{1,0:T(8,128)(2,1)S(1)} %get-tuple-element.48), channel_id=1, source_target_pairs={{0,8},{4,12},{8,4},{12,0},{1,9},{5,13},{9,5},{13,1},{2,10},{6,14},... | collective-permute-start | bytes 847880 | tf_op jit(solution)/shard_map/ppermute | solution.py:488
  27.3 15.5 %collective-permute-start.7 = (bf16[1024,128]{1,0:T(8,128)(2,1)S(1)}, bf16[1024,128]{1,0:T(8,128)(2,1)S(1)}, u32[]{:S(2)}, u32[]{:S(2)}) collective-permute-start(bf16[1024,128]{1,0:T(8,128)(2,1)S(1)} %get-tuple-element.64.theirs), channel_id=1, source_target_pairs={{0,1},{1,0},{2,3},{3,2},{4,5},{5,4},{6,7},{7,6},{8,9},{9,8},{10,11... | collective-permute-start | bytes 786440 | tf_op jit(solution)/shard_map/ppermute | solution.py:492
  36.4 7.8 %collective-permute-start.6 = (bf16[1024,128]{1,0:T(8,128)(2,1)S(1)}, bf16[1024,128]{1,0:T(8,128)(2,1)S(1)}, u32[]{:S(2)}, u32[]{:S(2)}) collective-permute-start(bf16[1024,128]{1,0:T(8,128)(2,1)S(1)} %get-tuple-element.62.theirs), channel_id=1, source_target_pairs={{0,1},{1,0},{2,3},{3,2},{4,5},{5,4},{6,7},{7,6},{8,9},{9,8},{10,11... | collective-permute-start | bytes 786440 | tf_op jit(solution)/shard_map/ppermute | solution.py:492
  38.6 11.4 %collective-permute-start.11 = (bf16[544,128]{1,0:T(8,128)(2,1)S(1)}, bf16[544,128]{1,0:T(8,128)(2,1)S(1)}, u32[]{:S(2)}, u32[]{:S(2)}) collective-permute-start(bf16[544,128]{1,0:T(8,128)(2,1)S(1)} %get-tuple-element.80), channel_id=1, source_target_pairs={{0,8},{4,12},{8,4},{12,0},{1,9},{5,13},{9,5},{13,1},{2,10},{6,14},... | collective-permute-start | bytes 417800 | tf_op jit(solution)/shard_map/ppermute | solution.py:488
  38.6 14.2 %collective-permute-start.13 = (bf16[544,128]{1,0:T(8,128)(2,1)S(1)}, bf16[544,128]{1,0:T(8,128)(2,1)S(1)}, u32[]{:S(2)}, u32[]{:S(2)}) collective-permute-start(bf16[544,128]{1,0:T(8,128)(2,1)S(1)} %get-tuple-element.84), channel_id=1, source_target_pairs={{0,8},{4,12},{8,4},{12,0},{1,9},{5,13},{9,5},{13,1},{2,10},{6,14},... | collective-permute-start | bytes 417800 | tf_op jit(solution)/shard_map/ppermute | solution.py:488
  45.7 3.1 %collective-permute-start.8 = (bf16[256,128]{1,0:T(8,128)(2,1)S(1)}, bf16[256,128]{1,0:T(8,128)(2,1)S(1)}, u32[]{:S(2)}, u32[]{:S(2)}) collective-permute-start(bf16[256,128]{1,0:T(8,128)(2,1)S(1)} %get-tuple-element.72.refs_0_), channel_id=1, source_target_pairs={{0,1},{1,0},{2,3},{3,2},{4,5},{5,4},{6,7},{7,6},{8,9},{9,8},{10,11... | collective-permute-start | bytes 196616 | tf_op jit(solution)/shard_map/ppermute | solution.py:492
  47.9 1.3 %collective-permute-start.9 = (bf16[256,128]{1,0:T(8,128)(2,1)S(1)}, bf16[256,128]{1,0:T(8,128)(2,1)S(1)}, u32[]{:S(2)}, u32[]{:S(2)}) collective-permute-start(bf16[256,128]{1,0:T(8,128)(2,1)S(1)} %get-tuple-element.73.refs_1_), channel_id=1, source_target_pairs={{0,1},{1,0},{2,3},{3,2},{4,5},{5,4},{6,7},{7,6},{8,9},{9,8},{10,11... | collective-permute-start | bytes 196616 | tf_op jit(solution)/shard_map/ppermute | solution.py:492
  49.8 1.2 %collective-permute-start.10 = (bf16[2,32,256]{2,1,0:T(8,128)(2,1)S(1)}, bf16[2,32,256]{2,1,0:T(8,128)(2,1)S(1)}, u32[]{:S(2)}, u32[]{:S(2)}) collective-permute-start(bf16[2,32,256]{2,1,0:T(8,128)(2,1)S(1)} %get-tuple-element.79), channel_id=1, source_target_pairs={{0,1},{1,0},{2,3},{3,2},{4,5},{5,4},{6,7},{7,6},{8,9},{9,8},{10,11... | collective-permute-start | bytes 98312 | tf_op jit(solution)/shard_map/ppermute | solution.py:492
  51.3 1.5 %collective-permute-start.12 = (f32[2,32,128]{2,1,0:T(8,128)S(1)}, f32[2,32,128]{2,1,0:T(8,128)S(1)}, u32[]{:S(2)}, u32[]{:S(2)}) collective-permute-start(f32[2,32,128]{2,1,0:T(8,128)S(1)} %get-tuple-element.83), channel_id=1, source_target_pairs={{0,1},{1,0},{2,3},{3,2},{4,5},{5,4},{6,7},{7,6},{8,9},{9,8},{10,11... | collective-permute-start | bytes 98312 | tf_op jit(solution)/shard_map/ppermute | solution.py:492

commit v17 on v16

--- a/solution.py
+++ b/solution.py
@@ -230,7 +230,9 @@
             part = slice(j * size.span + i * size.repeat, j * size.span + (i + 1) * size.repeat)
             value = anchor[i:i + 1, :] + scale * message[part, :].astype(F32)
             keep = (base + i * size.repeat).astype(F32) < length
-            out[part, :] = jnp.where(keep, value, jnp.float32(0.0)).astype(BF)
+            out[j][i * size.repeat:(i + 1) * size.repeat, :] = jnp.where(
+                keep, value, jnp.float32(0.0)
+            ).astype(BF)
 
 
 def rebuild_heads(size, parts, message, tables, mine, theirs):
@@ -393,16 +395,13 @@
         totals[j] = jnp.broadcast_to(total, totals.shape[1:])
 
 
-def lend_kernel(size, lent, message, tables, *refs):
-    _, _, theirs, given = refs[2:]
-    rebuild_half(size, message, tables, theirs, False)
-    for j in range(size.mine):
-        values = slice(j * size.span, (j + 1) * size.span)
-        given[j] = jnp.dot(lent[j], theirs[values, :], preferred_element_type=F32)
-
-
-def lent_store_kernel(size, k, theirs, mine, *refs):
-    keys, refs = tuple(refs[:size.mine]), refs[size.mine:]
+def theirs_kernel(size, message, tables, *refs):
+    rebuild_half(size, message, tables, refs[4:], False)
+
+
+def lent_store_kernel(size, k, mine, *refs):
+    many = size.mine
+    theirs, keys, refs = tuple(refs[:many]), tuple(refs[many:2 * many]), refs[2 * many:]
     cache, _, sems, more = refs[2:]
     copies = side_copies(size, k, (1,), cache, theirs, False, sems)
     copies += row_copies(size, k, (0,), cache, mine, keys, more)
@@ -412,16 +411,18 @@
         copy.wait()
 
 
-def last_kernel(size, k, weights, share, totals, got, message, tables, *refs):
-    cache, attended, mine, made, flat, sem, sems = refs[2:]
+def last_kernel(size, k, weights, lent, share, totals, message, tables, *refs):
+    others, refs = refs[:size.mine], refs[size.mine + 2:]
+    cache, attended, *rest = refs
+    mine, (made, flat, sem, sems) = tuple(rest[:size.mine]), rest[size.mine:]
     rebuild_half(size, message, tables, mine, True)
     copies = side_copies(size, k, (1,), cache, mine, True, sems)
     for copy in copies:
         copy.start()
     for j in range(size.mine):
-        values = slice(j * size.span, (j + 1) * size.span)
-        acc = share[j] + jnp.dot(weights[j], mine[values, :], preferred_element_type=F32)
-        flat[j] = (acc + got[j]) / totals[j]
+        acc = share[j] + jnp.dot(weights[j], mine[j][...], preferred_element_type=F32)
+        acc = acc + jnp.dot(lent[j], others[j][...], preferred_element_type=F32)
+        flat[j] = acc / totals[j]
     store_heads(size, k, flat, made, attended, sem, copies)
 
 
@@ -533,19 +534,20 @@
     )
     given = pltpu.VMEM((size.mine * size.span, HEAD_DIM), BF)
     if split:
-        state, (theirs, sums) = chained_call(
-            size, functools.partial(lend_kernel, size),
-            (swapped(lent), message[last, (1,), 0], tables), state, [given, wide], [], flops // 4,
+        head = pltpu.VMEM((size.span, HEAD_DIM), BF)
+        state, theirs = chained_call(
+            size, functools.partial(theirs_kernel, size), (message[last, (1,), 0], tables), state,
+            [head] * size.mine, [], flops // 8,
         )
-        got = swapped(sums)
+        others = [swapped(x) for x in theirs]
         state, _ = chained_call(
-            size, functools.partial(lent_store_kernel, size, last), (theirs, key_mine, *keys), state,
+            size, functools.partial(lent_store_kernel, size, last), (key_mine, *theirs, *keys), state,
             [], [sems, sems], 0,
         )
         state, _ = chained_call(
             size, functools.partial(last_kernel, size, last),
-            (weights, share, totals, got, message[last, (1,), 1], tables), state,
-            [], [given] + rows + [sems], flops // 4,
+            (weights, lent, share, totals, message[last, (1,), 1], tables, *others), state,
+            [], [head] * size.mine + rows + [sems], flops // 4,
         )
         return state
     state, (mine, theirs, kept, sums) = chained_call(

time: 54.7 us -> 54.3 us (level)
  starting transfers between devices: 17.2 us -> 18.2 us
  waiting for transfers between devices: 23.4 us -> 22.5 us
    ppermute x7, waiting for transfers between devices: 2.23 us -> 1.19 us  [swapped(): return lax.ppermute(x, 'sub', [(0, 1), (1, 0)])]
    ppermute x7, starting transfers between devices: 9.13 us -> 10.2 us  [swapped(): return lax.ppermute(x, 'sub', [(0, 1), (1, 0)])]
  transfers between devices with their start and end apart: 14 -> 14, of which waited for: 7 -> 6; matrix products, arithmetic and copies ran while one was open for 0% -> 0% of each run, Pallas kernels for 18% -> 18%
where the time goes in v17:
time: 54.3 us; the launch traced here: 53.7 us
  waiting for transfers between devices  22.5 us (41%)
  starting transfers between devices  18.2 us (34%)
  Pallas kernels  12.3 us (23%)
  between operations  0.73 us (1%)
    ppermute x7, waiting for transfers between devices, body(): msg = lax.ppermute(msg, 'pool', list(enumerate(far(n, k))))  21.3 us
    ppermute x7, starting transfers between devices, swapped(): return lax.ppermute(x, 'sub', [(0, 1), (1, 0)])  10.2 us
    ppermute x7, starting transfers between devices, body(): msg = lax.ppermute(msg, 'pool', list(enumerate(far(n, k))))  8.04 us
    pallas_call x7, Pallas kernels, chained_call(): pl.pallas_call(kernel, in_specs=[IN_VMEM] * many + [IN_HBM, IN_HBM], out_...  6.47 us
    pallas_call x2, Pallas kernels, pack(): pl.pallas_call(functools.partial(pack_kernel, size, plan), out_shape=shap...  4.14 us
    ppermute x7, waiting for transfers between devices, swapped(): return lax.ppermute(x, 'sub', [(0, 1), (1, 0)])  1.19 us
  transfers between devices with their start and end apart: 14, of which 6 were waited for; matrix products, arithmetic and copies ran while one was open for 0% of the time, Pallas kernels for 18%

profile of v17, /device:TPU:9, one launch (start us, length us, event | category | flops | bytes accessed | tf_op | source)
XLA Modules:
  0.0 53.7 jit_solution(14256068851737112929)
XLA Ops:
  0.6 1.7 %shard_map.89 = bf16[1088,128]{1,0:T(8,128)(2,1)S(1)} custom-call(s32[4]{0:T(128)} %route.3, s32[4]{0:T(128)} %lengths.3, bf16[4,2,256,512]{3,2,1,0:T(8,128)(2,1)} %deltas.3, bf16[4,2,16,512]{3,2,1,0:T(8,128)(2,1)} %anchors.3, bf16[4,2,512]{2,1,0:T(2,128)(2,1)} %scale.3), custom_call_target="tpu_custom_call" | custom-call | bytes 262144 | tf_op jit(solution)/shard_map/pallas_call | solution.py:144
  2.4 1.3 %collective-permute-start.5 = (bf16[1088,128]{1,0:T(8,128)(2,1)S(1)}, bf16[1088,128]{1,0:T(8,128)(2,1)S(1)}, u32[]{:S(2)}, u32[]{:S(2)}) collective-permute-start(bf16[1088,128]{1,0:T(8,128)(2,1)S(1)} %shard_map.89), channel_id=1, source_target_pairs={{0,12},{4,8},{8,0},{12,4},{1,13},{5,9},{9,1},{13,5},{2,14},{6,10},... | collective-permute-start | bytes 835592 | tf_op jit(solution)/shard_map/ppermute | solution.py:489
  3.7 2.4 %shard_map.87 = (bf16[1104,128]{1,0:T(8,128)(2,1)S(1)}, bf16[1104,128]{1,0:T(8,128)(2,1)S(1)}, bf16[1088,128]{1,0:T(8,128)(2,1)S(1)}, bf16[1104,128]{1,0:T(8,128...) custom-call(s32[4]{0:T(128)} %route.3, s32[4]{0:T(128)} %lengths.3, ...), custom_call_target="tpu_custom_call" | custom-call | bytes 1835008 | tf_op jit(solution)/shard_map/pallas_call | solution.py:144
  6.1 0.1 collective-permute-start.4
  6.2 2.3 %collective-permute-start.1 = (bf16[1104,128]{1,0:T(8,128)(2,1)S(1)}, bf16[1104,128]{1,0:T(8,128)(2,1)S(1)}, u32[]{:S(2)}, u32[]{:S(2)}) collective-permute-start(bf16[1104,128]{1,0:T(8,128)(2,1)S(1)} %get-tuple-element.49), channel_id=1, source_target_pairs={{0,4},{4,0},{8,12},{12,8},{1,5},{5,1},{9,13},{13,9},{2,6},{6,2},{1... | collective-permute-start | bytes 847880 | tf_op jit(solution)/shard_map/ppermute | solution.py:489
  8.5 0.1 collective-permute-start.2
  8.5 0.2 shard_map.88
  8.7 1.5 %collective-permute-start.3 = (bf16[1024,128]{1,0:T(8,128)(2,1)S(1)}, bf16[1024,128]{1,0:T(8,128)(2,1)S(1)}, u32[]{:S(2)}, u32[]{:S(2)}) collective-permute-start(bf16[1024,128]{1,0:T(8,128)(2,1)S(1)} %get-tuple-element.53.theirs), channel_id=1, source_target_pairs={{0,1},{1,0},{2,3},{3,2},{4,5},{5,4},{6,7},{7,6},{8,9},{9,8},{10,11... | collective-permute-start | bytes 786440 | tf_op jit(solution)/shard_map/ppermute | solution.py:493
  10.2 10.8 %collective-permute-done.5.refs_0_ = bf16[1088,128]{1,0:T(8,128)(2,1)S(1)} collective-permute-done((bf16[1088,128]{1,0:T(8,128)(2,1)S(1)}, bf16[1088,128]{1,0:T(8,128)(2,1)S(1)}, u32[]{:S(2)}, u32[]{:S(2)}) %collective-permute-start.5) | collective-permute-done | bytes 278560 | tf_op jit(solution)/shard_map/ppermute | solution.py:489
  21.1 0.0 collective-permute-start
  21.1 0.9 %shard_map.86 = (bf16[4,2,32,128]{3,2,1,0:T(8,128)(2,1)S(1)}, bf16[4,2,2,16,128]{4,3,2,1,0:T(8,128)(2,1)S(1)}) custom-call(bf16[4,4,2048]{2,1,0:T(4,128)(2,1)} %new_query.1, bf16[4,2,4,512]{3,2,1,0:T(4,128)(2,1)} %new_kv.1), custom_call_target="tpu_custom_call" | custom-call | tf_op jit(solution)/shard_map/pallas_call | solution.py:181
  22.0 5.1 %collective-permute-done.4.message.tables = bf16[1104,128]{1,0:T(8,128)(2,1)S(1)} collective-permute-done((bf16[1104,128]{1,0:T(8,128)(2,1)S(1)}, bf16[1104,128]{1,0:T(8,128)(2,1)S(1)}, u32[]{:S(2)}, u32[]{:S(2)}) %collective-permute-start.4) | collective-permute-done | bytes 282656 | tf_op jit(solution)/shard_map/ppermute | solution.py:489
  27.1 0.2 shard_map.90
  27.3 2.7 %collective-permute-start.7 = (bf16[1024,128]{1,0:T(8,128)(2,1)S(1)}, bf16[1024,128]{1,0:T(8,128)(2,1)S(1)}, u32[]{:S(2)}, u32[]{:S(2)}) collective-permute-start(bf16[1024,128]{1,0:T(8,128)(2,1)S(1)} %get-tuple-element.64.theirs), channel_id=1, source_target_pairs={{0,1},{1,0},{2,3},{3,2},{4,5},{5,4},{6,7},{7,6},{8,9},{9,8},{10,11... | collective-permute-start | bytes 786440 | tf_op jit(solution)/shard_map/ppermute | solution.py:493
  30.1 0.0 collective-permute-done.3.other
  30.1 1.3 %shard_map.91 = (bf16[4,2,256,512]{3,2,1,0:T(8,128)(2,1)}, bf16[4,4,2048]{2,1,0:T(4,128)(2,1)}) custom-call(bf16[4,2,32,128]{3,2,1,0:T(8,128)(2,1)S(1)} %get-tuple-element.46.query, bf16[4,2,2,16,128]{4,3,2,1,0:T(8,128)(2,1)S(1)} %get-tuple-element.47.new_kv, ...), custom_call_target="tpu_custom_call", output_to_operand_aliasing={{0}: (6, {}), {1}: (7, {})} | custom-call | flops 16777216 | bytes 1048576 | tf_op jit(solution)/shard_map/pallas_call | solution.py:456
  31.4 4.8 %collective-permute-done.2.refs_0_ = bf16[1088,128]{1,0:T(8,128)(2,1)S(1)} collective-permute-done((bf16[1088,128]{1,0:T(8,128)(2,1)S(1)}, bf16[1088,128]{1,0:T(8,128)(2,1)S(1)}, u32[]{:S(2)}, u32[]{:S(2)}) %collective-permute-start.2) | collective-permute-done | bytes 278560 | tf_op jit(solution)/shard_map/ppermute | solution.py:489
  36.2 0.0 collective-permute-done.1.message.tables
  36.2 0.2 shard_map.92
  36.4 2.2 %collective-permute-start.6 = (bf16[1024,128]{1,0:T(8,128)(2,1)S(1)}, bf16[1024,128]{1,0:T(8,128)(2,1)S(1)}, u32[]{:S(2)}, u32[]{:S(2)}) collective-permute-start(bf16[1024,128]{1,0:T(8,128)(2,1)S(1)} %get-tuple-element.62.theirs), channel_id=1, source_target_pairs={{0,1},{1,0},{2,3},{3,2},{4,5},{5,4},{6,7},{7,6},{8,9},{9,8},{10,11... | collective-permute-start | bytes 786440 | tf_op jit(solution)/shard_map/ppermute | solution.py:493
  38.6 0.0 collective-permute-start.11
  38.6 4.3 %collective-permute-start.10 = (bf16[544,128]{1,0:T(8,128)(2,1)S(1)}, bf16[544,128]{1,0:T(8,128)(2,1)S(1)}, u32[]{:S(2)}, u32[]{:S(2)}) collective-permute-start(bf16[544,128]{1,0:T(8,128)(2,1)S(1)} %get-tuple-element.80), channel_id=1, source_target_pairs={{0,8},{4,12},{8,4},{12,0},{1,9},{5,13},{9,5},{13,1},{2,10},{6,14},... | collective-permute-start | bytes 417800 | tf_op jit(solution)/shard_map/ppermute | solution.py:489
  42.9 0.0 collective-permute-done.7.other
  42.9 1.3 %shard_map.93 = (bf16[4,2,256,512]{3,2,1,0:T(8,128)(2,1)}, bf16[4,4,2048]{2,1,0:T(4,128)(2,1)}) custom-call(bf16[4,2,32,128]{3,2,1,0:T(8,128)(2,1)S(1)} %get-tuple-element.46.query, bf16[4,2,2,16,128]{4,3,2,1,0:T(8,128)(2,1)S(1)} %get-tuple-element.47.new_kv, ...), custom_call_target="tpu_custom_call", output_to_operand_aliasing={{0}: (6, {}), {1}: (7, {})} | custom-call | flops 16777216 | bytes 1048576 | tf_op jit(solution)/shard_map/pallas_call | solution.py:456
  44.2 0.0 collective-permute-done.6.other
  44.2 1.3 %shard_map.94 = (bf16[4,2,256,512]{3,2,1,0:T(8,128)(2,1)}, bf16[4,4,2048]{2,1,0:T(4,128)(2,1)}) custom-call(bf16[4,2,32,128]{3,2,1,0:T(8,128)(2,1)S(1)} %get-tuple-element.46.query, bf16[4,2,2,16,128]{4,3,2,1,0:T(8,128)(2,1)S(1)} %get-tuple-element.47.new_kv, ...), custom_call_target="tpu_custom_call", output_to_operand_aliasing={{0}: (6, {}), {1}: (7, {})} | custom-call | flops 16777216 | bytes 1048576 | tf_op jit(solution)/shard_map/pallas_call | solution.py:456
  45.6 0.0 collective-permute-done.message.tables
  45.6 0.1 shard_map.95
  45.7 2.2 %collective-permute-start.8 = (bf16[256,128]{1,0:T(8,128)(2,1)S(1)}, bf16[256,128]{1,0:T(8,128)(2,1)S(1)}, u32[]{:S(2)}, u32[]{:S(2)}) collective-permute-start(bf16[256,128]{1,0:T(8,128)(2,1)S(1)} %get-tuple-element.72.refs_2_), channel_id=1, source_target_pairs={{0,1},{1,0},{2,3},{3,2},{4,5},{5,4},{6,7},{7,6},{8,9},{9,8},{10,11... | collective-permute-start | bytes 196616 | tf_op jit(solution)/shard_map/ppermute | solution.py:493
  47.9 0.1 collective-permute-start.9
  48.0 0.8 %collective-permute-done.8.refs_0_ = bf16[256,128]{1,0:T(8,128)(2,1)S(1)} collective-permute-done((bf16[256,128]{1,0:T(8,128)(2,1)S(1)}, bf16[256,128]{1,0:T(8,128)(2,1)S(1)}, u32[]{:S(2)}, u32[]{:S(2)}) %collective-permute-start.8) | collective-permute-done | bytes 65568 | tf_op jit(solution)/shard_map/ppermute | solution.py:493
  48.8 0.4 collective-permute-done.9.refs_1_
  49.2 0.6 %shard_map.96 = (bf16[4,2,256,512]{3,2,1,0:T(8,128)(2,1)}, bf16[4,4,2048]{2,1,0:T(4,128)(2,1)}, bf16[2,32,256]{2,1,0:T(8,128)(2,1)S(1)}, bf16[2,32,256]{2,1,0:T(...) custom-call(bf16[4,2,32,128]{3,2,1,0:T(8,128)(2,1)S(1)} %get-tuple-e, ...), custom_call_target="tpu_custom_call", output_to_operand_aliasing={{0}: (6, {}), {1}: (7, {})} | custom-call | flops 8388608 | bytes 1048576 | tf_op jit(solution)/shard_map/pallas_call | solution.py:456
  49.8 0.0 collective-permute-done.11.message
  49.8 0.1 shard_map.97
  49.9 1.3 %collective-permute-start.12 = (bf16[256,128]{1,0:T(8,128)(2,1)S(1)}, bf16[256,128]{1,0:T(8,128)(2,1)S(1)}, u32[]{:S(2)}, u32[]{:S(2)}) collective-permute-start(bf16[256,128]{1,0:T(8,128)(2,1)S(1)} %get-tuple-element.84.refs_0_), channel_id=1, source_target_pairs={{0,1},{1,0},{2,3},{3,2},{4,5},{5,4},{6,7},{7,6},{8,9},{9,8},{10,11... | collective-permute-start | bytes 196616 | tf_op jit(solution)/shard_map/ppermute | solution.py:493
  51.2 0.1 collective-permute-start.13
  51.3 0.9 %shard_map.98 = (bf16[4,2,256,512]{3,2,1,0:T(8,128)(2,1)}, bf16[4,4,2048]{2,1,0:T(4,128)(2,1)}) custom-call(bf16[512,128]{1,0:T(8,128)(2,1)S(1)} %get-tuple-element.71.mine, bf16[256,128]{1,0:T(8,128)(2,1)S(1)} %get-tuple-element.84.refs_0_, bf16[256,128]{1,0:T(8,128)(2,1)S(1)} %get-tuple-element.85.refs_1_, ...), custom_call_target="tpu_custom_call", output_to_operand_aliasing={{0}: (5, {}), {1}: (6, {})} | custom-call | bytes 1048576 | tf_op jit(solution)/shard_map/pallas_call | solution.py:456
  52.2 0.6 %collective-permute-done.10.message = bf16[544,128]{1,0:T(8,128)(2,1)S(1)} collective-permute-done((bf16[544,128]{1,0:T(8,128)(2,1)S(1)}, bf16[544,128]{1,0:T(8,128)(2,1)S(1)}, u32[]{:S(2)}, u32[]{:S(2)}) %collective-permute-start.10) | collective-permute-done | bytes 139296 | tf_op jit(solution)/shard_map/ppermute | solution.py:489
  52.8 0.0 collective-permute-done.12.refs_0_
  52.8 0.0 collective-permute-done.13.refs_1_
  52.8 0.9 %shard_map.99 = (bf16[4,2,256,512]{3,2,1,0:T(8,128)(2,1)}, bf16[4,4,2048]{2,1,0:T(4,128)(2,1)}) custom-call(bf16[2,32,256]{2,1,0:T(8,128)(2,1)S(1)} %get-tuple-element.76.weights, bf16[2,32,256]{2,1,0:T(8,128)(2,1)S(1)} %get-tuple-element.77.lent, f32[2,32,128]{2,1,0:T(8,128)S(1)} %get-tuple-element.78.share, ...), custom_call_target="tpu_custom_call", output_to_operand_aliasing={{0}: (8, {}), {1}: (9, {})} | custom-call | flops 4194304 | bytes 1048576 | tf_op jit(solution)/shard_map/pallas_call | solution.py:456
Async XLA Ops:
  2.4 18.7 %collective-permute-start.5 = (bf16[1088,128]{1,0:T(8,128)(2,1)S(1)}, bf16[1088,128]{1,0:T(8,128)(2,1)S(1)}, u32[]{:S(2)}, u32[]{:S(2)}) collective-permute-start(bf16[1088,128]{1,0:T(8,128)(2,1)S(1)} %shard_map.89), channel_id=1, source_target_pairs={{0,12},{4,8},{8,0},{12,4},{1,13},{5,9},{9,1},{13,5},{2,14},{6,10},... | collective-permute-start | bytes 835592 | tf_op jit(solution)/shard_map/ppermute | solution.py:489
  6.1 21.0 %collective-permute-start.4 = (bf16[1104,128]{1,0:T(8,128)(2,1)S(1)}, bf16[1104,128]{1,0:T(8,128)(2,1)S(1)}, u32[]{:S(2)}, u32[]{:S(2)}) collective-permute-start(bf16[1104,128]{1,0:T(8,128)(2,1)S(1)} %get-tuple-element.54), channel_id=1, source_target_pairs={{0,12},{4,8},{8,0},{12,4},{1,13},{5,9},{9,1},{13,5},{2,14},{6,10},... | collective-permute-start | bytes 847880 | tf_op jit(solution)/shard_map/ppermute | solution.py:489
  6.2 30.0 %collective-permute-start.1 = (bf16[1104,128]{1,0:T(8,128)(2,1)S(1)}, bf16[1104,128]{1,0:T(8,128)(2,1)S(1)}, u32[]{:S(2)}, u32[]{:S(2)}) collective-permute-start(bf16[1104,128]{1,0:T(8,128)(2,1)S(1)} %get-tuple-element.49), channel_id=1, source_target_pairs={{0,4},{4,0},{8,12},{12,8},{1,5},{5,1},{9,13},{13,9},{2,6},{6,2},{1... | collective-permute-start | bytes 847880 | tf_op jit(solution)/shard_map/ppermute | solution.py:489
  8.5 27.7 %collective-permute-start.2 = (bf16[1088,128]{1,0:T(8,128)(2,1)S(1)}, bf16[1088,128]{1,0:T(8,128)(2,1)S(1)}, u32[]{:S(2)}, u32[]{:S(2)}) collective-permute-start(bf16[1088,128]{1,0:T(8,128)(2,1)S(1)} %get-tuple-element.50), channel_id=1, source_target_pairs={{0,4},{4,0},{8,12},{12,8},{1,5},{5,1},{9,13},{13,9},{2,6},{6,2},{1... | collective-permute-start | bytes 835592 | tf_op jit(solution)/shard_map/ppermute | solution.py:489
  8.7 21.3 %collective-permute-start.3 = (bf16[1024,128]{1,0:T(8,128)(2,1)S(1)}, bf16[1024,128]{1,0:T(8,128)(2,1)S(1)}, u32[]{:S(2)}, u32[]{:S(2)}) collective-permute-start(bf16[1024,128]{1,0:T(8,128)(2,1)S(1)} %get-tuple-element.53.theirs), channel_id=1, source_target_pairs={{0,1},{1,0},{2,3},{3,2},{4,5},{5,4},{6,7},{7,6},{8,9},{9,8},{10,11... | collective-permute-start | bytes 786440 | tf_op jit(solution)/shard_map/ppermute | solution.py:493
  21.1 24.5 %collective-permute-start = (bf16[1104,128]{1,0:T(8,128)(2,1)S(1)}, bf16[1104,128]{1,0:T(8,128)(2,1)S(1)}, u32[]{:S(2)}, u32[]{:S(2)}) collective-permute-start(bf16[1104,128]{1,0:T(8,128)(2,1)S(1)} %get-tuple-element.48), channel_id=1, source_target_pairs={{0,8},{4,12},{8,4},{12,0},{1,9},{5,13},{9,5},{13,1},{2,10},{6,14},... | collective-permute-start | bytes 847880 | tf_op jit(solution)/shard_map/ppermute | solution.py:489
  27.3 15.5 %collective-permute-start.7 = (bf16[1024,128]{1,0:T(8,128)(2,1)S(1)}, bf16[1024,128]{1,0:T(8,128)(2,1)S(1)}, u32[]{:S(2)}, u32[]{:S(2)}) collective-permute-start(bf16[1024,128]{1,0:T(8,128)(2,1)S(1)} %get-tuple-element.64.theirs), channel_id=1, source_target_pairs={{0,1},{1,0},{2,3},{3,2},{4,5},{5,4},{6,7},{7,6},{8,9},{9,8},{10,11... | collective-permute-start | bytes 786440 | tf_op jit(solution)/shard_map/ppermute | solution.py:493
  36.4 7.8 %collective-permute-start.6 = (bf16[1024,128]{1,0:T(8,128)(2,1)S(1)}, bf16[1024,128]{1,0:T(8,128)(2,1)S(1)}, u32[]{:S(2)}, u32[]{:S(2)}) collective-permute-start(bf16[1024,128]{1,0:T(8,128)(2,1)S(1)} %get-tuple-element.62.theirs), channel_id=1, source_target_pairs={{0,1},{1,0},{2,3},{3,2},{4,5},{5,4},{6,7},{7,6},{8,9},{9,8},{10,11... | collective-permute-start | bytes 786440 | tf_op jit(solution)/shard_map/ppermute | solution.py:493
  38.6 11.2 %collective-permute-start.11 = (bf16[544,128]{1,0:T(8,128)(2,1)S(1)}, bf16[544,128]{1,0:T(8,128)(2,1)S(1)}, u32[]{:S(2)}, u32[]{:S(2)}) collective-permute-start(bf16[544,128]{1,0:T(8,128)(2,1)S(1)} %get-tuple-element.81), channel_id=1, source_target_pairs={{0,8},{4,12},{8,4},{12,0},{1,9},{5,13},{9,5},{13,1},{2,10},{6,14},... | collective-permute-start | bytes 417800 | tf_op jit(solution)/shard_map/ppermute | solution.py:489
  38.6 14.2 %collective-permute-start.10 = (bf16[544,128]{1,0:T(8,128)(2,1)S(1)}, bf16[544,128]{1,0:T(8,128)(2,1)S(1)}, u32[]{:S(2)}, u32[]{:S(2)}) collective-permute-start(bf16[544,128]{1,0:T(8,128)(2,1)S(1)} %get-tuple-element.80), channel_id=1, source_target_pairs={{0,8},{4,12},{8,4},{12,0},{1,9},{5,13},{9,5},{13,1},{2,10},{6,14},... | collective-permute-start | bytes 417800 | tf_op jit(solution)/shard_map/ppermute | solution.py:489
  45.7 3.1 %collective-permute-start.8 = (bf16[256,128]{1,0:T(8,128)(2,1)S(1)}, bf16[256,128]{1,0:T(8,128)(2,1)S(1)}, u32[]{:S(2)}, u32[]{:S(2)}) collective-permute-start(bf16[256,128]{1,0:T(8,128)(2,1)S(1)} %get-tuple-element.72.refs_2_), channel_id=1, source_target_pairs={{0,1},{1,0},{2,3},{3,2},{4,5},{5,4},{6,7},{7,6},{8,9},{9,8},{10,11... | collective-permute-start | bytes 196616 | tf_op jit(solution)/shard_map/ppermute | solution.py:493
  47.9 1.3 %collective-permute-start.9 = (bf16[256,128]{1,0:T(8,128)(2,1)S(1)}, bf16[256,128]{1,0:T(8,128)(2,1)S(1)}, u32[]{:S(2)}, u32[]{:S(2)}) collective-permute-start(bf16[256,128]{1,0:T(8,128)(2,1)S(1)} %get-tuple-element.73.refs_3_), channel_id=1, source_target_pairs={{0,1},{1,0},{2,3},{3,2},{4,5},{5,4},{6,7},{7,6},{8,9},{9,8},{10,11... | collective-permute-start | bytes 196616 | tf_op jit(solution)/shard_map/ppermute | solution.py:493
  49.9 2.9 %collective-permute-start.12 = (bf16[256,128]{1,0:T(8,128)(2,1)S(1)}, bf16[256,128]{1,0:T(8,128)(2,1)S(1)}, u32[]{:S(2)}, u32[]{:S(2)}) collective-permute-start(bf16[256,128]{1,0:T(8,128)(2,1)S(1)} %get-tuple-element.84.refs_0_), channel_id=1, source_target_pairs={{0,1},{1,0},{2,3},{3,2},{4,5},{5,4},{6,7},{7,6},{8,9},{9,8},{10,11... | collective-permute-start | bytes 196616 | tf_op jit(solution)/shard_map/ppermute | solution.py:493
  51.2 1.6 %collective-permute-start.13 = (bf16[256,128]{1,0:T(8,128)(2,1)S(1)}, bf16[256,128]{1,0:T(8,128)(2,1)S(1)}, u32[]{:S(2)}, u32[]{:S(2)}) collective-permute-start(bf16[256,128]{1,0:T(8,128)(2,1)S(1)} %get-tuple-element.85.refs_1_), channel_id=1, source_target_pairs={{0,1},{1,0},{2,3},{3,2},{4,5},{5,4},{6,7},{7,6},{8,9},{9,8},{10,11... | collective-permute-start | bytes 196616 | tf_op jit(solution)/shard_map/ppermute | solution.py:493

commit v18 on v17

--- a/solution.py
+++ b/solution.py
@@ -526,13 +526,7 @@
     tables = message[last, (0,)]
     state, key_mine, theirs = rebuild(size, (0,), [tables], state, split)
     keys = theirs if split else (theirs,)
-    half = pltpu.VMEM((size.mine, size.wide, size.span), BF)
-    state, (weights, lent, share, totals) = chained_call(
-        size, functools.partial(weights_kernel, size, last, split),
-        (query, fresh, tables, key_mine, *[swapped(x) for x in keys]), state,
-        [half, half, wide, wide], [], flops // 2,
-    )
-    given = pltpu.VMEM((size.mine * size.span, HEAD_DIM), BF)
+    key_others = [swapped(x) for x in keys]
     if split:
         head = pltpu.VMEM((size.span, HEAD_DIM), BF)
         state, theirs = chained_call(
@@ -540,6 +534,14 @@
             [head] * size.mine, [], flops // 8,
         )
         others = [swapped(x) for x in theirs]
+    half = pltpu.VMEM((size.mine, size.wide, size.span), BF)
+    state, (weights, lent, share, totals) = chained_call(
+        size, functools.partial(weights_kernel, size, last, split),
+        (query, fresh, tables, key_mine, *key_others), state,
+        [half, half, wide, wide], [], flops // 2,
+    )
+    given = pltpu.VMEM((size.mine * size.span, HEAD_DIM), BF)
+    if split:
         state, _ = chained_call(
             size, functools.partial(lent_store_kernel, size, last), (key_mine, *theirs, *keys), state,
             [], [sems, sems], 0,

time: 54.3 us -> 54.7 us (level)
  starting transfers between devices: 18.2 us -> 19.8 us
  waiting for transfers between devices: 22.5 us -> 20.9 us
    ppermute x7, starting transfers between devices: 10.2 us -> 11.8 us  [swapped(): return lax.ppermute(x, 'sub', [(0, 1), (1, 0)])]
    ppermute x7, waiting for transfers between devices: 1.19 us -> 0.02 us  [swapped(): return lax.ppermute(x, 'sub', [(0, 1), (1, 0)])]
  transfers between devices with their start and end apart: 14 -> 14, of which waited for: 6 -> 4; matrix products, arithmetic and copies ran while one was open for 0% -> 0% of each run, Pallas kernels for 18% -> 18%
where the time goes in v18:
time: 54.7 us; the launch traced here: 53.8 us
  waiting for transfers between devices  20.9 us (38%)
  starting transfers between devices  19.8 us (36%)
  Pallas kernels  12.3 us (22%)
  between operations  0.75 us (1%)
    ppermute x7, waiting for transfers between devices, body(): msg = lax.ppermute(msg, 'pool', list(enumerate(far(n, k))))  20.9 us
    ppermute x7, starting transfers between devices, swapped(): return lax.ppermute(x, 'sub', [(0, 1), (1, 0)])  11.8 us
    ppermute x7, starting transfers between devices, body(): msg = lax.ppermute(msg, 'pool', list(enumerate(far(n, k))))  8.04 us
    pallas_call x7, Pallas kernels, chained_call(): pl.pallas_call(kernel, in_specs=[IN_VMEM] * many + [IN_HBM, IN_HBM], out_...  6.48 us
    pallas_call x2, Pallas kernels, pack(): pl.pallas_call(functools.partial(pack_kernel, size, plan), out_shape=shap...  4.14 us
  transfers between devices with their start and end apart: 14, of which 4 were waited for; matrix products, arithmetic and copies ran while one was open for 0% of the time, Pallas kernels for 18%

profile of v18, /device:TPU:9, one launch (start us, length us, event | category | flops | bytes accessed | tf_op | source)
XLA Modules:
  0.0 53.8 jit_solution(9834241397639968646)
XLA Ops:
  0.6 1.7 %shard_map.89 = bf16[1088,128]{1,0:T(8,128)(2,1)S(1)} custom-call(s32[4]{0:T(128)} %route.3, s32[4]{0:T(128)} %lengths.3, bf16[4,2,256,512]{3,2,1,0:T(8,128)(2,1)} %deltas.3, bf16[4,2,16,512]{3,2,1,0:T(8,128)(2,1)} %anchors.3, bf16[4,2,512]{2,1,0:T(2,128)(2,1)} %scale.3), custom_call_target="tpu_custom_call" | custom-call | bytes 262144 | tf_op jit(solution)/shard_map/pallas_call | solution.py:144
  2.4 1.3 %collective-permute-start.5 = (bf16[1088,128]{1,0:T(8,128)(2,1)S(1)}, bf16[1088,128]{1,0:T(8,128)(2,1)S(1)}, u32[]{:S(2)}, u32[]{:S(2)}) collective-permute-start(bf16[1088,128]{1,0:T(8,128)(2,1)S(1)} %shard_map.89), channel_id=1, source_target_pairs={{0,12},{4,8},{8,0},{12,4},{1,13},{5,9},{9,1},{13,5},{2,14},{6,10},... | collective-permute-start | bytes 835592 | tf_op jit(solution)/shard_map/ppermute | solution.py:489
  3.7 2.4 %shard_map.87 = (bf16[1104,128]{1,0:T(8,128)(2,1)S(1)}, bf16[1104,128]{1,0:T(8,128)(2,1)S(1)}, bf16[1088,128]{1,0:T(8,128)(2,1)S(1)}, bf16[1104,128]{1,0:T(8,128...) custom-call(s32[4]{0:T(128)} %route.3, s32[4]{0:T(128)} %lengths.3, ...), custom_call_target="tpu_custom_call" | custom-call | bytes 1835008 | tf_op jit(solution)/shard_map/pallas_call | solution.py:144
  6.1 0.1 collective-permute-start.4
  6.2 2.3 %collective-permute-start.1 = (bf16[1104,128]{1,0:T(8,128)(2,1)S(1)}, bf16[1104,128]{1,0:T(8,128)(2,1)S(1)}, u32[]{:S(2)}, u32[]{:S(2)}) collective-permute-start(bf16[1104,128]{1,0:T(8,128)(2,1)S(1)} %get-tuple-element.49), channel_id=1, source_target_pairs={{0,4},{4,0},{8,12},{12,8},{1,5},{5,1},{9,13},{13,9},{2,6},{6,2},{1... | collective-permute-start | bytes 847880 | tf_op jit(solution)/shard_map/ppermute | solution.py:489
  8.5 0.1 collective-permute-start.2
  8.5 0.2 shard_map.88
  8.7 1.5 %collective-permute-start.3 = (bf16[1024,128]{1,0:T(8,128)(2,1)S(1)}, bf16[1024,128]{1,0:T(8,128)(2,1)S(1)}, u32[]{:S(2)}, u32[]{:S(2)}) collective-permute-start(bf16[1024,128]{1,0:T(8,128)(2,1)S(1)} %get-tuple-element.53.theirs), channel_id=1, source_target_pairs={{0,1},{1,0},{2,3},{3,2},{4,5},{5,4},{6,7},{7,6},{8,9},{9,8},{10,11... | collective-permute-start | bytes 786440 | tf_op jit(solution)/shard_map/ppermute | solution.py:493
  10.2 10.8 %collective-permute-done.5.refs_0_ = bf16[1088,128]{1,0:T(8,128)(2,1)S(1)} collective-permute-done((bf16[1088,128]{1,0:T(8,128)(2,1)S(1)}, bf16[1088,128]{1,0:T(8,128)(2,1)S(1)}, u32[]{:S(2)}, u32[]{:S(2)}) %collective-permute-start.5) | collective-permute-done | bytes 278560 | tf_op jit(solution)/shard_map/ppermute | solution.py:489
  21.1 0.0 collective-permute-start
  21.1 0.9 %shard_map.86 = (bf16[4,2,32,128]{3,2,1,0:T(8,128)(2,1)S(1)}, bf16[4,2,2,16,128]{4,3,2,1,0:T(8,128)(2,1)S(1)}) custom-call(bf16[4,4,2048]{2,1,0:T(4,128)(2,1)} %new_query.1, bf16[4,2,4,512]{3,2,1,0:T(4,128)(2,1)} %new_kv.1), custom_call_target="tpu_custom_call" | custom-call | tf_op jit(solution)/shard_map/pallas_call | solution.py:181
  22.0 5.1 %collective-permute-done.4.message.tables = bf16[1104,128]{1,0:T(8,128)(2,1)S(1)} collective-permute-done((bf16[1104,128]{1,0:T(8,128)(2,1)S(1)}, bf16[1104,128]{1,0:T(8,128)(2,1)S(1)}, u32[]{:S(2)}, u32[]{:S(2)}) %collective-permute-start.4) | collective-permute-done | bytes 282656 | tf_op jit(solution)/shard_map/ppermute | solution.py:489
  27.1 0.2 shard_map.90
  27.3 2.7 %collective-permute-start.7 = (bf16[1024,128]{1,0:T(8,128)(2,1)S(1)}, bf16[1024,128]{1,0:T(8,128)(2,1)S(1)}, u32[]{:S(2)}, u32[]{:S(2)}) collective-permute-start(bf16[1024,128]{1,0:T(8,128)(2,1)S(1)} %get-tuple-element.64.theirs), channel_id=1, source_target_pairs={{0,1},{1,0},{2,3},{3,2},{4,5},{5,4},{6,7},{7,6},{8,9},{9,8},{10,11... | collective-permute-start | bytes 786440 | tf_op jit(solution)/shard_map/ppermute | solution.py:493
  30.1 0.0 collective-permute-done.3.other
  30.1 1.3 %shard_map.91 = (bf16[4,2,256,512]{3,2,1,0:T(8,128)(2,1)}, bf16[4,4,2048]{2,1,0:T(4,128)(2,1)}) custom-call(bf16[4,2,32,128]{3,2,1,0:T(8,128)(2,1)S(1)} %get-tuple-element.46.query, bf16[4,2,2,16,128]{4,3,2,1,0:T(8,128)(2,1)S(1)} %get-tuple-element.47.new_kv, ...), custom_call_target="tpu_custom_call", output_to_operand_aliasing={{0}: (6, {}), {1}: (7, {})} | custom-call | flops 16777216 | bytes 1048576 | tf_op jit(solution)/shard_map/pallas_call | solution.py:456
  31.4 4.8 %collective-permute-done.2.refs_0_ = bf16[1088,128]{1,0:T(8,128)(2,1)S(1)} collective-permute-done((bf16[1088,128]{1,0:T(8,128)(2,1)S(1)}, bf16[1088,128]{1,0:T(8,128)(2,1)S(1)}, u32[]{:S(2)}, u32[]{:S(2)}) %collective-permute-start.2) | collective-permute-done | bytes 278560 | tf_op jit(solution)/shard_map/ppermute | solution.py:489
  36.2 0.0 collective-permute-done.1.message.tables
  36.2 0.2 shard_map.92
  36.4 2.2 %collective-permute-start.6 = (bf16[1024,128]{1,0:T(8,128)(2,1)S(1)}, bf16[1024,128]{1,0:T(8,128)(2,1)S(1)}, u32[]{:S(2)}, u32[]{:S(2)}) collective-permute-start(bf16[1024,128]{1,0:T(8,128)(2,1)S(1)} %get-tuple-element.62.theirs), channel_id=1, source_target_pairs={{0,1},{1,0},{2,3},{3,2},{4,5},{5,4},{6,7},{7,6},{8,9},{9,8},{10,11... | collective-permute-start | bytes 786440 | tf_op jit(solution)/shard_map/ppermute | solution.py:493
  38.6 0.0 collective-permute-start.10
  38.6 4.3 %collective-permute-start.11 = (bf16[544,128]{1,0:T(8,128)(2,1)S(1)}, bf16[544,128]{1,0:T(8,128)(2,1)S(1)}, u32[]{:S(2)}, u32[]{:S(2)}) collective-permute-start(bf16[544,128]{1,0:T(8,128)(2,1)S(1)} %get-tuple-element.83), channel_id=1, source_target_pairs={{0,8},{4,12},{8,4},{12,0},{1,9},{5,13},{9,5},{13,1},{2,10},{6,14},... | collective-permute-start | bytes 417800 | tf_op jit(solution)/shard_map/ppermute | solution.py:489
  42.9 0.0 collective-permute-done.7.other
  42.9 1.3 %shard_map.93 = (bf16[4,2,256,512]{3,2,1,0:T(8,128)(2,1)}, bf16[4,4,2048]{2,1,0:T(4,128)(2,1)}) custom-call(bf16[4,2,32,128]{3,2,1,0:T(8,128)(2,1)S(1)} %get-tuple-element.46.query, bf16[4,2,2,16,128]{4,3,2,1,0:T(8,128)(2,1)S(1)} %get-tuple-element.47.new_kv, ...), custom_call_target="tpu_custom_call", output_to_operand_aliasing={{0}: (6, {}), {1}: (7, {})} | custom-call | flops 16777216 | bytes 1048576 | tf_op jit(solution)/shard_map/pallas_call | solution.py:456
  44.2 0.0 collective-permute-done.6.other
  44.2 1.3 %shard_map.94 = (bf16[4,2,256,512]{3,2,1,0:T(8,128)(2,1)}, bf16[4,4,2048]{2,1,0:T(4,128)(2,1)}) custom-call(bf16[4,2,32,128]{3,2,1,0:T(8,128)(2,1)S(1)} %get-tuple-element.46.query, bf16[4,2,2,16,128]{4,3,2,1,0:T(8,128)(2,1)S(1)} %get-tuple-element.47.new_kv, ...), custom_call_target="tpu_custom_call", output_to_operand_aliasing={{0}: (6, {}), {1}: (7, {})} | custom-call | flops 16777216 | bytes 1048576 | tf_op jit(solution)/shard_map/pallas_call | solution.py:456
  45.6 0.0 collective-permute-done.message.tables
  45.6 0.1 shard_map.95
  45.7 2.2 %collective-permute-start.8 = (bf16[256,128]{1,0:T(8,128)(2,1)S(1)}, bf16[256,128]{1,0:T(8,128)(2,1)S(1)}, u32[]{:S(2)}, u32[]{:S(2)}) collective-permute-start(bf16[256,128]{1,0:T(8,128)(2,1)S(1)} %get-tuple-element.72.refs_2_), channel_id=1, source_target_pairs={{0,1},{1,0},{2,3},{3,2},{4,5},{5,4},{6,7},{7,6},{8,9},{9,8},{10,11... | collective-permute-start | bytes 196616 | tf_op jit(solution)/shard_map/ppermute | solution.py:493
  47.9 0.1 collective-permute-start.9
  48.0 0.2 collective-permute-done.10.message
  48.2 0.1 shard_map.96
  48.3 2.9 %collective-permute-start.12 = (bf16[256,128]{1,0:T(8,128)(2,1)S(1)}, bf16[256,128]{1,0:T(8,128)(2,1)S(1)}, u32[]{:S(2)}, u32[]{:S(2)}) collective-permute-start(bf16[256,128]{1,0:T(8,128)(2,1)S(1)} %get-tuple-element.84.refs_0_), channel_id=1, source_target_pairs={{0,1},{1,0},{2,3},{3,2},{4,5},{5,4},{6,7},{7,6},{8,9},{9,8},{10,11... | collective-permute-start | bytes 196616 | tf_op jit(solution)/shard_map/ppermute | solution.py:493
  51.2 0.1 collective-permute-start.13
  51.3 0.0 collective-permute-done.8.refs_0_
  51.3 0.0 collective-permute-done.9.refs_1_
  51.3 0.6 %shard_map.97 = (bf16[4,2,256,512]{3,2,1,0:T(8,128)(2,1)}, bf16[4,4,2048]{2,1,0:T(4,128)(2,1)}, bf16[2,32,256]{2,1,0:T(8,128)(2,1)S(1)}, bf16[2,32,256]{2,1,0:T(...) custom-call(bf16[4,2,32,128]{3,2,1,0:T(8,128)(2,1)S(1)} %get-tuple-e, ...), custom_call_target="tpu_custom_call", output_to_operand_aliasing={{0}: (6, {}), {1}: (7, {})} | custom-call | flops 8388608 | bytes 1048576 | tf_op jit(solution)/shard_map/pallas_call | solution.py:456
  51.9 0.9 %shard_map.98 = (bf16[4,2,256,512]{3,2,1,0:T(8,128)(2,1)}, bf16[4,4,2048]{2,1,0:T(4,128)(2,1)}) custom-call(bf16[512,128]{1,0:T(8,128)(2,1)S(1)} %get-tuple-element.71.mine, bf16[256,128]{1,0:T(8,128)(2,1)S(1)} %get-tuple-element.84.refs_0_, bf16[256,128]{1,0:T(8,128)(2,1)S(1)} %get-tuple-element.85.refs_1_, ...), custom_call_target="tpu_custom_call", output_to_operand_aliasing={{0}: (5, {}), {1}: (6, {})} | custom-call | bytes 1048576 | tf_op jit(solution)/shard_map/pallas_call | solution.py:456
  52.8 0.0 collective-permute-done.11.message
  52.8 0.0 collective-permute-done.12.refs_0_
  52.8 0.0 collective-permute-done.13.refs_1_
  52.8 0.9 %shard_map.99 = (bf16[4,2,256,512]{3,2,1,0:T(8,128)(2,1)}, bf16[4,4,2048]{2,1,0:T(4,128)(2,1)}) custom-call(bf16[2,32,256]{2,1,0:T(8,128)(2,1)S(1)} %get-tuple-element.79.weights, bf16[2,32,256]{2,1,0:T(8,128)(2,1)S(1)} %get-tuple-element.80.lent, f32[2,32,128]{2,1,0:T(8,128)S(1)} %get-tuple-element.81.share, ...), custom_call_target="tpu_custom_call", output_to_operand_aliasing={{0}: (8, {}), {1}: (9, {})} | custom-call | flops 4194304 | bytes 1048576 | tf_op jit(solution)/shard_map/pallas_call | solution.py:456
Async XLA Ops:
  2.4 18.7 %collective-permute-start.5 = (bf16[1088,128]{1,0:T(8,128)(2,1)S(1)}, bf16[1088,128]{1,0:T(8,128)(2,1)S(1)}, u32[]{:S(2)}, u32[]{:S(2)}) collective-permute-start(bf16[1088,128]{1,0:T(8,128)(2,1)S(1)} %shard_map.89), channel_id=1, source_target_pairs={{0,12},{4,8},{8,0},{12,4},{1,13},{5,9},{9,1},{13,5},{2,14},{6,10},... | collective-permute-start | bytes 835592 | tf_op jit(solution)/shard_map/ppermute | solution.py:489
  6.1 21.0 %collective-permute-start.4 = (bf16[1104,128]{1,0:T(8,128)(2,1)S(1)}, bf16[1104,128]{1,0:T(8,128)(2,1)S(1)}, u32[]{:S(2)}, u32[]{:S(2)}) collective-permute-start(bf16[1104,128]{1,0:T(8,128)(2,1)S(1)} %get-tuple-element.54), channel_id=1, source_target_pairs={{0,12},{4,8},{8,0},{12,4},{1,13},{5,9},{9,1},{13,5},{2,14},{6,10},... | collective-permute-start | bytes 847880 | tf_op jit(solution)/shard_map/ppermute | solution.py:489
  6.2 30.0 %collective-permute-start.1 = (bf16[1104,128]{1,0:T(8,128)(2,1)S(1)}, bf16[1104,128]{1,0:T(8,128)(2,1)S(1)}, u32[]{:S(2)}, u32[]{:S(2)}) collective-permute-start(bf16[1104,128]{1,0:T(8,128)(2,1)S(1)} %get-tuple-element.49), channel_id=1, source_target_pairs={{0,4},{4,0},{8,12},{12,8},{1,5},{5,1},{9,13},{13,9},{2,6},{6,2},{1... | collective-permute-start | bytes 847880 | tf_op jit(solution)/shard_map/ppermute | solution.py:489
  8.5 27.7 %collective-permute-start.2 = (bf16[1088,128]{1,0:T(8,128)(2,1)S(1)}, bf16[1088,128]{1,0:T(8,128)(2,1)S(1)}, u32[]{:S(2)}, u32[]{:S(2)}) collective-permute-start(bf16[1088,128]{1,0:T(8,128)(2,1)S(1)} %get-tuple-element.50), channel_id=1, source_target_pairs={{0,4},{4,0},{8,12},{12,8},{1,5},{5,1},{9,13},{13,9},{2,6},{6,2},{1... | collective-permute-start | bytes 835592 | tf_op jit(solution)/shard_map/ppermute | solution.py:489
  8.7 21.3 %collective-permute-start.3 = (bf16[1024,128]{1,0:T(8,128)(2,1)S(1)}, bf16[1024,128]{1,0:T(8,128)(2,1)S(1)}, u32[]{:S(2)}, u32[]{:S(2)}) collective-permute-start(bf16[1024,128]{1,0:T(8,128)(2,1)S(1)} %get-tuple-element.53.theirs), channel_id=1, source_target_pairs={{0,1},{1,0},{2,3},{3,2},{4,5},{5,4},{6,7},{7,6},{8,9},{9,8},{10,11... | collective-permute-start | bytes 786440 | tf_op jit(solution)/shard_map/ppermute | solution.py:493
  21.1 24.5 %collective-permute-start = (bf16[1104,128]{1,0:T(8,128)(2,1)S(1)}, bf16[1104,128]{1,0:T(8,128)(2,1)S(1)}, u32[]{:S(2)}, u32[]{:S(2)}) collective-permute-start(bf16[1104,128]{1,0:T(8,128)(2,1)S(1)} %get-tuple-element.48), channel_id=1, source_target_pairs={{0,8},{4,12},{8,4},{12,0},{1,9},{5,13},{9,5},{13,1},{2,10},{6,14},... | collective-permute-start | bytes 847880 | tf_op jit(solution)/shard_map/ppermute | solution.py:489
  27.3 15.5 %collective-permute-start.7 = (bf16[1024,128]{1,0:T(8,128)(2,1)S(1)}, bf16[1024,128]{1,0:T(8,128)(2,1)S(1)}, u32[]{:S(2)}, u32[]{:S(2)}) collective-permute-start(bf16[1024,128]{1,0:T(8,128)(2,1)S(1)} %get-tuple-element.64.theirs), channel_id=1, source_target_pairs={{0,1},{1,0},{2,3},{3,2},{4,5},{5,4},{6,7},{7,6},{8,9},{9,8},{10,11... | collective-permute-start | bytes 786440 | tf_op jit(solution)/shard_map/ppermute | solution.py:493
  36.4 7.8 %collective-permute-start.6 = (bf16[1024,128]{1,0:T(8,128)(2,1)S(1)}, bf16[1024,128]{1,0:T(8,128)(2,1)S(1)}, u32[]{:S(2)}, u32[]{:S(2)}) collective-permute-start(bf16[1024,128]{1,0:T(8,128)(2,1)S(1)} %get-tuple-element.62.theirs), channel_id=1, source_target_pairs={{0,1},{1,0},{2,3},{3,2},{4,5},{5,4},{6,7},{7,6},{8,9},{9,8},{10,11... | collective-permute-start | bytes 786440 | tf_op jit(solution)/shard_map/ppermute | solution.py:493
  38.6 9.6 %collective-permute-start.10 = (bf16[544,128]{1,0:T(8,128)(2,1)S(1)}, bf16[544,128]{1,0:T(8,128)(2,1)S(1)}, u32[]{:S(2)}, u32[]{:S(2)}) collective-permute-start(bf16[544,128]{1,0:T(8,128)(2,1)S(1)} %get-tuple-element.74), channel_id=1, source_target_pairs={{0,8},{4,12},{8,4},{12,0},{1,9},{5,13},{9,5},{13,1},{2,10},{6,14},... | collective-permute-start | bytes 417800 | tf_op jit(solution)/shard_map/ppermute | solution.py:489
  38.6 14.2 %collective-permute-start.11 = (bf16[544,128]{1,0:T(8,128)(2,1)S(1)}, bf16[544,128]{1,0:T(8,128)(2,1)S(1)}, u32[]{:S(2)}, u32[]{:S(2)}) collective-permute-start(bf16[544,128]{1,0:T(8,128)(2,1)S(1)} %get-tuple-element.83), channel_id=1, source_target_pairs={{0,8},{4,12},{8,4},{12,0},{1,9},{5,13},{9,5},{13,1},{2,10},{6,14},... | collective-permute-start | bytes 417800 | tf_op jit(solution)/shard_map/ppermute | solution.py:489
  45.7 5.6 %collective-permute-start.8 = (bf16[256,128]{1,0:T(8,128)(2,1)S(1)}, bf16[256,128]{1,0:T(8,128)(2,1)S(1)}, u32[]{:S(2)}, u32[]{:S(2)}) collective-permute-start(bf16[256,128]{1,0:T(8,128)(2,1)S(1)} %get-tuple-element.72.refs_2_), channel_id=1, source_target_pairs={{0,1},{1,0},{2,3},{3,2},{4,5},{5,4},{6,7},{7,6},{8,9},{9,8},{10,11... | collective-permute-start | bytes 196616 | tf_op jit(solution)/shard_map/ppermute | solution.py:493
  47.9 3.4 %collective-permute-start.9 = (bf16[256,128]{1,0:T(8,128)(2,1)S(1)}, bf16[256,128]{1,0:T(8,128)(2,1)S(1)}, u32[]{:S(2)}, u32[]{:S(2)}) collective-permute-start(bf16[256,128]{1,0:T(8,128)(2,1)S(1)} %get-tuple-element.73.refs_3_), channel_id=1, source_target_pairs={{0,1},{1,0},{2,3},{3,2},{4,5},{5,4},{6,7},{7,6},{8,9},{9,8},{10,11... | collective-permute-start | bytes 196616 | tf_op jit(solution)/shard_map/ppermute | solution.py:493
  48.3 4.6 %collective-permute-start.12 = (bf16[256,128]{1,0:T(8,128)(2,1)S(1)}, bf16[256,128]{1,0:T(8,128)(2,1)S(1)}, u32[]{:S(2)}, u32[]{:S(2)}) collective-permute-start(bf16[256,128]{1,0:T(8,128)(2,1)S(1)} %get-tuple-element.84.refs_0_), channel_id=1, source_target_pairs={{0,1},{1,0},{2,3},{3,2},{4,5},{5,4},{6,7},{7,6},{8,9},{9,8},{10,11... | collective-permute-start | bytes 196616 | tf_op jit(solution)/shard_map/ppermute | solution.py:493
  51.2 1.6 %collective-permute-start.13 = (bf16[256,128]{1,0:T(8,128)(2,1)S(1)}, bf16[256,128]{1,0:T(8,128)(2,1)S(1)}, u32[]{:S(2)}, u32[]{:S(2)}) collective-permute-start(bf16[256,128]{1,0:T(8,128)(2,1)S(1)} %get-tuple-element.85.refs_1_), channel_id=1, source_target_pairs={{0,1},{1,0},{2,3},{3,2},{4,5},{5,4},{6,7},{7,6},{8,9},{9,8},{10,11... | collective-permute-start | bytes 196616 | tf_op jit(solution)/shard_map/ppermute | solution.py:493

commit v19 on v17

--- a/solution.py
+++ b/solution.py
@@ -516,10 +516,10 @@
         return state, mine, swapped(theirs), theirs
 
     state, held = None, []
-    for k in [0] + order[:-1]:
+    for k in [order[0], 0] + order[1:-1]:
         state, *each = take(k, both, state)
         held.append((k, *each))
-        if k:
+        if len(held) > 1:
             state = attend(*held.pop(0), state)
     state = attend(*held.pop(0), state)
     split = size.rest > 0

time: 54.3 us -> 58.1 us (1.070)
  waiting for transfers between devices: 22.5 us -> 31.2 us
  starting transfers between devices: 18.2 us -> 13.5 us
    ppermute x7, waiting for transfers between devices: 21.3 us -> 30.1 us  [body(): msg = lax.ppermute(msg, 'pool', list(enumerate(far(n, k))))]
    ppermute x7, starting transfers between devices: 10.2 us -> 4.33 us  [swapped(): return lax.ppermute(x, 'sub', [(0, 1), (1, 0)])]
    ppermute x7, starting transfers between devices: 8.04 us -> 9.22 us  [body(): msg = lax.ppermute(msg, 'pool', list(enumerate(far(n, k))))]
  transfers between devices with their start and end apart: 14 -> 14, of which waited for: 6 -> 5; matrix products, arithmetic and copies ran while one was open for 0% -> 0% of each run, Pallas kernels for 18% -> 15%
where the time goes in v19:
time: 58.1 us; the launch traced here: 57.8 us
  waiting for transfers between devices  31.2 us (54%)
  starting transfers between devices  13.5 us (23%)
  Pallas kernels  12.3 us (21%)
  between operations  0.73 us (1%)
    ppermute x7, waiting for transfers between devices, body(): msg = lax.ppermute(msg, 'pool', list(enumerate(far(n, k))))  30.1 us
    ppermute x7, starting transfers between devices, body(): msg = lax.ppermute(msg, 'pool', list(enumerate(far(n, k))))  9.22 us
    pallas_call x7, Pallas kernels, chained_call(): pl.pallas_call(kernel, in_specs=[IN_VMEM] * many + [IN_HBM, IN_HBM], out_...  6.47 us
    ppermute x7, starting transfers between devices, swapped(): return lax.ppermute(x, 'sub', [(0, 1), (1, 0)])  4.33 us
    pallas_call x2, Pallas kernels, pack(): pl.pallas_call(functools.partial(pack_kernel, size, plan), out_shape=shap...  4.15 us
    ppermute x7, waiting for transfers between devices, swapped(): return lax.ppermute(x, 'sub', [(0, 1), (1, 0)])  1.19 us
  transfers between devices with their start and end apart: 14, of which 5 were waited for; matrix products, arithmetic and copies ran while one was open for 0% of the time, Pallas kernels for 15%

profile of v19, /device:TPU:9, one launch (start us, length us, event | category | flops | bytes accessed | tf_op | source)
XLA Modules:
  0.0 57.8 jit_solution(7269213074829405264)
XLA Ops:
  0.6 2.4 %shard_map.87 = (bf16[1104,128]{1,0:T(8,128)(2,1)S(1)}, bf16[1104,128]{1,0:T(8,128)(2,1)S(1)}, bf16[1088,128]{1,0:T(8,128)(2,1)S(1)}, bf16[1104,128]{1,0:T(8,128...) custom-call(s32[4]{0:T(128)} %route.3, s32[4]{0:T(128)} %lengths.3, ...), custom_call_target="tpu_custom_call" | custom-call | bytes 1835008 | tf_op jit(solution)/shard_map/pallas_call | solution.py:144
  3.0 1.3 %collective-permute-start.3 = (bf16[1104,128]{1,0:T(8,128)(2,1)S(1)}, bf16[1104,128]{1,0:T(8,128)(2,1)S(1)}, u32[]{:S(2)}, u32[]{:S(2)}) collective-permute-start(bf16[1104,128]{1,0:T(8,128)(2,1)S(1)} %get-tuple-element.51), channel_id=1, source_target_pairs={{0,12},{4,8},{8,0},{12,4},{1,13},{5,9},{9,1},{13,5},{2,14},{6,10},... | collective-permute-start | bytes 847880 | tf_op jit(solution)/shard_map/ppermute | solution.py:489
  4.4 1.7 %shard_map.88 = bf16[1088,128]{1,0:T(8,128)(2,1)S(1)} custom-call(s32[4]{0:T(128)} %route.3, s32[4]{0:T(128)} %lengths.3, bf16[4,2,256,512]{3,2,1,0:T(8,128)(2,1)} %deltas.3, bf16[4,2,16,512]{3,2,1,0:T(8,128)(2,1)} %anchors.3, bf16[4,2,512]{2,1,0:T(2,128)(2,1)} %scale.3), custom_call_target="tpu_custom_call" | custom-call | bytes 262144 | tf_op jit(solution)/shard_map/pallas_call | solution.py:144
  6.1 0.1 collective-permute-start.4
  6.2 2.3 %collective-permute-start.1 = (bf16[1104,128]{1,0:T(8,128)(2,1)S(1)}, bf16[1104,128]{1,0:T(8,128)(2,1)S(1)}, u32[]{:S(2)}, u32[]{:S(2)}) collective-permute-start(bf16[1104,128]{1,0:T(8,128)(2,1)S(1)} %get-tuple-element.49), channel_id=1, source_target_pairs={{0,4},{4,0},{8,12},{12,8},{1,5},{5,1},{9,13},{13,9},{2,6},{6,2},{1... | collective-permute-start | bytes 847880 | tf_op jit(solution)/shard_map/ppermute | solution.py:489
  8.5 0.1 collective-permute-start.2
  8.5 19.3 %collective-permute-done.4.refs_0_ = bf16[1088,128]{1,0:T(8,128)(2,1)S(1)} collective-permute-done((bf16[1088,128]{1,0:T(8,128)(2,1)S(1)}, bf16[1088,128]{1,0:T(8,128)(2,1)S(1)}, u32[]{:S(2)}, u32[]{:S(2)}) %collective-permute-start.4) | collective-permute-done | bytes 278560 | tf_op jit(solution)/shard_map/ppermute | solution.py:489
  27.8 0.0 collective-permute-done.3.message.tables
  27.8 0.2 shard_map.89
  28.0 1.6 %collective-permute-start.5 = (bf16[1024,128]{1,0:T(8,128)(2,1)S(1)}, bf16[1024,128]{1,0:T(8,128)(2,1)S(1)}, u32[]{:S(2)}, u32[]{:S(2)}) collective-permute-start(bf16[1024,128]{1,0:T(8,128)(2,1)S(1)} %get-tuple-element.53.theirs), channel_id=1, source_target_pairs={{0,1},{1,0},{2,3},{3,2},{4,5},{5,4},{6,7},{7,6},{8,9},{9,8},{10,11... | collective-permute-start | bytes 786440 | tf_op jit(solution)/shard_map/ppermute | solution.py:493
  29.6 0.0 collective-permute-start
  29.6 0.9 %shard_map.86 = (bf16[4,2,32,128]{3,2,1,0:T(8,128)(2,1)S(1)}, bf16[4,2,2,16,128]{4,3,2,1,0:T(8,128)(2,1)S(1)}) custom-call(bf16[4,4,2048]{2,1,0:T(4,128)(2,1)} %new_query.1, bf16[4,2,4,512]{3,2,1,0:T(4,128)(2,1)} %new_kv.1), custom_call_target="tpu_custom_call" | custom-call | tf_op jit(solution)/shard_map/pallas_call | solution.py:181
  30.6 0.2 shard_map.90
  30.8 0.1 collective-permute-start.7
  30.9 0.0 collective-permute-done.5.other
  30.9 1.3 %shard_map.91 = (bf16[4,2,256,512]{3,2,1,0:T(8,128)(2,1)}, bf16[4,4,2048]{2,1,0:T(4,128)(2,1)}) custom-call(bf16[4,2,32,128]{3,2,1,0:T(8,128)(2,1)S(1)} %get-tuple-element.46.query, bf16[4,2,2,16,128]{4,3,2,1,0:T(8,128)(2,1)S(1)} %get-tuple-element.47.new_kv, ...), custom_call_target="tpu_custom_call", output_to_operand_aliasing={{0}: (6, {}), {1}: (7, {})} | custom-call | flops 16777216 | bytes 1048576 | tf_op jit(solution)/shard_map/pallas_call | solution.py:456
  32.2 0.0 collective-permute-done.2.refs_0_
  32.3 0.0 collective-permute-done.1.message.tables
  32.3 0.2 shard_map.92
  32.5 0.5 collective-permute-start.6
  33.0 4.9 %collective-permute-start.11 = (bf16[544,128]{1,0:T(8,128)(2,1)S(1)}, bf16[544,128]{1,0:T(8,128)(2,1)S(1)}, u32[]{:S(2)}, u32[]{:S(2)}) collective-permute-start(bf16[544,128]{1,0:T(8,128)(2,1)S(1)} %get-tuple-element.81), channel_id=1, source_target_pairs={{0,8},{4,12},{8,4},{12,0},{1,9},{5,13},{9,5},{13,1},{2,10},{6,14},... | collective-permute-start | bytes 417800 | tf_op jit(solution)/shard_map/ppermute | solution.py:489
  37.9 0.6 collective-permute-start.10
  38.4 0.0 collective-permute-done.7.other
  38.4 1.3 %shard_map.93 = (bf16[4,2,256,512]{3,2,1,0:T(8,128)(2,1)}, bf16[4,4,2048]{2,1,0:T(4,128)(2,1)}) custom-call(bf16[4,2,32,128]{3,2,1,0:T(8,128)(2,1)S(1)} %get-tuple-element.46.query, bf16[4,2,2,16,128]{4,3,2,1,0:T(8,128)(2,1)S(1)} %get-tuple-element.47.new_kv, ...), custom_call_target="tpu_custom_call", output_to_operand_aliasing={{0}: (6, {}), {1}: (7, {})} | custom-call | flops 16777216 | bytes 1048576 | tf_op jit(solution)/shard_map/pallas_call | solution.py:456
  39.8 0.0 collective-permute-done.6.other
  39.8 1.3 %shard_map.94 = (bf16[4,2,256,512]{3,2,1,0:T(8,128)(2,1)}, bf16[4,4,2048]{2,1,0:T(4,128)(2,1)}) custom-call(bf16[4,2,32,128]{3,2,1,0:T(8,128)(2,1)S(1)} %get-tuple-element.46.query, bf16[4,2,2,16,128]{4,3,2,1,0:T(8,128)(2,1)S(1)} %get-tuple-element.47.new_kv, ...), custom_call_target="tpu_custom_call", output_to_operand_aliasing={{0}: (6, {}), {1}: (7, {})} | custom-call | flops 16777216 | bytes 1048576 | tf_op jit(solution)/shard_map/pallas_call | solution.py:456
  41.1 9.8 %collective-permute-done.message.tables = bf16[1104,128]{1,0:T(8,128)(2,1)S(1)} collective-permute-done((bf16[1104,128]{1,0:T(8,128)(2,1)S(1)}, bf16[1104,128]{1,0:T(8,128)(2,1)S(1)}, u32[]{:S(2)}, u32[]{:S(2)}) %collective-permute-start) | collective-permute-done | bytes 282656 | tf_op jit(solution)/shard_map/ppermute | solution.py:489
  50.9 0.1 shard_map.95
  51.0 1.0 %collective-permute-start.8 = (bf16[256,128]{1,0:T(8,128)(2,1)S(1)}, bf16[256,128]{1,0:T(8,128)(2,1)S(1)}, u32[]{:S(2)}, u32[]{:S(2)}) collective-permute-start(bf16[256,128]{1,0:T(8,128)(2,1)S(1)} %get-tuple-element.72.refs_2_), channel_id=1, source_target_pairs={{0,1},{1,0},{2,3},{3,2},{4,5},{5,4},{6,7},{7,6},{8,9},{9,8},{10,11... | collective-permute-start | bytes 196616 | tf_op jit(solution)/shard_map/ppermute | solution.py:493
  52.0 0.1 collective-permute-start.9
  52.0 0.8 %collective-permute-done.8.refs_0_ = bf16[256,128]{1,0:T(8,128)(2,1)S(1)} collective-permute-done((bf16[256,128]{1,0:T(8,128)(2,1)S(1)}, bf16[256,128]{1,0:T(8,128)(2,1)S(1)}, u32[]{:S(2)}, u32[]{:S(2)}) %collective-permute-start.8) | collective-permute-done | bytes 65568 | tf_op jit(solution)/shard_map/ppermute | solution.py:493
  52.9 0.4 collective-permute-done.9.refs_1_
  53.2 0.6 %shard_map.96 = (bf16[4,2,256,512]{3,2,1,0:T(8,128)(2,1)}, bf16[4,4,2048]{2,1,0:T(4,128)(2,1)}, bf16[2,32,256]{2,1,0:T(8,128)(2,1)S(1)}, bf16[2,32,256]{2,1,0:T(...) custom-call(bf16[4,2,32,128]{3,2,1,0:T(8,128)(2,1)S(1)} %get-tuple-e, ...), custom_call_target="tpu_custom_call", output_to_operand_aliasing={{0}: (6, {}), {1}: (7, {})} | custom-call | flops 8388608 | bytes 1048576 | tf_op jit(solution)/shard_map/pallas_call | solution.py:456
  53.8 0.0 collective-permute-done.11.message
  53.9 0.1 shard_map.97
  53.9 1.0 %collective-permute-start.12 = (bf16[256,128]{1,0:T(8,128)(2,1)S(1)}, bf16[256,128]{1,0:T(8,128)(2,1)S(1)}, u32[]{:S(2)}, u32[]{:S(2)}) collective-permute-start(bf16[256,128]{1,0:T(8,128)(2,1)S(1)} %get-tuple-element.84.refs_0_), channel_id=1, source_target_pairs={{0,1},{1,0},{2,3},{3,2},{4,5},{5,4},{6,7},{7,6},{8,9},{9,8},{10,11... | collective-permute-start | bytes 196616 | tf_op jit(solution)/shard_map/ppermute | solution.py:493
  54.9 0.1 collective-permute-start.13
  55.0 0.9 %shard_map.98 = (bf16[4,2,256,512]{3,2,1,0:T(8,128)(2,1)}, bf16[4,4,2048]{2,1,0:T(4,128)(2,1)}) custom-call(bf16[512,128]{1,0:T(8,128)(2,1)S(1)} %get-tuple-element.71.mine, bf16[256,128]{1,0:T(8,128)(2,1)S(1)} %get-tuple-element.84.refs_0_, bf16[256,128]{1,0:T(8,128)(2,1)S(1)} %get-tuple-element.85.refs_1_, ...), custom_call_target="tpu_custom_call", output_to_operand_aliasing={{0}: (5, {}), {1}: (6, {})} | custom-call | bytes 1048576 | tf_op jit(solution)/shard_map/pallas_call | solution.py:456
  55.9 1.0 %collective-permute-done.10.message = bf16[544,128]{1,0:T(8,128)(2,1)S(1)} collective-permute-done((bf16[544,128]{1,0:T(8,128)(2,1)S(1)}, bf16[544,128]{1,0:T(8,128)(2,1)S(1)}, u32[]{:S(2)}, u32[]{:S(2)}) %collective-permute-start.10) | collective-permute-done | bytes 139296 | tf_op jit(solution)/shard_map/ppermute | solution.py:489
  56.9 0.0 collective-permute-done.12.refs_0_
  56.9 0.0 collective-permute-done.13.refs_1_
  56.9 0.9 %shard_map.99 = (bf16[4,2,256,512]{3,2,1,0:T(8,128)(2,1)}, bf16[4,4,2048]{2,1,0:T(4,128)(2,1)}) custom-call(bf16[2,32,256]{2,1,0:T(8,128)(2,1)S(1)} %get-tuple-element.76.weights, bf16[2,32,256]{2,1,0:T(8,128)(2,1)S(1)} %get-tuple-element.77.lent, f32[2,32,128]{2,1,0:T(8,128)S(1)} %get-tuple-element.78.share, ...), custom_call_target="tpu_custom_call", output_to_operand_aliasing={{0}: (8, {}), {1}: (9, {})} | custom-call | flops 4194304 | bytes 1048576 | tf_op jit(solution)/shard_map/pallas_call | solution.py:456
Async XLA Ops:
  3.0 24.8 %collective-permute-start.3 = (bf16[1104,128]{1,0:T(8,128)(2,1)S(1)}, bf16[1104,128]{1,0:T(8,128)(2,1)S(1)}, u32[]{:S(2)}, u32[]{:S(2)}) collective-permute-start(bf16[1104,128]{1,0:T(8,128)(2,1)S(1)} %get-tuple-element.51), channel_id=1, source_target_pairs={{0,12},{4,8},{8,0},{12,4},{1,13},{5,9},{9,1},{13,5},{2,14},{6,10},... | collective-permute-start | bytes 847880 | tf_op jit(solution)/shard_map/ppermute | solution.py:489
  6.1 21.7 %collective-permute-start.4 = (bf16[1088,128]{1,0:T(8,128)(2,1)S(1)}, bf16[1088,128]{1,0:T(8,128)(2,1)S(1)}, u32[]{:S(2)}, u32[]{:S(2)}) collective-permute-start(bf16[1088,128]{1,0:T(8,128)(2,1)S(1)} %shard_map.88), channel_id=1, source_target_pairs={{0,12},{4,8},{8,0},{12,4},{1,13},{5,9},{9,1},{13,5},{2,14},{6,10},... | collective-permute-start | bytes 835592 | tf_op jit(solution)/shard_map/ppermute | solution.py:489
  6.2 26.0 %collective-permute-start.1 = (bf16[1104,128]{1,0:T(8,128)(2,1)S(1)}, bf16[1104,128]{1,0:T(8,128)(2,1)S(1)}, u32[]{:S(2)}, u32[]{:S(2)}) collective-permute-start(bf16[1104,128]{1,0:T(8,128)(2,1)S(1)} %get-tuple-element.49), channel_id=1, source_target_pairs={{0,4},{4,0},{8,12},{12,8},{1,5},{5,1},{9,13},{13,9},{2,6},{6,2},{1... | collective-permute-start | bytes 847880 | tf_op jit(solution)/shard_map/ppermute | solution.py:489
  8.5 23.8 %collective-permute-start.2 = (bf16[1088,128]{1,0:T(8,128)(2,1)S(1)}, bf16[1088,128]{1,0:T(8,128)(2,1)S(1)}, u32[]{:S(2)}, u32[]{:S(2)}) collective-permute-start(bf16[1088,128]{1,0:T(8,128)(2,1)S(1)} %get-tuple-element.50), channel_id=1, source_target_pairs={{0,4},{4,0},{8,12},{12,8},{1,5},{5,1},{9,13},{13,9},{2,6},{6,2},{1... | collective-permute-start | bytes 835592 | tf_op jit(solution)/shard_map/ppermute | solution.py:489
  28.0 2.9 %collective-permute-start.5 = (bf16[1024,128]{1,0:T(8,128)(2,1)S(1)}, bf16[1024,128]{1,0:T(8,128)(2,1)S(1)}, u32[]{:S(2)}, u32[]{:S(2)}) collective-permute-start(bf16[1024,128]{1,0:T(8,128)(2,1)S(1)} %get-tuple-element.53.theirs), channel_id=1, source_target_pairs={{0,1},{1,0},{2,3},{3,2},{4,5},{5,4},{6,7},{7,6},{8,9},{9,8},{10,11... | collective-permute-start | bytes 786440 | tf_op jit(solution)/shard_map/ppermute | solution.py:493
  29.6 21.3 %collective-permute-start = (bf16[1104,128]{1,0:T(8,128)(2,1)S(1)}, bf16[1104,128]{1,0:T(8,128)(2,1)S(1)}, u32[]{:S(2)}, u32[]{:S(2)}) collective-permute-start(bf16[1104,128]{1,0:T(8,128)(2,1)S(1)} %get-tuple-element.48), channel_id=1, source_target_pairs={{0,8},{4,12},{8,4},{12,0},{1,9},{5,13},{9,5},{13,1},{2,10},{6,14},... | collective-permute-start | bytes 847880 | tf_op jit(solution)/shard_map/ppermute | solution.py:489
  30.8 7.7 %collective-permute-start.7 = (bf16[1024,128]{1,0:T(8,128)(2,1)S(1)}, bf16[1024,128]{1,0:T(8,128)(2,1)S(1)}, u32[]{:S(2)}, u32[]{:S(2)}) collective-permute-start(bf16[1024,128]{1,0:T(8,128)(2,1)S(1)} %get-tuple-element.64.theirs), channel_id=1, source_target_pairs={{0,1},{1,0},{2,3},{3,2},{4,5},{5,4},{6,7},{7,6},{8,9},{9,8},{10,11... | collective-permute-start | bytes 786440 | tf_op jit(solution)/shard_map/ppermute | solution.py:493
  32.5 7.3 %collective-permute-start.6 = (bf16[1024,128]{1,0:T(8,128)(2,1)S(1)}, bf16[1024,128]{1,0:T(8,128)(2,1)S(1)}, u32[]{:S(2)}, u32[]{:S(2)}) collective-permute-start(bf16[1024,128]{1,0:T(8,128)(2,1)S(1)} %get-tuple-element.62.theirs), channel_id=1, source_target_pairs={{0,1},{1,0},{2,3},{3,2},{4,5},{5,4},{6,7},{7,6},{8,9},{9,8},{10,11... | collective-permute-start | bytes 786440 | tf_op jit(solution)/shard_map/ppermute | solution.py:493
  33.0 20.9 %collective-permute-start.11 = (bf16[544,128]{1,0:T(8,128)(2,1)S(1)}, bf16[544,128]{1,0:T(8,128)(2,1)S(1)}, u32[]{:S(2)}, u32[]{:S(2)}) collective-permute-start(bf16[544,128]{1,0:T(8,128)(2,1)S(1)} %get-tuple-element.81), channel_id=1, source_target_pairs={{0,8},{4,12},{8,4},{12,0},{1,9},{5,13},{9,5},{13,1},{2,10},{6,14},... | collective-permute-start | bytes 417800 | tf_op jit(solution)/shard_map/ppermute | solution.py:489
  37.9 19.0 %collective-permute-start.10 = (bf16[544,128]{1,0:T(8,128)(2,1)S(1)}, bf16[544,128]{1,0:T(8,128)(2,1)S(1)}, u32[]{:S(2)}, u32[]{:S(2)}) collective-permute-start(bf16[544,128]{1,0:T(8,128)(2,1)S(1)} %get-tuple-element.80), channel_id=1, source_target_pairs={{0,8},{4,12},{8,4},{12,0},{1,9},{5,13},{9,5},{13,1},{2,10},{6,14},... | collective-permute-start | bytes 417800 | tf_op jit(solution)/shard_map/ppermute | solution.py:489
  51.0 1.9 %collective-permute-start.8 = (bf16[256,128]{1,0:T(8,128)(2,1)S(1)}, bf16[256,128]{1,0:T(8,128)(2,1)S(1)}, u32[]{:S(2)}, u32[]{:S(2)}) collective-permute-start(bf16[256,128]{1,0:T(8,128)(2,1)S(1)} %get-tuple-element.72.refs_2_), channel_id=1, source_target_pairs={{0,1},{1,0},{2,3},{3,2},{4,5},{5,4},{6,7},{7,6},{8,9},{9,8},{10,11... | collective-permute-start | bytes 196616 | tf_op jit(solution)/shard_map/ppermute | solution.py:493
  52.0 1.3 %collective-permute-start.9 = (bf16[256,128]{1,0:T(8,128)(2,1)S(1)}, bf16[256,128]{1,0:T(8,128)(2,1)S(1)}, u32[]{:S(2)}, u32[]{:S(2)}) collective-permute-start(bf16[256,128]{1,0:T(8,128)(2,1)S(1)} %get-tuple-element.73.refs_3_), channel_id=1, source_target_pairs={{0,1},{1,0},{2,3},{3,2},{4,5},{5,4},{6,7},{7,6},{8,9},{9,8},{10,11... | collective-permute-start | bytes 196616 | tf_op jit(solution)/shard_map/ppermute | solution.py:493
  53.9 2.9 %collective-permute-start.12 = (bf16[256,128]{1,0:T(8,128)(2,1)S(1)}, bf16[256,128]{1,0:T(8,128)(2,1)S(1)}, u32[]{:S(2)}, u32[]{:S(2)}) collective-permute-start(bf16[256,128]{1,0:T(8,128)(2,1)S(1)} %get-tuple-element.84.refs_0_), channel_id=1, source_target_pairs={{0,1},{1,0},{2,3},{3,2},{4,5},{5,4},{6,7},{7,6},{8,9},{9,8},{10,11... | collective-permute-start | bytes 196616 | tf_op jit(solution)/shard_map/ppermute | solution.py:493
  54.9 2.0 %collective-permute-start.13 = (bf16[256,128]{1,0:T(8,128)(2,1)S(1)}, bf16[256,128]{1,0:T(8,128)(2,1)S(1)}, u32[]{:S(2)}, u32[]{:S(2)}) collective-permute-start(bf16[256,128]{1,0:T(8,128)(2,1)S(1)} %get-tuple-element.85.refs_1_), channel_id=1, source_target_pairs={{0,1},{1,0},{2,3},{3,2},{4,5},{5,4},{6,7},{7,6},{8,9},{9,8},{10,11... | collective-permute-start | bytes 196616 | tf_op jit(solution)/shard_map/ppermute | solution.py:493
